TPU v7x, 32 devices: a whole 2x2x4 slice. The times are simulated.
32 devices in a mesh: lat: 4 (over y, core), lon: 8 (over z, x).
Axes of the slice: x: 2, y: 2, z: 4, core: 2. Of those that a mesh axis runs over, the one named last changes fastest.
Arguments:
- obs_feat: bfloat16 [64, 393216], P(None, ('lat', 'lon')), may hold values from -6 to 6
- obs_offset: bfloat16 [2, 393216], P(None, ('lat', 'lon')), may hold values from 0 to 8
- block_tile: int32 [3072, 1], P(('lat', 'lon')), may hold values from 0 to 31; in each aligned block of 96 rows (0 to 95, 96 to 191, ...) at most 6 rows name the same one
- block_patch: int32 [3072], P(('lat', 'lon')), may hold values from 0 to 23
- embed_weight: bfloat16 [64, 256], replicated, may hold values from -3 to 3
- grid_base: bfloat16 [128, 384, 256], P('lat', 'lon'), may hold values from -3 to 3
- norm_gain: float32 [256], replicated, may hold values from 0.5 to 1.5
- qkv_weight: bfloat16 [256, 768], replicated, may hold values from -1 to 1
- out_weight: bfloat16 [256, 256], replicated, may hold values from -0.375 to 0.375
- mlp_gain: float32 [256], replicated, may hold values from 0.5 to 1.5
- up_weight: bfloat16 [256, 1024], replicated, may hold values from -0.375 to 0.375
- down_weight: bfloat16 [1024, 256], replicated, may hold values from -0.1875 to 0.1875
- decode_weight: bfloat16 [256, 64], replicated, may hold values from -0.75 to 0.75
Outputs:
- grid_latent: bfloat16 [128, 384, 256], P('lat', 'lon')
- obs_out: bfloat16 [64, 393216], P(None, ('lat', 'lon'))
Inputs may be any that keep to these rules, and one draw needn't show every extreme that they name: `block_tile`: among the 96 blocks of one device, at most 6 name the same tile, a bound that some block reaches.
All inputs are finite; a program needn't handle non-finite values.
Results may differ from a plain program's by a relative error of at most 0.015.
Values may be sent and summed in bfloat16 or wider, within the bound.
No kernel may reach another device: no remote copies, remote signals or barrier semaphores. Data moves between devices by JAX's collectives and lax.ppermute only.
A program may use at most 192 MiB of HBM per device.

v0:
```python
import jax
import jax.numpy as jnp
from jax import lax
from jax.sharding import PartitionSpec as P

HEAD_DIM = 32
WIN = 8
PATCH = 8
BLK = 128


epsilon = 1e-05
spread_coef = 0.5


def with_halo(array, sides, width):
    for axis, dim in sides:
        size, length = (lax.axis_size(axis), array.shape[dim])
        up = [(i, (i + 1) % size) for i in range(size)]
        down = [(j, i) for i, j in up]
        last = lax.slice_in_dim(array, length - width, length, axis=dim)
        initial = lax.slice_in_dim(array, 0, width, axis=dim)
        before = lax.ppermute(last, axis, up)
        after = lax.ppermute(initial, axis, down)
        array = jnp.concatenate([before, array, after], axis=dim)
    return array


def normalize(values, gain_row):
    center = jnp.mean(values, axis=-1, keepdims=True)
    centered = values - center
    variance = jnp.mean(centered * centered, axis=-1, keepdims=True)
    return centered * lax.rsqrt(variance + epsilon) * gain_row


def patch_weights(offsets):
    cell_ids = jnp.arange(PATCH * PATCH, dtype=jnp.int32)
    row_center = (cell_ids // PATCH).astype(jnp.float32) + 0.5
    col_center = (cell_ids % PATCH).astype(jnp.float32) + 0.5
    row_gap = row_center[:, None, None] - offsets[0][None]
    col_gap = col_center[:, None, None] - offsets[1][None]
    return jnp.exp(-spread_coef * (row_gap * row_gap + col_gap * col_gap)).astype(jnp.bfloat16)


def weighted_mean(weights, values):
    numerator = jnp.einsum("cso,csf->fso", weights, values, preferred_element_type=jnp.float32)
    denominator = jnp.sum(weights.astype(jnp.float32), axis=0)
    return (numerator / denominator[None]).astype(jnp.bfloat16)


def local(
    obs_feat,
    obs_offset,
    block_tile,
    block_patch,
    embed_weight,
    grid_base,
    norm_gain,
    qkv_weight,
    out_weight,
    mlp_gain,
    up_weight,
    down_weight,
    decode_weight,
):
    lat_devices = lax.axis_size("lat")
    lon_devices = lax.axis_size("lon")
    devices = lat_devices * lon_devices
    feat_width, obs_count = obs_feat.shape
    blocks = obs_count // BLK
    capacity = max(2, 2 * blocks // devices)
    slot_total = devices * capacity
    tile_ids = block_tile[:, 0]
    hit_table = (tile_ids[:, None] == jnp.arange(devices, dtype=jnp.int32)[None, :]).astype(
        jnp.int32
    )
    earlier = jnp.cumsum(hit_table, axis=0) - hit_table
    slot_rank = jnp.sum(earlier * hit_table, axis=1)
    slot_index = tile_ids * capacity + slot_rank
    slot_source = (
        jnp.zeros((slot_total,), jnp.int32)
        .at[slot_index]
        .set(jnp.arange(1, blocks + 1, dtype=jnp.int32))
    )
    slot_live = slot_source > 0
    source_index = jnp.maximum(slot_source - 1, 0)
    feat_blocks = obs_feat.reshape(feat_width, blocks, BLK)
    own_offsets = obs_offset.reshape(2, blocks, BLK)
    tag_row = jnp.broadcast_to(
        (block_patch + 1).astype(jnp.bfloat16)[None, :, None], (1, blocks, BLK)
    )
    meta_blocks = jnp.concatenate([own_offsets, tag_row], axis=0)
    zero_value = jnp.zeros((), jnp.bfloat16)
    send_feat = jnp.where(
        slot_live[None, :, None], jnp.take(feat_blocks, source_index, axis=1), zero_value
    )
    send_meta = jnp.where(
        slot_live[None, :, None], jnp.take(meta_blocks, source_index, axis=1), zero_value
    )
    recv_feat, recv_meta = (
        lax.all_to_all(
            send_feat.reshape(feat_width, devices, capacity, BLK),
            ("lat", "lon"),
            split_axis=1,
            concat_axis=1,
            tiled=True,
        ),
        lax.all_to_all(
            send_meta.reshape(3, devices, capacity, BLK),
            ("lat", "lon"),
            split_axis=1,
            concat_axis=1,
            tiled=True,
        ),
    )
    recv_feat = recv_feat.reshape(feat_width, slot_total, BLK)
    recv_meta = recv_meta.reshape(3, slot_total, BLK)
    tile_rows, tile_cols, channels = grid_base.shape
    patch_rows = tile_rows // PATCH
    patch_cols = tile_cols // PATCH
    patch_total = patch_rows * patch_cols
    patch_ids = recv_meta[2, :, 0].astype(jnp.float32).astype(jnp.int32) - 1
    slot_weights = patch_weights(recv_meta[0:2].astype(jnp.float32))
    slot_sums = jnp.einsum(
        "cso,fso->scf", slot_weights, recv_feat, preferred_element_type=jnp.float32
    )
    slot_mass = jnp.sum(slot_weights.astype(jnp.float32), axis=2).T
    owner_table = (patch_ids[None, :] == jnp.arange(patch_total, dtype=jnp.int32)[:, None]).astype(
        jnp.float32
    )
    patch_sums = jnp.einsum("ps,scf->pcf", owner_table, slot_sums, precision=lax.Precision.HIGHEST)
    patch_mass = jnp.dot(owner_table, slot_mass, precision=lax.Precision.HIGHEST)
    encoded = (patch_sums / (1.0 + patch_mass[:, :, None])).astype(jnp.bfloat16)
    encoded = (
        encoded.reshape(patch_rows, patch_cols, PATCH, PATCH, feat_width)
        .transpose(0, 2, 1, 3, 4)
        .reshape(tile_rows * tile_cols, feat_width)
    )
    lifted = jnp.dot(encoded, embed_weight, preferred_element_type=jnp.float32)
    grid_start = (grid_base.reshape(-1, channels).astype(jnp.float32) + lifted).astype(jnp.bfloat16)
    normed = normalize(grid_start.astype(jnp.float32), norm_gain).astype(jnp.bfloat16)
    margin = WIN // 2
    ext_rows = tile_rows + 2 * margin
    ext_cols = tile_cols + 2 * margin
    packed_own = jnp.dot(normed, qkv_weight, preferred_element_type=jnp.float32).astype(
        jnp.bfloat16
    )
    packed = with_halo(
        packed_own.reshape(tile_rows, tile_cols, 3 * channels), (("lat", 0), ("lon", 1)), margin
    )
    win_rows = ext_rows // WIN
    win_cols = ext_cols // WIN
    head_count = channels // HEAD_DIM
    windows = packed.reshape(win_rows, WIN, win_cols, WIN, 3, head_count, HEAD_DIM)
    lat_cells = tile_rows * lat_devices
    global_row = lax.axis_index("lat") * tile_rows - margin + jnp.arange(ext_rows, dtype=jnp.int32)
    row_side = (
        (global_row >= 0).astype(jnp.int32) + (global_row >= lat_cells).astype(jnp.int32)
    ).reshape(win_rows, WIN)
    same_side = row_side[:, :, None] == row_side[:, None, :]
    scores = jnp.einsum(
        "aibjhd,akblhd->abhijkl",
        windows[..., 0, :, :],
        windows[..., 1, :, :],
        preferred_element_type=jnp.float32,
    ) * HEAD_DIM ** (-0.5)
    scores = jnp.where(same_side[:, None, None, :, None, :, None], scores, -1e30)
    scores = scores.reshape(win_rows, win_cols, head_count, WIN, WIN, WIN * WIN)
    row_top = jnp.max(scores, axis=-1, keepdims=True)
    raised = jnp.exp(scores - row_top)
    attn_probs = (raised / jnp.sum(raised, axis=-1, keepdims=True)).astype(jnp.bfloat16)
    attn_probs = attn_probs.reshape(win_rows, win_cols, head_count, WIN, WIN, WIN, WIN)
    attended = jnp.einsum(
        "abhijkl,akblhd->aibjhd",
        attn_probs,
        windows[..., 2, :, :],
        preferred_element_type=jnp.float32,
    ).astype(jnp.bfloat16)
    attended = attended.reshape(ext_rows, ext_cols, channels)
    attended = attended[margin : margin + tile_rows, margin : margin + tile_cols].reshape(
        -1, channels
    )
    residual = grid_start.astype(jnp.float32) + jnp.dot(
        attended, out_weight, preferred_element_type=jnp.float32
    )
    normed_mlp = normalize(residual, mlp_gain).astype(jnp.bfloat16)
    hidden = jax.nn.gelu(jnp.dot(normed_mlp, up_weight, preferred_element_type=jnp.float32)).astype(
        jnp.bfloat16
    )
    latent = (residual + jnp.dot(hidden, down_weight, preferred_element_type=jnp.float32)).astype(
        jnp.bfloat16
    )
    projected = jnp.dot(latent, decode_weight, preferred_element_type=jnp.float32).astype(
        jnp.bfloat16
    )
    patch_values = (
        projected.reshape(patch_rows, PATCH, patch_cols, PATCH, feat_width)
        .transpose(1, 3, 0, 2, 4)
        .reshape(PATCH * PATCH, patch_total, feat_width)
    )
    slot_values = jnp.take(patch_values, jnp.clip(patch_ids, 0, patch_total - 1), axis=1)
    inner_a = slot_values.shape[0]
    inner_b = slot_values.shape[2]
    back_blocks = lax.all_to_all(
        slot_values.reshape(inner_a, devices, capacity, inner_b),
        ("lat", "lon"),
        split_axis=1,
        concat_axis=1,
        tiled=True,
    )
    returned = jnp.take(back_blocks.reshape(inner_a, slot_total, inner_b), slot_index, axis=1)
    own_weights = patch_weights(own_offsets.astype(jnp.float32))
    returned = weighted_mean(own_weights, returned)
    obs_out = returned.reshape(feat_width, obs_count)
    return (latent.reshape(tile_rows, tile_cols, channels), obs_out)


def solution(mesh):
    placed = (
        P(None, ("lat", "lon")),
        P(None, ("lat", "lon")),
        P(("lat", "lon"), None),
        P(("lat", "lon")),
        P(),
        P("lat", "lon", None),
        P(),
        P(),
        P(),
        P(),
        P(),
        P(),
        P(),
    )
    return jax.shard_map(
        local,
        mesh=mesh,
        in_specs=placed,
        out_specs=(P("lat", "lon", None), P(None, ("lat", "lon"))),
        check_vma=False,
    )
```

profile of v0, /device:TPU:0, one launch (start us, length us, event | category | flops | bytes accessed | tf_op | source)
XLA Modules:
  0.0 345.1 jit_solution(14295580401112757698)
XLA Ops:
  8.4 7.3 %all-to-all-start = ((bf16[3,32,6,128]{3,2,0,1:T(8,128)(2,1)}), bf16[3,32,6,128]{3,2,0,1:T(8,128)(2,1)S(1)}, u32[]{:S(2)}, u32[]{:S(2)}) async-start(bf16[3,32,6,128]{3,2,0,1:T(8,128)(2,1)} %copy.46), calls=%async_computation | async-start | bytes 393216 | tf_op jit(solution)/shard_map/all_to_all | solution.py:108
  18.9 3.4 select_select_fusion
  24.2 4.1 %all-to-all-start.1 = ((bf16[64,32,6,128]{3,0,2,1:T(8,128)(2,1)}), bf16[64,32,6,128]{3,0,2,1:T(8,128)(2,1)}, u32[]{:S(2)}, u32[]{:S(2)}) async-start(bf16[64,32,6,128]{3,0,2,1:T(8,128)(2,1)} %select_select_fusion), calls=%async_computation.1 | async-start | bytes 6291456 | tf_op jit(solution)/shard_map/all_to_all | solution.py:101
  31.0 69.8 %all-to-all-done.1 = bf16[64,32,6,128]{3,0,2,1:T(8,128)(2,1)} async-done(((bf16[64,32,6,128]{3,0,2,1:T(8,128)(2,1)}), bf16[64,32,6,128]{3,0,2,1:T(8,128)(2,1)}, u32[]{:S(2)}, u32[]{:S(2)}) %all-to-all-start.1) | async-done | bytes 3145760 | tf_op jit(solution)/shard_map/all_to_all | solution.py:101
  100.9 3.8 %fusion.15 = f32[192,64,64]{2,1,0:T(8,128)S(1)} fusion(bf16[64,192,128]{2,0,1:T(8,128)(2,1)} %bitcast.10, f32[192,128]{1,0:T(8,128)S(1)} %sub.120, f32[64]{0:T(128)S(1)} %get-tuple-element.25, f32[192,128]{1,0:T(8,128)S(1)} %sub.116, f32[64]{0:T(128)S(1)} %get-tuple-element.26), kind=kOutput, calls=%fused_computation.40 | convolution fusion | flops 212336640 | bytes 6488576 | tf_op jit(solution)/shard_map/cso,fso->scf/dot_general | solution.py:124
  104.7 5.7 %fusion.28 = bf16[24,64,64]{2,0,1:T(8,128)(2,1)S(1)} fusion(f32[192,64,64]{2,1,0:T(8,128)S(1)} %fusion.15, f32[24,64]{0,1:T(8,128)S(1)} %copy.50, s32[192]{0:T(256)S(1)} %get-tuple-element.3), kind=kOutput, calls=%fused_computation.56 | convolution fusion | flops 226693632 | bytes 3349248 | tf_op jit(solution)/shard_map/ps,scf->pcf/dot_general | solution.py:131
  114.9 6.7 %collective-permute-done = bf16[4,48,768]{2,1,0:T(8,128)(2,1)S(1)} collective-permute-done((bf16[4,48,768]{2,1,0:T(8,128)(2,1)S(1)}, bf16[4,48,768]{2,1,0:T(8,128)(2,1)S(1)}, u32[]{:S(2)}, u32[]{:S(2)}) %collective-permute-start) | collective-permute-done | bytes 294944 | tf_op jit(solution)/shard_map/ppermute | solution.py:23
  121.8 4.7 %collective-permute-start.3 = (bf16[40,4,768]{2,1,0:T(4,128)(2,1)S(1)}, bf16[40,4,768]{2,1,0:T(4,128)(2,1)S(1)}, u32[]{:S(2)}, u32[]{:S(2)}) collective-permute-start(bf16[40,4,768]{2,1,0:T(4,128)(2,1)S(1)} %get-tuple-element.10), channel_id=1, source_target_pairs={{1,0},{2,1},{3,2},{4,3},{5,4},{6,5},{7,6},{0,7},{9,8},{10,9},{11,1... | collective-permute-start | bytes 737288 | tf_op jit(solution)/shard_map/ppermute | solution.py:24
  127.8 5.6 %collective-permute-done.2 = bf16[40,4,768]{2,1,0:T(4,128)(2,1)S(1)} collective-permute-done((bf16[40,4,768]{2,1,0:T(4,128)(2,1)S(1)}, bf16[40,4,768]{2,1,0:T(4,128)(2,1)S(1)}, u32[]{:S(2)}, u32[]{:S(2)}) %collective-permute-start.2) | collective-permute-done | bytes 245792 | tf_op jit(solution)/shard_map/ppermute | solution.py:23
  135.6 4.7 %pad_maximum_fusion = bf16[40,56,768]{2,1,0:T(8,128)(2,1)} fusion(bf16[40,4,768]{2,1,0:T(4,128)(2,1)S(1)} %collective-permute-done.3, bf16[4,48,768]{2,1,0:T(8,128)(2,1)S(1)} %collective-permute-done.1, bf16[32,48,768]{2,1,0:T(8,128)(2,1)} %bitcast.114, bf16[4,48,768]{2,1,0:T(8,128)(2,1)S(1)} %collective-permute-done, ...), kind=kLoop, calls=%fused_computation.30 | loop fusion | flops 17203200 | bytes 6881280 | tf_op jit(solution)/shard_map/concatenate | solution.py:25
  140.4 16.2 %reshape.241 = bf16[5,8,7,8,3,8,32]{6,5,4,3,2,1,0:T(8,128)(2,1)} reshape(bf16[40,56,768]{2,1,0:T(8,128)(2,1)} %pad_maximum_fusion) | data formatting | bytes 6881280 | tf_op jit(solution)/shard_map/reshape | solution.py:154
  156.6 10.8 %fusion.65 = (bf16[5,8,7,8,1,8,32]{6,5,4,3,2,1,0:T(8,128)(2,1)}, bf16[5,8,7,8,1,8,32]{6,5,4,3,2,1,0:T(8,128)(2,1)}, bf16[5,8,7,8,1,8,32]{6,5,4,3,2,1,0:T(8,128)(2,1)}) fusion(bf16[5,8,7,8,3,8,32]{6,5,4,3,2,1,0:T(8,128)(2,1)} %reshape.241), kind=kLoop, calls=%fused_computation.126 | loop fusion | bytes 6881280 | tf_op jit(solution)/shard_map/slice | solution.py:176
  167.4 36.1 %fusion = (f32[5,7,8,8,8]{4,3,2,1,0:T(8,128)S(1)}, f32[5,7,8,8,8,8,8]{4,6,5,3,2,1,0:T(8,128)}) fusion(pred[5,8,8]{2,1,0:T(8,128)(4,1)S(1)} %broadcast_compare_fusion, bf16[5,8,7,8,1,8,32]{6,5,4,3,2,1,0:T(8,128)(2,1)} %get-tuple-element.8, bf16[5,8,7,8,1,8,32]{6,5,4,3,2,1,0:T(8,128)(2,1)} %get-tuple-element.7), kind=kOutput, calls=%fused_computation.8 | convolution fusion | flops 76823040 | bytes 6953280 | tf_op jit(solution)/shard_map/aibjhd,akblhd->abhijkl/dot_general | solution.py:161
  203.5 24.0 %fusion.1 = f32[5,7,8,8,8]{4,3,2,1,0:T(8,128)S(1)} fusion(f32[5,7,8,8,8,8,8]{4,6,5,3,2,1,0:T(8,128)} %get-tuple-element.22, f32[5,7,8,8,8]{4,3,2,1,0:T(8,128)S(1)} %get-tuple-element.21, pred[5,8,8]{2,1,0:T(8,128)(4,1)S(1)} %broadcast_compare_fusion), kind=kLoop, calls=%fused_computation.9 | loop fusion | flops 4569600 | bytes 4731200 | tf_op jit(solution)/shard_map/reduce_sum | solution.py:171
  227.6 31.1 %fusion.13 = bf16[5,8,7,8,8,32]{5,3,1,4,2,0:T(8,128)(2,1)} fusion(f32[5,7,8,8,8,8,8]{4,6,5,3,2,1,0:T(8,128)} %get-tuple-element.22, f32[5,7,8,8,8]{4,3,2,1,0:T(8,128)S(1)} %fusion.1, f32[5,7,8,8,8]{4,3,2,1,0:T(8,128)S(1)} %get-tuple-element.21, pred[5,8,8]{2,1,0:T(8,128)(4,1)S(1)} %broadcast_compare_fusion, ...), kind=kOutput, calls=%fused_computation.25 | convolution fusion | flops 79708160 | bytes 7024960 | tf_op jit(solution)/shard_map/abhijkl,akblhd->aibjhd/dot_general | solution.py:173
  258.6 9.7 %copy.57 = bf16[5,8,7,8,8,32]{5,4,3,2,1,0:T(8,128)(2,1)} copy(bf16[5,8,7,8,8,32]{5,3,1,4,2,0:T(8,128)(2,1)} %fusion.13) | data formatting | bytes 2293760 | tf_op jit(solution)/shard_map/convert_element_type | solution.py:178
  268.3 6.0 %reshape.242 = bf16[40,56,256]{2,1,0:T(8,128)(2,1)S(1)} reshape(bf16[5,8,7,8,8,32]{5,4,3,2,1,0:T(8,128)(2,1)} %copy.57) | data formatting | bytes 2293760 | tf_op jit(solution)/shard_map/reshape | solution.py:179
  275.8 3.7 %fusion.16 = bf16[1536,256]{1,0:T(8,128)(2,1)S(1)} fusion(f32[1536,256]{1,0:T(8,128)S(1)} %get-tuple-element.24, bf16[1024,256]{1,0:T(8,128)(2,1)} %param.24, bf16[256,1024]{1,0:T(8,128)(2,1)} %param.23, f32[256]{0:T(256)S(1)} %copy-done.17, f32[1536]{0:T(1024)S(1)} %add_rsqrt_fusion, f32[1536]{0:T(1024)S(1)} %broadcast_multiply_fusion), kind=kOutput, calls=%fused_computation.41 | convolution fusion | flops 1627127808 | bytes 3421184 | tf_op jit(solution)/shard_map/dot_general | solution.py:190
  281.1 2.8 gather_fusion.2
  284.0 3.3 fusion.71
  287.3 6.2 %reshape.302 = bf16[32,2,12288]{2,1,0:T(2,128)(2,1)} reshape(bf16[32,6,64,64]{3,2,1,0:T(8,128)(2,1)} %fusion.71) | data formatting | bytes 3145728
  293.5 3.1 all-to-all-start.2
  298.0 37.4 %all-to-all-done.2 = bf16[32,2,12288]{2,1,0:T(2,128)(2,1)S(1)} async-done(((bf16[32,2,12288]{2,1,0:T(2,128)(2,1)}), bf16[32,2,12288]{2,1,0:T(2,128)(2,1)S(1)}, u32[]{:S(2)}, u32[]{:S(2)}) %all-to-all-start.2) | async-done | bytes 1572896 | tf_op jit(solution)/shard_map/all_to_all | solution.py:204
  335.5 3.3 reshape.303
  (110 shorter events, 34.0 us)
Async XLA Ops:
  0.6 15.1 %copy-start = (bf16[64,12288]{1,0:T(8,128)(2,1)S(1)}, bf16[64,12288]{1,0:T(8,128)(2,1)}, u32[]{:S(2)}) copy-start(bf16[64,12288]{1,0:T(8,128)(2,1)} %param.13) | copy-start | bytes 4718596
  8.4 15.9 %all-to-all-start = ((bf16[3,32,6,128]{3,2,0,1:T(8,128)(2,1)}), bf16[3,32,6,128]{3,2,0,1:T(8,128)(2,1)S(1)}, u32[]{:S(2)}, u32[]{:S(2)}) async-start(bf16[3,32,6,128]{3,2,0,1:T(8,128)(2,1)} %copy.46), calls=%async_computation | async-start | bytes 393216 | tf_op jit(solution)/shard_map/all_to_all | solution.py:108
  24.2 76.6 %all-to-all-start.1 = ((bf16[64,32,6,128]{3,0,2,1:T(8,128)(2,1)}), bf16[64,32,6,128]{3,0,2,1:T(8,128)(2,1)}, u32[]{:S(2)}, u32[]{:S(2)}) async-start(bf16[64,32,6,128]{3,0,2,1:T(8,128)(2,1)} %select_select_fusion), calls=%async_computation.1 | async-start | bytes 6291456 | tf_op jit(solution)/shard_map/all_to_all | solution.py:101
  28.4 76.3 %copy-start.18 = (f32[64]{0:T(128)}, f32[64]{0:T(128)S(1)}, u32[]{:S(2)}) copy-start(f32[64]{0:T(128)S(1)} %get-tuple-element.25) | copy-start | bytes 772
  28.4 76.3 %copy-start.20 = (f32[64]{0:T(128)}, f32[64]{0:T(128)S(1)}, u32[]{:S(2)}) copy-start(f32[64]{0:T(128)S(1)} %get-tuple-element.26) | copy-start | bytes 772
  104.7 5.9 %copy-start.5 = (bf16[32,48,256]{2,1,0:T(8,128)(2,1)S(1)}, bf16[32,48,256]{2,1,0:T(8,128)(2,1)}, u32[]{:S(2)}) copy-start(bf16[32,48,256]{2,1,0:T(8,128)(2,1)} %param.18) | copy-start | bytes 2359300
  104.7 5.9 %copy-start.10 = (bf16[64,256]{1,0:T(8,128)(2,1)S(1)}, bf16[64,256]{1,0:T(8,128)(2,1)}, u32[]{:S(2)}) copy-start(bf16[64,256]{1,0:T(8,128)(2,1)} %param.17) | copy-start | bytes 98308
  111.1 1.9 copy-start.2
  112.9 8.6 %copy-start.4 = (bf16[1536,768]{1,0:T(8,128)(2,1)}, bf16[1536,768]{1,0:T(8,128)(2,1)S(1)}, u32[]{:S(2)}) copy-start(bf16[1536,768]{1,0:T(8,128)(2,1)S(1)} %convolution_convert_fusion) | copy-start | bytes 7077892
  113.0 8.5 %collective-permute-start = (bf16[4,48,768]{2,1,0:T(8,128)(2,1)S(1)}, bf16[4,48,768]{2,1,0:T(8,128)(2,1)S(1)}, u32[]{:S(2)}, u32[]{:S(2)}) collective-permute-start(bf16[4,48,768]{2,1,0:T(8,128)(2,1)S(1)} %bitcast.127), channel_id=1, source_target_pairs={{0,8},{8,16},{16,24},{24,0},{1,9},{9,17},{17,25},{25,1},{2,10},{10... | collective-permute-start | bytes 884744 | tf_op jit(solution)/shard_map/ppermute | solution.py:23
  113.1 8.5 %collective-permute-start.1 = (bf16[4,48,768]{2,1,0:T(8,128)(2,1)S(1)}, bf16[4,48,768]{2,1,0:T(8,128)(2,1)S(1)}, u32[]{:S(2)}, u32[]{:S(2)}) collective-permute-start(bf16[4,48,768]{2,1,0:T(8,128)(2,1)S(1)} %bitcast.126), channel_id=1, source_target_pairs={{8,0},{16,8},{24,16},{0,24},{9,1},{17,9},{25,17},{1,25},{10,2},{18... | collective-permute-start | bytes 884744 | tf_op jit(solution)/shard_map/ppermute | solution.py:24
  121.8 11.7 %collective-permute-start.2 = (bf16[40,4,768]{2,1,0:T(4,128)(2,1)S(1)}, bf16[40,4,768]{2,1,0:T(4,128)(2,1)S(1)}, u32[]{:S(2)}, u32[]{:S(2)}) collective-permute-start(bf16[40,4,768]{2,1,0:T(4,128)(2,1)S(1)} %get-tuple-element.9), channel_id=1, source_target_pairs={{0,1},{1,2},{2,3},{3,4},{4,5},{5,6},{6,7},{7,0},{8,9},{9,10},{10,1... | collective-permute-start | bytes 737288 | tf_op jit(solution)/shard_map/ppermute | solution.py:23
  121.8 13.8 %collective-permute-start.3 = (bf16[40,4,768]{2,1,0:T(4,128)(2,1)S(1)}, bf16[40,4,768]{2,1,0:T(4,128)(2,1)S(1)}, u32[]{:S(2)}, u32[]{:S(2)}) collective-permute-start(bf16[40,4,768]{2,1,0:T(4,128)(2,1)S(1)} %get-tuple-element.10), channel_id=1, source_target_pairs={{1,0},{2,1},{3,2},{4,3},{5,4},{6,5},{7,6},{0,7},{9,8},{10,9},{11,1... | collective-permute-start | bytes 737288 | tf_op jit(solution)/shard_map/ppermute | solution.py:24
  268.3 6.4 %copy-start.3 = (f32[1536,256]{1,0:T(8,128)S(1)}, f32[1536,256]{1,0:T(8,128)}, u32[]{:S(2)}) copy-start(f32[1536,256]{1,0:T(8,128)} %copy-done.2) | copy-start | bytes 4718596
  268.3 6.5 %copy-start.9 = (bf16[256,256]{1,0:T(8,128)(2,1)S(1)}, bf16[256,256]{1,0:T(8,128)(2,1)}, u32[]{:S(2)}) copy-start(bf16[256,256]{1,0:T(8,128)(2,1)} %param.21) | copy-start | bytes 393220
  275.8 4.6 %copy-start.11 = (bf16[256,64]{0,1:T(8,128)(2,1)S(1)}, bf16[256,64]{0,1:T(8,128)(2,1)}, u32[]{:S(2)}) copy-start(bf16[256,64]{0,1:T(8,128)(2,1)} %param.25) | copy-start | bytes 98308
  281.1 2.9 copy-start.12
  287.3 9.3 %copy-start.14 = (s32[96,1]{0,1:T(1,128)S(1)}, s32[96,1]{0,1:T(1,128)}, u32[]{:S(2)}) copy-start(s32[96,1]{0,1:T(1,128)} %copy-done.13) | copy-start | bytes 1156
  287.3 9.4 %copy-start.8 = (bf16[2,12288]{1,0:T(2,128)(2,1)S(1)}, bf16[2,12288]{1,0:T(2,128)(2,1)}, u32[]{:S(2)}) copy-start(bf16[2,12288]{1,0:T(2,128)(2,1)} %param.14) | copy-start | bytes 147460
  287.3 9.5 %copy-start.19 = (f32[64]{0:T(128)S(1)}, f32[64]{0:T(128)}, u32[]{:S(2)}) copy-start(f32[64]{0:T(128)} %copy-done.18) | copy-start | bytes 772
  287.3 9.5 %copy-start.21 = (f32[64]{0:T(128)S(1)}, f32[64]{0:T(128)}, u32[]{:S(2)}) copy-start(f32[64]{0:T(128)} %copy-done.20) | copy-start | bytes 772
  293.5 41.9 %all-to-all-start.2 = ((bf16[32,2,12288]{2,1,0:T(2,128)(2,1)}), bf16[32,2,12288]{2,1,0:T(2,128)(2,1)S(1)}, u32[]{:S(2)}, u32[]{:S(2)}) async-start(bf16[32,2,12288]{2,1,0:T(2,128)(2,1)} %reshape.302), calls=%async_computation.2 | async-start | bytes 3145728 | tf_op jit(solution)/shard_map/all_to_all | solution.py:204
  298.0 43.5 %copy-start.16 = (pred[96]{0:T(512)(128)(4,1)S(1)}, pred[96]{0:T(512)(128)(4,1)}, u32[]{:S(2)}) copy-start(pred[96]{0:T(512)(128)(4,1)} %get-tuple-element.4) | copy-start | bytes 292
  341.5 3.4 copy-start.1
  (5 other events, 5.2 us)
where the time goes:
time: 349 us; the launch traced here: 345 us
  waiting for transfers between devices  124 us (36%)
  matrix products  85.1 us (24%)
  local copies, waits for them, and re-layouts  67.6 us (19%)
  other arithmetic  46.2 us (13%)
  starting transfers between devices  21.1 us (6%)
    all_to_all x1, waiting for transfers between devices, local(): lax.all_to_all(send_feat.reshape(feat_width, devices, capacity, BLK), ('l...  69.8 us
    all_to_all x1, waiting for transfers between devices, local(): lax.all_to_all(slot_values.reshape(inner_a, devices, capacity, inner_b),...  37.4 us
    dot_general x1, matrix products, local(): jnp.einsum('aibjhd,akblhd->abhijkl', windows[..., 0, :, :], windows[...,...  36.1 us
    dot_general x1, matrix products, local(): jnp.einsum('abhijkl,akblhd->aibjhd', attn_probs, windows[..., 2, :, :], p...  31.1 us
    reduce_sum x1, other arithmetic, local(): jnp.sum(raised, axis=-1, keepdims=True)  24 us
    reshape x1, local copies, waits for them, and re-layouts, local(): packed.reshape(win_rows, WIN, win_cols, WIN, 3, head_count, HEAD_DIM)  16.2 us
    ppermute x2, waiting for transfers between devices, with_halo(): before = lax.ppermute(last, axis, up)  12.2 us
    slice x1, local copies, waits for them, and re-layouts, local(): windows[..., 2, :, :]  10.8 us
  transfers between devices with their start and end apart: 7, of which 6 were waited for; matrix products, arithmetic and copies ran while one was open for 3% of the time, Pallas kernels for 0%

commit v1 on v0

v1 whole, which is shorter than its diff:
```python
import jax
import jax.numpy as jnp
from jax import lax
from jax.experimental import pallas as pl
from jax.experimental.pallas import tpu as pltpu
from jax.sharding import PartitionSpec as P

HEAD_DIM = 32
WIN = 8
PATCH = 8
BLK = 128
CELLS = PATCH * PATCH
LANES = 2 * CELLS

epsilon = 1e-05
spread_coef = 0.5

NT = (((1,), (1,)), ((), ()))
TN = (((0,), (0,)), ((), ()))


def params(**extra):
    return pltpu.CompilerParams(vmem_limit_bytes=56 * 1024 * 1024, **extra)


def vmem():
    return pl.BlockSpec(memory_space=pltpu.VMEM)


def smem():
    return pl.BlockSpec(memory_space=pltpu.SMEM)


def normalize(values, gain_row):
    center = jnp.mean(values, axis=-1, keepdims=True)
    centered = values - center
    variance = jnp.mean(centered * centered, axis=-1, keepdims=True)
    return centered * lax.rsqrt(variance + epsilon) * gain_row


def block_weights(offsets):
    axis_id = lax.broadcasted_iota(jnp.int32, (PATCH, BLK), 0).astype(jnp.float32) + 0.5
    row_gap = axis_id - offsets[0:1]
    col_gap = axis_id - offsets[1:2]
    row_gap = row_gap * row_gap
    col_gap = col_gap * col_gap
    total = row_gap[:, None, :] + col_gap[None, :, :]
    return jnp.exp(-spread_coef * total).reshape(CELLS, BLK).astype(jnp.bfloat16)


def meta_rows(pairs):
    return -(-3 * pairs // 16) * 16


def encode_blocks(capacity, devices, tile_ref, patch_ref, feat_ref, offset_ref, send_ref, slot_ref, count_ref):
    blocks = feat_ref.shape[1] // BLK
    feat_width = feat_ref.shape[0]
    pairs = capacity // 2
    meta = meta_rows(pairs)
    chunk = pairs * feat_width + meta
    send_ref[...] = jnp.zeros_like(send_ref)

    def clear(t, _):
        count_ref[t] = 0
        return 0

    lax.fori_loop(0, devices, clear, 0)
    lane_half = lax.broadcasted_iota(jnp.int32, (feat_width, LANES), 1) // CELLS
    meta_half = lax.broadcasted_iota(jnp.int32, (meta, LANES), 1) // CELLS
    meta_row = lax.broadcasted_iota(jnp.int32, (meta, LANES), 0)
    ones = jnp.ones((16, BLK), jnp.bfloat16)

    def one(b):
        tile = tile_ref[b]
        rank = count_ref[tile]
        count_ref[tile] = rank + 1
        slot_ref[b] = tile * capacity + rank
        pair = rank // 2
        half = rank % 2
        col = pl.multiple_of(b * BLK, BLK)
        feat = jnp.concatenate([feat_ref[:, pl.ds(col, BLK)], ones], axis=0)
        weights = block_weights(offset_ref[:, pl.ds(col, BLK)].astype(jnp.float32))
        twice = jnp.concatenate([weights, weights], axis=0)
        sums = lax.dot_general(feat, twice, NT, preferred_element_type=jnp.float32)
        row = pl.multiple_of(tile * chunk + pair * feat_width, 16)
        old = send_ref[pl.ds(row, feat_width), :].astype(jnp.float32)
        send_ref[pl.ds(row, feat_width), :] = jnp.where(
            lane_half == half, sums[:feat_width], old
        ).astype(jnp.bfloat16)
        mass = sums[feat_width : feat_width + 1]
        high = mass.astype(jnp.bfloat16).astype(jnp.float32)
        low = mass - high
        tag = (patch_ref[b] + 1).astype(jnp.float32)
        row = pl.multiple_of(tile * chunk + pairs * feat_width, 16)
        old = send_ref[pl.ds(row, meta), :].astype(jnp.float32)
        new = jnp.where(
            meta_row == pair,
            high,
            jnp.where(
                meta_row == pairs + pair, low, jnp.where(meta_row == 2 * pairs + pair, tag, old)
            ),
        )
        send_ref[pl.ds(row, meta), :] = jnp.where(meta_half == half, new, old).astype(jnp.bfloat16)

    unroll = 4 if blocks % 4 == 0 else 1

    def body(i, _):
        for u in range(unroll):
            one(i * unroll + u)
        return 0

    lax.fori_loop(0, blocks // unroll, body, 0)


def start_tile(capacity, devices, id_ref, recv_ref, embed_ref, base_ref, start_ref, acc_ref):
    feat_width, channels = embed_ref.shape
    tile_rows, tile_cols, _ = base_ref.shape
    pairs = capacity // 2
    meta = meta_rows(pairs)
    chunk = pairs * feat_width + meta
    patch_rows, patch_cols = tile_rows // PATCH, tile_cols // PATCH
    acc_ref[...] = jnp.zeros_like(acc_ref)
    first = lax.broadcasted_iota(jnp.int32, (feat_width + 8, LANES), 1) < CELLS

    def gather(d, _):
        base = pl.multiple_of(d * chunk, 16)
        tags = recv_ref[pl.ds(base + pairs * feat_width, meta), :].astype(jnp.float32)
        for k in range(pairs):
            sums = recv_ref[pl.ds(base + k * feat_width, feat_width), :].astype(jnp.float32)
            mass = tags[k : k + 1] + tags[pairs + k : pairs + k + 1]
            both = jnp.concatenate([sums, jnp.broadcast_to(mass, (8, LANES))], axis=0)
            slot = d * capacity + 2 * k
            a = id_ref[slot]
            acc_ref[a] += jnp.where(first, both, 0.0)
            b = id_ref[slot + 1]
            acc_ref[b] += jnp.where(first, 0.0, both)
        return 0

    lax.fori_loop(0, devices, gather, 0)
    head = lax.broadcasted_iota(jnp.int32, (feat_width, LANES), 1) < CELLS
    embed = embed_ref[...]

    def encoded(p):
        total = acc_ref[p]
        total = total + pltpu.roll(total, CELLS, 1)
        return total[:feat_width] / (1.0 + total[feat_width : feat_width + 1])

    def lift(pr, _):
        parts = []
        for pc in range(0, patch_cols, 2):
            p = pr * patch_cols + pc
            pair = jnp.where(head, encoded(p), encoded(p + 1)).astype(jnp.bfloat16)
            parts.append(lax.dot_general(pair, embed, TN, preferred_element_type=jnp.float32))
        lifted = jnp.concatenate(parts, axis=0).reshape(patch_cols, PATCH, PATCH, channels)
        lifted = lifted.transpose(1, 0, 2, 3).reshape(PATCH, tile_cols, channels)
        rows = pl.ds(pr * PATCH, PATCH)
        start_ref[rows] = (base_ref[rows].astype(jnp.float32) + lifted).astype(jnp.bfloat16)
        return 0

    lax.fori_loop(0, patch_rows, lift, 0)


def grid_block(
    capacity, devices, lat_cells, place_ref, id_ref, ext_ref, norm_ref, qkv_ref, out_ref, mlp_ref,
    up_ref, down_ref, decode_ref, latent_ref, back_ref, packed_ref, att_ref, proj_ref,
):
    ext_rows, ext_cols, channels = ext_ref.shape
    tile_rows, tile_cols, _ = latent_ref.shape
    margin = WIN // 2
    win_rows, win_cols = ext_rows // WIN, ext_cols // WIN
    patch_rows, patch_cols = tile_rows // PATCH, tile_cols // PATCH
    tokens = WIN * WIN
    group = 128
    heads = group // HEAD_DIM
    feat_width = decode_ref.shape[0]
    pairs = capacity // 2
    scale = HEAD_DIM ** (-0.5)
    norm_gain = norm_ref[...]
    head_of = lax.broadcasted_iota(jnp.int32, (tokens, group), 1) // HEAD_DIM
    key_row = lax.broadcasted_iota(jnp.int32, (tokens, heads * tokens), 0) // WIN
    query_row = lax.broadcasted_iota(jnp.int32, (tokens, heads * tokens), 1) % tokens // WIN

    def attend(wr, _):
        rows = pl.ds(wr * WIN, WIN)
        cells = ext_ref[rows].reshape(WIN, win_cols, WIN, channels).transpose(1, 0, 2, 3)
        normed = normalize(cells.reshape(win_cols * tokens, channels), norm_gain)
        packed_ref[...] = jnp.dot(
            normed.astype(jnp.bfloat16), qkv_ref[...], preferred_element_type=jnp.float32
        ).astype(jnp.bfloat16)
        top = place_ref[0] * tile_rows - margin + wr * WIN
        side = lambda r: (r >= 0).astype(jnp.int32) + (r >= lat_cells).astype(jnp.int32)
        bias = jnp.where(side(top + key_row) == side(top + query_row), 0.0, -1e30)
        for w in range(win_cols):
            span = slice(w * tokens, (w + 1) * tokens)
            for g in range(channels // group):
                at = lambda i: slice(i * channels + g * group, i * channels + (g + 1) * group)
                query = packed_ref[span, at(0)]
                key = packed_ref[span, at(1)]
                value = packed_ref[span, at(2)]
                stack = jnp.concatenate(
                    [jnp.where(head_of == h, query, jnp.zeros_like(query)) for h in range(heads)],
                    axis=0,
                )
                scores = lax.dot_general(key, stack, NT, preferred_element_type=jnp.float32)
                scores = scores + bias
                peak = jnp.max(scores, axis=0, keepdims=True)
                raised = jnp.exp((scores - peak) * scale)
                total = jnp.sum(raised, axis=0, keepdims=True)
                probs = (raised * (1.0 / total)).astype(jnp.bfloat16)
                mixed = lax.dot_general(probs, value, TN, preferred_element_type=jnp.float32)
                picked = mixed[:tokens]
                for h in range(1, heads):
                    picked = jnp.where(head_of == h, mixed[h * tokens : (h + 1) * tokens], picked)
                att_ref[rows, w * WIN : (w + 1) * WIN, g * group : (g + 1) * group] = picked.reshape(
                    WIN, WIN, group
                )
        return 0

    lax.fori_loop(0, win_rows, attend, 0)
    mlp_gain = mlp_ref[...]

    def by_patch(values):
        values = values.reshape(PATCH, patch_cols, PATCH, channels).transpose(1, 0, 2, 3)
        return values.reshape(patch_cols * CELLS, channels)

    def finish(pr, _):
        rows = pl.ds(margin + pr * PATCH, PATCH)
        attended = by_patch(att_ref[rows, margin : margin + tile_cols, :]).astype(jnp.bfloat16)
        begun = by_patch(ext_ref[rows, margin : margin + tile_cols, :])
        residual = begun + jnp.dot(attended, out_ref[...], preferred_element_type=jnp.float32)
        normed = normalize(residual, mlp_gain).astype(jnp.bfloat16)
        hidden = jax.nn.gelu(
            jnp.dot(normed, up_ref[...], preferred_element_type=jnp.float32)
        ).astype(jnp.bfloat16)
        latent = residual + jnp.dot(hidden, down_ref[...], preferred_element_type=jnp.float32)
        placed = latent.reshape(patch_cols, PATCH, PATCH, channels).transpose(1, 0, 2, 3)
        latent_ref[pl.ds(pr * PATCH, PATCH)] = placed.reshape(PATCH, tile_cols, channels).astype(
            jnp.bfloat16
        )
        latent = latent.astype(jnp.bfloat16)
        for pc in range(patch_cols):
            cells = latent[pc * CELLS : (pc + 1) * CELLS]
            proj_ref[pr * patch_cols + pc] = lax.dot_general(
                decode_ref[...],
                jnp.concatenate([cells, cells], axis=0),
                NT,
                preferred_element_type=jnp.float32,
            )
        return 0

    lax.fori_loop(0, patch_rows, finish, 0)
    first = lax.broadcasted_iota(jnp.int32, (feat_width, LANES), 1) < CELLS

    def reply(d, _):
        for k in range(pairs):
            slot = d * capacity + 2 * k
            pair = jnp.where(first, proj_ref[id_ref[slot]], proj_ref[id_ref[slot + 1]])
            row = pl.multiple_of((d * pairs + k) * feat_width, 16)
            back_ref[pl.ds(row, feat_width), :] = pair.astype(jnp.bfloat16)
        return 0

    lax.fori_loop(0, devices, reply, 0)


def decode_blocks(slot_ref, back_ref, offset_ref, out_ref):
    feat_width, count = out_ref.shape
    blocks = count // BLK

    def one(b):
        slot = slot_ref[b]
        col = pl.multiple_of(b * BLK, BLK)
        weights = block_weights(offset_ref[:, pl.ds(col, BLK)].astype(jnp.float32))
        total = jnp.sum(weights.astype(jnp.float32), axis=0, keepdims=True)
        nothing = jnp.zeros_like(weights)
        low = slot % 2 == 0
        both = jnp.concatenate(
            [jnp.where(low, weights, nothing), jnp.where(low, nothing, weights)], axis=0
        )
        values = back_ref[pl.ds(pl.multiple_of(slot // 2 * feat_width, 16), feat_width), :]
        mean = jnp.dot(values, both, preferred_element_type=jnp.float32) / total
        out_ref[:, pl.ds(col, BLK)] = mean.astype(jnp.bfloat16)

    unroll = 4 if blocks % 4 == 0 else 1

    def body(i, _):
        for u in range(unroll):
            one(i * unroll + u)
        return 0

    lax.fori_loop(0, blocks // unroll, body, 0)


def with_halo(array, sides, width):
    for axis, dim in sides:
        size, length = (lax.axis_size(axis), array.shape[dim])
        up = [(i, (i + 1) % size) for i in range(size)]
        down = [(j, i) for i, j in up]
        last = lax.slice_in_dim(array, length - width, length, axis=dim)
        initial = lax.slice_in_dim(array, 0, width, axis=dim)
        before = lax.ppermute(last, axis, up)
        after = lax.ppermute(initial, axis, down)
        array = jnp.concatenate([before, array, after], axis=dim)
    return array


def local(
    obs_feat,
    obs_offset,
    block_tile,
    block_patch,
    embed_weight,
    grid_base,
    norm_gain,
    qkv_weight,
    out_weight,
    mlp_gain,
    up_weight,
    down_weight,
    decode_weight,
):
    lat_devices = lax.axis_size("lat")
    lon_devices = lax.axis_size("lon")
    devices = lat_devices * lon_devices
    feat_width, obs_count = obs_feat.shape
    blocks = obs_count // BLK
    capacity = max(2, 2 * blocks // devices)
    capacity += capacity % 2
    pairs = capacity // 2
    tile_rows, tile_cols, channels = grid_base.shape
    patch_total = (tile_rows // PATCH) * (tile_cols // PATCH)
    chunk = pairs * feat_width + meta_rows(pairs)

    send, slots = pl.pallas_call(
        lambda *refs: encode_blocks(capacity, devices, *refs),
        out_shape=(
            jax.ShapeDtypeStruct((devices * chunk, LANES), jnp.bfloat16),
            jax.ShapeDtypeStruct((blocks,), jnp.int32),
        ),
        in_specs=[smem(), smem(), vmem(), vmem()],
        out_specs=(vmem(), smem()),
        scratch_shapes=[pltpu.SMEM((devices,), jnp.int32)],
        compiler_params=params(),
        name="encode_blocks",
    )(block_tile.reshape(blocks), block_patch, obs_feat, obs_offset)

    recv = lax.all_to_all(
        send.reshape(devices, chunk, LANES), ("lat", "lon"), split_axis=0, concat_axis=0, tiled=True
    )
    tags = recv[:, pairs * feat_width + 2 * pairs : pairs * feat_width + 3 * pairs, 0 :: CELLS]
    ids = jnp.clip(tags.astype(jnp.float32).astype(jnp.int32) - 1, 0, patch_total - 1).reshape(-1)

    start = pl.pallas_call(
        lambda *refs: start_tile(capacity, devices, *refs),
        out_shape=jax.ShapeDtypeStruct(grid_base.shape, jnp.bfloat16),
        in_specs=[smem(), vmem(), vmem(), vmem()],
        out_specs=vmem(),
        scratch_shapes=[pltpu.VMEM((patch_total, feat_width + 8, LANES), jnp.float32)],
        compiler_params=params(),
        name="start_tile",
    )(ids, recv.reshape(devices * chunk, LANES), embed_weight, grid_base)

    margin = WIN // 2
    ext = with_halo(start, (("lat", 0), ("lon", 1)), margin).astype(jnp.float32)
    ext_rows, ext_cols, _ = ext.shape
    place = lax.axis_index("lat").astype(jnp.int32).reshape(1)

    latent, back = pl.pallas_call(
        lambda *refs: grid_block(capacity, devices, tile_rows * lat_devices, *refs),
        out_shape=(
            jax.ShapeDtypeStruct(grid_base.shape, jnp.bfloat16),
            jax.ShapeDtypeStruct((devices * pairs * feat_width, LANES), jnp.bfloat16),
        ),
        in_specs=[smem(), smem()] + [vmem()] * 8,
        out_specs=(vmem(), vmem()),
        scratch_shapes=[
            pltpu.VMEM((ext_cols // WIN * WIN * WIN, 3 * channels), jnp.bfloat16),
            pltpu.VMEM((ext_rows, ext_cols, channels), jnp.float32),
            pltpu.VMEM((patch_total, feat_width, LANES), jnp.float32),
        ],
        compiler_params=params(),
        name="grid_block",
    )(
        place,
        ids,
        ext,
        norm_gain.reshape(1, channels),
        qkv_weight,
        out_weight,
        mlp_gain.reshape(1, channels),
        up_weight,
        down_weight,
        decode_weight.T,
    )

    returned = lax.all_to_all(
        back.reshape(devices, pairs * feat_width, LANES),
        ("lat", "lon"),
        split_axis=0,
        concat_axis=0,
        tiled=True,
    )
    obs_out = pl.pallas_call(
        decode_blocks,
        out_shape=jax.ShapeDtypeStruct((feat_width, obs_count), jnp.bfloat16),
        in_specs=[smem(), vmem(), vmem()],
        out_specs=vmem(),
        compiler_params=params(),
        name="decode_blocks",
    )(slots, returned.reshape(devices * pairs * feat_width, LANES), obs_offset)
    return (latent, obs_out)


def solution(mesh):
    placed = (
        P(None, ("lat", "lon")),
        P(None, ("lat", "lon")),
        P(("lat", "lon"), None),
        P(("lat", "lon")),
        P(),
        P("lat", "lon", None),
        P(),
        P(),
        P(),
        P(),
        P(),
        P(),
        P(),
    )
    return jax.shard_map(
        local,
        mesh=mesh,
        in_specs=placed,
        out_specs=(P("lat", "lon", None), P(None, ("lat", "lon"))),
        check_vma=False,
    )
```

time: 349 us -> 154 us (0.44); the launches traced: 345 us -> 154 us
  waiting for transfers between devices: 124 us -> 5.47 us
  blocking collectives: 0 us -> 92.8 us
  matrix products: 85.1 us -> 0 us
  local copies, waits for them, and re-layouts: 67.6 us -> 2.12 us
  Pallas kernels: 0 us -> 42.3 us
  other arithmetic: 46.2 us -> 4.06 us
  starting transfers between devices: 21.1 us -> 6.59 us
    all_to_all x3 -> x0, waiting for transfers between devices: 109 us -> none  [the longest x1 69.8 us: local(): lax.all_to_all(send_feat.reshape(feat_width, devices, capacity, BLK), ('l...]
    all_to_all x0 -> x2, blocking collectives: none -> 92.8 us  [the longest x1 48.9 us: local(): lax.all_to_all(send.reshape(devices, chunk, LANES), ('lat', 'lon'), split...]
    dot_general x11 -> x0, matrix products: 85.1 us -> none  [the longest x1 36.1 us: local(): jnp.einsum('aibjhd,akblhd->abhijkl', windows[..., 0, :, :], windows[...,...]
    pallas_call x0 -> x4, Pallas kernels: none -> 42.3 us  [the longest x1 20.5 us: local(): pl.pallas_call(lambda *refs: grid_block(capacity, devices, tile_rows * la...]
    reduce_sum x6 -> x0, other arithmetic: 29 us -> none  [the longest x1 24 us: local(): jnp.sum(raised, axis=-1, keepdims=True)]
    reshape x5 -> x1, local copies, waits for them, and re-layouts: 24.1 us -> 0.78 us  [local(): jnp.clip(tags.astype(jnp.float32).astype(jnp.int32) - 1, 0, patch_total - 1)]
    all_to_all x3 -> x0, starting transfers between devices: 14.5 us -> none  [the longest x1 7.3 us: local(): lax.all_to_all(send_meta.reshape(3, devices, capacity, BLK), ('lat', 'lon...]
    slice x4 -> x1, local copies, waits for them, and re-layouts: 11.3 us -> 0.28 us  [local(): recv[:, pairs * feat_width + 2 * pairs:pairs * feat_width + 3 * pairs, 0:...]
  transfers between devices with their start and end apart: 7 -> 4, of which waited for: 6 -> 2; matrix products, arithmetic and copies ran while one was open for 3% -> 0% of each run, Pallas kernels for 0% -> 0%
where the time goes in v1:
time: 154 us
  blocking collectives  92.8 us (60%)
  Pallas kernels  42.3 us (27%)
  starting transfers between devices  6.59 us (4%)
  waiting for transfers between devices  5.47 us (4%)
  other arithmetic  4.06 us (3%)
  local copies, waits for them, and re-layouts  2.12 us (1%)
    all_to_all x1, blocking collectives, local(): lax.all_to_all(send.reshape(devices, chunk, LANES), ('lat', 'lon'), split...  48.9 us
    all_to_all x1, blocking collectives, local(): lax.all_to_all(back.reshape(devices, pairs * feat_width, LANES), ('lat',...  43.9 us
    pallas_call x1, Pallas kernels, local(): pl.pallas_call(lambda *refs: grid_block(capacity, devices, tile_rows * la...  20.5 us
    pallas_call x1, Pallas kernels, local(): pl.pallas_call(lambda *refs: encode_blocks(capacity, devices, *refs), out...  9.14 us
    pallas_call x1, Pallas kernels, local(): pl.pallas_call(decode_blocks, out_shape=jax.ShapeDtypeStruct((feat_width,...  7.37 us
    ppermute x2, starting transfers between devices, with_halo(): after = lax.ppermute(initial, axis, down)  5.73 us
    ppermute x2, waiting for transfers between devices, with_halo(): before = lax.ppermute(last, axis, up)  5.46 us
    pallas_call x1, Pallas kernels, local(): pl.pallas_call(lambda *refs: start_tile(capacity, devices, *refs), out_sh...  5.3 us
  transfers between devices with their start and end apart: 4, of which 2 were waited for; matrix products, arithmetic and copies ran while one was open for 0% of the time, Pallas kernels for 0%

profile of v1, /device:TPU:0, one launch (start us, length us, event | category | flops | bytes accessed | tf_op | source)
XLA Modules:
  0.0 154.0 jit_solution(15028456337408092329)
XLA Ops:
  0.6 9.1 %encode_blocks.1 = (bf16[6656,128]{1,0:T(8,128)(2,1)}, s32[96]{0:T(128)}) custom-call(s32[96]{0:T(128)} %bitcast.16, s32[96]{0:T(128)} %refs_1_.1, bf16[64,12288]{1,0:T(8,128)(2,1)} %refs_2_.2, bf16[2,12288]{1,0:T(2,128)(2,1)} %offset_ref.1), custom_call_target="tpu_custom_call" | custom-call | tf_op jit(solution)/shard_map/encode_blocks/pallas_call | solution.py:333
  9.8 48.9 %all_to_all.10 = bf16[32,208,128]{2,1,0:T(8,128)(2,1)S(1)} all-to-all(bf16[32,208,128]{2,1,0:T(8,128)(2,1)} %bitcast.11), channel_id=1, replica_groups=mesh['lat'=4,'lon'=8] {'lat','lon'}, dimensions={0} | all-to-all | bytes 3407872 | tf_op jit(solution)/shard_map/all_to_all | solution.py:346
  58.7 0.0 copy-start
  58.7 0.3 slice.15
  59.1 0.8 reshape.34.refs_0_.refs_1_
  59.8 0.1 copy-done
  59.9 5.3 %start_tile.1 = bf16[32,48,256]{2,1,0:T(8,128)(2,1)} custom-call(s32[192]{0:T(256)} %reshape.34.refs_0_.refs_1_, bf16[6656,128]{1,0:T(8,128)(2,1)} %bitcast.9, bf16[64,256]{1,0:T(8,128)(2,1)} %refs_2_.3, bf16[32,48,256]{2,1,0:T(8,128)(2,1)} %refs_3_.3), custom_call_target="tpu_custom_call" | custom-call | tf_op jit(solution)/shard_map/start_tile/pallas_call | solution.py:352
  65.2 1.0 fusion
  66.2 0.1 collective-permute-start
  66.3 1.7 %collective-permute-start.1 = (bf16[4,48,256]{2,1,0:T(8,128)(2,1)S(1)}, bf16[4,48,256]{2,1,0:T(8,128)(2,1)S(1)}, u32[]{:S(2)}, u32[]{:S(2)}) collective-permute-start(bf16[4,48,256]{2,1,0:T(8,128)(2,1)S(1)} %get-tuple-element.13), channel_id=1, source_target_pairs={{8,0},{16,8},{24,16},{0,24},{9,1},{17,9},{25,17},{1,25},{10,2},{18... | collective-permute-start | bytes 294920 | tf_op jit(solution)/shard_map/ppermute | solution.py:301
  68.0 2.8 %collective-permute-done = bf16[4,48,256]{2,1,0:T(8,128)(2,1)S(1)} collective-permute-done((bf16[4,48,256]{2,1,0:T(8,128)(2,1)S(1)}, bf16[4,48,256]{2,1,0:T(8,128)(2,1)S(1)}, u32[]{:S(2)}, u32[]{:S(2)}) %collective-permute-start) | collective-permute-done | bytes 98336 | tf_op jit(solution)/shard_map/ppermute | solution.py:300
  70.8 0.0 collective-permute-done.1
  70.8 1.0 pad_maximum_fusion.2
  71.8 0.8 collective-permute-start.2
  72.6 4.0 %collective-permute-start.3 = (bf16[40,4,256]{2,1,0:T(4,128)(2,1)S(1)}, bf16[40,4,256]{2,1,0:T(4,128)(2,1)S(1)}, u32[]{:S(2)}, u32[]{:S(2)}) collective-permute-start(bf16[40,4,256]{2,1,0:T(4,128)(2,1)S(1)} %get-tuple-element.11), channel_id=1, source_target_pairs={{1,0},{2,1},{3,2},{4,3},{5,4},{6,5},{7,6},{0,7},{9,8},{10,9},{11,1... | collective-permute-start | bytes 245768 | tf_op jit(solution)/shard_map/ppermute | solution.py:301
  76.6 2.7 %collective-permute-done.2 = bf16[40,4,256]{2,1,0:T(4,128)(2,1)S(1)} collective-permute-done((bf16[40,4,256]{2,1,0:T(4,128)(2,1)S(1)}, bf16[40,4,256]{2,1,0:T(4,128)(2,1)S(1)}, u32[]{:S(2)}, u32[]{:S(2)}) %collective-permute-start.2) | collective-permute-done | bytes 81952 | tf_op jit(solution)/shard_map/ppermute | solution.py:300
  79.3 0.0 collective-permute-done.3
  79.3 3.0 %maximum_convert_fusion.refs_2_ = f32[40,56,256]{2,1,0:T(8,128)} fusion(bf16[40,4,256]{2,1,0:T(4,128)(2,1)S(1)} %collective-permute-done.3, bf16[4,48,256]{2,1,0:T(8,128)(2,1)S(1)} %collective-permute-done.1, bf16[32,48,256]{2,1,0:T(8,128)(2,1)} %start_tile.1, bf16[4,48,256]{2,1,0:T(8,128)(2,1)S(1)} %collective-permute-done, ...), kind=kLoop, calls=%fused_computation | loop fusion | flops 5734400 | bytes 3440640 | tf_op jit(solution)/shard_map/convert_element_type | solution.py:363
  82.3 20.5 %grid_block.1 = (bf16[32,48,256]{2,1,0:T(8,128)(2,1)}, bf16[6144,128]{1,0:T(8,128)(2,1)}) custom-call(s32[1]{0:T(128)} %bitcast.refs_0_, s32[192]{0:T(256)} %reshape.34.refs_0_.refs_1_, f32[40,56,256]{2,1,0:T(8,128)} %maximum_convert_fusion.refs_2_, f32[1,256]{1,0:T(1,128)} %bitcast.14, bf16[256,768]{1,0:T(8,128)(2,1)} %refs_4_.1, bf16[256,256]{1,0:T(8,128)(2,1)} %refs_5_.1, ...), custom_call_target="tpu_custom_call" | custom-call | tf_op jit(solution)/shard_map/grid_block/pallas_call | solution.py:367
  102.8 43.9 %all_to_all.11 = bf16[32,192,128]{2,1,0:T(8,128)(2,1)} all-to-all(bf16[32,192,128]{2,1,0:T(8,128)(2,1)} %bitcast.12), channel_id=1, replica_groups=mesh['lat'=4,'lon'=8] {'lat','lon'}, dimensions={0} | all-to-all | bytes 3145728 | tf_op jit(solution)/shard_map/all_to_all | solution.py:395
  146.6 7.4 %decode_blocks.1 = bf16[64,12288]{1,0:T(8,128)(2,1)} custom-call(s32[96]{0:T(128)} %get-tuple-element.8.slot_ref, bf16[6144,128]{1,0:T(8,128)(2,1)} %bitcast.10, bf16[2,12288]{1,0:T(2,128)(2,1)} %offset_ref.1), custom_call_target="tpu_custom_call" | custom-call | tf_op jit(solution)/shard_map/decode_blocks/pallas_call | solution.py:402
  (1 shorter events, 0.0 us)
Async XLA Ops:
  58.7 1.2 copy-start
  66.2 4.6 %collective-permute-start = (bf16[4,48,256]{2,1,0:T(8,128)(2,1)S(1)}, bf16[4,48,256]{2,1,0:T(8,128)(2,1)S(1)}, u32[]{:S(2)}, u32[]{:S(2)}) collective-permute-start(bf16[4,48,256]{2,1,0:T(8,128)(2,1)S(1)} %get-tuple-element.12), channel_id=1, source_target_pairs={{0,8},{8,16},{16,24},{24,0},{1,9},{9,17},{17,25},{25,1},{2,10},{10... | collective-permute-start | bytes 294920 | tf_op jit(solution)/shard_map/ppermute | solution.py:300
  66.3 4.5 %collective-permute-start.1 = (bf16[4,48,256]{2,1,0:T(8,128)(2,1)S(1)}, bf16[4,48,256]{2,1,0:T(8,128)(2,1)S(1)}, u32[]{:S(2)}, u32[]{:S(2)}) collective-permute-start(bf16[4,48,256]{2,1,0:T(8,128)(2,1)S(1)} %get-tuple-element.13), channel_id=1, source_target_pairs={{8,0},{16,8},{24,16},{0,24},{9,1},{17,9},{25,17},{1,25},{10,2},{18... | collective-permute-start | bytes 294920 | tf_op jit(solution)/shard_map/ppermute | solution.py:301
  71.8 7.5 %collective-permute-start.2 = (bf16[40,4,256]{2,1,0:T(4,128)(2,1)S(1)}, bf16[40,4,256]{2,1,0:T(4,128)(2,1)S(1)}, u32[]{:S(2)}, u32[]{:S(2)}) collective-permute-start(bf16[40,4,256]{2,1,0:T(4,128)(2,1)S(1)} %get-tuple-element.10), channel_id=1, source_target_pairs={{0,1},{1,2},{2,3},{3,4},{4,5},{5,6},{6,7},{7,0},{8,9},{9,10},{10,1... | collective-permute-start | bytes 245768 | tf_op jit(solution)/shard_map/ppermute | solution.py:300
  72.6 6.7 %collective-permute-start.3 = (bf16[40,4,256]{2,1,0:T(4,128)(2,1)S(1)}, bf16[40,4,256]{2,1,0:T(4,128)(2,1)S(1)}, u32[]{:S(2)}, u32[]{:S(2)}) collective-permute-start(bf16[40,4,256]{2,1,0:T(4,128)(2,1)S(1)} %get-tuple-element.11), channel_id=1, source_target_pairs={{1,0},{2,1},{3,2},{4,3},{5,4},{6,5},{7,6},{0,7},{9,8},{10,9},{11,1... | collective-permute-start | bytes 245768 | tf_op jit(solution)/shard_map/ppermute | solution.py:301

commit v2 on v1

--- a/solution.py
+++ b/solution.py
@@ -1,3 +1,5 @@
+import math
+
 import jax
 import jax.numpy as jnp
 from jax import lax
@@ -19,8 +21,8 @@
 TN = (((0,), (0,)), ((), ()))
 
 
-def params(**extra):
-    return pltpu.CompilerParams(vmem_limit_bytes=56 * 1024 * 1024, **extra)
+def params(mib):
+    return pltpu.CompilerParams(vmem_limit_bytes=mib * 1024 * 1024)
 
 
 def vmem():
@@ -102,7 +104,7 @@
         )
         send_ref[pl.ds(row, meta), :] = jnp.where(meta_half == half, new, old).astype(jnp.bfloat16)
 
-    unroll = 4 if blocks % 4 == 0 else 1
+    unroll = 32 if blocks % 32 == 0 else 1
 
     def body(i, _):
         for u in range(unroll):
@@ -136,7 +138,7 @@
             acc_ref[b] += jnp.where(first, 0.0, both)
         return 0
 
-    lax.fori_loop(0, devices, gather, 0)
+    lax.fori_loop(0, devices, gather, 0, unroll=4)
     head = lax.broadcasted_iota(jnp.int32, (feat_width, LANES), 1) < CELLS
     embed = embed_ref[...]
 
@@ -157,67 +159,105 @@
         start_ref[rows] = (base_ref[rows].astype(jnp.float32) + lifted).astype(jnp.bfloat16)
         return 0
 
-    lax.fori_loop(0, patch_rows, lift, 0)
+    lax.fori_loop(0, patch_rows, lift, 0, unroll=True)
 
 
 def grid_block(
     capacity, devices, lat_cells, place_ref, id_ref, ext_ref, norm_ref, qkv_ref, out_ref, mlp_ref,
-    up_ref, down_ref, decode_ref, latent_ref, back_ref, packed_ref, att_ref, proj_ref,
+    up_ref, down_ref, decode_ref, latent_ref, back_ref, turned_ref, key_ref, pack_ref, att_ref,
+    mixed_ref, proj_ref, score_ref, prob_ref,
 ):
     ext_rows, ext_cols, channels = ext_ref.shape
     tile_rows, tile_cols, _ = latent_ref.shape
     margin = WIN // 2
     win_rows, win_cols = ext_rows // WIN, ext_cols // WIN
+    win_pairs = -(-win_cols // 2)
     patch_rows, patch_cols = tile_rows // PATCH, tile_cols // PATCH
     tokens = WIN * WIN
     group = 128
     heads = group // HEAD_DIM
-    feat_width = decode_ref.shape[0]
+    feat_width = decode_ref.shape[1]
     pairs = capacity // 2
-    scale = HEAD_DIM ** (-0.5)
+    scale = HEAD_DIM ** (-0.5) / math.log(2.0)
     norm_gain = norm_ref[...]
-    head_of = lax.broadcasted_iota(jnp.int32, (tokens, group), 1) // HEAD_DIM
-    key_row = lax.broadcasted_iota(jnp.int32, (tokens, heads * tokens), 0) // WIN
-    query_row = lax.broadcasted_iota(jnp.int32, (tokens, heads * tokens), 1) % tokens // WIN
-
-    def attend(wr, _):
+    turned_ref[:channels] = qkv_ref[:, :channels].T
+    turned_ref[channels:] = qkv_ref[:, 2 * channels :].T
+    shape = (tokens, heads * LANES)
+    own = lax.broadcasted_iota(jnp.int32, shape, 1) % LANES < tokens
+    key_row = lax.broadcasted_iota(jnp.int32, (tokens, LANES), 0) // WIN
+    query_row = lax.broadcasted_iota(jnp.int32, (tokens, LANES), 1) % tokens // WIN
+    nothing = jnp.zeros(shape, jnp.bfloat16)
+    empty = jnp.zeros((HEAD_DIM, LANES), jnp.bfloat16)
+
+    def attend(wr):
         rows = pl.ds(wr * WIN, WIN)
         cells = ext_ref[rows].reshape(WIN, win_cols, WIN, channels).transpose(1, 0, 2, 3)
         normed = normalize(cells.reshape(win_cols * tokens, channels), norm_gain)
-        packed_ref[...] = jnp.dot(
-            normed.astype(jnp.bfloat16), qkv_ref[...], preferred_element_type=jnp.float32
+        normed = normed.astype(jnp.bfloat16)
+        if win_cols % 2:
+            normed = jnp.concatenate([normed, jnp.zeros((tokens, channels), jnp.bfloat16)], axis=0)
+        key_ref[...] = jnp.dot(
+            normed, qkv_ref[:, channels : 2 * channels], preferred_element_type=jnp.float32
         ).astype(jnp.bfloat16)
-        top = place_ref[0] * tile_rows - margin + wr * WIN
-        side = lambda r: (r >= 0).astype(jnp.int32) + (r >= lat_cells).astype(jnp.int32)
-        bias = jnp.where(side(top + key_row) == side(top + query_row), 0.0, -1e30)
+        pack_ref[...] = lax.dot_general(
+            turned_ref[...], normed, NT, preferred_element_type=jnp.float32
+        ).astype(jnp.bfloat16)
+        edge = wr in (0, win_rows - 1)
+        if edge:
+            top = place_ref[0] * tile_rows - margin + wr * WIN
+            side = lambda r: (r >= 0).astype(jnp.int32) + (r >= lat_cells).astype(jnp.int32)
+            bias = jnp.where(side(top + key_row) == side(top + query_row), 0.0, -1e30)
+            bias = jnp.concatenate([bias] * heads, axis=1)
+        parts = [(p, g) for p in range(win_pairs) for g in range(channels // group)]
+        for n, (p, g) in enumerate(parts):
+            span = slice(p * LANES, (p + 1) * LANES)
+            at = slice(g * group, (g + 1) * group)
+            query = pack_ref[at, span]
+            stack = jnp.concatenate(
+                [
+                    jnp.concatenate(
+                        [
+                            query[h * HEAD_DIM : (h + 1) * HEAD_DIM] if i == h else empty
+                            for i in range(heads)
+                        ],
+                        axis=0,
+                    )
+                    for h in range(heads)
+                ],
+                axis=1,
+            )
+            scores = jnp.dot(key_ref[span, at], stack, preferred_element_type=jnp.float32)
+            scores = jnp.where(own, scores[:tokens], scores[tokens:])
+            score_ref[n] = scores + bias if edge else scores
+        for n, (p, g) in enumerate(parts):
+            scores = score_ref[n]
+            peak = jnp.max(scores, axis=0, keepdims=True)
+            raised = jnp.exp2((scores - peak) * scale)
+            total = jnp.sum(raised, axis=0, keepdims=True)
+            probs = (raised * (1.0 / total)).astype(jnp.bfloat16)
+            prob_ref[n, :tokens] = jnp.where(own, probs, nothing)
+            prob_ref[n, tokens:] = jnp.where(own, nothing, probs)
+        for n, (p, g) in enumerate(parts):
+            span = slice(p * LANES, (p + 1) * LANES)
+            for h in range(0, heads, 2):
+                at = g * group + h * HEAD_DIM
+                both = jnp.dot(
+                    pack_ref[channels + at : channels + at + 2 * HEAD_DIM, span],
+                    prob_ref[n, :, h * LANES : (h + 2) * LANES],
+                    preferred_element_type=jnp.float32,
+                ).astype(jnp.bfloat16)
+                att_ref[at : at + HEAD_DIM, span] = both[:HEAD_DIM, :LANES]
+                att_ref[at + HEAD_DIM : at + 2 * HEAD_DIM, span] = both[HEAD_DIM:, LANES:]
+        mixed = lax.dot_general(att_ref[...], out_ref[...], TN, preferred_element_type=jnp.float32)
         for w in range(win_cols):
-            span = slice(w * tokens, (w + 1) * tokens)
-            for g in range(channels // group):
-                at = lambda i: slice(i * channels + g * group, i * channels + (g + 1) * group)
-                query = packed_ref[span, at(0)]
-                key = packed_ref[span, at(1)]
-                value = packed_ref[span, at(2)]
-                stack = jnp.concatenate(
-                    [jnp.where(head_of == h, query, jnp.zeros_like(query)) for h in range(heads)],
-                    axis=0,
-                )
-                scores = lax.dot_general(key, stack, NT, preferred_element_type=jnp.float32)
-                scores = scores + bias
-                peak = jnp.max(scores, axis=0, keepdims=True)
-                raised = jnp.exp((scores - peak) * scale)
-                total = jnp.sum(raised, axis=0, keepdims=True)
-                probs = (raised * (1.0 / total)).astype(jnp.bfloat16)
-                mixed = lax.dot_general(probs, value, TN, preferred_element_type=jnp.float32)
-                picked = mixed[:tokens]
-                for h in range(1, heads):
-                    picked = jnp.where(head_of == h, mixed[h * tokens : (h + 1) * tokens], picked)
-                att_ref[rows, w * WIN : (w + 1) * WIN, g * group : (g + 1) * group] = picked.reshape(
-                    WIN, WIN, group
-                )
-        return 0
-
-    lax.fori_loop(0, win_rows, attend, 0)
+            mixed_ref[rows, w * WIN : (w + 1) * WIN, :] = mixed[w * tokens : (w + 1) * tokens].reshape(
+                WIN, WIN, channels
+            )
+
+    for wr in range(win_rows):
+        attend(wr)
     mlp_gain = mlp_ref[...]
+    first = lax.broadcasted_iota(jnp.int32, (feat_width, LANES), 1) < CELLS
 
     def by_patch(values):
         values = values.reshape(PATCH, patch_cols, PATCH, channels).transpose(1, 0, 2, 3)
@@ -225,9 +265,8 @@
 
     def finish(pr, _):
         rows = pl.ds(margin + pr * PATCH, PATCH)
-        attended = by_patch(att_ref[rows, margin : margin + tile_cols, :]).astype(jnp.bfloat16)
-        begun = by_patch(ext_ref[rows, margin : margin + tile_cols, :])
-        residual = begun + jnp.dot(attended, out_ref[...], preferred_element_type=jnp.float32)
+        inner = slice(margin, margin + tile_cols)
+        residual = by_patch(ext_ref[rows, inner, :] + mixed_ref[rows, inner, :])
         normed = normalize(residual, mlp_gain).astype(jnp.bfloat16)
         hidden = jax.nn.gelu(
             jnp.dot(normed, up_ref[...], preferred_element_type=jnp.float32)
@@ -238,18 +277,15 @@
             jnp.bfloat16
         )
         latent = latent.astype(jnp.bfloat16)
-        for pc in range(patch_cols):
-            cells = latent[pc * CELLS : (pc + 1) * CELLS]
-            proj_ref[pr * patch_cols + pc] = lax.dot_general(
-                decode_ref[...],
-                jnp.concatenate([cells, cells], axis=0),
-                NT,
-                preferred_element_type=jnp.float32,
-            )
-        return 0
-
-    lax.fori_loop(0, patch_rows, finish, 0)
-    first = lax.broadcasted_iota(jnp.int32, (feat_width, LANES), 1) < CELLS
+        projected = jnp.dot(latent, decode_ref[...], preferred_element_type=jnp.float32)
+        for pc in range(0, patch_cols, 2):
+            turned = projected[pc * CELLS : pc * CELLS + LANES].T
+            swapped = pltpu.roll(turned, CELLS, 1)
+            proj_ref[pr * patch_cols + pc] = jnp.where(first, turned, swapped)
+            proj_ref[pr * patch_cols + pc + 1] = jnp.where(first, swapped, turned)
+        return 0
+
+    lax.fori_loop(0, patch_rows, finish, 0, unroll=True)
 
     def reply(d, _):
         for k in range(pairs):
@@ -277,10 +313,10 @@
             [jnp.where(low, weights, nothing), jnp.where(low, nothing, weights)], axis=0
         )
         values = back_ref[pl.ds(pl.multiple_of(slot // 2 * feat_width, 16), feat_width), :]
-        mean = jnp.dot(values, both, preferred_element_type=jnp.float32) / total
+        mean = jnp.dot(values, both, preferred_element_type=jnp.float32) * (1.0 / total)
         out_ref[:, pl.ds(col, BLK)] = mean.astype(jnp.bfloat16)
 
-    unroll = 4 if blocks % 4 == 0 else 1
+    unroll = 32 if blocks % 32 == 0 else 1
 
     def body(i, _):
         for u in range(unroll):
@@ -339,7 +375,7 @@
         in_specs=[smem(), smem(), vmem(), vmem()],
         out_specs=(vmem(), smem()),
         scratch_shapes=[pltpu.SMEM((devices,), jnp.int32)],
-        compiler_params=params(),
+        compiler_params=params(8),
         name="encode_blocks",
     )(block_tile.reshape(blocks), block_patch, obs_feat, obs_offset)
 
@@ -355,13 +391,14 @@
         in_specs=[smem(), vmem(), vmem(), vmem()],
         out_specs=vmem(),
         scratch_shapes=[pltpu.VMEM((patch_total, feat_width + 8, LANES), jnp.float32)],
-        compiler_params=params(),
+        compiler_params=params(8),
         name="start_tile",
     )(ids, recv.reshape(devices * chunk, LANES), embed_weight, grid_base)
 
     margin = WIN // 2
     ext = with_halo(start, (("lat", 0), ("lon", 1)), margin).astype(jnp.float32)
     ext_rows, ext_cols, _ = ext.shape
+    padded = -(-ext_cols // (2 * WIN)) * LANES
     place = lax.axis_index("lat").astype(jnp.int32).reshape(1)
 
     latent, back = pl.pallas_call(
@@ -373,11 +410,16 @@
         in_specs=[smem(), smem()] + [vmem()] * 8,
         out_specs=(vmem(), vmem()),
         scratch_shapes=[
-            pltpu.VMEM((ext_cols // WIN * WIN * WIN, 3 * channels), jnp.bfloat16),
+            pltpu.VMEM((2 * channels, channels), jnp.bfloat16),
+            pltpu.VMEM((padded, channels), jnp.bfloat16),
+            pltpu.VMEM((2 * channels, padded), jnp.bfloat16),
+            pltpu.VMEM((channels, padded), jnp.bfloat16),
             pltpu.VMEM((ext_rows, ext_cols, channels), jnp.float32),
             pltpu.VMEM((patch_total, feat_width, LANES), jnp.float32),
+            pltpu.VMEM((padded * channels // LANES // 128, WIN * WIN, 4 * LANES), jnp.float32),
+            pltpu.VMEM((padded * channels // LANES // 128, LANES, 4 * LANES), jnp.bfloat16),
         ],
-        compiler_params=params(),
+        compiler_params=params(20),
         name="grid_block",
     )(
         place,
@@ -389,7 +431,7 @@
         mlp_gain.reshape(1, channels),
         up_weight,
         down_weight,
-        decode_weight.T,
+        decode_weight,
     )
 
     returned = lax.all_to_all(
@@ -404,7 +446,7 @@
         out_shape=jax.ShapeDtypeStruct((feat_width, obs_count), jnp.bfloat16),
         in_specs=[smem(), vmem(), vmem()],
         out_specs=vmem(),
-        compiler_params=params(),
+        compiler_params=params(8),
         name="decode_blocks",
     )(slots, returned.reshape(devices * pairs * feat_width, LANES), obs_offset)
     return (latent, obs_out)

time: 154 us -> 132 us (0.86)
  Pallas kernels: 42.3 us -> 22.5 us
  other arithmetic: 4.06 us -> 0.56 us
  local copies, waits for them, and re-layouts: 2.12 us -> 4.11 us
    pallas_call x1, Pallas kernels: 20.5 us -> 12 us  [local(): pl.pallas_call(lambda *refs: grid_block(capacity, devices, tile_rows * la...]
    pallas_call x1, Pallas kernels: 9.14 us -> 4.11 us  [local(): pl.pallas_call(lambda *refs: encode_blocks(capacity, devices, *refs), out...]
    pallas_call x1, Pallas kernels: 7.37 us -> 3.78 us  [local(): pl.pallas_call(decode_blocks, out_shape=jax.ShapeDtypeStruct((feat_width,...]
    unnamed x2 -> x29, local copies, waits for them, and re-layouts: 0.11 us -> 3.68 us
    pallas_call x1, Pallas kernels: 5.3 us -> 2.64 us  [local(): pl.pallas_call(lambda *refs: start_tile(capacity, devices, *refs), out_sh...]
    convert_element_type x1, other arithmetic: 2.98 us -> 0.45 us  [local(): ext = with_halo(start, (('lat', 0), ('lon', 1)), margin).astype(jnp.float32)]
where the time goes in v2:
time: 132 us
  blocking collectives  92.3 us (70%)
  Pallas kernels  22.5 us (17%)
  starting transfers between devices  6.58 us (5%)
  waiting for transfers between devices  5.29 us (4%)
  local copies, waits for them, and re-layouts  4.11 us (3%)
    all_to_all x1, blocking collectives, local(): lax.all_to_all(send.reshape(devices, chunk, LANES), ('lat', 'lon'), split...  48.7 us
    all_to_all x1, blocking collectives, local(): lax.all_to_all(back.reshape(devices, pairs * feat_width, LANES), ('lat',...  43.5 us
    pallas_call x1, Pallas kernels, local(): pl.pallas_call(lambda *refs: grid_block(capacity, devices, tile_rows * la...  12 us
    ppermute x2, starting transfers between devices, with_halo(): after = lax.ppermute(initial, axis, down)  5.66 us
    ppermute x2, waiting for transfers between devices, with_halo(): before = lax.ppermute(last, axis, up)  5.28 us
    pallas_call x1, Pallas kernels, local(): pl.pallas_call(lambda *refs: encode_blocks(capacity, devices, *refs), out...  4.11 us
    pallas_call x1, Pallas kernels, local(): pl.pallas_call(decode_blocks, out_shape=jax.ShapeDtypeStruct((feat_width,...  3.78 us
    unnamed x29, local copies, waits for them, and re-layouts  3.68 us
  transfers between devices with their start and end apart: 4, of which 2 were waited for; matrix products, arithmetic and copies ran while one was open for 0% of the time, Pallas kernels for 0%

profile of v2, /device:TPU:0, one launch (start us, length us, event | category | flops | bytes accessed | tf_op | source)
XLA Modules:
  0.0 132.1 jit_solution(2758652367357043680)
XLA Ops:
  0.6 1.4 %copy-done = bf16[64,12288]{1,0:T(8,128)(2,1)S(1)} copy-done((bf16[64,12288]{1,0:T(8,128)(2,1)S(1)}, bf16[64,12288]{1,0:T(8,128)(2,1)}, u32[]{:S(2)}) %copy-start) | copy-done | bytes 1572888
  2.0 0.8 copy-done.5
  2.8 0.7 copy-done.11
  3.5 0.7 copy-done.12
  4.2 4.1 %encode_blocks.1 = (bf16[6656,128]{1,0:T(8,128)(2,1)S(1)}, s32[96]{0:T(128)S(1)}) custom-call(s32[96]{0:T(128)S(1)} %bitcast.14, s32[96]{0:T(128)S(1)} %copy-done.12, bf16[64,12288]{1,0:T(8,128)(2,1)S(1)} %copy-done, bf16[2,12288]{1,0:T(2,128)(2,1)S(1)} %copy-done.5), custom_call_target="tpu_custom_call" | custom-call | tf_op jit(solution)/shard_map/encode_blocks/pallas_call | solution.py:369
  8.3 48.7 %all_to_all.10 = bf16[32,208,128]{2,1,0:T(8,128)(2,1)S(1)} all-to-all(bf16[32,208,128]{2,1,0:T(8,128)(2,1)S(1)} %bitcast.10), channel_id=1, replica_groups=mesh['lat'=4,'lon'=8] {'lat','lon'}, dimensions={0} | all-to-all | bytes 3407872 | tf_op jit(solution)/shard_map/all_to_all | solution.py:382
  57.0 0.3 slice.15
  57.3 0.1 reshape.34.refs_0_.refs_1_
  57.5 0.0 copy-start.13
  57.5 2.6 %start_tile.1 = bf16[32,48,256]{2,1,0:T(8,128)(2,1)S(1)} custom-call(s32[192]{0:T(256)S(1)} %reshape.34.refs_0_.refs_1_, bf16[6656,128]{1,0:T(8,128)(2,1)S(1)} %bitcast.8, bf16[64,256]{1,0:T(8,128)(2,1)S(1)} %copy-done.8, bf16[32,48,256]{2,1,0:T(8,128)(2,1)S(1)} %copy-done.1), custom_call_target="tpu_custom_call" | custom-call | tf_op jit(solution)/shard_map/start_tile/pallas_call | solution.py:388
  60.2 0.1 collective-permute-start
  60.3 0.0 copy-start.2
  60.3 0.0 copy-start.3
  60.3 1.7 %collective-permute-start.1 = (bf16[4,48,256]{2,1,0:T(8,128)(2,1)S(1)}, bf16[4,48,256]{2,1,0:T(8,128)(2,1)S(1)}, u32[]{:S(2)}, u32[]{:S(2)}) collective-permute-start(bf16[4,48,256]{2,1,0:T(8,128)(2,1)S(1)} %get-tuple-element.13), channel_id=1, source_target_pairs={{8,0},{16,8},{24,16},{0,24},{9,1},{17,9},{25,17},{1,25},{10,2},{18... | collective-permute-start | bytes 294920 | tf_op jit(solution)/shard_map/ppermute | solution.py:337
  62.1 2.3 %collective-permute-done = bf16[4,48,256]{2,1,0:T(8,128)(2,1)S(1)} collective-permute-done((bf16[4,48,256]{2,1,0:T(8,128)(2,1)S(1)}, bf16[4,48,256]{2,1,0:T(8,128)(2,1)S(1)}, u32[]{:S(2)}, u32[]{:S(2)}) %collective-permute-start) | collective-permute-done | bytes 98336 | tf_op jit(solution)/shard_map/ppermute | solution.py:336
  64.4 0.1 pad_maximum_fusion.2
  64.5 0.9 collective-permute-start.2
  65.3 3.9 %collective-permute-start.3 = (bf16[40,4,256]{2,1,0:T(4,128)(2,1)S(1)}, bf16[40,4,256]{2,1,0:T(4,128)(2,1)S(1)}, u32[]{:S(2)}, u32[]{:S(2)}) collective-permute-start(bf16[40,4,256]{2,1,0:T(4,128)(2,1)S(1)} %get-tuple-element.11), channel_id=1, source_target_pairs={{1,0},{2,1},{3,2},{4,3},{5,4},{6,5},{7,6},{0,7},{9,8},{10,9},{11,1... | collective-permute-start | bytes 245768 | tf_op jit(solution)/shard_map/ppermute | solution.py:337
  69.3 0.1 copy.23.refs_9_
  69.4 3.0 %collective-permute-done.2 = bf16[40,4,256]{2,1,0:T(4,128)(2,1)S(1)} collective-permute-done((bf16[40,4,256]{2,1,0:T(4,128)(2,1)S(1)}, bf16[40,4,256]{2,1,0:T(4,128)(2,1)S(1)}, u32[]{:S(2)}, u32[]{:S(2)}) %collective-permute-start.2) | collective-permute-done | bytes 81952 | tf_op jit(solution)/shard_map/ppermute | solution.py:336
  72.3 0.5 maximum_convert_fusion.refs_2_
  72.8 12.0 %grid_block.1 = (bf16[32,48,256]{2,1,0:T(8,128)(2,1)}, bf16[6144,128]{1,0:T(8,128)(2,1)S(1)}) custom-call(s32[1]{0:T(128)} %bitcast.refs_0_, s32[192]{0:T(256)S(1)} %reshape.34.refs_0_.refs_1_, f32[40,56,256]{2,1,0:T(8,128)S(1)} %maximum_convert_fusion.refs_2_, f32[1,256]{1,0:T(1,128)S(1)} %bitcast.12, bf16[256,768]{1,0:T(8,128)(2,1)S(1)} %copy-done.4, ...), custom_call_target="tpu_custom_call" | custom-call | tf_op jit(solution)/shard_map/grid_block/pallas_call | solution.py:404
  84.8 43.5 %all_to_all.11 = bf16[32,192,128]{2,1,0:T(8,128)(2,1)S(1)} all-to-all(bf16[32,192,128]{2,1,0:T(8,128)(2,1)S(1)} %bitcast.11), channel_id=1, replica_groups=mesh['lat'=4,'lon'=8] {'lat','lon'}, dimensions={0} | all-to-all | bytes 3145728 | tf_op jit(solution)/shard_map/all_to_all | solution.py:437
  128.4 3.8 %decode_blocks.1 = bf16[64,12288]{1,0:T(8,128)(2,1)} custom-call(s32[96]{0:T(128)S(1)} %get-tuple-element.8.slot_ref, bf16[6144,128]{1,0:T(8,128)(2,1)S(1)} %bitcast.9, bf16[2,12288]{1,0:T(2,128)(2,1)S(1)} %copy-done.6), custom_call_target="tpu_custom_call" | custom-call | tf_op jit(solution)/shard_map/decode_blocks/pallas_call | solution.py:444
  (25 shorter events, 0.1 us)
Async XLA Ops:
  0.6 1.4 %copy-start = (bf16[64,12288]{1,0:T(8,128)(2,1)S(1)}, bf16[64,12288]{1,0:T(8,128)(2,1)}, u32[]{:S(2)}) copy-start(bf16[64,12288]{1,0:T(8,128)(2,1)} %refs_2_.2) | copy-start | bytes 4718596
  2.0 0.8 copy-start.5
  2.8 0.7 copy-start.11
  3.5 0.7 copy-start.12
  4.2 53.3 %copy-start.1 = (bf16[32,48,256]{2,1,0:T(8,128)(2,1)S(1)}, bf16[32,48,256]{2,1,0:T(8,128)(2,1)}, u32[]{:S(2)}) copy-start(bf16[32,48,256]{2,1,0:T(8,128)(2,1)} %refs_3_.3) | copy-start | bytes 2359300
  4.2 53.3 %copy-start.8 = (bf16[64,256]{1,0:T(8,128)(2,1)S(1)}, bf16[64,256]{1,0:T(8,128)(2,1)}, u32[]{:S(2)}) copy-start(bf16[64,256]{1,0:T(8,128)(2,1)} %refs_2_.3) | copy-start | bytes 98308
  57.5 11.8 %copy-start.13 = (bf16[256,64]{0,1:T(8,128)(2,1)S(1)}, bf16[256,64]{0,1:T(8,128)(2,1)}, u32[]{:S(2)}) copy-start(bf16[256,64]{0,1:T(8,128)(2,1)} %param.25) | copy-start | bytes 98308
  60.2 4.2 %collective-permute-start = (bf16[4,48,256]{2,1,0:T(8,128)(2,1)S(1)}, bf16[4,48,256]{2,1,0:T(8,128)(2,1)S(1)}, u32[]{:S(2)}, u32[]{:S(2)}) collective-permute-start(bf16[4,48,256]{2,1,0:T(8,128)(2,1)S(1)} %get-tuple-element.12), channel_id=1, source_target_pairs={{0,8},{8,16},{16,24},{24,0},{1,9},{9,17},{17,25},{25,1},{2,10},{10... | collective-permute-start | bytes 294920 | tf_op jit(solution)/shard_map/ppermute | solution.py:336
  60.3 12.5 %copy-start.2 = (bf16[256,1024]{1,0:T(8,128)(2,1)S(1)}, bf16[256,1024]{1,0:T(8,128)(2,1)}, u32[]{:S(2)}) copy-start(bf16[256,1024]{1,0:T(8,128)(2,1)} %refs_7_.1) | copy-start | bytes 1572868
  60.3 12.5 %copy-start.3 = (bf16[1024,256]{1,0:T(8,128)(2,1)S(1)}, bf16[1024,256]{1,0:T(8,128)(2,1)}, u32[]{:S(2)}) copy-start(bf16[1024,256]{1,0:T(8,128)(2,1)} %refs_8_.1) | copy-start | bytes 1572868
  60.3 12.5 %copy-start.4 = (bf16[256,768]{1,0:T(8,128)(2,1)S(1)}, bf16[256,768]{1,0:T(8,128)(2,1)}, u32[]{:S(2)}) copy-start(bf16[256,768]{1,0:T(8,128)(2,1)} %refs_4_.1) | copy-start | bytes 1179652
  60.3 12.5 %copy-start.7 = (bf16[256,256]{1,0:T(8,128)(2,1)S(1)}, bf16[256,256]{1,0:T(8,128)(2,1)}, u32[]{:S(2)}) copy-start(bf16[256,256]{1,0:T(8,128)(2,1)} %refs_5_.1) | copy-start | bytes 393220
  60.3 12.5 %copy-start.9 = (f32[256]{0:T(256)S(1)}, f32[256]{0:T(256)}, u32[]{:S(2)}) copy-start(f32[256]{0:T(256)} %param.19) | copy-start | bytes 3076
  60.3 12.5 %copy-start.10 = (f32[256]{0:T(256)S(1)}, f32[256]{0:T(256)}, u32[]{:S(2)}) copy-start(f32[256]{0:T(256)} %param.22) | copy-start | bytes 3076
  60.3 4.1 %collective-permute-start.1 = (bf16[4,48,256]{2,1,0:T(8,128)(2,1)S(1)}, bf16[4,48,256]{2,1,0:T(8,128)(2,1)S(1)}, u32[]{:S(2)}, u32[]{:S(2)}) collective-permute-start(bf16[4,48,256]{2,1,0:T(8,128)(2,1)S(1)} %get-tuple-element.13), channel_id=1, source_target_pairs={{8,0},{16,8},{24,16},{0,24},{9,1},{17,9},{25,17},{1,25},{10,2},{18... | collective-permute-start | bytes 294920 | tf_op jit(solution)/shard_map/ppermute | solution.py:337
  64.5 7.8 %collective-permute-start.2 = (bf16[40,4,256]{2,1,0:T(4,128)(2,1)S(1)}, bf16[40,4,256]{2,1,0:T(4,128)(2,1)S(1)}, u32[]{:S(2)}, u32[]{:S(2)}) collective-permute-start(bf16[40,4,256]{2,1,0:T(4,128)(2,1)S(1)} %get-tuple-element.10), channel_id=1, source_target_pairs={{0,1},{1,2},{2,3},{3,4},{4,5},{5,6},{6,7},{7,0},{8,9},{9,10},{10,1... | collective-permute-start | bytes 245768 | tf_op jit(solution)/shard_map/ppermute | solution.py:336
  65.3 7.0 %collective-permute-start.3 = (bf16[40,4,256]{2,1,0:T(4,128)(2,1)S(1)}, bf16[40,4,256]{2,1,0:T(4,128)(2,1)S(1)}, u32[]{:S(2)}, u32[]{:S(2)}) collective-permute-start(bf16[40,4,256]{2,1,0:T(4,128)(2,1)S(1)} %get-tuple-element.11), channel_id=1, source_target_pairs={{1,0},{2,1},{3,2},{4,3},{5,4},{6,5},{7,6},{0,7},{9,8},{10,9},{11,1... | collective-permute-start | bytes 245768 | tf_op jit(solution)/shard_map/ppermute | solution.py:337
  84.8 43.5 %copy-start.6 = (bf16[2,12288]{1,0:T(2,128)(2,1)S(1)}, bf16[2,12288]{1,0:T(2,128)(2,1)}, u32[]{:S(2)}) copy-start(bf16[2,12288]{1,0:T(2,128)(2,1)} %offset_ref.1) | copy-start | bytes 147460

commit v3 on v2

--- a/solution.py
+++ b/solution.py
@@ -5,6 +5,7 @@
 from jax import lax
 from jax.experimental import pallas as pl
 from jax.experimental.pallas import tpu as pltpu
+from jax.sharding import Mesh
 from jax.sharding import PartitionSpec as P
 
 HEAD_DIM = 32
@@ -54,7 +55,10 @@
     return -(-3 * pairs // 16) * 16
 
 
-def encode_blocks(capacity, devices, tile_ref, patch_ref, feat_ref, offset_ref, send_ref, slot_ref, count_ref):
+def encode_blocks(capacity, shape, place_ref, tile_ref, patch_ref, feat_ref, offset_ref, send_ref, slot_ref, count_ref):
+    lat, depth, width = shape
+    plane = lat * width
+    devices = plane * depth
     blocks = feat_ref.shape[1] // BLK
     feat_width = feat_ref.shape[0]
     pairs = capacity // 2
@@ -76,7 +80,11 @@
         tile = tile_ref[b]
         rank = count_ref[tile]
         count_ref[tile] = rank + 1
-        slot_ref[b] = tile * capacity + rank
+        lon = tile % (depth * width)
+        partner = (tile // (depth * width) * width + lon % width) ^ place_ref[0]
+        hop = (lon // width + depth - place_ref[1]) % depth
+        piece = jnp.where(hop == 0, partner, plane + partner * (depth - 1) + hop - 1)
+        slot_ref[b] = piece * capacity + rank
         pair = rank // 2
         half = rank % 2
         col = pl.multiple_of(b * BLK, BLK)
@@ -84,7 +92,7 @@
         weights = block_weights(offset_ref[:, pl.ds(col, BLK)].astype(jnp.float32))
         twice = jnp.concatenate([weights, weights], axis=0)
         sums = lax.dot_general(feat, twice, NT, preferred_element_type=jnp.float32)
-        row = pl.multiple_of(tile * chunk + pair * feat_width, 16)
+        row = pl.multiple_of(piece * chunk + pair * feat_width, 16)
         old = send_ref[pl.ds(row, feat_width), :].astype(jnp.float32)
         send_ref[pl.ds(row, feat_width), :] = jnp.where(
             lane_half == half, sums[:feat_width], old
@@ -93,7 +101,7 @@
         high = mass.astype(jnp.bfloat16).astype(jnp.float32)
         low = mass - high
         tag = (patch_ref[b] + 1).astype(jnp.float32)
-        row = pl.multiple_of(tile * chunk + pairs * feat_width, 16)
+        row = pl.multiple_of(piece * chunk + pairs * feat_width, 16)
         old = send_ref[pl.ds(row, meta), :].astype(jnp.float32)
         new = jnp.where(
             meta_row == pair,
@@ -114,58 +122,89 @@
     lax.fori_loop(0, blocks // unroll, body, 0)
 
 
-def start_tile(capacity, devices, id_ref, recv_ref, embed_ref, base_ref, start_ref, acc_ref):
+def dense_rows(pairs, feat_width):
+    return pairs * feat_width + -(-2 * pairs // 16) * 16
+
+
+def add_chunk(capacity, feat_width, id_ref, slot, recv_ref, base, acc_ref):
+    pairs = capacity // 2
+    first = lax.broadcasted_iota(jnp.int32, (feat_width + 8, LANES), 1) < CELLS
+    tags = recv_ref[base + pairs * feat_width : base + pairs * feat_width + meta_rows(pairs), :]
+    tags = tags.astype(jnp.float32)
+    for k in range(pairs):
+        at = base + k * feat_width
+        sums = recv_ref[at : at + feat_width, :].astype(jnp.float32)
+        mass = tags[k : k + 1] + tags[pairs + k : pairs + k + 1]
+        both = jnp.concatenate([sums, jnp.broadcast_to(mass, (8, LANES))], axis=0)
+        acc_ref[id_ref[slot + 2 * k]] += jnp.where(first, both, 0.0)
+        acc_ref[id_ref[slot + 2 * k + 1]] += jnp.where(first, 0.0, both)
+
+
+def paired(acc_ref, j):
+    first = lax.broadcasted_iota(jnp.int32, acc_ref.shape[1:], 1) < CELLS
+    even, odd = acc_ref[2 * j], acc_ref[2 * j + 1]
+    even, odd = even + pltpu.roll(even, CELLS, 1), odd + pltpu.roll(odd, CELLS, 1)
+    return jnp.where(first, even, odd)
+
+
+def gather_planes(capacity, plane, hops, feat_width, id_ref, *refs):
+    pieces, outs, acc_ref = refs[:plane], refs[plane : plane + hops], refs[plane + hops]
+    pairs = capacity // 2
+    chunk = pairs * feat_width + meta_rows(pairs)
+    patch_pairs = acc_ref.shape[1] // 2
+    acc_ref[...] = jnp.zeros_like(acc_ref)
+    for r in range(plane):
+        for hop in range(hops):
+            slot = (r * hops + hop) * capacity
+            add_chunk(capacity, feat_width, id_ref, slot, pieces[r], hop * chunk, acc_ref.at[hop])
+    for hop in range(hops):
+        masses = []
+        for j in range(patch_pairs):
+            pair = paired(acc_ref.at[hop], j)
+            outs[hop][j * feat_width : (j + 1) * feat_width, :] = pair[:feat_width].astype(
+                jnp.bfloat16
+            )
+            masses.append(pair[feat_width : feat_width + 1])
+        masses = jnp.concatenate(masses, axis=0)
+        high = masses.astype(jnp.bfloat16).astype(jnp.float32)
+        spare = outs[hop].shape[0] - patch_pairs * (feat_width + 2)
+        rows = [high, masses - high] + ([jnp.zeros((spare, LANES), jnp.float32)] if spare else [])
+        outs[hop][patch_pairs * feat_width :, :] = jnp.concatenate(rows, axis=0).astype(jnp.bfloat16)
+
+
+def start_tile(capacity, plane, hops, id_ref, *refs):
+    pieces, parts = refs[:plane], refs[plane : plane + hops]
+    embed_ref, base_ref, start_ref, acc_ref = refs[plane + hops :]
     feat_width, channels = embed_ref.shape
     tile_rows, tile_cols, _ = base_ref.shape
-    pairs = capacity // 2
-    meta = meta_rows(pairs)
-    chunk = pairs * feat_width + meta
     patch_rows, patch_cols = tile_rows // PATCH, tile_cols // PATCH
+    patch_pairs = patch_rows * patch_cols // 2
     acc_ref[...] = jnp.zeros_like(acc_ref)
-    first = lax.broadcasted_iota(jnp.int32, (feat_width + 8, LANES), 1) < CELLS
-
-    def gather(d, _):
-        base = pl.multiple_of(d * chunk, 16)
-        tags = recv_ref[pl.ds(base + pairs * feat_width, meta), :].astype(jnp.float32)
-        for k in range(pairs):
-            sums = recv_ref[pl.ds(base + k * feat_width, feat_width), :].astype(jnp.float32)
-            mass = tags[k : k + 1] + tags[pairs + k : pairs + k + 1]
-            both = jnp.concatenate([sums, jnp.broadcast_to(mass, (8, LANES))], axis=0)
-            slot = d * capacity + 2 * k
-            a = id_ref[slot]
-            acc_ref[a] += jnp.where(first, both, 0.0)
-            b = id_ref[slot + 1]
-            acc_ref[b] += jnp.where(first, 0.0, both)
-        return 0
-
-    lax.fori_loop(0, devices, gather, 0, unroll=4)
-    head = lax.broadcasted_iota(jnp.int32, (feat_width, LANES), 1) < CELLS
+    for r in range(plane):
+        add_chunk(capacity, feat_width, id_ref, r * capacity, pieces[r], 0, acc_ref)
     embed = embed_ref[...]
-
-    def encoded(p):
-        total = acc_ref[p]
-        total = total + pltpu.roll(total, CELLS, 1)
-        return total[:feat_width] / (1.0 + total[feat_width : feat_width + 1])
-
-    def lift(pr, _):
-        parts = []
-        for pc in range(0, patch_cols, 2):
-            p = pr * patch_cols + pc
-            pair = jnp.where(head, encoded(p), encoded(p + 1)).astype(jnp.bfloat16)
-            parts.append(lax.dot_general(pair, embed, TN, preferred_element_type=jnp.float32))
-        lifted = jnp.concatenate(parts, axis=0).reshape(patch_cols, PATCH, PATCH, channels)
+    mass_rows = [part[patch_pairs * feat_width :, :].astype(jnp.float32) for part in parts]
+    for pr in range(patch_rows):
+        lifted = []
+        for pc in range(patch_cols // 2):
+            j = pr * (patch_cols // 2) + pc
+            pair = paired(acc_ref, j)
+            sums, mass = pair[:feat_width], pair[feat_width : feat_width + 1]
+            for part, rows in zip(parts, mass_rows):
+                sums = sums + part[j * feat_width : (j + 1) * feat_width, :].astype(jnp.float32)
+                mass = mass + (rows[j : j + 1] + rows[patch_pairs + j : patch_pairs + j + 1])
+            encoded = (sums * (1.0 / (1.0 + mass))).astype(jnp.bfloat16)
+            lifted.append(lax.dot_general(encoded, embed, TN, preferred_element_type=jnp.float32))
+        lifted = jnp.concatenate(lifted, axis=0).reshape(patch_cols, PATCH, PATCH, channels)
         lifted = lifted.transpose(1, 0, 2, 3).reshape(PATCH, tile_cols, channels)
-        rows = pl.ds(pr * PATCH, PATCH)
+        rows = slice(pr * PATCH, (pr + 1) * PATCH)
         start_ref[rows] = (base_ref[rows].astype(jnp.float32) + lifted).astype(jnp.bfloat16)
-        return 0
-
-    lax.fori_loop(0, patch_rows, lift, 0, unroll=True)
 
 
 def grid_block(
-    capacity, devices, lat_cells, place_ref, id_ref, ext_ref, norm_ref, qkv_ref, out_ref, mlp_ref,
-    up_ref, down_ref, decode_ref, latent_ref, back_ref, turned_ref, key_ref, pack_ref, att_ref,
-    mixed_ref, proj_ref, score_ref, prob_ref,
+    lat_cells, place_ref, ext_ref, norm_ref, qkv_ref, out_ref, mlp_ref,
+    up_ref, down_ref, decode_ref, latent_ref, proj_ref, turned_ref, key_ref, pack_ref, att_ref,
+    mixed_ref, score_ref, prob_ref,
 ):
     ext_rows, ext_cols, channels = ext_ref.shape
     tile_rows, tile_cols, _ = latent_ref.shape
@@ -177,7 +216,6 @@
     group = 128
     heads = group // HEAD_DIM
     feat_width = decode_ref.shape[1]
-    pairs = capacity // 2
     scale = HEAD_DIM ** (-0.5) / math.log(2.0)
     norm_gain = norm_ref[...]
     turned_ref[:channels] = qkv_ref[:, :channels].T
@@ -204,7 +242,7 @@
         ).astype(jnp.bfloat16)
         edge = wr in (0, win_rows - 1)
         if edge:
-            top = place_ref[0] * tile_rows - margin + wr * WIN
+            top = place_ref[2] * tile_rows - margin + wr * WIN
             side = lambda r: (r >= 0).astype(jnp.int32) + (r >= lat_cells).astype(jnp.int32)
             bias = jnp.where(side(top + key_row) == side(top + query_row), 0.0, -1e30)
             bias = jnp.concatenate([bias] * heads, axis=1)
@@ -257,7 +295,6 @@
     for wr in range(win_rows):
         attend(wr)
     mlp_gain = mlp_ref[...]
-    first = lax.broadcasted_iota(jnp.int32, (feat_width, LANES), 1) < CELLS
 
     def by_patch(values):
         values = values.reshape(PATCH, patch_cols, PATCH, channels).transpose(1, 0, 2, 3)
@@ -280,25 +317,42 @@
         projected = jnp.dot(latent, decode_ref[...], preferred_element_type=jnp.float32)
         for pc in range(0, patch_cols, 2):
             turned = projected[pc * CELLS : pc * CELLS + LANES].T
-            swapped = pltpu.roll(turned, CELLS, 1)
-            proj_ref[pr * patch_cols + pc] = jnp.where(first, turned, swapped)
-            proj_ref[pr * patch_cols + pc + 1] = jnp.where(first, swapped, turned)
+            j = pr * (patch_cols // 2) + pc // 2
+            proj_ref[pl.ds(pl.multiple_of(j * feat_width, 16), feat_width), :] = turned.astype(
+                jnp.bfloat16
+            )
         return 0
 
     lax.fori_loop(0, patch_rows, finish, 0, unroll=True)
 
-    def reply(d, _):
-        for k in range(pairs):
-            slot = d * capacity + 2 * k
-            pair = jnp.where(first, proj_ref[id_ref[slot]], proj_ref[id_ref[slot + 1]])
-            row = pl.multiple_of((d * pairs + k) * feat_width, 16)
-            back_ref[pl.ds(row, feat_width), :] = pair.astype(jnp.bfloat16)
-        return 0
-
-    lax.fori_loop(0, devices, reply, 0)
-
-
-def decode_blocks(slot_ref, back_ref, offset_ref, out_ref):
+
+def reply_patches(capacity, plane, tiles, feat_width, id_ref, *refs):
+    tile_refs, out_ref, both_ref = refs[:tiles], refs[tiles], refs[tiles + 1]
+    pairs = capacity // 2
+    first = lax.broadcasted_iota(jnp.int32, (feat_width, LANES), 1) < CELLS
+    for t in range(tiles):
+        for j in range(both_ref.shape[1] // 2):
+            pair = tile_refs[t][j * feat_width : (j + 1) * feat_width, :].astype(jnp.float32)
+            swapped = pltpu.roll(pair, CELLS, 1)
+            both_ref[t, 2 * j] = jnp.where(first, pair, swapped)
+            both_ref[t, 2 * j + 1] = jnp.where(first, swapped, pair)
+    for r in range(plane):
+        for t in range(tiles):
+            for k in range(pairs):
+                slot = (r * tiles + t) * capacity + 2 * k
+                pair = jnp.where(
+                    first, both_ref[t, id_ref[slot]], both_ref[t, id_ref[slot + 1]]
+                )
+                at = ((r * tiles + t) * pairs + k) * feat_width
+                out_ref[at : at + feat_width, :] = pair.astype(jnp.bfloat16)
+
+
+def decode_blocks(slot_ref, offset_ref, *refs):
+    pieces, out_ref, back_ref = refs[:-2], refs[-2], refs[-1]
+    at = 0
+    for piece in pieces:
+        back_ref[at : at + piece.shape[0], :] = piece[...]
+        at += piece.shape[0]
     feat_width, count = out_ref.shape
     blocks = count // BLK
 
@@ -328,7 +382,7 @@
 
 def with_halo(array, sides, width):
     for axis, dim in sides:
-        size, length = (lax.axis_size(axis), array.shape[dim])
+        size, length = (axis_count(axis), array.shape[dim])
         up = [(i, (i + 1) % size) for i in range(size)]
         down = [(j, i) for i, j in up]
         last = lax.slice_in_dim(array, length - width, length, axis=dim)
@@ -337,6 +391,24 @@
         after = lax.ppermute(initial, axis, down)
         array = jnp.concatenate([before, array, after], axis=dim)
     return array
+
+
+def axis_count(axes):
+    axes = axes if isinstance(axes, tuple) else (axes,)
+    return math.prod([lax.axis_size(axis) for axis in axes])
+
+
+def swap_in_plane(arrays):
+    plane = len(arrays)
+    return arrays[:1] + [
+        lax.ppermute(arrays[r], ("lat", "x"), [(i, i ^ r) for i in range(plane)])
+        for r in range(1, plane)
+    ]
+
+
+def shift_planes(array, hop):
+    depth = lax.axis_size("z")
+    return lax.ppermute(array, "z", [(i, (i + hop) % depth) for i in range(depth)])
 
 
 def local(
@@ -354,9 +426,9 @@
     down_weight,
     decode_weight,
 ):
-    lat_devices = lax.axis_size("lat")
-    lon_devices = lax.axis_size("lon")
-    devices = lat_devices * lon_devices
+    lat, depth, width = (lax.axis_size(axis) for axis in ("lat", "z", "x"))
+    plane, hops = lat * width, depth - 1
+    devices = plane * depth
     feat_width, obs_count = obs_feat.shape
     blocks = obs_count // BLK
     capacity = max(2, 2 * blocks // devices)
@@ -365,49 +437,75 @@
     tile_rows, tile_cols, channels = grid_base.shape
     patch_total = (tile_rows // PATCH) * (tile_cols // PATCH)
     chunk = pairs * feat_width + meta_rows(pairs)
+    dense = dense_rows(patch_total // 2, feat_width)
+    lat_id = lax.axis_index("lat").astype(jnp.int32)
+    place = jnp.stack(
+        [lat_id * width + lax.axis_index("x"), lax.axis_index("z"), lat_id]
+    ).astype(jnp.int32)
 
     send, slots = pl.pallas_call(
-        lambda *refs: encode_blocks(capacity, devices, *refs),
+        lambda *refs: encode_blocks(capacity, (lat, depth, width), *refs),
         out_shape=(
             jax.ShapeDtypeStruct((devices * chunk, LANES), jnp.bfloat16),
             jax.ShapeDtypeStruct((blocks,), jnp.int32),
         ),
-        in_specs=[smem(), smem(), vmem(), vmem()],
+        in_specs=[smem(), smem(), smem(), vmem(), vmem()],
         out_specs=(vmem(), smem()),
         scratch_shapes=[pltpu.SMEM((devices,), jnp.int32)],
         compiler_params=params(8),
         name="encode_blocks",
-    )(block_tile.reshape(blocks), block_patch, obs_feat, obs_offset)
-
-    recv = lax.all_to_all(
-        send.reshape(devices, chunk, LANES), ("lat", "lon"), split_axis=0, concat_axis=0, tiled=True
-    )
-    tags = recv[:, pairs * feat_width + 2 * pairs : pairs * feat_width + 3 * pairs, 0 :: CELLS]
-    ids = jnp.clip(tags.astype(jnp.float32).astype(jnp.int32) - 1, 0, patch_total - 1).reshape(-1)
+    )(place, block_tile.reshape(blocks), block_patch, obs_feat, obs_offset)
+
+    def cut(array, start, rows):
+        return [
+            lax.slice_in_dim(array, start + r * rows, start + (r + 1) * rows) for r in range(plane)
+        ]
+
+    def ids_of(pieces, tiles):
+        at = pairs * feat_width + 2 * pairs
+        tags = jnp.stack(
+            [p.reshape(tiles, chunk, LANES)[:, at : at + pairs, 0::CELLS] for p in pieces]
+        )
+        ids = tags.astype(jnp.float32).astype(jnp.int32) - 1
+        return jnp.clip(ids, 0, patch_total - 1).reshape(-1)
+
+    far = swap_in_plane(cut(send, plane * chunk, hops * chunk))
+    near = swap_in_plane(cut(send, 0, chunk))
+    far_ids = ids_of(far, hops)
+    sums = pl.pallas_call(
+        lambda *refs: gather_planes(capacity, plane, hops, feat_width, *refs),
+        out_shape=[jax.ShapeDtypeStruct((dense, LANES), jnp.bfloat16)] * hops,
+        in_specs=[smem()] + [vmem()] * plane,
+        out_specs=[vmem()] * hops,
+        scratch_shapes=[pltpu.VMEM((hops, patch_total, feat_width + 8, LANES), jnp.float32)],
+        compiler_params=params(8),
+        name="gather_planes",
+    )(far_ids, *far)
+    parts = [shift_planes(sums[hop], hop + 1) for hop in range(hops)]
+    near_ids = ids_of(near, 1)
 
     start = pl.pallas_call(
-        lambda *refs: start_tile(capacity, devices, *refs),
+        lambda *refs: start_tile(capacity, plane, hops, *refs),
         out_shape=jax.ShapeDtypeStruct(grid_base.shape, jnp.bfloat16),
-        in_specs=[smem(), vmem(), vmem(), vmem()],
+        in_specs=[smem()] + [vmem()] * (plane + hops + 2),
         out_specs=vmem(),
         scratch_shapes=[pltpu.VMEM((patch_total, feat_width + 8, LANES), jnp.float32)],
         compiler_params=params(8),
         name="start_tile",
-    )(ids, recv.reshape(devices * chunk, LANES), embed_weight, grid_base)
+    )(near_ids, *near, *parts, embed_weight, grid_base)
 
     margin = WIN // 2
-    ext = with_halo(start, (("lat", 0), ("lon", 1)), margin).astype(jnp.float32)
+    ext = with_halo(start, (("lat", 0), (("z", "x"), 1)), margin).astype(jnp.float32)
     ext_rows, ext_cols, _ = ext.shape
     padded = -(-ext_cols // (2 * WIN)) * LANES
-    place = lax.axis_index("lat").astype(jnp.int32).reshape(1)
-
-    latent, back = pl.pallas_call(
-        lambda *refs: grid_block(capacity, devices, tile_rows * lat_devices, *refs),
+
+    latent, projected = pl.pallas_call(
+        lambda *refs: grid_block(tile_rows * lat, *refs),
         out_shape=(
             jax.ShapeDtypeStruct(grid_base.shape, jnp.bfloat16),
-            jax.ShapeDtypeStruct((devices * pairs * feat_width, LANES), jnp.bfloat16),
+            jax.ShapeDtypeStruct((patch_total // 2 * feat_width, LANES), jnp.bfloat16),
         ),
-        in_specs=[smem(), smem()] + [vmem()] * 8,
+        in_specs=[smem()] + [vmem()] * 8,
         out_specs=(vmem(), vmem()),
         scratch_shapes=[
             pltpu.VMEM((2 * channels, channels), jnp.bfloat16),
@@ -415,7 +513,6 @@
             pltpu.VMEM((2 * channels, padded), jnp.bfloat16),
             pltpu.VMEM((channels, padded), jnp.bfloat16),
             pltpu.VMEM((ext_rows, ext_cols, channels), jnp.float32),
-            pltpu.VMEM((patch_total, feat_width, LANES), jnp.float32),
             pltpu.VMEM((padded * channels // LANES // 128, WIN * WIN, 4 * LANES), jnp.float32),
             pltpu.VMEM((padded * channels // LANES // 128, LANES, 4 * LANES), jnp.bfloat16),
         ],
@@ -423,7 +520,6 @@
         name="grid_block",
     )(
         place,
-        ids,
         ext,
         norm_gain.reshape(1, channels),
         qkv_weight,
@@ -434,32 +530,48 @@
         decode_weight,
     )
 
-    returned = lax.all_to_all(
-        back.reshape(devices, pairs * feat_width, LANES),
-        ("lat", "lon"),
-        split_axis=0,
-        concat_axis=0,
-        tiled=True,
-    )
+    def reply(ids, tiles, name):
+        count = len(tiles)
+        rows = count * pairs * feat_width
+        out = pl.pallas_call(
+            lambda *refs: reply_patches(capacity, plane, count, feat_width, *refs),
+            out_shape=jax.ShapeDtypeStruct((plane * rows, LANES), jnp.bfloat16),
+            in_specs=[smem()] + [vmem()] * count,
+            out_specs=vmem(),
+            scratch_shapes=[pltpu.VMEM((count, patch_total, feat_width, LANES), jnp.float32)],
+            compiler_params=params(8),
+            name=name,
+        )(ids, *tiles)
+        return swap_in_plane(cut(out, 0, rows))
+
+    others = [shift_planes(projected, -hop) for hop in range(1, depth)]
+    near_back = reply(near_ids, [projected], "reply_near")
+    far_back = reply(far_ids, others, "reply_far")
+
     obs_out = pl.pallas_call(
         decode_blocks,
         out_shape=jax.ShapeDtypeStruct((feat_width, obs_count), jnp.bfloat16),
-        in_specs=[smem(), vmem(), vmem()],
+        in_specs=[smem(), vmem()] + [vmem()] * (2 * plane),
         out_specs=vmem(),
-        compiler_params=params(8),
+        scratch_shapes=[pltpu.VMEM((devices * pairs * feat_width, LANES), jnp.bfloat16)],
+        compiler_params=params(10),
         name="decode_blocks",
-    )(slots, returned.reshape(devices * pairs * feat_width, LANES), obs_offset)
+    )(slots, obs_offset, *near_back, *far_back)
     return (latent, obs_out)
 
 
 def solution(mesh):
+    lat, lon = mesh.devices.shape
+    width = lat // 2 if lat % 2 == 0 and lon % (lat // 2) == 0 else 1
+    split = Mesh(mesh.devices.reshape(lat, lon // width, width), ("lat", "z", "x"))
+    every = ("lat", "z", "x")
     placed = (
-        P(None, ("lat", "lon")),
-        P(None, ("lat", "lon")),
-        P(("lat", "lon"), None),
-        P(("lat", "lon")),
-        P(),
-        P("lat", "lon", None),
+        P(None, every),
+        P(None, every),
+        P(every, None),
+        P(every),
+        P(),
+        P("lat", ("z", "x"), None),
         P(),
         P(),
         P(),
@@ -470,8 +582,8 @@
     )
     return jax.shard_map(
         local,
-        mesh=mesh,
+        mesh=split,
         in_specs=placed,
-        out_specs=(P("lat", "lon", None), P(None, ("lat", "lon"))),
+        out_specs=(P("lat", ("z", "x"), None), P(None, every)),
         check_vma=False,
     )

time: 132 us -> 145 us (1.098); the launches traced: 132 us -> 143 us
  blocking collectives: 92.3 us -> 0 us
  waiting for transfers between devices: 5.29 us -> 54.7 us
  starting transfers between devices: 6.58 us -> 51.8 us
  local copies, waits for them, and re-layouts: 4.11 us -> 9.32 us
  Pallas kernels: 22.5 us -> 25.6 us
    all_to_all x2 -> x0, blocking collectives: 92.3 us -> none  [the longest x1 48.7 us: local(): lax.all_to_all(send.reshape(devices, chunk, LANES), ('lat', 'lon'), split...]
    ppermute x0 -> x34, waiting for transfers between devices: none -> 49.5 us  [the longest x28 26.5 us: swap_in_plane(): lax.ppermute(arrays[r], ('lat', 'x'), [(i, i ^ r) for i in range(plane)])]
    ppermute x0 -> x34, starting transfers between devices: none -> 41.9 us  [the longest x28 31.5 us: swap_in_plane(): lax.ppermute(arrays[r], ('lat', 'x'), [(i, i ^ r) for i in range(plane)])]
    pallas_call x3 -> x6, Pallas kernels: 18.7 us -> 21.7 us  [the longest x1 11.1 us: local(): pl.pallas_call(lambda *refs: grid_block(tile_rows * lat, *refs), out_shap...]
    another operation x0 -> x18, local copies, waits for them, and re-layouts: none -> 2.35 us  [ids_of(): jnp.stack([p.reshape(tiles, chunk, LANES)[:, at:at + pairs, 0::CELLS] for...]
    ppermute x2, starting transfers between devices: 5.66 us -> 7.68 us  [with_halo(): after = lax.ppermute(initial, axis, down)]
    slice x1 -> x20, local copies, waits for them, and re-layouts: 0.28 us -> 1.8 us  [the longest x16 1.57 us: ids_of(): p.reshape(tiles, chunk, LANES)[:, at:at + pairs, 0::CELLS]]
    unnamed x29 -> x37, local copies, waits for them, and re-layouts: 3.68 us -> 4.66 us
  transfers between devices with their start and end apart: 4 -> 38, of which waited for: 2 -> 17; matrix products, arithmetic and copies ran while one was open for 0% -> 3% of each run, Pallas kernels for 0% -> 1%
where the time goes in v3:
time: 145 us; the launch traced here: 143 us
  waiting for transfers between devices  54.7 us (38%)
  starting transfers between devices  51.8 us (36%)
  Pallas kernels  25.6 us (18%)
  local copies, waits for them, and re-layouts  9.32 us (6%)
    ppermute x28, starting transfers between devices, swap_in_plane(): lax.ppermute(arrays[r], ('lat', 'x'), [(i, i ^ r) for i in range(plane)])  31.5 us
    ppermute x28, waiting for transfers between devices, swap_in_plane(): lax.ppermute(arrays[r], ('lat', 'x'), [(i, i ^ r) for i in range(plane)])  26.5 us
    ppermute x6, waiting for transfers between devices, shift_planes(): lax.ppermute(array, 'z', [(i, (i + hop) % depth) for i in range(depth)])  23 us
    pallas_call x1, Pallas kernels, local(): pl.pallas_call(lambda *refs: grid_block(tile_rows * lat, *refs), out_shap...  11.1 us
    ppermute x6, starting transfers between devices, shift_planes(): lax.ppermute(array, 'z', [(i, (i + hop) % depth) for i in range(depth)])  10.4 us
    ppermute x2, starting transfers between devices, with_halo(): after = lax.ppermute(initial, axis, down)  7.68 us
    pallas_call x1, Pallas kernels, local(): pl.pallas_call(lambda *refs: encode_blocks(capacity, (lat, depth, width),...  4.94 us
    ppermute x2, waiting for transfers between devices, with_halo(): before = lax.ppermute(last, axis, up)  4.84 us
  transfers between devices with their start and end apart: 38, of which 17 were waited for; matrix products, arithmetic and copies ran while one was open for 3% of the time, Pallas kernels for 1%

profile of v3, /device:TPU:0, one launch (start us, length us, event | category | flops | bytes accessed | tf_op | source)
XLA Modules:
  0.0 143.0 jit_solution(3519827184455985833)
XLA Ops:
  4.2 4.9 %encode_blocks.1 = (bf16[6656,128]{1,0:T(8,128)(2,1)S(1)}, s32[96]{0:T(128)S(1)}) custom-call(s32[3]{0:T(128)S(1)} %pad_add_fusion.refs_0_, s32[96]{0:T(128)S(1)} %bitcast.58, s32[96]{0:T(128)S(1)} %copy-done.12, bf16[64,12288]{1,0:T(8,128)(2,1)S(1)} %copy-done, bf16[2,12288]{1,0:T(2,128)(2,1)S(1)} %copy-done.5), custom_call_target="tpu_custom_call" | custom-call | tf_op jit(solution)/shard_map/encode_blocks/pallas_call | solution.py:446
  9.3 3.4 %collective-permute-start.6 = (bf16[208,128]{1,0:T(8,128)(2,1)S(1)}, bf16[208,128]{1,0:T(8,128)(2,1)S(1)}, u32[]{:S(2)}, u32[]{:S(2)}) collective-permute-start(bf16[208,128]{1,0:T(8,128)(2,1)S(1)} %get-tuple-element.26), channel_id=1, source_target_pairs={{0,25},{1,24},{8,17},{9,16},{16,9},{17,8},{24,1},{25,0},{2,27},{3,... | collective-permute-start | bytes 159752 | tf_op jit(solution)/shard_map/ppermute | solution.py:404
  14.6 3.1 %collective-permute-start.4 = (bf16[208,128]{1,0:T(8,128)(2,1)S(1)}, bf16[208,128]{1,0:T(8,128)(2,1)S(1)}, u32[]{:S(2)}, u32[]{:S(2)}) collective-permute-start(bf16[208,128]{1,0:T(8,128)(2,1)S(1)} %get-tuple-element.28), channel_id=1, source_target_pairs={{0,17},{1,16},{8,25},{9,24},{16,1},{17,0},{24,9},{25,8},{2,19},{3,... | collective-permute-start | bytes 159752 | tf_op jit(solution)/shard_map/ppermute | solution.py:404
  18.3 5.9 %collective-permute-done.5.refs_7_ = bf16[208,128]{1,0:T(8,128)(2,1)S(1)} collective-permute-done((bf16[208,128]{1,0:T(8,128)(2,1)S(1)}, bf16[208,128]{1,0:T(8,128)(2,1)S(1)}, u32[]{:S(2)}, u32[]{:S(2)}) %collective-permute-start.5) | collective-permute-done | bytes 53280 | tf_op jit(solution)/shard_map/ppermute | solution.py:404
  28.3 2.9 %collective-permute-start.11 = (bf16[624,128]{1,0:T(8,128)(2,1)S(1)}, bf16[624,128]{1,0:T(8,128)(2,1)S(1)}, u32[]{:S(2)}, u32[]{:S(2)}) collective-permute-start(bf16[624,128]{1,0:T(8,128)(2,1)S(1)} %get-tuple-element.18), channel_id=1, source_target_pairs={{0,17},{1,16},{8,25},{9,24},{16,1},{17,0},{24,9},{25,8},{2,19},{3,... | collective-permute-start | bytes 479240 | tf_op jit(solution)/shard_map/ppermute | solution.py:404
  37.2 2.1 %collective-permute-done.10.refs_5_ = bf16[624,128]{1,0:T(8,128)(2,1)S(1)} collective-permute-done((bf16[624,128]{1,0:T(8,128)(2,1)S(1)}, bf16[624,128]{1,0:T(8,128)(2,1)S(1)}, u32[]{:S(2)}, u32[]{:S(2)}) %collective-permute-start.10) | collective-permute-done | bytes 159776 | tf_op jit(solution)/shard_map/ppermute | solution.py:404
  40.4 2.3 %collective-permute-done.7.refs_2_ = bf16[624,128]{1,0:T(8,128)(2,1)S(1)} collective-permute-done((bf16[624,128]{1,0:T(8,128)(2,1)S(1)}, bf16[624,128]{1,0:T(8,128)(2,1)S(1)}, u32[]{:S(2)}, u32[]{:S(2)}) %collective-permute-start.7) | collective-permute-done | bytes 159776 | tf_op jit(solution)/shard_map/ppermute | solution.py:404
  43.6 2.4 %gather_planes.1 = (bf16[800,128]{1,0:T(8,128)(2,1)S(1)}, bf16[800,128]{1,0:T(8,128)(2,1)S(1)}, bf16[800,128]{1,0:T(8,128)(2,1)S(1)}) custom-call(s32[144]{0:T(256)S(1)} %min.25.refs_0_, bf16[624,128]{1,0:T(8,128)(2,1)S(1)} %get-tuple-element.23.refs_1_, bf16[624,128]{1,0:T(8,128)(2,1)S(1)} %collective-permute-done.7.refs_2_, ...), custom_call_target="tpu_custom_call" | custom-call | tf_op jit(solution)/shard_map/gather_planes/pallas_call | solution.py:475
  47.6 2.6 %collective-permute-start.15 = (bf16[800,128]{1,0:T(8,128)(2,1)S(1)}, bf16[800,128]{1,0:T(8,128)(2,1)S(1)}, u32[]{:S(2)}, u32[]{:S(2)}) collective-permute-start(bf16[800,128]{1,0:T(8,128)(2,1)S(1)} %get-tuple-element.11), channel_id=1, source_target_pairs={{0,4},{2,6},{4,0},{6,2},{1,5},{3,7},{5,1},{7,3},{8,12},{10,14},{12... | collective-permute-start | bytes 614408 | tf_op jit(solution)/shard_map/ppermute | solution.py:411
  51.8 4.2 %collective-permute-done.14.refs_9_ = bf16[800,128]{1,0:T(8,128)(2,1)S(1)} collective-permute-done((bf16[800,128]{1,0:T(8,128)(2,1)S(1)}, bf16[800,128]{1,0:T(8,128)(2,1)S(1)}, u32[]{:S(2)}, u32[]{:S(2)}) %collective-permute-start.14) | collective-permute-done | bytes 204832 | tf_op jit(solution)/shard_map/ppermute | solution.py:411
  55.9 7.0 %collective-permute-done.15.refs_10_ = bf16[800,128]{1,0:T(8,128)(2,1)S(1)} collective-permute-done((bf16[800,128]{1,0:T(8,128)(2,1)S(1)}, bf16[800,128]{1,0:T(8,128)(2,1)S(1)}, u32[]{:S(2)}, u32[]{:S(2)}) %collective-permute-start.15) | collective-permute-done | bytes 204832 | tf_op jit(solution)/shard_map/ppermute | solution.py:411
  66.4 2.3 %collective-permute-done.17 = bf16[4,48,256]{2,1,0:T(8,128)(2,1)S(1)} collective-permute-done((bf16[4,48,256]{2,1,0:T(8,128)(2,1)S(1)}, bf16[4,48,256]{2,1,0:T(8,128)(2,1)S(1)}, u32[]{:S(2)}, u32[]{:S(2)}) %collective-permute-start.17) | collective-permute-done | bytes 98336 | tf_op jit(solution)/shard_map/ppermute | solution.py:390
  69.1 2.2 %collective-permute-start.19 = (bf16[40,4,256]{2,1,0:T(4,128)(2,1)S(1)}, bf16[40,4,256]{2,1,0:T(4,128)(2,1)S(1)}, u32[]{:S(2)}, u32[]{:S(2)}) collective-permute-start(bf16[40,4,256]{2,1,0:T(4,128)(2,1)S(1)} %get-tuple-element.41), channel_id=1, source_target_pairs={{0,1},{1,2},{2,3},{3,4},{4,5},{5,6},{6,7},{7,0},{8,9},{9,10},{10,1... | collective-permute-start | bytes 245768 | tf_op jit(solution)/shard_map/ppermute | solution.py:390
  71.3 6.0 %collective-permute-start.20 = (bf16[40,4,256]{2,1,0:T(4,128)(2,1)S(1)}, bf16[40,4,256]{2,1,0:T(4,128)(2,1)S(1)}, u32[]{:S(2)}, u32[]{:S(2)}) collective-permute-start(bf16[40,4,256]{2,1,0:T(4,128)(2,1)S(1)} %get-tuple-element.42), channel_id=1, source_target_pairs={{1,0},{2,1},{3,2},{4,3},{5,4},{6,5},{7,6},{0,7},{9,8},{10,9},{11,1... | collective-permute-start | bytes 245768 | tf_op jit(solution)/shard_map/ppermute | solution.py:391
  77.4 2.5 %collective-permute-done.19 = bf16[40,4,256]{2,1,0:T(4,128)(2,1)S(1)} collective-permute-done((bf16[40,4,256]{2,1,0:T(4,128)(2,1)S(1)}, bf16[40,4,256]{2,1,0:T(4,128)(2,1)S(1)}, u32[]{:S(2)}, u32[]{:S(2)}) %collective-permute-start.19) | collective-permute-done | bytes 81952 | tf_op jit(solution)/shard_map/ppermute | solution.py:390
  80.5 11.1 %grid_block.1 = (bf16[32,48,256]{2,1,0:T(8,128)(2,1)}, bf16[768,128]{1,0:T(8,128)(2,1)S(1)}) custom-call(s32[3]{0:T(128)S(1)} %pad_add_fusion.refs_0_, f32[40,56,256]{2,1,0:T(8,128)S(1)} %maximum_convert_fusion.refs_1_, f32[1,256]{1,0:T(1,128)S(1)} %bitcast.56, bf16[256,768]{1,0:T(8,128)(2,1)S(1)} %copy-done.4, bf16[256,256]{1,0:T(8,128)(2,1)S(1)} %copy-done.7, ...), custom_call_target="tpu_custom_call" | custom-call | tf_op jit(solution)/shard_map/grid_block/pallas_call | solution.py:502
  91.6 2.0 %collective-permute-start.30 = (bf16[768,128]{1,0:T(8,128)(2,1)S(1)}, bf16[768,128]{1,0:T(8,128)(2,1)S(1)}, u32[]{:S(2)}, u32[]{:S(2)}) collective-permute-start(bf16[768,128]{1,0:T(8,128)(2,1)S(1)} %get-tuple-element.15.refs_1_), channel_id=1, source_target_pairs={{0,2},{2,4},{4,6},{6,0},{1,3},{3,5},{5,7},{7,1},{8,10},{10,12},{12... | collective-permute-start | bytes 589832 | tf_op jit(solution)/shard_map/ppermute | solution.py:411
  97.3 4.0 %collective-permute-done.30.refs_3_ = bf16[768,128]{1,0:T(8,128)(2,1)S(1)} collective-permute-done((bf16[768,128]{1,0:T(8,128)(2,1)S(1)}, bf16[768,128]{1,0:T(8,128)(2,1)S(1)}, u32[]{:S(2)}, u32[]{:S(2)}) %collective-permute-start.30) | collective-permute-done | bytes 196640 | tf_op jit(solution)/shard_map/ppermute | solution.py:411
  101.3 7.8 %collective-permute-done.29.refs_2_ = bf16[768,128]{1,0:T(8,128)(2,1)S(1)} collective-permute-done((bf16[768,128]{1,0:T(8,128)(2,1)S(1)}, bf16[768,128]{1,0:T(8,128)(2,1)S(1)}, u32[]{:S(2)}, u32[]{:S(2)}) %collective-permute-start.29) | collective-permute-done | bytes 196640 | tf_op jit(solution)/shard_map/ppermute | solution.py:411
  115.8 6.3 %collective-permute-done.26.refs_6_ = bf16[192,128]{1,0:T(8,128)(2,1)S(1)} collective-permute-done((bf16[192,128]{1,0:T(8,128)(2,1)S(1)}, bf16[192,128]{1,0:T(8,128)(2,1)S(1)}, u32[]{:S(2)}, u32[]{:S(2)}) %collective-permute-start.26) | collective-permute-done | bytes 49184 | tf_op jit(solution)/shard_map/ppermute | solution.py:404
  131.0 2.2 %collective-permute-done.35.refs_13_ = bf16[576,128]{1,0:T(8,128)(2,1)S(1)} collective-permute-done((bf16[576,128]{1,0:T(8,128)(2,1)S(1)}, bf16[576,128]{1,0:T(8,128)(2,1)S(1)}, u32[]{:S(2)}, u32[]{:S(2)}) %collective-permute-start.35) | collective-permute-done | bytes 147488 | tf_op jit(solution)/shard_map/ppermute | solution.py:404
  133.2 2.7 %collective-permute-done.34.refs_12_ = bf16[576,128]{1,0:T(8,128)(2,1)S(1)} collective-permute-done((bf16[576,128]{1,0:T(8,128)(2,1)S(1)}, bf16[576,128]{1,0:T(8,128)(2,1)S(1)}, u32[]{:S(2)}, u32[]{:S(2)}) %collective-permute-start.34) | collective-permute-done | bytes 147488 | tf_op jit(solution)/shard_map/ppermute | solution.py:404
  136.3 2.9 %collective-permute-done.31.refs_9_ = bf16[576,128]{1,0:T(8,128)(2,1)S(1)} collective-permute-done((bf16[576,128]{1,0:T(8,128)(2,1)S(1)}, bf16[576,128]{1,0:T(8,128)(2,1)S(1)}, u32[]{:S(2)}, u32[]{:S(2)}) %collective-permute-start.31) | collective-permute-done | bytes 147488 | tf_op jit(solution)/shard_map/ppermute | solution.py:404
  139.1 3.8 %decode_blocks.1 = bf16[64,12288]{1,0:T(8,128)(2,1)} custom-call(s32[96]{0:T(128)S(1)} %get-tuple-element.14.slot_ref, bf16[2,12288]{1,0:T(2,128)(2,1)S(1)} %copy-done.6, bf16[192,128]{1,0:T(8,128)(2,1)S(1)} %get-tuple-element.52.refs_0_, bf16[192,128]{1,0:T(8,128)(2,1)S(1)} %collective-permute-done.21.refs_1_, ...), custom_call_target="tpu_custom_call" | custom-call | tf_op jit(solution)/shard_map/decode_blocks/pallas_call | solution.py:551
  (144 shorter events, 45.5 us)
Async XLA Ops:
  9.3 8.5 %collective-permute-start.6 = (bf16[208,128]{1,0:T(8,128)(2,1)S(1)}, bf16[208,128]{1,0:T(8,128)(2,1)S(1)}, u32[]{:S(2)}, u32[]{:S(2)}) collective-permute-start(bf16[208,128]{1,0:T(8,128)(2,1)S(1)} %get-tuple-element.26), channel_id=1, source_target_pairs={{0,25},{1,24},{8,17},{9,16},{16,9},{17,8},{24,1},{25,0},{2,27},{3,... | collective-permute-start | bytes 159752 | tf_op jit(solution)/shard_map/ppermute | solution.py:404
  12.7 19.0 %collective-permute-start.13 = (bf16[624,128]{1,0:T(8,128)(2,1)S(1)}, bf16[624,128]{1,0:T(8,128)(2,1)S(1)}, u32[]{:S(2)}, u32[]{:S(2)}) collective-permute-start(bf16[624,128]{1,0:T(8,128)(2,1)S(1)} %get-tuple-element.16), channel_id=1, source_target_pairs={{0,25},{1,24},{8,17},{9,16},{16,9},{17,8},{24,1},{25,0},{2,27},{3,... | collective-permute-start | bytes 479240 | tf_op jit(solution)/shard_map/ppermute | solution.py:404
  12.8 19.1 %collective-permute-start.12 = (bf16[624,128]{1,0:T(8,128)(2,1)S(1)}, bf16[624,128]{1,0:T(8,128)(2,1)S(1)}, u32[]{:S(2)}, u32[]{:S(2)}) collective-permute-start(bf16[624,128]{1,0:T(8,128)(2,1)S(1)} %get-tuple-element.17), channel_id=1, source_target_pairs={{0,24},{1,25},{8,16},{9,17},{16,8},{17,9},{24,0},{25,1},{2,26},{3,... | collective-permute-start | bytes 479240 | tf_op jit(solution)/shard_map/ppermute | solution.py:404
  14.5 9.7 %collective-permute-start.5 = (bf16[208,128]{1,0:T(8,128)(2,1)S(1)}, bf16[208,128]{1,0:T(8,128)(2,1)S(1)}, u32[]{:S(2)}, u32[]{:S(2)}) collective-permute-start(bf16[208,128]{1,0:T(8,128)(2,1)S(1)} %get-tuple-element.27), channel_id=1, source_target_pairs={{0,24},{1,25},{8,16},{9,17},{16,8},{17,9},{24,0},{25,1},{2,26},{3,... | collective-permute-start | bytes 159752 | tf_op jit(solution)/shard_map/ppermute | solution.py:404
  14.6 11.5 %collective-permute-start.4 = (bf16[208,128]{1,0:T(8,128)(2,1)S(1)}, bf16[208,128]{1,0:T(8,128)(2,1)S(1)}, u32[]{:S(2)}, u32[]{:S(2)}) collective-permute-start(bf16[208,128]{1,0:T(8,128)(2,1)S(1)} %get-tuple-element.28), channel_id=1, source_target_pairs={{0,17},{1,16},{8,25},{9,24},{16,1},{17,0},{24,9},{25,8},{2,19},{3,... | collective-permute-start | bytes 159752 | tf_op jit(solution)/shard_map/ppermute | solution.py:404
  17.8 8.8 %collective-permute-start.3 = (bf16[208,128]{1,0:T(8,128)(2,1)S(1)}, bf16[208,128]{1,0:T(8,128)(2,1)S(1)}, u32[]{:S(2)}, u32[]{:S(2)}) collective-permute-start(bf16[208,128]{1,0:T(8,128)(2,1)S(1)} %get-tuple-element.29), channel_id=1, source_target_pairs={{0,16},{1,17},{8,24},{9,25},{16,0},{17,1},{24,8},{25,9},{2,18},{3,... | collective-permute-start | bytes 159752 | tf_op jit(solution)/shard_map/ppermute | solution.py:404
  28.3 8.5 %collective-permute-start.11 = (bf16[624,128]{1,0:T(8,128)(2,1)S(1)}, bf16[624,128]{1,0:T(8,128)(2,1)S(1)}, u32[]{:S(2)}, u32[]{:S(2)}) collective-permute-start(bf16[624,128]{1,0:T(8,128)(2,1)S(1)} %get-tuple-element.18), channel_id=1, source_target_pairs={{0,17},{1,16},{8,25},{9,24},{16,1},{17,0},{24,9},{25,8},{2,19},{3,... | collective-permute-start | bytes 479240 | tf_op jit(solution)/shard_map/ppermute | solution.py:404
  32.0 10.8 %collective-permute-start.7 = (bf16[624,128]{1,0:T(8,128)(2,1)S(1)}, bf16[624,128]{1,0:T(8,128)(2,1)S(1)}, u32[]{:S(2)}, u32[]{:S(2)}) collective-permute-start(bf16[624,128]{1,0:T(8,128)(2,1)S(1)} %get-tuple-element.22), channel_id=1, source_target_pairs={{0,1},{1,0},{8,9},{9,8},{16,17},{17,16},{24,25},{25,24},{2,3},{3,2... | collective-permute-start | bytes 479240 | tf_op jit(solution)/shard_map/ppermute | solution.py:404
  46.0 10.0 %collective-permute-start.14 = (bf16[800,128]{1,0:T(8,128)(2,1)S(1)}, bf16[800,128]{1,0:T(8,128)(2,1)S(1)}, u32[]{:S(2)}, u32[]{:S(2)}) collective-permute-start(bf16[800,128]{1,0:T(8,128)(2,1)S(1)} %get-tuple-element.10), channel_id=1, source_target_pairs={{0,2},{2,4},{4,6},{6,0},{1,3},{3,5},{5,7},{7,1},{8,10},{10,12},{12... | collective-permute-start | bytes 614408 | tf_op jit(solution)/shard_map/ppermute | solution.py:411
  47.6 15.3 %collective-permute-start.15 = (bf16[800,128]{1,0:T(8,128)(2,1)S(1)}, bf16[800,128]{1,0:T(8,128)(2,1)S(1)}, u32[]{:S(2)}, u32[]{:S(2)}) collective-permute-start(bf16[800,128]{1,0:T(8,128)(2,1)S(1)} %get-tuple-element.11), channel_id=1, source_target_pairs={{0,4},{2,6},{4,0},{6,2},{1,5},{3,7},{5,1},{7,3},{8,12},{10,14},{12... | collective-permute-start | bytes 614408 | tf_op jit(solution)/shard_map/ppermute | solution.py:411
  50.2 12.8 %collective-permute-start.16 = (bf16[800,128]{1,0:T(8,128)(2,1)S(1)}, bf16[800,128]{1,0:T(8,128)(2,1)S(1)}, u32[]{:S(2)}, u32[]{:S(2)}) collective-permute-start(bf16[800,128]{1,0:T(8,128)(2,1)S(1)} %get-tuple-element.12), channel_id=1, source_target_pairs={{0,6},{2,0},{4,2},{6,4},{1,7},{3,1},{5,3},{7,5},{8,14},{10,8},{12,... | collective-permute-start | bytes 614408 | tf_op jit(solution)/shard_map/ppermute | solution.py:411
  69.1 10.9 %collective-permute-start.19 = (bf16[40,4,256]{2,1,0:T(4,128)(2,1)S(1)}, bf16[40,4,256]{2,1,0:T(4,128)(2,1)S(1)}, u32[]{:S(2)}, u32[]{:S(2)}) collective-permute-start(bf16[40,4,256]{2,1,0:T(4,128)(2,1)S(1)} %get-tuple-element.41), channel_id=1, source_target_pairs={{0,1},{1,2},{2,3},{3,4},{4,5},{5,6},{6,7},{7,0},{8,9},{9,10},{10,1... | collective-permute-start | bytes 245768 | tf_op jit(solution)/shard_map/ppermute | solution.py:390
  71.3 8.7 %collective-permute-start.20 = (bf16[40,4,256]{2,1,0:T(4,128)(2,1)S(1)}, bf16[40,4,256]{2,1,0:T(4,128)(2,1)S(1)}, u32[]{:S(2)}, u32[]{:S(2)}) collective-permute-start(bf16[40,4,256]{2,1,0:T(4,128)(2,1)S(1)} %get-tuple-element.42), channel_id=1, source_target_pairs={{1,0},{2,1},{3,2},{4,3},{5,4},{6,5},{7,6},{0,7},{9,8},{10,9},{11,1... | collective-permute-start | bytes 245768 | tf_op jit(solution)/shard_map/ppermute | solution.py:391
  91.6 9.7 %collective-permute-start.30 = (bf16[768,128]{1,0:T(8,128)(2,1)S(1)}, bf16[768,128]{1,0:T(8,128)(2,1)S(1)}, u32[]{:S(2)}, u32[]{:S(2)}) collective-permute-start(bf16[768,128]{1,0:T(8,128)(2,1)S(1)} %get-tuple-element.15.refs_1_), channel_id=1, source_target_pairs={{0,2},{2,4},{4,6},{6,0},{1,3},{3,5},{5,7},{7,1},{8,10},{10,12},{12... | collective-permute-start | bytes 589832 | tf_op jit(solution)/shard_map/ppermute | solution.py:411
  93.6 15.5 %collective-permute-start.29 = (bf16[768,128]{1,0:T(8,128)(2,1)S(1)}, bf16[768,128]{1,0:T(8,128)(2,1)S(1)}, u32[]{:S(2)}, u32[]{:S(2)}) collective-permute-start(bf16[768,128]{1,0:T(8,128)(2,1)S(1)} %get-tuple-element.15.refs_1_), channel_id=1, source_target_pairs={{0,4},{2,6},{4,0},{6,2},{1,5},{3,7},{5,1},{7,3},{8,12},{10,14},{12... | collective-permute-start | bytes 589832 | tf_op jit(solution)/shard_map/ppermute | solution.py:411
  95.2 13.9 %collective-permute-start.28 = (bf16[768,128]{1,0:T(8,128)(2,1)S(1)}, bf16[768,128]{1,0:T(8,128)(2,1)S(1)}, u32[]{:S(2)}, u32[]{:S(2)}) collective-permute-start(bf16[768,128]{1,0:T(8,128)(2,1)S(1)} %get-tuple-element.15.refs_1_), channel_id=1, source_target_pairs={{0,6},{2,0},{4,2},{6,4},{1,7},{3,1},{5,3},{7,5},{8,14},{10,8},{12,... | collective-permute-start | bytes 589832 | tf_op jit(solution)/shard_map/ppermute | solution.py:411
  97.2 17.3 %collective-permute-start.27 = (bf16[192,128]{1,0:T(8,128)(2,1)S(1)}, bf16[192,128]{1,0:T(8,128)(2,1)S(1)}, u32[]{:S(2)}, u32[]{:S(2)}) collective-permute-start(bf16[192,128]{1,0:T(8,128)(2,1)S(1)} %get-tuple-element.45), channel_id=1, source_target_pairs={{0,25},{1,24},{8,17},{9,16},{16,9},{17,8},{24,1},{25,0},{2,27},{3,... | collective-permute-start | bytes 147464 | tf_op jit(solution)/shard_map/ppermute | solution.py:404
  110.2 18.6 %collective-permute-start.37 = (bf16[576,128]{1,0:T(8,128)(2,1)S(1)}, bf16[576,128]{1,0:T(8,128)(2,1)S(1)}, u32[]{:S(2)}, u32[]{:S(2)}) collective-permute-start(bf16[576,128]{1,0:T(8,128)(2,1)S(1)} %get-tuple-element.33), channel_id=1, source_target_pairs={{0,25},{1,24},{8,17},{9,16},{16,9},{17,8},{24,1},{25,0},{2,27},{3,... | collective-permute-start | bytes 442376 | tf_op jit(solution)/shard_map/ppermute | solution.py:404
  111.0 18.2 %collective-permute-start.36 = (bf16[576,128]{1,0:T(8,128)(2,1)S(1)}, bf16[576,128]{1,0:T(8,128)(2,1)S(1)}, u32[]{:S(2)}, u32[]{:S(2)}) collective-permute-start(bf16[576,128]{1,0:T(8,128)(2,1)S(1)} %get-tuple-element.34), channel_id=1, source_target_pairs={{0,24},{1,25},{8,16},{9,17},{16,8},{17,9},{24,0},{25,1},{2,26},{3,... | collective-permute-start | bytes 442376 | tf_op jit(solution)/shard_map/ppermute | solution.py:404
  112.6 9.4 %collective-permute-start.26 = (bf16[192,128]{1,0:T(8,128)(2,1)S(1)}, bf16[192,128]{1,0:T(8,128)(2,1)S(1)}, u32[]{:S(2)}, u32[]{:S(2)}) collective-permute-start(bf16[192,128]{1,0:T(8,128)(2,1)S(1)} %get-tuple-element.46), channel_id=1, source_target_pairs={{0,24},{1,25},{8,16},{9,17},{16,8},{17,9},{24,0},{25,1},{2,26},{3,... | collective-permute-start | bytes 147464 | tf_op jit(solution)/shard_map/ppermute | solution.py:404
  112.7 10.6 %collective-permute-start.25 = (bf16[192,128]{1,0:T(8,128)(2,1)S(1)}, bf16[192,128]{1,0:T(8,128)(2,1)S(1)}, u32[]{:S(2)}, u32[]{:S(2)}) collective-permute-start(bf16[192,128]{1,0:T(8,128)(2,1)S(1)} %get-tuple-element.47), channel_id=1, source_target_pairs={{0,17},{1,16},{8,25},{9,24},{16,1},{17,0},{24,9},{25,8},{2,19},{3,... | collective-permute-start | bytes 147464 | tf_op jit(solution)/shard_map/ppermute | solution.py:404
  114.5 9.2 %collective-permute-start.24 = (bf16[192,128]{1,0:T(8,128)(2,1)S(1)}, bf16[192,128]{1,0:T(8,128)(2,1)S(1)}, u32[]{:S(2)}, u32[]{:S(2)}) collective-permute-start(bf16[192,128]{1,0:T(8,128)(2,1)S(1)} %get-tuple-element.48), channel_id=1, source_target_pairs={{0,16},{1,17},{8,24},{9,25},{16,0},{17,1},{24,8},{25,9},{2,18},{3,... | collective-permute-start | bytes 147464 | tf_op jit(solution)/shard_map/ppermute | solution.py:404
  127.4 8.5 %collective-permute-start.34 = (bf16[576,128]{1,0:T(8,128)(2,1)S(1)}, bf16[576,128]{1,0:T(8,128)(2,1)S(1)}, u32[]{:S(2)}, u32[]{:S(2)}) collective-permute-start(bf16[576,128]{1,0:T(8,128)(2,1)S(1)} %get-tuple-element.36), channel_id=1, source_target_pairs={{0,16},{1,17},{8,24},{9,25},{16,0},{17,1},{24,8},{25,9},{2,18},{3,... | collective-permute-start | bytes 442376 | tf_op jit(solution)/shard_map/ppermute | solution.py:404
  129.2 9.9 %collective-permute-start.31 = (bf16[576,128]{1,0:T(8,128)(2,1)S(1)}, bf16[576,128]{1,0:T(8,128)(2,1)S(1)}, u32[]{:S(2)}, u32[]{:S(2)}) collective-permute-start(bf16[576,128]{1,0:T(8,128)(2,1)S(1)} %get-tuple-element.39), channel_id=1, source_target_pairs={{0,1},{1,0},{8,9},{9,8},{16,17},{17,16},{24,25},{25,24},{2,3},{3,2... | collective-permute-start | bytes 442376 | tf_op jit(solution)/shard_map/ppermute | solution.py:404
  (28 other events, 268.2 us)

commit v4 on v3

--- a/solution.py
+++ b/solution.py
@@ -55,7 +55,10 @@
     return -(-3 * pairs // 16) * 16
 
 
-def encode_blocks(capacity, shape, place_ref, tile_ref, patch_ref, feat_ref, offset_ref, send_ref, slot_ref, count_ref):
+def encode_blocks(
+    capacity, shape, place_ref, tile_ref, patch_ref, feat_ref, offset_ref, near_ref, far_ref,
+    slot_ref, send_ref, count_ref,
+):
     lat, depth, width = shape
     plane = lat * width
     devices = plane * depth
@@ -81,7 +84,7 @@
         rank = count_ref[tile]
         count_ref[tile] = rank + 1
         lon = tile % (depth * width)
-        partner = (tile // (depth * width) * width + lon % width) ^ place_ref[0]
+        partner = (tile // (depth * width) * width + lon % width)
         hop = (lon // width + depth - place_ref[1]) % depth
         piece = jnp.where(hop == 0, partner, plane + partner * (depth - 1) + hop - 1)
         slot_ref[b] = piece * capacity + rank
@@ -120,6 +123,8 @@
         return 0
 
     lax.fori_loop(0, blocks // unroll, body, 0)
+    near_ref[...] = send_ref[: near_ref.shape[0]]
+    far_ref[...] = send_ref[near_ref.shape[0] :]
 
 
 def dense_rows(pairs, feat_width):
@@ -147,16 +152,18 @@
     return jnp.where(first, even, odd)
 
 
-def gather_planes(capacity, plane, hops, feat_width, id_ref, *refs):
-    pieces, outs, acc_ref = refs[:plane], refs[plane : plane + hops], refs[plane + hops]
+def gather_planes(capacity, plane, hops, feat_width, id_ref, recv_ref, *refs):
+    outs, acc_ref = refs[:hops], refs[hops]
     pairs = capacity // 2
     chunk = pairs * feat_width + meta_rows(pairs)
     patch_pairs = acc_ref.shape[1] // 2
     acc_ref[...] = jnp.zeros_like(acc_ref)
     for r in range(plane):
         for hop in range(hops):
-            slot = (r * hops + hop) * capacity
-            add_chunk(capacity, feat_width, id_ref, slot, pieces[r], hop * chunk, acc_ref.at[hop])
+            n = r * hops + hop
+            add_chunk(
+                capacity, feat_width, id_ref, n * capacity, recv_ref, n * chunk, acc_ref.at[hop]
+            )
     for hop in range(hops):
         masses = []
         for j in range(patch_pairs):
@@ -172,16 +179,17 @@
         outs[hop][patch_pairs * feat_width :, :] = jnp.concatenate(rows, axis=0).astype(jnp.bfloat16)
 
 
-def start_tile(capacity, plane, hops, id_ref, *refs):
-    pieces, parts = refs[:plane], refs[plane : plane + hops]
-    embed_ref, base_ref, start_ref, acc_ref = refs[plane + hops :]
+def start_tile(capacity, plane, hops, id_ref, recv_ref, *refs):
+    parts = refs[:hops]
+    embed_ref, base_ref, start_ref, acc_ref = refs[hops:]
+    chunk = recv_ref.shape[0] // plane
     feat_width, channels = embed_ref.shape
     tile_rows, tile_cols, _ = base_ref.shape
     patch_rows, patch_cols = tile_rows // PATCH, tile_cols // PATCH
     patch_pairs = patch_rows * patch_cols // 2
     acc_ref[...] = jnp.zeros_like(acc_ref)
     for r in range(plane):
-        add_chunk(capacity, feat_width, id_ref, r * capacity, pieces[r], 0, acc_ref)
+        add_chunk(capacity, feat_width, id_ref, r * capacity, recv_ref, r * chunk, acc_ref)
     embed = embed_ref[...]
     mass_rows = [part[patch_pairs * feat_width :, :].astype(jnp.float32) for part in parts]
     for pr in range(patch_rows):
@@ -398,12 +406,11 @@
     return math.prod([lax.axis_size(axis) for axis in axes])
 
 
-def swap_in_plane(arrays):
-    plane = len(arrays)
-    return arrays[:1] + [
-        lax.ppermute(arrays[r], ("lat", "x"), [(i, i ^ r) for i in range(plane)])
-        for r in range(1, plane)
-    ]
+def swap_in_plane(array):
+    plane = axis_count(("lat", "x"))
+    parts = array.reshape(plane, -1, LANES)
+    parts = lax.all_to_all(parts, ("lat", "x"), split_axis=0, concat_axis=0, tiled=True)
+    return parts.reshape(array.shape)
 
 
 def shift_planes(array, hop):
@@ -443,56 +450,54 @@
         [lat_id * width + lax.axis_index("x"), lax.axis_index("z"), lat_id]
     ).astype(jnp.int32)
 
-    send, slots = pl.pallas_call(
+    send_near, send_far, slots = pl.pallas_call(
         lambda *refs: encode_blocks(capacity, (lat, depth, width), *refs),
         out_shape=(
-            jax.ShapeDtypeStruct((devices * chunk, LANES), jnp.bfloat16),
+            jax.ShapeDtypeStruct((plane * chunk, LANES), jnp.bfloat16),
+            jax.ShapeDtypeStruct((plane * hops * chunk, LANES), jnp.bfloat16),
             jax.ShapeDtypeStruct((blocks,), jnp.int32),
         ),
         in_specs=[smem(), smem(), smem(), vmem(), vmem()],
-        out_specs=(vmem(), smem()),
-        scratch_shapes=[pltpu.SMEM((devices,), jnp.int32)],
-        compiler_params=params(8),
+        out_specs=(vmem(), vmem(), smem()),
+        scratch_shapes=[
+            pltpu.VMEM((devices * chunk, LANES), jnp.bfloat16),
+            pltpu.SMEM((devices,), jnp.int32),
+        ],
+        compiler_params=params(10),
         name="encode_blocks",
     )(place, block_tile.reshape(blocks), block_patch, obs_feat, obs_offset)
 
-    def cut(array, start, rows):
-        return [
-            lax.slice_in_dim(array, start + r * rows, start + (r + 1) * rows) for r in range(plane)
-        ]
-
-    def ids_of(pieces, tiles):
+    def ids_of(recv, tiles):
         at = pairs * feat_width + 2 * pairs
-        tags = jnp.stack(
-            [p.reshape(tiles, chunk, LANES)[:, at : at + pairs, 0::CELLS] for p in pieces]
-        )
+        tags = recv.reshape(plane * tiles, chunk, LANES)[:, at : at + pairs, 0::CELLS]
         ids = tags.astype(jnp.float32).astype(jnp.int32) - 1
         return jnp.clip(ids, 0, patch_total - 1).reshape(-1)
 
-    far = swap_in_plane(cut(send, plane * chunk, hops * chunk))
-    near = swap_in_plane(cut(send, 0, chunk))
+    far = swap_in_plane(send_far)
     far_ids = ids_of(far, hops)
     sums = pl.pallas_call(
         lambda *refs: gather_planes(capacity, plane, hops, feat_width, *refs),
         out_shape=[jax.ShapeDtypeStruct((dense, LANES), jnp.bfloat16)] * hops,
-        in_specs=[smem()] + [vmem()] * plane,
+        in_specs=[smem(), vmem()],
         out_specs=[vmem()] * hops,
         scratch_shapes=[pltpu.VMEM((hops, patch_total, feat_width + 8, LANES), jnp.float32)],
         compiler_params=params(8),
         name="gather_planes",
-    )(far_ids, *far)
+    )(far_ids, far)
+    send_near, sums = lax.optimization_barrier((send_near, sums))
     parts = [shift_planes(sums[hop], hop + 1) for hop in range(hops)]
+    near = swap_in_plane(send_near)
     near_ids = ids_of(near, 1)
 
     start = pl.pallas_call(
         lambda *refs: start_tile(capacity, plane, hops, *refs),
         out_shape=jax.ShapeDtypeStruct(grid_base.shape, jnp.bfloat16),
-        in_specs=[smem()] + [vmem()] * (plane + hops + 2),
+        in_specs=[smem()] + [vmem()] * (hops + 3),
         out_specs=vmem(),
         scratch_shapes=[pltpu.VMEM((patch_total, feat_width + 8, LANES), jnp.float32)],
         compiler_params=params(8),
         name="start_tile",
-    )(near_ids, *near, *parts, embed_weight, grid_base)
+    )(near_ids, near, *parts, embed_weight, grid_base)
 
     margin = WIN // 2
     ext = with_halo(start, (("lat", 0), (("z", "x"), 1)), margin).astype(jnp.float32)
@@ -542,7 +547,7 @@
             compiler_params=params(8),
             name=name,
         )(ids, *tiles)
-        return swap_in_plane(cut(out, 0, rows))
+        return swap_in_plane(out)
 
     others = [shift_planes(projected, -hop) for hop in range(1, depth)]
     near_back = reply(near_ids, [projected], "reply_near")
@@ -551,12 +556,12 @@
     obs_out = pl.pallas_call(
         decode_blocks,
         out_shape=jax.ShapeDtypeStruct((feat_width, obs_count), jnp.bfloat16),
-        in_specs=[smem(), vmem()] + [vmem()] * (2 * plane),
+        in_specs=[smem(), vmem()] + [vmem()] * 2,
         out_specs=vmem(),
         scratch_shapes=[pltpu.VMEM((devices * pairs * feat_width, LANES), jnp.bfloat16)],
         compiler_params=params(10),
         name="decode_blocks",
-    )(slots, obs_offset, *near_back, *far_back)
+    )(slots, obs_offset, near_back, far_back)
     return (latent, obs_out)
 
 

time: 145 us -> 135 us (0.931)
  blocking collectives: 0 us -> 42.5 us
  starting transfers between devices: 51.8 us -> 26 us
  waiting for transfers between devices: 54.7 us -> 31.7 us
  local copies, waits for them, and re-layouts: 9.32 us -> 4.19 us
    all_to_all x0 -> x2, blocking collectives: none -> 42.5 us  [swap_in_plane(): lax.all_to_all(parts, ('lat', 'x'), split_axis=0, concat_axis=0, tiled=True)]
    ppermute x28 -> x0, starting transfers between devices: 31.5 us -> none  [swap_in_plane(): lax.ppermute(arrays[r], ('lat', 'x'), [(i, i ^ r) for i in range(plane)])]
    ppermute x28 -> x0, waiting for transfers between devices: 26.5 us -> none  [swap_in_plane(): lax.ppermute(arrays[r], ('lat', 'x'), [(i, i ^ r) for i in range(plane)])]
    all_to_all x0 -> x2, starting transfers between devices: none -> 7.06 us  [swap_in_plane(): lax.all_to_all(parts, ('lat', 'x'), split_axis=0, concat_axis=0, tiled=True)]
    all_to_all x0 -> x2, waiting for transfers between devices: none -> 2.58 us  [swap_in_plane(): lax.all_to_all(parts, ('lat', 'x'), split_axis=0, concat_axis=0, tiled=True)]
    another operation x18 -> x0, local copies, waits for them, and re-layouts: 2.35 us -> none  [ids_of(): jnp.stack([p.reshape(tiles, chunk, LANES)[:, at:at + pairs, 0::CELLS] for...]
    slice x20 -> x2, local copies, waits for them, and re-layouts: 1.8 us -> 0.25 us  [ids_of(): tags = recv.reshape(plane * tiles, chunk, LANES)[:, at:at + pairs, 0::CELLS]]
    unnamed x37 -> x29, local copies, waits for them, and re-layouts: 4.66 us -> 3.69 us
  transfers between devices with their start and end apart: 38 -> 12, of which waited for: 17 -> 9; matrix products, arithmetic and copies ran while one was open for 3% -> 0% of each run, Pallas kernels for 1% -> 1%
where the time goes in v4:
time: 135 us; the launch traced here: 132 us
  blocking collectives  42.5 us (31%)
  waiting for transfers between devices  31.7 us (23%)
  Pallas kernels  26.5 us (20%)
  starting transfers between devices  26 us (19%)
  local copies, waits for them, and re-layouts  4.19 us (3%)
    all_to_all x2, blocking collectives, swap_in_plane(): lax.all_to_all(parts, ('lat', 'x'), split_axis=0, concat_axis=0, tiled=True)  42.5 us
    ppermute x6, waiting for transfers between devices, shift_planes(): lax.ppermute(array, 'z', [(i, (i + hop) % depth) for i in range(depth)])  23 us
    pallas_call x1, Pallas kernels, local(): pl.pallas_call(lambda *refs: grid_block(tile_rows * lat, *refs), out_shap...  11 us
    ppermute x6, starting transfers between devices, shift_planes(): lax.ppermute(array, 'z', [(i, (i + hop) % depth) for i in range(depth)])  10 us
    ppermute x2, starting transfers between devices, with_halo(): after = lax.ppermute(initial, axis, down)  7.34 us
    all_to_all x2, starting transfers between devices, swap_in_plane(): lax.all_to_all(parts, ('lat', 'x'), split_axis=0, concat_axis=0, tiled=True)  7.06 us
    pallas_call x1, Pallas kernels, local(): pl.pallas_call(lambda *refs: encode_blocks(capacity, (lat, depth, width),...  5.18 us
    ppermute x2, waiting for transfers between devices, with_halo(): before = lax.ppermute(last, axis, up)  4.37 us
  transfers between devices with their start and end apart: 12, of which 9 were waited for; matrix products, arithmetic and copies ran while one was open for 0% of the time, Pallas kernels for 1%

profile of v4, /device:TPU:0, one launch (start us, length us, event | category | flops | bytes accessed | tf_op | source)
XLA Modules:
  0.0 132.3 jit_solution(14916396064896213325)
XLA Ops:
  4.2 5.2 %encode_blocks.1 = (bf16[1664,128]{1,0:T(8,128)(2,1)}, bf16[4992,128]{1,0:T(8,128)(2,1)S(1)}, s32[96]{0:T(128)S(1)}) custom-call(s32[3]{0:T(128)S(1)} %pad_add_fusion.refs_0_, s32[96]{0:T(128)S(1)} %bitcast.24, s32[96]{0:T(128)S(1)} %copy-done.12, bf16[64,12288]{1,0:T(8,128)(2,1)S(1)} %copy-done, bf16[2,12288]{1,0:T(2,128)(2,1)S(1)} %copy-done.5), custom_call_target="tpu_custom_call" | custom-call | tf_op jit(solution)/shard_map/encode_blocks/pallas_call | solution.py:453
  9.4 22.4 %all_to_all.20 = bf16[8,624,128]{2,1,0:T(8,128)(2,1)S(1)} all-to-all(bf16[8,624,128]{2,1,0:T(8,128)(2,1)S(1)} %bitcast.21), channel_id=1, replica_groups=mesh['lat'=4,'z'=4,'x'=2] {'lat','x'}, dimensions={0} | all-to-all | bytes 2555904 | tf_op jit(solution)/shard_map/all_to_all | solution.py:412
  32.2 2.4 %gather_planes.1 = (bf16[800,128]{1,0:T(8,128)(2,1)S(1)}, bf16[800,128]{1,0:T(8,128)(2,1)S(1)}, bf16[800,128]{1,0:T(8,128)(2,1)S(1)}) custom-call(s32[144]{0:T(256)S(1)} %reshape.45.refs_0_, bf16[4992,128]{1,0:T(8,128)(2,1)S(1)} %bitcast.16), custom_call_target="tpu_custom_call" | custom-call | tf_op jit(solution)/shard_map/gather_planes/pallas_call | solution.py:478
  34.6 3.5 %all-to-all-start.1 = ((bf16[8,208,128]{2,1,0:T(8,128)(2,1)}), bf16[8,208,128]{2,1,0:T(8,128)(2,1)S(1)}, u32[]{:S(2)}, u32[]{:S(2)}) async-start(bf16[8,208,128]{2,1,0:T(8,128)(2,1)} %bitcast.7), calls=%async_computation.1 | async-start | bytes 851968 | tf_op jit(solution)/shard_map/all_to_all | solution.py:412
  38.1 1.6 %collective-permute-start = (bf16[800,128]{1,0:T(8,128)(2,1)S(1)}, bf16[800,128]{1,0:T(8,128)(2,1)S(1)}, u32[]{:S(2)}, u32[]{:S(2)}) collective-permute-start(bf16[800,128]{1,0:T(8,128)(2,1)S(1)} %get-tuple-element.20), channel_id=1, source_target_pairs={{0,2},{2,4},{4,6},{6,0},{1,3},{3,5},{5,7},{7,1},{8,10},{10,12},{12... | collective-permute-start | bytes 614408 | tf_op jit(solution)/shard_map/ppermute | solution.py:418
  39.7 2.6 %collective-permute-start.1 = (bf16[800,128]{1,0:T(8,128)(2,1)S(1)}, bf16[800,128]{1,0:T(8,128)(2,1)S(1)}, u32[]{:S(2)}, u32[]{:S(2)}) collective-permute-start(bf16[800,128]{1,0:T(8,128)(2,1)S(1)} %get-tuple-element.21), channel_id=1, source_target_pairs={{0,4},{2,6},{4,0},{6,2},{1,5},{3,7},{5,1},{7,3},{8,12},{10,14},{12... | collective-permute-start | bytes 614408 | tf_op jit(solution)/shard_map/ppermute | solution.py:418
  43.7 2.6 %all-to-all-done.1 = bf16[8,208,128]{2,1,0:T(8,128)(2,1)S(1)} async-done(((bf16[8,208,128]{2,1,0:T(8,128)(2,1)}), bf16[8,208,128]{2,1,0:T(8,128)(2,1)S(1)}, u32[]{:S(2)}, u32[]{:S(2)}) %all-to-all-start.1) | async-done | bytes 426016 | tf_op jit(solution)/shard_map/all_to_all | solution.py:412
  46.5 1.5 %collective-permute-done.refs_2_ = bf16[800,128]{1,0:T(8,128)(2,1)S(1)} collective-permute-done((bf16[800,128]{1,0:T(8,128)(2,1)S(1)}, bf16[800,128]{1,0:T(8,128)(2,1)S(1)}, u32[]{:S(2)}, u32[]{:S(2)}) %collective-permute-start) | collective-permute-done | bytes 204832 | tf_op jit(solution)/shard_map/ppermute | solution.py:418
  48.0 8.3 %collective-permute-done.1.refs_3_ = bf16[800,128]{1,0:T(8,128)(2,1)S(1)} collective-permute-done((bf16[800,128]{1,0:T(8,128)(2,1)S(1)}, bf16[800,128]{1,0:T(8,128)(2,1)S(1)}, u32[]{:S(2)}, u32[]{:S(2)}) %collective-permute-start.1) | collective-permute-done | bytes 204832 | tf_op jit(solution)/shard_map/ppermute | solution.py:418
  56.3 1.6 %start_tile.1 = bf16[32,48,256]{2,1,0:T(8,128)(2,1)S(1)} custom-call(s32[48]{0:T(128)S(1)} %reshape.48.refs_0_, bf16[1664,128]{1,0:T(8,128)(2,1)S(1)} %bitcast.19, bf16[800,128]{1,0:T(8,128)(2,1)S(1)} %collective-permute-done.refs_2_, bf16[800,128]{1,0:T(8,128)(2,1)S(1)} %collective-permute-done.1.refs_3_, ...), custom_call_target="tpu_custom_call" | custom-call | tf_op jit(solution)/shard_map/start_tile/pallas_call | solution.py:492
  58.0 1.7 %collective-permute-start.4 = (bf16[4,48,256]{2,1,0:T(8,128)(2,1)S(1)}, bf16[4,48,256]{2,1,0:T(8,128)(2,1)S(1)}, u32[]{:S(2)}, u32[]{:S(2)}) collective-permute-start(bf16[4,48,256]{2,1,0:T(8,128)(2,1)S(1)} %get-tuple-element.29), channel_id=1, source_target_pairs={{8,0},{16,8},{24,16},{0,24},{9,1},{17,9},{25,17},{1,25},{10,2},{18... | collective-permute-start | bytes 294920 | tf_op jit(solution)/shard_map/ppermute | solution.py:399
  59.8 2.2 %collective-permute-done.3 = bf16[4,48,256]{2,1,0:T(8,128)(2,1)S(1)} collective-permute-done((bf16[4,48,256]{2,1,0:T(8,128)(2,1)S(1)}, bf16[4,48,256]{2,1,0:T(8,128)(2,1)S(1)}, u32[]{:S(2)}, u32[]{:S(2)}) %collective-permute-start.3) | collective-permute-done | bytes 98336 | tf_op jit(solution)/shard_map/ppermute | solution.py:398
  62.3 1.5 %collective-permute-start.5 = (bf16[40,4,256]{2,1,0:T(4,128)(2,1)S(1)}, bf16[40,4,256]{2,1,0:T(4,128)(2,1)S(1)}, u32[]{:S(2)}, u32[]{:S(2)}) collective-permute-start(bf16[40,4,256]{2,1,0:T(4,128)(2,1)S(1)} %get-tuple-element.26), channel_id=1, source_target_pairs={{0,1},{1,2},{2,3},{3,4},{4,5},{5,6},{6,7},{7,0},{8,9},{9,10},{10,1... | collective-permute-start | bytes 245768 | tf_op jit(solution)/shard_map/ppermute | solution.py:398
  63.8 5.6 %collective-permute-start.6 = (bf16[40,4,256]{2,1,0:T(4,128)(2,1)S(1)}, bf16[40,4,256]{2,1,0:T(4,128)(2,1)S(1)}, u32[]{:S(2)}, u32[]{:S(2)}) collective-permute-start(bf16[40,4,256]{2,1,0:T(4,128)(2,1)S(1)} %get-tuple-element.27), channel_id=1, source_target_pairs={{1,0},{2,1},{3,2},{4,3},{5,4},{6,5},{7,6},{0,7},{9,8},{10,9},{11,1... | collective-permute-start | bytes 245768 | tf_op jit(solution)/shard_map/ppermute | solution.py:399
  69.5 2.2 %collective-permute-done.5 = bf16[40,4,256]{2,1,0:T(4,128)(2,1)S(1)} collective-permute-done((bf16[40,4,256]{2,1,0:T(4,128)(2,1)S(1)}, bf16[40,4,256]{2,1,0:T(4,128)(2,1)S(1)}, u32[]{:S(2)}, u32[]{:S(2)}) %collective-permute-start.5) | collective-permute-done | bytes 81952 | tf_op jit(solution)/shard_map/ppermute | solution.py:398
  71.6 1.6 %collective-permute-done.6 = bf16[40,4,256]{2,1,0:T(4,128)(2,1)S(1)} collective-permute-done((bf16[40,4,256]{2,1,0:T(4,128)(2,1)S(1)}, bf16[40,4,256]{2,1,0:T(4,128)(2,1)S(1)}, u32[]{:S(2)}, u32[]{:S(2)}) %collective-permute-start.6) | collective-permute-done | bytes 81952 | tf_op jit(solution)/shard_map/ppermute | solution.py:399
  73.7 11.0 %grid_block.1 = (bf16[32,48,256]{2,1,0:T(8,128)(2,1)}, bf16[768,128]{1,0:T(8,128)(2,1)S(1)}) custom-call(s32[3]{0:T(128)S(1)} %pad_add_fusion.refs_0_, f32[40,56,256]{2,1,0:T(8,128)S(1)} %maximum_convert_fusion.refs_1_, f32[1,256]{1,0:T(1,128)S(1)} %bitcast.22, bf16[256,768]{1,0:T(8,128)(2,1)S(1)} %copy-done.4, bf16[256,256]{1,0:T(8,128)(2,1)S(1)} %copy-done.7, ...), custom_call_target="tpu_custom_call" | custom-call | tf_op jit(solution)/shard_map/grid_block/pallas_call | solution.py:507
  86.2 3.6 %all-to-all-start.2 = ((bf16[8,192,128]{2,1,0:T(8,128)(2,1)}), bf16[8,192,128]{2,1,0:T(8,128)(2,1)S(1)}, u32[]{:S(2)}, u32[]{:S(2)}) async-start(bf16[8,192,128]{2,1,0:T(8,128)(2,1)} %bitcast.11), calls=%async_computation.2 | async-start | bytes 786432 | tf_op jit(solution)/shard_map/all_to_all | solution.py:412
  89.8 2.0 %collective-permute-start.9 = (bf16[768,128]{1,0:T(8,128)(2,1)S(1)}, bf16[768,128]{1,0:T(8,128)(2,1)S(1)}, u32[]{:S(2)}, u32[]{:S(2)}) collective-permute-start(bf16[768,128]{1,0:T(8,128)(2,1)S(1)} %get-tuple-element.25.refs_1_), channel_id=1, source_target_pairs={{0,2},{2,4},{4,6},{6,0},{1,3},{3,5},{5,7},{7,1},{8,10},{10,12},{12... | collective-permute-start | bytes 589832 | tf_op jit(solution)/shard_map/ppermute | solution.py:418
  91.8 1.9 %collective-permute-start.8 = (bf16[768,128]{1,0:T(8,128)(2,1)S(1)}, bf16[768,128]{1,0:T(8,128)(2,1)S(1)}, u32[]{:S(2)}, u32[]{:S(2)}) collective-permute-start(bf16[768,128]{1,0:T(8,128)(2,1)S(1)} %get-tuple-element.25.refs_1_), channel_id=1, source_target_pairs={{0,4},{2,6},{4,0},{6,2},{1,5},{3,7},{5,1},{7,3},{8,12},{10,14},{12... | collective-permute-start | bytes 589832 | tf_op jit(solution)/shard_map/ppermute | solution.py:418
  94.2 5.2 %collective-permute-done.9.refs_3_ = bf16[768,128]{1,0:T(8,128)(2,1)S(1)} collective-permute-done((bf16[768,128]{1,0:T(8,128)(2,1)S(1)}, bf16[768,128]{1,0:T(8,128)(2,1)S(1)}, u32[]{:S(2)}, u32[]{:S(2)}) %collective-permute-start.9) | collective-permute-done | bytes 196640 | tf_op jit(solution)/shard_map/ppermute | solution.py:418
  99.5 7.9 %collective-permute-done.8.refs_2_ = bf16[768,128]{1,0:T(8,128)(2,1)S(1)} collective-permute-done((bf16[768,128]{1,0:T(8,128)(2,1)S(1)}, bf16[768,128]{1,0:T(8,128)(2,1)S(1)}, u32[]{:S(2)}, u32[]{:S(2)}) %collective-permute-start.8) | collective-permute-done | bytes 196640 | tf_op jit(solution)/shard_map/ppermute | solution.py:418
  108.5 20.1 %all_to_all.21 = bf16[8,576,128]{2,1,0:T(8,128)(2,1)S(1)} all-to-all(bf16[8,576,128]{2,1,0:T(8,128)(2,1)S(1)} %bitcast.17), channel_id=1, replica_groups=mesh['lat'=4,'z'=4,'x'=2] {'lat','x'}, dimensions={0} | all-to-all | bytes 2359296 | tf_op jit(solution)/shard_map/all_to_all | solution.py:412
  128.5 3.8 %decode_blocks.1 = bf16[64,12288]{1,0:T(8,128)(2,1)} custom-call(s32[96]{0:T(128)S(1)} %get-tuple-element.24.slot_ref, bf16[2,12288]{1,0:T(2,128)(2,1)S(1)} %copy-done.6, bf16[1536,128]{1,0:T(8,128)(2,1)S(1)} %bitcast.20, bf16[4608,128]{1,0:T(8,128)(2,1)S(1)} %bitcast.18), custom_call_target="tpu_custom_call" | custom-call | tf_op jit(solution)/shard_map/decode_blocks/pallas_call | solution.py:556
  (48 shorter events, 9.5 us)
Async XLA Ops:
  0.7 1.4 %copy-start = (bf16[64,12288]{1,0:T(8,128)(2,1)S(1)}, bf16[64,12288]{1,0:T(8,128)(2,1)}, u32[]{:S(2)}) copy-start(bf16[64,12288]{1,0:T(8,128)(2,1)} %refs_3_.2) | copy-start | bytes 4718596
  2.1 0.8 copy-start.5
  9.4 46.8 %copy-start.1 = (bf16[32,48,256]{2,1,0:T(8,128)(2,1)S(1)}, bf16[32,48,256]{2,1,0:T(8,128)(2,1)}, u32[]{:S(2)}) copy-start(bf16[32,48,256]{2,1,0:T(8,128)(2,1)} %refs_6_.2) | copy-start | bytes 2359300
  9.4 46.8 %copy-start.8 = (bf16[64,256]{1,0:T(8,128)(2,1)S(1)}, bf16[64,256]{1,0:T(8,128)(2,1)}, u32[]{:S(2)}) copy-start(bf16[64,256]{1,0:T(8,128)(2,1)} %refs_5_.1) | copy-start | bytes 98308
  34.6 11.6 %all-to-all-start.1 = ((bf16[8,208,128]{2,1,0:T(8,128)(2,1)}), bf16[8,208,128]{2,1,0:T(8,128)(2,1)S(1)}, u32[]{:S(2)}, u32[]{:S(2)}) async-start(bf16[8,208,128]{2,1,0:T(8,128)(2,1)} %bitcast.7), calls=%async_computation.1 | async-start | bytes 851968 | tf_op jit(solution)/shard_map/all_to_all | solution.py:412
  38.1 31.3 %copy-start.13 = (bf16[256,64]{0,1:T(8,128)(2,1)S(1)}, bf16[256,64]{0,1:T(8,128)(2,1)}, u32[]{:S(2)}) copy-start(bf16[256,64]{0,1:T(8,128)(2,1)} %param.25) | copy-start | bytes 98308
  38.1 9.9 %collective-permute-start = (bf16[800,128]{1,0:T(8,128)(2,1)S(1)}, bf16[800,128]{1,0:T(8,128)(2,1)S(1)}, u32[]{:S(2)}, u32[]{:S(2)}) collective-permute-start(bf16[800,128]{1,0:T(8,128)(2,1)S(1)} %get-tuple-element.20), channel_id=1, source_target_pairs={{0,2},{2,4},{4,6},{6,0},{1,3},{3,5},{5,7},{7,1},{8,10},{10,12},{12... | collective-permute-start | bytes 614408 | tf_op jit(solution)/shard_map/ppermute | solution.py:418
  39.7 16.5 %collective-permute-start.1 = (bf16[800,128]{1,0:T(8,128)(2,1)S(1)}, bf16[800,128]{1,0:T(8,128)(2,1)S(1)}, u32[]{:S(2)}, u32[]{:S(2)}) collective-permute-start(bf16[800,128]{1,0:T(8,128)(2,1)S(1)} %get-tuple-element.21), channel_id=1, source_target_pairs={{0,4},{2,6},{4,0},{6,2},{1,5},{3,7},{5,1},{7,3},{8,12},{10,14},{12... | collective-permute-start | bytes 614408 | tf_op jit(solution)/shard_map/ppermute | solution.py:418
  42.3 13.9 %collective-permute-start.2 = (bf16[800,128]{1,0:T(8,128)(2,1)S(1)}, bf16[800,128]{1,0:T(8,128)(2,1)S(1)}, u32[]{:S(2)}, u32[]{:S(2)}) collective-permute-start(bf16[800,128]{1,0:T(8,128)(2,1)S(1)} %get-tuple-element.22), channel_id=1, source_target_pairs={{0,6},{2,0},{4,2},{6,4},{1,7},{3,1},{5,3},{7,5},{8,14},{10,8},{12,... | collective-permute-start | bytes 614408 | tf_op jit(solution)/shard_map/ppermute | solution.py:418
  57.9 4.1 %collective-permute-start.3 = (bf16[4,48,256]{2,1,0:T(8,128)(2,1)S(1)}, bf16[4,48,256]{2,1,0:T(8,128)(2,1)S(1)}, u32[]{:S(2)}, u32[]{:S(2)}) collective-permute-start(bf16[4,48,256]{2,1,0:T(8,128)(2,1)S(1)} %get-tuple-element.28), channel_id=1, source_target_pairs={{0,8},{8,16},{16,24},{24,0},{1,9},{9,17},{17,25},{25,1},{2,10},{10... | collective-permute-start | bytes 294920 | tf_op jit(solution)/shard_map/ppermute | solution.py:398
  57.9 15.7 %copy-start.2 = (bf16[256,1024]{1,0:T(8,128)(2,1)S(1)}, bf16[256,1024]{1,0:T(8,128)(2,1)}, u32[]{:S(2)}) copy-start(bf16[256,1024]{1,0:T(8,128)(2,1)} %refs_6_.3) | copy-start | bytes 1572868
  57.9 15.7 %copy-start.3 = (bf16[1024,256]{1,0:T(8,128)(2,1)S(1)}, bf16[1024,256]{1,0:T(8,128)(2,1)}, u32[]{:S(2)}) copy-start(bf16[1024,256]{1,0:T(8,128)(2,1)} %refs_7_.1) | copy-start | bytes 1572868
  58.0 15.7 %copy-start.4 = (bf16[256,768]{1,0:T(8,128)(2,1)S(1)}, bf16[256,768]{1,0:T(8,128)(2,1)}, u32[]{:S(2)}) copy-start(bf16[256,768]{1,0:T(8,128)(2,1)} %refs_3_.3) | copy-start | bytes 1179652
  58.0 15.7 %copy-start.7 = (bf16[256,256]{1,0:T(8,128)(2,1)S(1)}, bf16[256,256]{1,0:T(8,128)(2,1)}, u32[]{:S(2)}) copy-start(bf16[256,256]{1,0:T(8,128)(2,1)} %refs_4_.3) | copy-start | bytes 393220
  58.0 15.7 %copy-start.9 = (f32[256]{0:T(256)S(1)}, f32[256]{0:T(256)}, u32[]{:S(2)}) copy-start(f32[256]{0:T(256)} %param.19) | copy-start | bytes 3076
  58.0 15.7 %copy-start.10 = (f32[256]{0:T(256)S(1)}, f32[256]{0:T(256)}, u32[]{:S(2)}) copy-start(f32[256]{0:T(256)} %param.22) | copy-start | bytes 3076
  58.0 4.2 %collective-permute-start.4 = (bf16[4,48,256]{2,1,0:T(8,128)(2,1)S(1)}, bf16[4,48,256]{2,1,0:T(8,128)(2,1)S(1)}, u32[]{:S(2)}, u32[]{:S(2)}) collective-permute-start(bf16[4,48,256]{2,1,0:T(8,128)(2,1)S(1)} %get-tuple-element.29), channel_id=1, source_target_pairs={{8,0},{16,8},{24,16},{0,24},{9,1},{17,9},{25,17},{1,25},{10,2},{18... | collective-permute-start | bytes 294920 | tf_op jit(solution)/shard_map/ppermute | solution.py:399
  62.3 9.4 %collective-permute-start.5 = (bf16[40,4,256]{2,1,0:T(4,128)(2,1)S(1)}, bf16[40,4,256]{2,1,0:T(4,128)(2,1)S(1)}, u32[]{:S(2)}, u32[]{:S(2)}) collective-permute-start(bf16[40,4,256]{2,1,0:T(4,128)(2,1)S(1)} %get-tuple-element.26), channel_id=1, source_target_pairs={{0,1},{1,2},{2,3},{3,4},{4,5},{5,6},{6,7},{7,0},{8,9},{9,10},{10,1... | collective-permute-start | bytes 245768 | tf_op jit(solution)/shard_map/ppermute | solution.py:398
  63.8 9.4 %collective-permute-start.6 = (bf16[40,4,256]{2,1,0:T(4,128)(2,1)S(1)}, bf16[40,4,256]{2,1,0:T(4,128)(2,1)S(1)}, u32[]{:S(2)}, u32[]{:S(2)}) collective-permute-start(bf16[40,4,256]{2,1,0:T(4,128)(2,1)S(1)} %get-tuple-element.27), channel_id=1, source_target_pairs={{1,0},{2,1},{3,2},{4,3},{5,4},{6,5},{7,6},{0,7},{9,8},{10,9},{11,1... | collective-permute-start | bytes 245768 | tf_op jit(solution)/shard_map/ppermute | solution.py:399
  86.2 42.3 %copy-start.6 = (bf16[2,12288]{1,0:T(2,128)(2,1)S(1)}, bf16[2,12288]{1,0:T(2,128)(2,1)}, u32[]{:S(2)}) copy-start(bf16[2,12288]{1,0:T(2,128)(2,1)} %offset_ref.1) | copy-start | bytes 147460
  86.2 22.3 %all-to-all-start.2 = ((bf16[8,192,128]{2,1,0:T(8,128)(2,1)}), bf16[8,192,128]{2,1,0:T(8,128)(2,1)S(1)}, u32[]{:S(2)}, u32[]{:S(2)}) async-start(bf16[8,192,128]{2,1,0:T(8,128)(2,1)} %bitcast.11), calls=%async_computation.2 | async-start | bytes 786432 | tf_op jit(solution)/shard_map/all_to_all | solution.py:412
  89.8 9.7 %collective-permute-start.9 = (bf16[768,128]{1,0:T(8,128)(2,1)S(1)}, bf16[768,128]{1,0:T(8,128)(2,1)S(1)}, u32[]{:S(2)}, u32[]{:S(2)}) collective-permute-start(bf16[768,128]{1,0:T(8,128)(2,1)S(1)} %get-tuple-element.25.refs_1_), channel_id=1, source_target_pairs={{0,2},{2,4},{4,6},{6,0},{1,3},{3,5},{5,7},{7,1},{8,10},{10,12},{12... | collective-permute-start | bytes 589832 | tf_op jit(solution)/shard_map/ppermute | solution.py:418
  91.8 15.7 %collective-permute-start.8 = (bf16[768,128]{1,0:T(8,128)(2,1)S(1)}, bf16[768,128]{1,0:T(8,128)(2,1)S(1)}, u32[]{:S(2)}, u32[]{:S(2)}) collective-permute-start(bf16[768,128]{1,0:T(8,128)(2,1)S(1)} %get-tuple-element.25.refs_1_), channel_id=1, source_target_pairs={{0,4},{2,6},{4,0},{6,2},{1,5},{3,7},{5,1},{7,3},{8,12},{10,14},{12... | collective-permute-start | bytes 589832 | tf_op jit(solution)/shard_map/ppermute | solution.py:418
  93.7 13.8 %collective-permute-start.7 = (bf16[768,128]{1,0:T(8,128)(2,1)S(1)}, bf16[768,128]{1,0:T(8,128)(2,1)S(1)}, u32[]{:S(2)}, u32[]{:S(2)}) collective-permute-start(bf16[768,128]{1,0:T(8,128)(2,1)S(1)} %get-tuple-element.25.refs_1_), channel_id=1, source_target_pairs={{0,6},{2,0},{4,2},{6,4},{1,7},{3,1},{5,3},{7,5},{8,14},{10,8},{12,... | collective-permute-start | bytes 589832 | tf_op jit(solution)/shard_map/ppermute | solution.py:418
  (2 other events, 1.3 us)

commit v5 on v4

--- a/solution.py
+++ b/solution.py
@@ -56,17 +56,29 @@
 
 
 def encode_blocks(
-    capacity, shape, place_ref, tile_ref, patch_ref, feat_ref, offset_ref, near_ref, far_ref,
-    slot_ref, send_ref, count_ref,
+    capacity, shape, place_ref, tile_hbm, patch_hbm, feat_hbm, offset_hbm, near_ref, far_ref,
+    slot_ref, send_ref, tile_ref, patch_ref, feat_ref, offset_ref, count_ref, sems,
 ):
     lat, depth, width = shape
-    plane = lat * width
-    devices = plane * depth
+    devices = lat * depth * width
+    feat_width = feat_ref.shape[0]
     blocks = feat_ref.shape[1] // BLK
-    feat_width = feat_ref.shape[0]
+    step = sems.shape[0] - 3
+    size = blocks // step
     pairs = capacity // 2
     meta = meta_rows(pairs)
     chunk = pairs * feat_width + meta
+    small = [
+        pltpu.make_async_copy(tile_hbm, tile_ref, sems.at[step]),
+        pltpu.make_async_copy(patch_hbm, patch_ref, sems.at[step + 1]),
+        pltpu.make_async_copy(offset_hbm, offset_ref, sems.at[step + 2]),
+    ]
+    large = []
+    for i in range(step):
+        span = pl.ds(i * size * BLK, size * BLK)
+        large.append(pltpu.make_async_copy(feat_hbm.at[:, span], feat_ref.at[:, span], sems.at[i]))
+    for copy in small + large:
+        copy.start()
     send_ref[...] = jnp.zeros_like(send_ref)
 
     def clear(t, _):
@@ -84,9 +96,9 @@
         rank = count_ref[tile]
         count_ref[tile] = rank + 1
         lon = tile % (depth * width)
-        partner = (tile // (depth * width) * width + lon % width)
+        partner = tile // (depth * width) * width + lon % width
         hop = (lon // width + depth - place_ref[1]) % depth
-        piece = jnp.where(hop == 0, partner, plane + partner * (depth - 1) + hop - 1)
+        piece = jnp.where(hop == 0, partner, lat * width + partner * (depth - 1) + hop - 1)
         slot_ref[b] = piece * capacity + rank
         pair = rank // 2
         half = rank % 2
@@ -115,14 +127,12 @@
         )
         send_ref[pl.ds(row, meta), :] = jnp.where(meta_half == half, new, old).astype(jnp.bfloat16)
 
-    unroll = 32 if blocks % 32 == 0 else 1
-
-    def body(i, _):
-        for u in range(unroll):
-            one(i * unroll + u)
-        return 0
-
-    lax.fori_loop(0, blocks // unroll, body, 0)
+    for copy in small:
+        copy.wait()
+    for i in range(step):
+        large[i].wait()
+        for b in range(i * size, (i + 1) * size):
+            one(b)
     near_ref[...] = send_ref[: near_ref.shape[0]]
     far_ref[...] = send_ref[near_ref.shape[0] :]
 
@@ -179,24 +189,29 @@
         outs[hop][patch_pairs * feat_width :, :] = jnp.concatenate(rows, axis=0).astype(jnp.bfloat16)
 
 
-def start_tile(capacity, plane, hops, id_ref, recv_ref, *refs):
+def gather_own(capacity, plane, feat_width, id_ref, recv_ref, own_ref, acc_ref):
+    chunk = recv_ref.shape[0] // plane
+    acc_ref[...] = jnp.zeros_like(acc_ref)
+    for r in range(plane):
+        add_chunk(capacity, feat_width, id_ref, r * capacity, recv_ref, r * chunk, acc_ref)
+    for j in range(own_ref.shape[0]):
+        own_ref[j] = paired(acc_ref, j)
+
+
+def start_tile(hops, own_ref, *refs):
     parts = refs[:hops]
-    embed_ref, base_ref, start_ref, acc_ref = refs[hops:]
-    chunk = recv_ref.shape[0] // plane
+    embed_ref, base_ref, start_ref = refs[hops:]
     feat_width, channels = embed_ref.shape
     tile_rows, tile_cols, _ = base_ref.shape
     patch_rows, patch_cols = tile_rows // PATCH, tile_cols // PATCH
     patch_pairs = patch_rows * patch_cols // 2
-    acc_ref[...] = jnp.zeros_like(acc_ref)
-    for r in range(plane):
-        add_chunk(capacity, feat_width, id_ref, r * capacity, recv_ref, r * chunk, acc_ref)
     embed = embed_ref[...]
     mass_rows = [part[patch_pairs * feat_width :, :].astype(jnp.float32) for part in parts]
     for pr in range(patch_rows):
         lifted = []
         for pc in range(patch_cols // 2):
             j = pr * (patch_cols // 2) + pc
-            pair = paired(acc_ref, j)
+            pair = own_ref[j]
             sums, mass = pair[:feat_width], pair[feat_width : feat_width + 1]
             for part, rows in zip(parts, mass_rows):
                 sums = sums + part[j * feat_width : (j + 1) * feat_width, :].astype(jnp.float32)
@@ -209,141 +224,241 @@
         start_ref[rows] = (base_ref[rows].astype(jnp.float32) + lifted).astype(jnp.bfloat16)
 
 
-def grid_block(
-    lat_cells, place_ref, ext_ref, norm_ref, qkv_ref, out_ref, mlp_ref,
-    up_ref, down_ref, decode_ref, latent_ref, proj_ref, turned_ref, key_ref, pack_ref, att_ref,
-    mixed_ref, score_ref, prob_ref,
+def turn_weights(qkv_ref, turned_ref):
+    channels = qkv_ref.shape[0]
+    turned_ref[:channels] = qkv_ref[:, :channels].T
+    turned_ref[channels:] = qkv_ref[:, 2 * channels :].T
+
+
+def attend(
+    cells_ref, windows, side, norm_gain, qkv_ref, out_ref, turned_ref, key_ref, pack_ref, att_ref,
+    score_ref, prob_ref,
+):
+    channels = qkv_ref.shape[0]
+    tokens = WIN * WIN
+    group = 128
+    heads = group // HEAD_DIM
+    count = -(-len(windows) // 2)
+    size = count * LANES
+    scale = HEAD_DIM ** (-0.5) / math.log(2.0)
+    shape = (tokens, heads * LANES)
+    own = lax.broadcasted_iota(jnp.int32, shape, 1) % LANES < tokens
+    nothing = jnp.zeros(shape, jnp.bfloat16)
+    empty = jnp.zeros((HEAD_DIM, LANES), jnp.bfloat16)
+    cells = jnp.concatenate(
+        [
+            cells_ref[row : row + WIN, col : col + WIN, :].reshape(tokens, channels)
+            for row, col in windows
+        ],
+        axis=0,
+    )
+    normed = normalize(cells, norm_gain).astype(jnp.bfloat16)
+    if len(windows) % 2:
+        normed = jnp.concatenate([normed, jnp.zeros((tokens, channels), jnp.bfloat16)], axis=0)
+    key_ref[:size] = jnp.dot(
+        normed, qkv_ref[:, channels : 2 * channels], preferred_element_type=jnp.float32
+    ).astype(jnp.bfloat16)
+    pack_ref[:, :size] = lax.dot_general(
+        turned_ref[...], normed, NT, preferred_element_type=jnp.float32
+    ).astype(jnp.bfloat16)
+    if side is not None:
+        key_row = lax.broadcasted_iota(jnp.int32, (tokens, LANES), 0) // WIN
+        query_row = lax.broadcasted_iota(jnp.int32, (tokens, LANES), 1) % tokens // WIN
+        bias = jnp.where(side(key_row) == side(query_row), 0.0, -1e30)
+        bias = jnp.concatenate([bias] * heads, axis=1)
+    parts = [(p, g) for p in range(count) for g in range(channels // group)]
+    for n, (p, g) in enumerate(parts):
+        span = slice(p * LANES, (p + 1) * LANES)
+        at = slice(g * group, (g + 1) * group)
+        query = pack_ref[at, span]
+        stack = jnp.concatenate(
+            [
+                jnp.concatenate(
+                    [
+                        query[h * HEAD_DIM : (h + 1) * HEAD_DIM] if i == h else empty
+                        for i in range(heads)
+                    ],
+                    axis=0,
+                )
+                for h in range(heads)
+            ],
+            axis=1,
+        )
+        scores = jnp.dot(key_ref[span, at], stack, preferred_element_type=jnp.float32)
+        scores = jnp.where(own, scores[:tokens], scores[tokens:])
+        score_ref[n] = scores if side is None else scores + bias
+    for n in range(len(parts)):
+        scores = score_ref[n]
+        peak = jnp.max(scores, axis=0, keepdims=True)
+        raised = jnp.exp2((scores - peak) * scale)
+        total = jnp.sum(raised, axis=0, keepdims=True)
+        probs = (raised * (1.0 / total)).astype(jnp.bfloat16)
+        prob_ref[n, :tokens] = jnp.where(own, probs, nothing)
+        prob_ref[n, tokens:] = jnp.where(own, nothing, probs)
+    for n, (p, g) in enumerate(parts):
+        span = slice(p * LANES, (p + 1) * LANES)
+        for h in range(0, heads, 2):
+            at = g * group + h * HEAD_DIM
+            both = jnp.dot(
+                pack_ref[channels + at : channels + at + 2 * HEAD_DIM, span],
+                prob_ref[n, :, h * LANES : (h + 2) * LANES],
+                preferred_element_type=jnp.float32,
+            ).astype(jnp.bfloat16)
+            att_ref[at : at + HEAD_DIM, span] = both[:HEAD_DIM, :LANES]
+            att_ref[at + HEAD_DIM : at + 2 * HEAD_DIM, span] = both[HEAD_DIM:, LANES:]
+    mixed = lax.dot_general(
+        att_ref[:, :size], out_ref[...], TN, preferred_element_type=jnp.float32
+    )
+    return [
+        mixed[w * tokens : (w + 1) * tokens].reshape(WIN, WIN, channels)
+        for w in range(len(windows))
+    ]
+
+
+def finish(begun, mixed, mlp_gain, up_ref, down_ref, decode_ref):
+    residual = jnp.concatenate([a.reshape(CELLS, -1) + b.reshape(CELLS, -1) for a, b in zip(begun, mixed)])
+    normed = normalize(residual, mlp_gain).astype(jnp.bfloat16)
+    hidden = jax.nn.gelu(jnp.dot(normed, up_ref[...], preferred_element_type=jnp.float32))
+    latent = residual + jnp.dot(
+        hidden.astype(jnp.bfloat16), down_ref[...], preferred_element_type=jnp.float32
+    )
+    projected = jnp.dot(
+        latent.astype(jnp.bfloat16), decode_ref[...], preferred_element_type=jnp.float32
+    )
+    turned = [
+        projected[i * CELLS : i * CELLS + LANES].T.astype(jnp.bfloat16)
+        for i in range(0, len(begun), 2)
+    ]
+    return latent, turned
+
+
+def patch_order(patch_rows, patch_cols):
+    inner = lambda r, c: 0 < r < patch_rows - 1 and 0 < c < patch_cols - 1
+    every = [(r, c) for r in range(patch_rows) for c in range(patch_cols)]
+    first = [at for at in every if inner(*at)]
+    sides = [at for at in every if 0 < at[0] < patch_rows - 1 and not inner(*at)]
+    ends = [at for at in every if not 0 < at[0] < patch_rows - 1]
+    return first, sides, ends
+
+
+def inner_block(
+    start_ref, norm_ref, qkv_ref, out_ref, mlp_ref, up_ref, down_ref, decode_ref, latent_ref,
+    proj_ref, mixed_ref, cells_ref, turned_ref, key_ref, pack_ref, att_ref, score_ref, prob_ref,
+):
+    tile_rows, tile_cols, channels = cells_ref.shape
+    margin = WIN // 2
+    feat_width = decode_ref.shape[1]
+    cells_ref[...] = start_ref[...].astype(jnp.float32)
+    turn_weights(qkv_ref, turned_ref)
+    for row in range(0, tile_rows - WIN, WIN):
+        cols = range(0, tile_cols - WIN, WIN)
+        mixed = attend(
+            cells_ref, [(row + margin, col + margin) for col in cols], None, norm_ref[...],
+            qkv_ref, out_ref, turned_ref, key_ref, pack_ref, att_ref, score_ref, prob_ref,
+        )
+        for col, block in zip(cols, mixed):
+            mixed_ref[row : row + WIN, col : col + WIN, :] = block
+    first, _, _ = patch_order(tile_rows // PATCH, tile_cols // PATCH)
+    done = 0
+    for pr in sorted(set(r for r, _ in first)):
+        here = [c for r, c in first if r == pr]
+        row = pr * PATCH
+        latent, turned = finish(
+            [cells_ref[row : row + PATCH, c * PATCH : (c + 1) * PATCH, :] for c in here],
+            [
+                mixed_ref[
+                    row - margin : row - margin + PATCH,
+                    c * PATCH - margin : c * PATCH - margin + PATCH,
+                    :,
+                ]
+                for c in here
+            ],
+            mlp_ref[...], up_ref, down_ref, decode_ref,
+        )
+        placed = latent.reshape(len(here), PATCH, PATCH, channels).transpose(1, 0, 2, 3)
+        latent_ref[row - PATCH : row] = placed.reshape(PATCH, len(here) * PATCH, channels).astype(
+            jnp.bfloat16
+        )
+        for pair in turned:
+            proj_ref[done : done + feat_width, :] = pair
+            done += feat_width
+
+
+def outer_block(
+    lat_cells, place_ref, ext_ref, inner_latent_ref, inner_proj_ref, inner_mixed_ref, norm_ref, qkv_ref, out_ref,
+    mlp_ref, up_ref, down_ref, decode_ref, latent_ref, proj_ref, mixed_ref, turned_ref, key_ref,
+    pack_ref, att_ref, score_ref, prob_ref,
 ):
     ext_rows, ext_cols, channels = ext_ref.shape
     tile_rows, tile_cols, _ = latent_ref.shape
     margin = WIN // 2
-    win_rows, win_cols = ext_rows // WIN, ext_cols // WIN
-    win_pairs = -(-win_cols // 2)
-    patch_rows, patch_cols = tile_rows // PATCH, tile_cols // PATCH
-    tokens = WIN * WIN
-    group = 128
-    heads = group // HEAD_DIM
     feat_width = decode_ref.shape[1]
-    scale = HEAD_DIM ** (-0.5) / math.log(2.0)
-    norm_gain = norm_ref[...]
-    turned_ref[:channels] = qkv_ref[:, :channels].T
-    turned_ref[channels:] = qkv_ref[:, 2 * channels :].T
-    shape = (tokens, heads * LANES)
-    own = lax.broadcasted_iota(jnp.int32, shape, 1) % LANES < tokens
-    key_row = lax.broadcasted_iota(jnp.int32, (tokens, LANES), 0) // WIN
-    query_row = lax.broadcasted_iota(jnp.int32, (tokens, LANES), 1) % tokens // WIN
-    nothing = jnp.zeros(shape, jnp.bfloat16)
-    empty = jnp.zeros((HEAD_DIM, LANES), jnp.bfloat16)
-
-    def attend(wr):
-        rows = pl.ds(wr * WIN, WIN)
-        cells = ext_ref[rows].reshape(WIN, win_cols, WIN, channels).transpose(1, 0, 2, 3)
-        normed = normalize(cells.reshape(win_cols * tokens, channels), norm_gain)
-        normed = normed.astype(jnp.bfloat16)
-        if win_cols % 2:
-            normed = jnp.concatenate([normed, jnp.zeros((tokens, channels), jnp.bfloat16)], axis=0)
-        key_ref[...] = jnp.dot(
-            normed, qkv_ref[:, channels : 2 * channels], preferred_element_type=jnp.float32
-        ).astype(jnp.bfloat16)
-        pack_ref[...] = lax.dot_general(
-            turned_ref[...], normed, NT, preferred_element_type=jnp.float32
-        ).astype(jnp.bfloat16)
-        edge = wr in (0, win_rows - 1)
-        if edge:
-            top = place_ref[2] * tile_rows - margin + wr * WIN
-            side = lambda r: (r >= 0).astype(jnp.int32) + (r >= lat_cells).astype(jnp.int32)
-            bias = jnp.where(side(top + key_row) == side(top + query_row), 0.0, -1e30)
-            bias = jnp.concatenate([bias] * heads, axis=1)
-        parts = [(p, g) for p in range(win_pairs) for g in range(channels // group)]
-        for n, (p, g) in enumerate(parts):
-            span = slice(p * LANES, (p + 1) * LANES)
-            at = slice(g * group, (g + 1) * group)
-            query = pack_ref[at, span]
-            stack = jnp.concatenate(
-                [
-                    jnp.concatenate(
-                        [
-                            query[h * HEAD_DIM : (h + 1) * HEAD_DIM] if i == h else empty
-                            for i in range(heads)
-                        ],
-                        axis=0,
-                    )
-                    for h in range(heads)
-                ],
-                axis=1,
+    last_row, last_col = ext_rows - WIN, ext_cols - WIN
+    top = place_ref[2] * tile_rows - margin
+    turn_weights(qkv_ref, turned_ref)
+
+    def place(windows, side):
+        mixed = attend(
+            ext_ref, windows, side, norm_ref[...], qkv_ref, out_ref, turned_ref, key_ref,
+            pack_ref, att_ref, score_ref, prob_ref,
+        )
+        for (row, col), block in zip(windows, mixed):
+            mixed_ref[row : row + WIN, col : col + WIN, :] = block
+
+    for row in (0, last_row):
+        side = lambda r: (top + row + r >= 0).astype(jnp.int32) + (
+            top + row + r >= lat_cells
+        ).astype(jnp.int32)
+        place([(row, col) for col in range(0, ext_cols, WIN)], side)
+    place([(row, col) for row in range(WIN, last_row, WIN) for col in (0, last_col)], None)
+    mixed_ref[WIN:last_row, WIN:last_col, :] = inner_mixed_ref[...]
+    _, sides, ends = patch_order(tile_rows // PATCH, tile_cols // PATCH)
+    done = inner_proj_ref.shape[0]
+    proj_ref[:done, :] = inner_proj_ref[...]
+
+    def patches(here):
+        at = [
+            (
+                slice(r * PATCH + margin, (r + 1) * PATCH + margin),
+                slice(c * PATCH + margin, (c + 1) * PATCH + margin),
             )
-            scores = jnp.dot(key_ref[span, at], stack, preferred_element_type=jnp.float32)
-            scores = jnp.where(own, scores[:tokens], scores[tokens:])
-            score_ref[n] = scores + bias if edge else scores
-        for n, (p, g) in enumerate(parts):
-            scores = score_ref[n]
-            peak = jnp.max(scores, axis=0, keepdims=True)
-            raised = jnp.exp2((scores - peak) * scale)
-            total = jnp.sum(raised, axis=0, keepdims=True)
-            probs = (raised * (1.0 / total)).astype(jnp.bfloat16)
-            prob_ref[n, :tokens] = jnp.where(own, probs, nothing)
-            prob_ref[n, tokens:] = jnp.where(own, nothing, probs)
-        for n, (p, g) in enumerate(parts):
-            span = slice(p * LANES, (p + 1) * LANES)
-            for h in range(0, heads, 2):
-                at = g * group + h * HEAD_DIM
-                both = jnp.dot(
-                    pack_ref[channels + at : channels + at + 2 * HEAD_DIM, span],
-                    prob_ref[n, :, h * LANES : (h + 2) * LANES],
-                    preferred_element_type=jnp.float32,
-                ).astype(jnp.bfloat16)
-                att_ref[at : at + HEAD_DIM, span] = both[:HEAD_DIM, :LANES]
-                att_ref[at + HEAD_DIM : at + 2 * HEAD_DIM, span] = both[HEAD_DIM:, LANES:]
-        mixed = lax.dot_general(att_ref[...], out_ref[...], TN, preferred_element_type=jnp.float32)
-        for w in range(win_cols):
-            mixed_ref[rows, w * WIN : (w + 1) * WIN, :] = mixed[w * tokens : (w + 1) * tokens].reshape(
-                WIN, WIN, channels
-            )
-
-    for wr in range(win_rows):
-        attend(wr)
-    mlp_gain = mlp_ref[...]
-
-    def by_patch(values):
-        values = values.reshape(PATCH, patch_cols, PATCH, channels).transpose(1, 0, 2, 3)
-        return values.reshape(patch_cols * CELLS, channels)
-
-    def finish(pr, _):
-        rows = pl.ds(margin + pr * PATCH, PATCH)
-        inner = slice(margin, margin + tile_cols)
-        residual = by_patch(ext_ref[rows, inner, :] + mixed_ref[rows, inner, :])
-        normed = normalize(residual, mlp_gain).astype(jnp.bfloat16)
-        hidden = jax.nn.gelu(
-            jnp.dot(normed, up_ref[...], preferred_element_type=jnp.float32)
-        ).astype(jnp.bfloat16)
-        latent = residual + jnp.dot(hidden, down_ref[...], preferred_element_type=jnp.float32)
-        placed = latent.reshape(patch_cols, PATCH, PATCH, channels).transpose(1, 0, 2, 3)
-        latent_ref[pl.ds(pr * PATCH, PATCH)] = placed.reshape(PATCH, tile_cols, channels).astype(
-            jnp.bfloat16
+            for r, c in here
+        ]
+        latent, turned = finish(
+            [ext_ref[r, c, :] for r, c in at],
+            [mixed_ref[r, c, :] for r, c in at],
+            mlp_ref[...], up_ref, down_ref, decode_ref,
         )
-        latent = latent.astype(jnp.bfloat16)
-        projected = jnp.dot(latent, decode_ref[...], preferred_element_type=jnp.float32)
-        for pc in range(0, patch_cols, 2):
-            turned = projected[pc * CELLS : pc * CELLS + LANES].T
-            j = pr * (patch_cols // 2) + pc // 2
-            proj_ref[pl.ds(pl.multiple_of(j * feat_width, 16), feat_width), :] = turned.astype(
-                jnp.bfloat16
-            )
-        return 0
-
-    lax.fori_loop(0, patch_rows, finish, 0, unroll=True)
-
-
-def reply_patches(capacity, plane, tiles, feat_width, id_ref, *refs):
+        for i, pair in enumerate(turned):
+            at = done + i * feat_width
+            proj_ref[at : at + feat_width, :] = pair
+        return latent.reshape(len(here), PATCH, PATCH, channels), len(turned) * feat_width
+
+    latent, used = patches(sides)
+    done += used
+    for pr in sorted(set(r for r, _ in sides)):
+        left, right = [latent[i] for i, (r, _) in enumerate(sides) if r == pr]
+        inner = inner_latent_ref[(pr - 1) * PATCH : pr * PATCH].astype(jnp.float32)
+        whole = jnp.concatenate([left, inner, right], axis=1)
+        latent_ref[pr * PATCH : (pr + 1) * PATCH] = whole.astype(jnp.bfloat16)
+    for pr in sorted(set(r for r, _ in ends)):
+        latent, used = patches([at for at in ends if at[0] == pr])
+        done += used
+        placed = latent.transpose(1, 0, 2, 3).reshape(PATCH, tile_cols, channels)
+        latent_ref[pr * PATCH : (pr + 1) * PATCH] = placed.astype(jnp.bfloat16)
+
+
+def reply_patches(capacity, plane, tiles, order, feat_width, id_ref, *refs):
     tile_refs, out_ref, both_ref = refs[:tiles], refs[tiles], refs[tiles + 1]
     pairs = capacity // 2
     first = lax.broadcasted_iota(jnp.int32, (feat_width, LANES), 1) < CELLS
     for t in range(tiles):
-        for j in range(both_ref.shape[1] // 2):
-            pair = tile_refs[t][j * feat_width : (j + 1) * feat_width, :].astype(jnp.float32)
+        for i in range(0, len(order), 2):
+            at = i // 2 * feat_width
+            pair = tile_refs[t][at : at + feat_width, :].astype(jnp.float32)
             swapped = pltpu.roll(pair, CELLS, 1)
-            both_ref[t, 2 * j] = jnp.where(first, pair, swapped)
-            both_ref[t, 2 * j + 1] = jnp.where(first, swapped, pair)
+            both_ref[t, order[i]] = jnp.where(first, pair, swapped)
+            both_ref[t, order[i + 1]] = jnp.where(first, swapped, pair)
     for r in range(plane):
         for t in range(tiles):
             for k in range(pairs):
@@ -355,12 +470,9 @@
                 out_ref[at : at + feat_width, :] = pair.astype(jnp.bfloat16)
 
 
-def decode_blocks(slot_ref, offset_ref, *refs):
-    pieces, out_ref, back_ref = refs[:-2], refs[-2], refs[-1]
-    at = 0
-    for piece in pieces:
-        back_ref[at : at + piece.shape[0], :] = piece[...]
-        at += piece.shape[0]
+def decode_blocks(slot_ref, offset_ref, near_ref, far_ref, out_ref, back_ref):
+    back_ref[: near_ref.shape[0], :] = near_ref[...]
+    back_ref[near_ref.shape[0] :, :] = far_ref[...]
     feat_width, count = out_ref.shape
     blocks = count // BLK
 
@@ -411,6 +523,17 @@
     parts = array.reshape(plane, -1, LANES)
     parts = lax.all_to_all(parts, ("lat", "x"), split_axis=0, concat_axis=0, tiled=True)
     return parts.reshape(array.shape)
+
+
+def swap_at_once(gains, array):
+    def apart(array):
+        lat, width = lax.axis_size("lat"), lax.axis_size("x")
+        parts = array.reshape(lat, width, -1, LANES)
+        for dim, axis in enumerate(("lat", "x")):
+            parts = lax.all_to_all(parts, axis, split_axis=dim, concat_axis=dim, tiled=True)
+        return parts.reshape(array.shape)
+
+    return lax.cond(gains[0] > 0.0, swap_in_plane, apart, array)
 
 
 def shift_planes(array, hop):
@@ -450,6 +573,7 @@
         [lat_id * width + lax.axis_index("x"), lax.axis_index("z"), lat_id]
     ).astype(jnp.int32)
 
+    steps = 3 if blocks % 3 == 0 else 1
     send_near, send_far, slots = pl.pallas_call(
         lambda *refs: encode_blocks(capacity, (lat, depth, width), *refs),
         out_shape=(
@@ -457,11 +581,16 @@
             jax.ShapeDtypeStruct((plane * hops * chunk, LANES), jnp.bfloat16),
             jax.ShapeDtypeStruct((blocks,), jnp.int32),
         ),
-        in_specs=[smem(), smem(), smem(), vmem(), vmem()],
+        in_specs=[smem()] + [pl.BlockSpec(memory_space=pltpu.HBM)] * 4,
         out_specs=(vmem(), vmem(), smem()),
         scratch_shapes=[
             pltpu.VMEM((devices * chunk, LANES), jnp.bfloat16),
+            pltpu.SMEM((blocks,), jnp.int32),
+            pltpu.SMEM((blocks,), jnp.int32),
+            pltpu.VMEM(obs_feat.shape, jnp.bfloat16),
+            pltpu.VMEM(obs_offset.shape, jnp.bfloat16),
             pltpu.SMEM((devices,), jnp.int32),
+            pltpu.SemaphoreType.DMA((steps + 3,)),
         ],
         compiler_params=params(10),
         name="encode_blocks",
@@ -481,77 +610,108 @@
         in_specs=[smem(), vmem()],
         out_specs=[vmem()] * hops,
         scratch_shapes=[pltpu.VMEM((hops, patch_total, feat_width + 8, LANES), jnp.float32)],
-        compiler_params=params(8),
+        compiler_params=params(10),
         name="gather_planes",
     )(far_ids, far)
-    send_near, sums = lax.optimization_barrier((send_near, sums))
     parts = [shift_planes(sums[hop], hop + 1) for hop in range(hops)]
-    near = swap_in_plane(send_near)
+    send_near, _ = lax.optimization_barrier((send_near, sums))
+    near = swap_at_once(norm_gain, send_near)
     near_ids = ids_of(near, 1)
-
-    start = pl.pallas_call(
-        lambda *refs: start_tile(capacity, plane, hops, *refs),
-        out_shape=jax.ShapeDtypeStruct(grid_base.shape, jnp.bfloat16),
-        in_specs=[smem()] + [vmem()] * (hops + 3),
+    own = pl.pallas_call(
+        lambda *refs: gather_own(capacity, plane, feat_width, *refs),
+        out_shape=jax.ShapeDtypeStruct((patch_total // 2, feat_width + 8, LANES), jnp.float32),
+        in_specs=[smem(), vmem()],
         out_specs=vmem(),
         scratch_shapes=[pltpu.VMEM((patch_total, feat_width + 8, LANES), jnp.float32)],
-        compiler_params=params(8),
+        compiler_params=params(10),
+        cost_estimate=pl.CostEstimate(flops=10**9, bytes_accessed=10**7, transcendentals=0),
+        name="gather_own",
+    )(near_ids, near)
+
+    start = pl.pallas_call(
+        lambda *refs: start_tile(hops, *refs),
+        out_shape=jax.ShapeDtypeStruct(grid_base.shape, jnp.bfloat16),
+        in_specs=[vmem()] * (hops + 3),
+        out_specs=vmem(),
+        compiler_params=params(10),
         name="start_tile",
-    )(near_ids, near, *parts, embed_weight, grid_base)
+    )(own, *parts, embed_weight, grid_base)
 
     margin = WIN // 2
     ext = with_halo(start, (("lat", 0), (("z", "x"), 1)), margin).astype(jnp.float32)
     ext_rows, ext_cols, _ = ext.shape
-    padded = -(-ext_cols // (2 * WIN)) * LANES
+    group = 128
+    gains = (norm_gain.reshape(1, channels), mlp_gain.reshape(1, channels))
+    weights = (gains[0], qkv_weight, out_weight, gains[1], up_weight, down_weight, decode_weight)
+    patch_rows, patch_cols = tile_rows // PATCH, tile_cols // PATCH
+    inner, sides, ends = patch_order(patch_rows, patch_cols)
+    order = [r * patch_cols + c for r, c in inner + sides + ends]
+    inner_cells = (tile_rows - 2 * PATCH, tile_cols - 2 * PATCH, channels)
+    inner_mixed = (tile_rows - WIN, tile_cols - WIN, channels)
+
+    def scratch(windows):
+        count = -(-windows // 2)
+        parts = count * channels // group
+        lanes = group // HEAD_DIM * LANES
+        return [
+            pltpu.VMEM((2 * channels, channels), jnp.bfloat16),
+            pltpu.VMEM((count * LANES, channels), jnp.bfloat16),
+            pltpu.VMEM((2 * channels, count * LANES), jnp.bfloat16),
+            pltpu.VMEM((channels, count * LANES), jnp.bfloat16),
+            pltpu.VMEM((parts, WIN * WIN, lanes), jnp.float32),
+            pltpu.VMEM((parts, LANES, lanes), jnp.bfloat16),
+        ]
+
+    latent_inner, proj_inner, mixed_inner = pl.pallas_call(
+        inner_block,
+        out_shape=(
+            jax.ShapeDtypeStruct(inner_cells, jnp.bfloat16),
+            jax.ShapeDtypeStruct((len(inner) // 2 * feat_width, LANES), jnp.bfloat16),
+            jax.ShapeDtypeStruct(inner_mixed, jnp.float32),
+        ),
+        in_specs=[vmem()] * 8,
+        out_specs=(vmem(), vmem(), vmem()),
+        scratch_shapes=[pltpu.VMEM(grid_base.shape, jnp.float32)]
+        + scratch(tile_cols // WIN - 1),
+        compiler_params=params(16),
+        cost_estimate=pl.CostEstimate(flops=6 * 10**9, bytes_accessed=10**7, transcendentals=0),
+        name="inner_block",
+    )(start, *weights)
 
     latent, projected = pl.pallas_call(
-        lambda *refs: grid_block(tile_rows * lat, *refs),
+        lambda *refs: outer_block(tile_rows * lat, *refs),
         out_shape=(
             jax.ShapeDtypeStruct(grid_base.shape, jnp.bfloat16),
             jax.ShapeDtypeStruct((patch_total // 2 * feat_width, LANES), jnp.bfloat16),
         ),
-        in_specs=[smem()] + [vmem()] * 8,
+        in_specs=[smem()] + [vmem()] * 11,
         out_specs=(vmem(), vmem()),
-        scratch_shapes=[
-            pltpu.VMEM((2 * channels, channels), jnp.bfloat16),
-            pltpu.VMEM((padded, channels), jnp.bfloat16),
-            pltpu.VMEM((2 * channels, padded), jnp.bfloat16),
-            pltpu.VMEM((channels, padded), jnp.bfloat16),
-            pltpu.VMEM((ext_rows, ext_cols, channels), jnp.float32),
-            pltpu.VMEM((padded * channels // LANES // 128, WIN * WIN, 4 * LANES), jnp.float32),
-            pltpu.VMEM((padded * channels // LANES // 128, LANES, 4 * LANES), jnp.bfloat16),
-        ],
+        scratch_shapes=[pltpu.VMEM((ext_rows, ext_cols, channels), jnp.float32)]
+        + scratch(max(ext_cols // WIN, 2 * (ext_rows // WIN - 2))),
         compiler_params=params(20),
-        name="grid_block",
-    )(
-        place,
-        ext,
-        norm_gain.reshape(1, channels),
-        qkv_weight,
-        out_weight,
-        mlp_gain.reshape(1, channels),
-        up_weight,
-        down_weight,
-        decode_weight,
-    )
+        cost_estimate=pl.CostEstimate(flops=8 * 10**9, bytes_accessed=10**7, transcendentals=0),
+        name="outer_block",
+    )(place, ext, latent_inner, proj_inner, mixed_inner, *weights)
 
     def reply(ids, tiles, name):
         count = len(tiles)
-        rows = count * pairs * feat_width
-        out = pl.pallas_call(
-            lambda *refs: reply_patches(capacity, plane, count, feat_width, *refs),
-            out_shape=jax.ShapeDtypeStruct((plane * rows, LANES), jnp.bfloat16),
+        return pl.pallas_call(
+            lambda *refs: reply_patches(capacity, plane, count, order, feat_width, *refs),
+            out_shape=jax.ShapeDtypeStruct(
+                (plane * count * pairs * feat_width, LANES), jnp.bfloat16
+            ),
             in_specs=[smem()] + [vmem()] * count,
             out_specs=vmem(),
             scratch_shapes=[pltpu.VMEM((count, patch_total, feat_width, LANES), jnp.float32)],
-            compiler_params=params(8),
+            compiler_params=params(12),
+            cost_estimate=pl.CostEstimate(flops=10**9, bytes_accessed=10**7, transcendentals=0),
             name=name,
         )(ids, *tiles)
-        return swap_in_plane(out)
 
     others = [shift_planes(projected, -hop) for hop in range(1, depth)]
-    near_back = reply(near_ids, [projected], "reply_near")
-    far_back = reply(far_ids, others, "reply_far")
+    near_reply = reply(near_ids, [projected], "reply_near")
+    near_back = swap_at_once(norm_gain, near_reply)
+    far_back = swap_in_plane(reply(far_ids, others, "reply_far"))
 
     obs_out = pl.pallas_call(
         decode_blocks,

time: 135 us -> 125 us (0.926); the launches traced: 132 us -> 124 us
  waiting for transfers between devices: 31.7 us -> 25.3 us
  starting transfers between devices: 26 us -> 21.9 us
  local copies, waits for them, and re-layouts: 4.19 us -> 7.11 us
  blocking collectives: 42.5 us -> 39.8 us
  Pallas kernels: 26.5 us -> 28.1 us
    ppermute x6, waiting for transfers between devices: 23 us -> 6.91 us  [shift_planes(): lax.ppermute(array, 'z', [(i, (i + hop) % depth) for i in range(depth)])]
    all_to_all x2 -> x1, waiting for transfers between devices: 2.58 us -> 16.2 us  [swap_in_plane(): lax.all_to_all(parts, ('lat', 'x'), split_axis=0, concat_axis=0, tiled=True)]
    all_to_all x2 -> x3, blocking collectives: 42.5 us -> 39.8 us  [swap_in_plane(): lax.all_to_all(parts, ('lat', 'x'), split_axis=0, concat_axis=0, tiled=True)]
    unnamed x29 -> x33, local copies, waits for them, and re-layouts: 3.69 us -> 6.09 us
    ppermute x2, waiting for transfers between devices: 4.37 us -> 2.18 us  [with_halo(): before = lax.ppermute(last, axis, up)]
    all_to_all x2 -> x1, starting transfers between devices: 7.06 us -> 5.18 us  [swap_in_plane(): lax.all_to_all(parts, ('lat', 'x'), split_axis=0, concat_axis=0, tiled=True)]
    ppermute x2, waiting for transfers between devices: 1.78 us -> 0.01 us  [with_halo(): after = lax.ppermute(initial, axis, down)]
    ppermute x6, starting transfers between devices: 10 us -> 8.3 us  [shift_planes(): lax.ppermute(array, 'z', [(i, (i + hop) % depth) for i in range(depth)])]
  transfers between devices with their start and end apart: 12 -> 11, of which waited for: 9 -> 3; matrix products, arithmetic and copies ran while one was open for 0% -> 1% of each run, Pallas kernels for 1% -> 5%
where the time goes in v5:
time: 125 us; the launch traced here: 124 us
  blocking collectives  39.8 us (32%)
  Pallas kernels  28.1 us (22%)
  waiting for transfers between devices  25.3 us (20%)
  starting transfers between devices  21.9 us (18%)
  local copies, waits for them, and re-layouts  7.11 us (6%)
  between operations  1.5 us (1%)
    all_to_all x3, blocking collectives, swap_in_plane(): lax.all_to_all(parts, ('lat', 'x'), split_axis=0, concat_axis=0, tiled=True)  39.8 us
    all_to_all x1, waiting for transfers between devices, swap_in_plane(): lax.all_to_all(parts, ('lat', 'x'), split_axis=0, concat_axis=0, tiled=True)  16.2 us
    ppermute x6, starting transfers between devices, shift_planes(): lax.ppermute(array, 'z', [(i, (i + hop) % depth) for i in range(depth)])  8.3 us
    pallas_call x1, Pallas kernels, local(): pl.pallas_call(lambda *refs: outer_block(tile_rows * lat, *refs), out_sha...  7.79 us
    ppermute x2, starting transfers between devices, with_halo(): after = lax.ppermute(initial, axis, down)  6.92 us
    ppermute x6, waiting for transfers between devices, shift_planes(): lax.ppermute(array, 'z', [(i, (i + hop) % depth) for i in range(depth)])  6.91 us
    unnamed x33, local copies, waits for them, and re-layouts  6.09 us
    pallas_call x1, Pallas kernels, local(): pl.pallas_call(lambda *refs: encode_blocks(capacity, (lat, depth, width),...  5.72 us
  transfers between devices with their start and end apart: 11, of which 3 were waited for; matrix products, arithmetic and copies ran while one was open for 1% of the time, Pallas kernels for 5%

profile of v5, /device:TPU:0, one launch (start us, length us, event | category | flops | bytes accessed | tf_op | source)
XLA Modules:
  0.0 124.4 jit_solution(1721913886354511518)
XLA Ops:
  0.7 1.4 %copy-done = bf16[64,12288]{1,0:T(8,128)(2,1)S(1)} copy-done((bf16[64,12288]{1,0:T(8,128)(2,1)S(1)}, bf16[64,12288]{1,0:T(8,128)(2,1)}, u32[]{:S(2)}) %copy-start) | copy-done | bytes 1572888
  4.2 5.7 %encode_blocks.1 = (bf16[1664,128]{1,0:T(8,128)(2,1)S(1)}, bf16[4992,128]{1,0:T(8,128)(2,1)}, s32[96]{0:T(128)S(1)}) custom-call(s32[3]{0:T(128)S(1)} %pad_add_fusion.refs_0_, s32[96]{0:T(128)S(1)} %bitcast.25, s32[96]{0:T(128)S(1)} %copy-done.6, bf16[64,12288]{1,0:T(8,128)(2,1)S(1)} %copy-done, bf16[2,12288]{1,0:T(2,128)(2,1)S(1)} %copy-done.2), custom_call_target="tpu_custom_call" | custom-call | tf_op jit(solution)/shard_map/encode_blocks/pallas_call | solution.py:577
  10.0 5.2 %all-to-all-start.6 = ((bf16[8,624,128]{2,1,0:T(8,128)(2,1)}), bf16[8,624,128]{2,1,0:T(8,128)(2,1)S(1)}, u32[]{:S(2)}, u32[]{:S(2)}) async-start(bf16[8,624,128]{2,1,0:T(8,128)(2,1)} %bitcast.13), calls=%async_computation.6 | async-start | bytes 2555904 | tf_op jit(solution)/shard_map/all_to_all | solution.py:524
  16.3 16.2 %all-to-all-done.6 = bf16[8,624,128]{2,1,0:T(8,128)(2,1)S(1)} async-done(((bf16[8,624,128]{2,1,0:T(8,128)(2,1)}), bf16[8,624,128]{2,1,0:T(8,128)(2,1)S(1)}, u32[]{:S(2)}, u32[]{:S(2)}) %all-to-all-start.6) | async-done | bytes 1277984 | tf_op jit(solution)/shard_map/all_to_all | solution.py:524
  32.9 2.8 %gather_planes.1 = (bf16[800,128]{1,0:T(8,128)(2,1)}, bf16[800,128]{1,0:T(8,128)(2,1)}, bf16[800,128]{1,0:T(8,128)(2,1)S(1)}) custom-call(s32[144]{0:T(256)S(1)} %reshape.64.refs_0_, bf16[4992,128]{1,0:T(8,128)(2,1)S(1)} %bitcast.22), custom_call_target="tpu_custom_call" | custom-call | tf_op jit(solution)/shard_map/gather_planes/pallas_call | solution.py:607
  35.7 1.6 %collective-permute-start = (bf16[800,128]{1,0:T(8,128)(2,1)}, bf16[800,128]{1,0:T(8,128)(2,1)S(1)}, u32[]{:S(2)}, u32[]{:S(2)}) collective-permute-start(bf16[800,128]{1,0:T(8,128)(2,1)} %get-tuple-element.26), channel_id=1, source_target_pairs={{0,2},{2,4},{4,6},{6,0},{1,3},{3,5},{5,7},{7,1},{8,10},{10,12},{12... | collective-permute-start | bytes 614408 | tf_op jit(solution)/shard_map/ppermute | solution.py:541
  37.3 2.6 %collective-permute-start.1 = (bf16[800,128]{1,0:T(8,128)(2,1)}, bf16[800,128]{1,0:T(8,128)(2,1)S(1)}, u32[]{:S(2)}, u32[]{:S(2)}) collective-permute-start(bf16[800,128]{1,0:T(8,128)(2,1)} %get-tuple-element.27), channel_id=1, source_target_pairs={{0,4},{2,6},{4,0},{6,2},{1,5},{3,7},{5,1},{7,3},{8,12},{10,14},{12... | collective-permute-start | bytes 614408 | tf_op jit(solution)/shard_map/ppermute | solution.py:541
  39.9 1.3 %collective-permute-start.2 = (bf16[800,128]{1,0:T(8,128)(2,1)S(1)}, bf16[800,128]{1,0:T(8,128)(2,1)S(1)}, u32[]{:S(2)}, u32[]{:S(2)}) collective-permute-start(bf16[800,128]{1,0:T(8,128)(2,1)S(1)} %get-tuple-element.28), channel_id=1, source_target_pairs={{0,6},{2,0},{4,2},{6,4},{1,7},{3,1},{5,3},{7,5},{8,14},{10,8},{12,... | collective-permute-start | bytes 614408 | tf_op jit(solution)/shard_map/ppermute | solution.py:541
  41.2 10.6 %conditional.2 = (bf16[1664,128]{1,0:T(8,128)(2,1)S(1)}) conditional(s32[]{:T(128)} %bitcast.11, bf16[1664,128]{1,0:T(8,128)(2,1)S(1)} %get-tuple-element.29, bf16[1664,128]{1,0:T(8,128)(2,1)S(1)} %get-tuple-element.29), branch_computations={%region_0.1_spmd, %region_1.2_spmd} | conditional | bytes 3407880 | solution.py:536
  41.2 10.6 %all_to_all.36 = bf16[8,208,128]{2,1,0:T(8,128)(2,1)S(1)} all-to-all(bf16[8,208,128]{2,1,0:T(8,128)(2,1)S(1)} %bitcast.31), channel_id=1, replica_groups=mesh['lat'=4,'z'=4,'x'=2] {'lat','x'}, dimensions={0} | all-to-all | bytes 851968 | tf_op jit(solution)/shard_map/cond/branch_1_fun/all_to_all | solution.py:524
  52.1 1.2 gather_own.1.refs_0_
  54.2 1.4 %collective-permute-start.4 = (bf16[4,48,256]{2,1,0:T(8,128)(2,1)S(1)}, bf16[4,48,256]{2,1,0:T(8,128)(2,1)S(1)}, u32[]{:S(2)}, u32[]{:S(2)}) collective-permute-start(bf16[4,48,256]{2,1,0:T(8,128)(2,1)S(1)} %get-tuple-element.39), channel_id=1, source_target_pairs={{8,0},{16,8},{24,16},{0,24},{9,1},{17,9},{25,17},{1,25},{10,2},{18... | collective-permute-start | bytes 294920 | tf_op jit(solution)/shard_map/ppermute | solution.py:511
  55.7 2.2 %collective-permute-done.3 = bf16[4,48,256]{2,1,0:T(8,128)(2,1)S(1)} collective-permute-done((bf16[4,48,256]{2,1,0:T(8,128)(2,1)S(1)}, bf16[4,48,256]{2,1,0:T(8,128)(2,1)S(1)}, u32[]{:S(2)}, u32[]{:S(2)}) %collective-permute-start.3) | collective-permute-done | bytes 98336 | tf_op jit(solution)/shard_map/ppermute | solution.py:510
  58.0 1.1 collective-permute-start.5
  59.1 5.5 %collective-permute-start.6 = (bf16[40,4,256]{2,1,0:T(4,128)(2,1)S(1)}, bf16[40,4,256]{2,1,0:T(4,128)(2,1)S(1)}, u32[]{:S(2)}, u32[]{:S(2)}) collective-permute-start(bf16[40,4,256]{2,1,0:T(4,128)(2,1)S(1)} %get-tuple-element.37), channel_id=1, source_target_pairs={{1,0},{2,1},{3,2},{4,3},{5,4},{6,5},{7,6},{0,7},{9,8},{10,9},{11,1... | collective-permute-start | bytes 245768 | tf_op jit(solution)/shard_map/ppermute | solution.py:511
  66.5 4.6 %inner_block.1 = (bf16[16,32,256]{2,1,0:T(8,128)(2,1)S(1)}, bf16[256,128]{1,0:T(8,128)(2,1)S(1)}, f32[24,40,256]{2,1,0:T(8,128)S(1)}) custom-call(bf16[32,48,256]{2,1,0:T(8,128)(2,1)S(1)} %start_tile.1.start_ref, f32[1,256]{1,0:T(1,128)S(1)} %bitcast.26, bf16[256,768]{1,0:T(8,128)(2,1)S(1)} %copy-done.9, bf16[256,256]{1,0:T(8,128)(2,1)S(1)} %copy-done.11, ...), custom_call_target="tpu_custom_call" | custom-call | flops 6000000000 | bytes 10000000 | tf_op jit(solution)/shard_map/inner_block/pallas_call | solution.py:665
  72.1 7.8 %outer_block.1 = (bf16[32,48,256]{2,1,0:T(8,128)(2,1)}, bf16[768,128]{1,0:T(8,128)(2,1)S(1)}) custom-call(s32[3]{0:T(128)S(1)} %pad_add_fusion.refs_0_, f32[40,56,256]{2,1,0:T(8,128)S(1)} %maximum_convert_fusion.refs_1_, bf16[16,32,256]{2,1,0:T(8,128)(2,1)S(1)} %get-tuple-element.30.refs_2_, bf16[256,128]{1,0:T(8,128)(2,1)S(1)} %get-tuple-element.31.refs_3_, ...), custom_call_target="tpu_custom_call" | custom-call | flops 8000000000 | bytes 10000000 | tf_op jit(solution)/shard_map/outer_block/pallas_call | solution.py:681
  79.9 2.2 %collective-permute-start.7 = (bf16[768,128]{1,0:T(8,128)(2,1)S(1)}, bf16[768,128]{1,0:T(8,128)(2,1)S(1)}, u32[]{:S(2)}, u32[]{:S(2)}) collective-permute-start(bf16[768,128]{1,0:T(8,128)(2,1)S(1)} %get-tuple-element.35.refs_1_), channel_id=1, source_target_pairs={{0,6},{2,0},{4,2},{6,4},{1,7},{3,1},{5,3},{7,5},{8,14},{10,8},{12,... | collective-permute-start | bytes 589832 | tf_op jit(solution)/shard_map/ppermute | solution.py:541
  83.4 10.4 %conditional.3 = (bf16[1536,128]{1,0:T(8,128)(2,1)S(1)}) conditional(s32[]{:T(128)} %bitcast.11, bf16[1536,128]{1,0:T(8,128)(2,1)S(1)} %reply_near.1, bf16[1536,128]{1,0:T(8,128)(2,1)S(1)} %reply_near.1), branch_computations={%region_2.3_spmd, %region_3.4_spmd} | conditional | bytes 3145736 | solution.py:536
  83.5 10.4 %all_to_all.39 = bf16[8,192,128]{2,1,0:T(8,128)(2,1)S(1)} all-to-all(bf16[8,192,128]{2,1,0:T(8,128)(2,1)S(1)} %bitcast.33), channel_id=1, replica_groups=mesh['lat'=4,'z'=4,'x'=2] {'lat','x'}, dimensions={0} | all-to-all | bytes 786432 | tf_op jit(solution)/shard_map/cond/branch_1_fun/all_to_all | solution.py:524
  93.8 6.9 %collective-permute-done.8.refs_2_ = bf16[768,128]{1,0:T(8,128)(2,1)S(1)} collective-permute-done((bf16[768,128]{1,0:T(8,128)(2,1)S(1)}, bf16[768,128]{1,0:T(8,128)(2,1)S(1)}, u32[]{:S(2)}, u32[]{:S(2)}) %collective-permute-start.8) | collective-permute-done | bytes 196640 | tf_op jit(solution)/shard_map/ppermute | solution.py:541
  100.7 1.0 reply_far.1
  101.7 18.8 %all_to_all.40 = bf16[8,576,128]{2,1,0:T(8,128)(2,1)S(1)} all-to-all(bf16[8,576,128]{2,1,0:T(8,128)(2,1)S(1)} %bitcast.24), channel_id=1, replica_groups=mesh['lat'=4,'z'=4,'x'=2] {'lat','x'}, dimensions={0} | all-to-all | bytes 2359296 | tf_op jit(solution)/shard_map/all_to_all | solution.py:524
  120.6 3.8 %decode_blocks.1 = bf16[64,12288]{1,0:T(8,128)(2,1)} custom-call(s32[96]{0:T(128)S(1)} %get-tuple-element.34.slot_ref, bf16[2,12288]{1,0:T(2,128)(2,1)S(1)} %copy-done.3, bf16[1536,128]{1,0:T(8,128)(2,1)S(1)} %get-tuple-element.41.near_ref, bf16[4608,128]{1,0:T(8,128)(2,1)S(1)} %bitcast.23), custom_call_target="tpu_custom_call" | custom-call | tf_op jit(solution)/shard_map/decode_blocks/pallas_call | solution.py:716
  (56 shorter events, 8.5 us)
Async XLA Ops:
  0.6 14.5 %copy-start.13 = (f32[256]{0:T(256)S(1)}, f32[256]{0:T(256)}, u32[]{:S(2)}) copy-start(f32[256]{0:T(256)} %param.23) | copy-start | bytes 3076
  0.7 1.4 %copy-start = (bf16[64,12288]{1,0:T(8,128)(2,1)S(1)}, bf16[64,12288]{1,0:T(8,128)(2,1)}, u32[]{:S(2)}) copy-start(bf16[64,12288]{1,0:T(8,128)(2,1)} %refs_3_.1) | copy-start | bytes 4718596
  10.0 22.6 %all-to-all-start.6 = ((bf16[8,624,128]{2,1,0:T(8,128)(2,1)}), bf16[8,624,128]{2,1,0:T(8,128)(2,1)S(1)}, u32[]{:S(2)}, u32[]{:S(2)}) async-start(bf16[8,624,128]{2,1,0:T(8,128)(2,1)} %bitcast.13), calls=%async_computation.6 | async-start | bytes 2555904 | tf_op jit(solution)/shard_map/all_to_all | solution.py:524
  35.7 17.6 %collective-permute-start = (bf16[800,128]{1,0:T(8,128)(2,1)}, bf16[800,128]{1,0:T(8,128)(2,1)S(1)}, u32[]{:S(2)}, u32[]{:S(2)}) collective-permute-start(bf16[800,128]{1,0:T(8,128)(2,1)} %get-tuple-element.26), channel_id=1, source_target_pairs={{0,2},{2,4},{4,6},{6,0},{1,3},{3,5},{5,7},{7,1},{8,10},{10,12},{12... | collective-permute-start | bytes 614408 | tf_op jit(solution)/shard_map/ppermute | solution.py:541
  37.3 16.1 %collective-permute-start.1 = (bf16[800,128]{1,0:T(8,128)(2,1)}, bf16[800,128]{1,0:T(8,128)(2,1)S(1)}, u32[]{:S(2)}, u32[]{:S(2)}) collective-permute-start(bf16[800,128]{1,0:T(8,128)(2,1)} %get-tuple-element.27), channel_id=1, source_target_pairs={{0,4},{2,6},{4,0},{6,2},{1,5},{3,7},{5,1},{7,3},{8,12},{10,14},{12... | collective-permute-start | bytes 614408 | tf_op jit(solution)/shard_map/ppermute | solution.py:541
  39.9 13.4 %collective-permute-start.2 = (bf16[800,128]{1,0:T(8,128)(2,1)S(1)}, bf16[800,128]{1,0:T(8,128)(2,1)S(1)}, u32[]{:S(2)}, u32[]{:S(2)}) collective-permute-start(bf16[800,128]{1,0:T(8,128)(2,1)S(1)} %get-tuple-element.28), channel_id=1, source_target_pairs={{0,6},{2,0},{4,2},{6,4},{1,7},{3,1},{5,3},{7,5},{8,14},{10,8},{12,... | collective-permute-start | bytes 614408 | tf_op jit(solution)/shard_map/ppermute | solution.py:541
  51.8 1.5 %copy-start.1 = (bf16[32,48,256]{2,1,0:T(8,128)(2,1)S(1)}, bf16[32,48,256]{2,1,0:T(8,128)(2,1)}, u32[]{:S(2)}) copy-start(bf16[32,48,256]{2,1,0:T(8,128)(2,1)} %refs_5_.1) | copy-start | bytes 2359300
  51.8 1.5 %copy-start.4 = (bf16[64,256]{1,0:T(8,128)(2,1)S(1)}, bf16[64,256]{1,0:T(8,128)(2,1)}, u32[]{:S(2)}) copy-start(bf16[64,256]{1,0:T(8,128)(2,1)} %refs_4_.3) | copy-start | bytes 98308
  53.3 2.3 %copy-start.15 = (bf16[256,64]{0,1:T(8,128)(2,1)S(1)}, bf16[256,64]{0,1:T(8,128)(2,1)}, u32[]{:S(2)}) copy-start(bf16[256,64]{0,1:T(8,128)(2,1)} %param.29) | copy-start | bytes 98308
  53.3 11.3 %copy-start.7 = (bf16[256,1024]{1,0:T(8,128)(2,1)S(1)}, bf16[256,1024]{1,0:T(8,128)(2,1)}, u32[]{:S(2)}) copy-start(bf16[256,1024]{1,0:T(8,128)(2,1)} %refs_9_.1) | copy-start | bytes 1572868
  53.3 11.3 %copy-start.8 = (bf16[1024,256]{1,0:T(8,128)(2,1)S(1)}, bf16[1024,256]{1,0:T(8,128)(2,1)}, u32[]{:S(2)}) copy-start(bf16[1024,256]{1,0:T(8,128)(2,1)} %refs_10_.1) | copy-start | bytes 1572868
  53.3 11.3 %copy-start.14 = (f32[256]{0:T(256)S(1)}, f32[256]{0:T(256)}, u32[]{:S(2)}) copy-start(f32[256]{0:T(256)} %param.26) | copy-start | bytes 3076
  53.8 4.1 %collective-permute-start.3 = (bf16[4,48,256]{2,1,0:T(8,128)(2,1)S(1)}, bf16[4,48,256]{2,1,0:T(8,128)(2,1)S(1)}, u32[]{:S(2)}, u32[]{:S(2)}) collective-permute-start(bf16[4,48,256]{2,1,0:T(8,128)(2,1)S(1)} %get-tuple-element.38), channel_id=1, source_target_pairs={{0,8},{8,16},{16,24},{24,0},{1,9},{9,17},{17,25},{25,1},{2,10},{10... | collective-permute-start | bytes 294920 | tf_op jit(solution)/shard_map/ppermute | solution.py:510
  54.2 3.7 %collective-permute-start.4 = (bf16[4,48,256]{2,1,0:T(8,128)(2,1)S(1)}, bf16[4,48,256]{2,1,0:T(8,128)(2,1)S(1)}, u32[]{:S(2)}, u32[]{:S(2)}) collective-permute-start(bf16[4,48,256]{2,1,0:T(8,128)(2,1)S(1)} %get-tuple-element.39), channel_id=1, source_target_pairs={{8,0},{16,8},{24,16},{0,24},{9,1},{17,9},{25,17},{1,25},{10,2},{18... | collective-permute-start | bytes 294920 | tf_op jit(solution)/shard_map/ppermute | solution.py:511
  58.0 13.1 %collective-permute-start.5 = (bf16[40,4,256]{2,1,0:T(4,128)(2,1)S(1)}, bf16[40,4,256]{2,1,0:T(4,128)(2,1)S(1)}, u32[]{:S(2)}, u32[]{:S(2)}) collective-permute-start(bf16[40,4,256]{2,1,0:T(4,128)(2,1)S(1)} %get-tuple-element.36), channel_id=1, source_target_pairs={{0,1},{1,2},{2,3},{3,4},{4,5},{5,6},{6,7},{7,0},{8,9},{9,10},{10,1... | collective-permute-start | bytes 245768 | tf_op jit(solution)/shard_map/ppermute | solution.py:510
  59.1 12.0 %collective-permute-start.6 = (bf16[40,4,256]{2,1,0:T(4,128)(2,1)S(1)}, bf16[40,4,256]{2,1,0:T(4,128)(2,1)S(1)}, u32[]{:S(2)}, u32[]{:S(2)}) collective-permute-start(bf16[40,4,256]{2,1,0:T(4,128)(2,1)S(1)} %get-tuple-element.37), channel_id=1, source_target_pairs={{1,0},{2,1},{3,2},{4,3},{5,4},{6,5},{7,6},{0,7},{9,8},{10,9},{11,1... | collective-permute-start | bytes 245768 | tf_op jit(solution)/shard_map/ppermute | solution.py:511
  64.6 1.0 copy-start.9
  65.6 0.9 copy-start.11
  71.1 1.0 copy-start.10
  71.1 1.0 copy-start.12
  79.9 13.9 %collective-permute-start.7 = (bf16[768,128]{1,0:T(8,128)(2,1)S(1)}, bf16[768,128]{1,0:T(8,128)(2,1)S(1)}, u32[]{:S(2)}, u32[]{:S(2)}) collective-permute-start(bf16[768,128]{1,0:T(8,128)(2,1)S(1)} %get-tuple-element.35.refs_1_), channel_id=1, source_target_pairs={{0,6},{2,0},{4,2},{6,4},{1,7},{3,1},{5,3},{7,5},{8,14},{10,8},{12,... | collective-permute-start | bytes 589832 | tf_op jit(solution)/shard_map/ppermute | solution.py:541
  82.1 18.6 %collective-permute-start.8 = (bf16[768,128]{1,0:T(8,128)(2,1)S(1)}, bf16[768,128]{1,0:T(8,128)(2,1)S(1)}, u32[]{:S(2)}, u32[]{:S(2)}) collective-permute-start(bf16[768,128]{1,0:T(8,128)(2,1)S(1)} %get-tuple-element.35.refs_1_), channel_id=1, source_target_pairs={{0,4},{2,6},{4,0},{6,2},{1,5},{3,7},{5,1},{7,3},{8,12},{10,14},{12... | collective-permute-start | bytes 589832 | tf_op jit(solution)/shard_map/ppermute | solution.py:541
  82.6 18.1 %collective-permute-start.9 = (bf16[768,128]{1,0:T(8,128)(2,1)S(1)}, bf16[768,128]{1,0:T(8,128)(2,1)S(1)}, u32[]{:S(2)}, u32[]{:S(2)}) collective-permute-start(bf16[768,128]{1,0:T(8,128)(2,1)S(1)} %get-tuple-element.35.refs_1_), channel_id=1, source_target_pairs={{0,2},{2,4},{4,6},{6,0},{1,3},{3,5},{5,7},{7,1},{8,10},{10,12},{12... | collective-permute-start | bytes 589832 | tf_op jit(solution)/shard_map/ppermute | solution.py:541
  93.8 26.7 %copy-start.3 = (bf16[2,12288]{1,0:T(2,128)(2,1)S(1)}, bf16[2,12288]{1,0:T(2,128)(2,1)}, u32[]{:S(2)}) copy-start(bf16[2,12288]{1,0:T(2,128)(2,1)} %offset_ref.1) | copy-start | bytes 147460
  (3 other events, 2.1 us)

commit v6 on v5

--- a/solution.py
+++ b/solution.py
@@ -97,7 +97,7 @@
         count_ref[tile] = rank + 1
         lon = tile % (depth * width)
         partner = tile // (depth * width) * width + lon % width
-        hop = (lon // width + depth - place_ref[1]) % depth
+        hop = lon // width ^ place_ref[1]
         piece = jnp.where(hop == 0, partner, lat * width + partner * (depth - 1) + hop - 1)
         slot_ref[b] = piece * capacity + rank
         pair = rank // 2
@@ -141,9 +141,8 @@
     return pairs * feat_width + -(-2 * pairs // 16) * 16
 
 
-def add_chunk(capacity, feat_width, id_ref, slot, recv_ref, base, acc_ref):
+def add_chunk(capacity, feat_width, id_ref, slot, recv_ref, base, low_ref, high_ref):
     pairs = capacity // 2
-    first = lax.broadcasted_iota(jnp.int32, (feat_width + 8, LANES), 1) < CELLS
     tags = recv_ref[base + pairs * feat_width : base + pairs * feat_width + meta_rows(pairs), :]
     tags = tags.astype(jnp.float32)
     for k in range(pairs):
@@ -151,33 +150,34 @@
         sums = recv_ref[at : at + feat_width, :].astype(jnp.float32)
         mass = tags[k : k + 1] + tags[pairs + k : pairs + k + 1]
         both = jnp.concatenate([sums, jnp.broadcast_to(mass, (8, LANES))], axis=0)
-        acc_ref[id_ref[slot + 2 * k]] += jnp.where(first, both, 0.0)
-        acc_ref[id_ref[slot + 2 * k + 1]] += jnp.where(first, 0.0, both)
-
-
-def paired(acc_ref, j):
-    first = lax.broadcasted_iota(jnp.int32, acc_ref.shape[1:], 1) < CELLS
-    even, odd = acc_ref[2 * j], acc_ref[2 * j + 1]
-    even, odd = even + pltpu.roll(even, CELLS, 1), odd + pltpu.roll(odd, CELLS, 1)
+        low_ref[id_ref[slot + 2 * k]] += both
+        high_ref[id_ref[slot + 2 * k + 1]] += both
+
+
+def paired(low_ref, high_ref, j):
+    first = lax.broadcasted_iota(jnp.int32, low_ref.shape[1:], 1) < CELLS
+    even = low_ref[2 * j] + pltpu.roll(high_ref[2 * j], CELLS, 1)
+    odd = high_ref[2 * j + 1] + pltpu.roll(low_ref[2 * j + 1], CELLS, 1)
     return jnp.where(first, even, odd)
 
 
 def gather_planes(capacity, plane, hops, feat_width, id_ref, recv_ref, *refs):
-    outs, acc_ref = refs[:hops], refs[hops]
+    outs, lows, highs = refs[:hops], refs[hops : 2 * hops], refs[2 * hops :]
     pairs = capacity // 2
     chunk = pairs * feat_width + meta_rows(pairs)
-    patch_pairs = acc_ref.shape[1] // 2
-    acc_ref[...] = jnp.zeros_like(acc_ref)
+    patch_pairs = lows[0].shape[0] // 2
+    for ref in lows + highs:
+        ref[...] = jnp.zeros_like(ref)
     for r in range(plane):
         for hop in range(hops):
             n = r * hops + hop
             add_chunk(
-                capacity, feat_width, id_ref, n * capacity, recv_ref, n * chunk, acc_ref.at[hop]
+                capacity, feat_width, id_ref, n * capacity, recv_ref, n * chunk, lows[hop], highs[hop]
             )
     for hop in range(hops):
         masses = []
         for j in range(patch_pairs):
-            pair = paired(acc_ref.at[hop], j)
+            pair = paired(lows[hop], highs[hop], j)
             outs[hop][j * feat_width : (j + 1) * feat_width, :] = pair[:feat_width].astype(
                 jnp.bfloat16
             )
@@ -189,13 +189,17 @@
         outs[hop][patch_pairs * feat_width :, :] = jnp.concatenate(rows, axis=0).astype(jnp.bfloat16)
 
 
-def gather_own(capacity, plane, feat_width, id_ref, recv_ref, own_ref, acc_ref):
+def gather_own(capacity, plane, feat_width, id_ref, recv_ref, *refs):
+    own_ref, low_ref, high_ref = refs[-3:]
     chunk = recv_ref.shape[0] // plane
-    acc_ref[...] = jnp.zeros_like(acc_ref)
+    low_ref[...] = jnp.zeros_like(low_ref)
+    high_ref[...] = jnp.zeros_like(high_ref)
     for r in range(plane):
-        add_chunk(capacity, feat_width, id_ref, r * capacity, recv_ref, r * chunk, acc_ref)
+        add_chunk(
+            capacity, feat_width, id_ref, r * capacity, recv_ref, r * chunk, low_ref, high_ref
+        )
     for j in range(own_ref.shape[0]):
-        own_ref[j] = paired(acc_ref, j)
+        own_ref[j] = paired(low_ref, high_ref, j)
 
 
 def start_tile(hops, own_ref, *refs):
@@ -322,11 +326,14 @@
     latent = residual + jnp.dot(
         hidden.astype(jnp.bfloat16), down_ref[...], preferred_element_type=jnp.float32
     )
-    projected = jnp.dot(
-        latent.astype(jnp.bfloat16), decode_ref[...], preferred_element_type=jnp.float32
-    )
+    rounded = latent.astype(jnp.bfloat16)
     turned = [
-        projected[i * CELLS : i * CELLS + LANES].T.astype(jnp.bfloat16)
+        lax.dot_general(
+            decode_ref[...],
+            rounded[i * CELLS : i * CELLS + LANES],
+            NT,
+            preferred_element_type=jnp.float32,
+        ).astype(jnp.bfloat16)
         for i in range(0, len(begun), 2)
     ]
     return latent, turned
@@ -347,7 +354,7 @@
 ):
     tile_rows, tile_cols, channels = cells_ref.shape
     margin = WIN // 2
-    feat_width = decode_ref.shape[1]
+    feat_width = decode_ref.shape[0]
     cells_ref[...] = start_ref[...].astype(jnp.float32)
     turn_weights(qkv_ref, turned_ref)
     for row in range(0, tile_rows - WIN, WIN):
@@ -392,7 +399,7 @@
     ext_rows, ext_cols, channels = ext_ref.shape
     tile_rows, tile_cols, _ = latent_ref.shape
     margin = WIN // 2
-    feat_width = decode_ref.shape[1]
+    feat_width = decode_ref.shape[0]
     last_row, last_col = ext_rows - WIN, ext_cols - WIN
     top = place_ref[2] * tile_rows - margin
     turn_weights(qkv_ref, turned_ref)
@@ -536,9 +543,9 @@
     return lax.cond(gains[0] > 0.0, swap_in_plane, apart, array)
 
 
-def shift_planes(array, hop):
+def swap_planes(array, hop):
     depth = lax.axis_size("z")
-    return lax.ppermute(array, "z", [(i, (i + hop) % depth) for i in range(depth)])
+    return lax.ppermute(array, "z", [(i, i ^ hop) for i in range(depth)])
 
 
 def local(
@@ -592,7 +599,7 @@
             pltpu.SMEM((devices,), jnp.int32),
             pltpu.SemaphoreType.DMA((steps + 3,)),
         ],
-        compiler_params=params(10),
+        compiler_params=params(61),
         name="encode_blocks",
     )(place, block_tile.reshape(blocks), block_patch, obs_feat, obs_offset)
 
@@ -609,24 +616,24 @@
         out_shape=[jax.ShapeDtypeStruct((dense, LANES), jnp.bfloat16)] * hops,
         in_specs=[smem(), vmem()],
         out_specs=[vmem()] * hops,
-        scratch_shapes=[pltpu.VMEM((hops, patch_total, feat_width + 8, LANES), jnp.float32)],
-        compiler_params=params(10),
+        scratch_shapes=[pltpu.VMEM((patch_total, feat_width + 8, LANES), jnp.float32)] * (2 * hops),
+        compiler_params=params(14),
         name="gather_planes",
     )(far_ids, far)
-    parts = [shift_planes(sums[hop], hop + 1) for hop in range(hops)]
+    parts = [swap_planes(sums[hop - 1], hop) for hop in range(hops, 0, -1)]
     send_near, _ = lax.optimization_barrier((send_near, sums))
     near = swap_at_once(norm_gain, send_near)
     near_ids = ids_of(near, 1)
     own = pl.pallas_call(
         lambda *refs: gather_own(capacity, plane, feat_width, *refs),
         out_shape=jax.ShapeDtypeStruct((patch_total // 2, feat_width + 8, LANES), jnp.float32),
-        in_specs=[smem(), vmem()],
+        in_specs=[smem()] + [vmem()] * 3,
         out_specs=vmem(),
-        scratch_shapes=[pltpu.VMEM((patch_total, feat_width + 8, LANES), jnp.float32)],
+        scratch_shapes=[pltpu.VMEM((patch_total, feat_width + 8, LANES), jnp.float32)] * 2,
         compiler_params=params(10),
         cost_estimate=pl.CostEstimate(flops=10**9, bytes_accessed=10**7, transcendentals=0),
         name="gather_own",
-    )(near_ids, near)
+    )(near_ids, near, qkv_weight, out_weight)
 
     start = pl.pallas_call(
         lambda *refs: start_tile(hops, *refs),
@@ -642,7 +649,7 @@
     ext_rows, ext_cols, _ = ext.shape
     group = 128
     gains = (norm_gain.reshape(1, channels), mlp_gain.reshape(1, channels))
-    weights = (gains[0], qkv_weight, out_weight, gains[1], up_weight, down_weight, decode_weight)
+    weights = (gains[0], qkv_weight, out_weight, gains[1], up_weight, down_weight, decode_weight.T)
     patch_rows, patch_cols = tile_rows // PATCH, tile_cols // PATCH
     inner, sides, ends = patch_order(patch_rows, patch_cols)
     order = [r * patch_cols + c for r, c in inner + sides + ends]
@@ -708,7 +715,7 @@
             name=name,
         )(ids, *tiles)
 
-    others = [shift_planes(projected, -hop) for hop in range(1, depth)]
+    others = [swap_planes(projected, hop) for hop in range(hops, 0, -1)][::-1]
     near_reply = reply(near_ids, [projected], "reply_near")
     near_back = swap_at_once(norm_gain, near_reply)
     far_back = swap_in_plane(reply(far_ids, others, "reply_far"))

time: 125 us -> 119 us (0.952); the launches traced: 124 us -> 117 us
  local copies, waits for them, and re-layouts: 7.11 us -> 1.27 us
  starting transfers between devices: 21.9 us -> 20.6 us
    unnamed x33 -> x24, local copies, waits for them, and re-layouts: 6.09 us -> 0.26 us
    ppermute x2, starting transfers between devices: 6.92 us -> 5.51 us  [with_halo(): after = lax.ppermute(initial, axis, down)]
  transfers between devices with their start and end apart: 11 -> 11, of which waited for: 3 -> 4; matrix products, arithmetic and copies ran while one was open for 1% -> 1% of each run, Pallas kernels for 5% -> 6%
where the time goes in v6:
time: 119 us; the launch traced here: 117 us
  blocking collectives  40.2 us (34%)
  Pallas kernels  27.5 us (23%)
  waiting for transfers between devices  24.5 us (21%)
  starting transfers between devices  20.6 us (17%)
  between operations  1.52 us (1%)
  local copies, waits for them, and re-layouts  1.27 us (1%)
  other arithmetic  1.24 us (1%)
    all_to_all x3, blocking collectives, swap_in_plane(): lax.all_to_all(parts, ('lat', 'x'), split_axis=0, concat_axis=0, tiled=True)  40.2 us
    all_to_all x1, waiting for transfers between devices, swap_in_plane(): lax.all_to_all(parts, ('lat', 'x'), split_axis=0, concat_axis=0, tiled=True)  16.2 us
    ppermute x6, starting transfers between devices, swap_planes(): return lax.ppermute(array, 'z', [(i, i ^ hop) for i in range(depth)])  8.84 us
    pallas_call x1, Pallas kernels, local(): pl.pallas_call(lambda *refs: outer_block(tile_rows * lat, *refs), out_sha...  7.81 us
    pallas_call x1, Pallas kernels, local(): pl.pallas_call(lambda *refs: encode_blocks(capacity, (lat, depth, width),...  6.05 us
    ppermute x6, waiting for transfers between devices, swap_planes(): return lax.ppermute(array, 'z', [(i, i ^ hop) for i in range(depth)])  5.99 us
    ppermute x2, starting transfers between devices, with_halo(): after = lax.ppermute(initial, axis, down)  5.51 us
    all_to_all x1, starting transfers between devices, swap_in_plane(): lax.all_to_all(parts, ('lat', 'x'), split_axis=0, concat_axis=0, tiled=True)  5.19 us
  transfers between devices with their start and end apart: 11, of which 4 were waited for; matrix products, arithmetic and copies ran while one was open for 1% of the time, Pallas kernels for 6%

profile of v6, /device:TPU:0, one launch (start us, length us, event | category | flops | bytes accessed | tf_op | source)
XLA Modules:
  0.0 116.8 jit_solution(9149550859756561762)
XLA Ops:
  1.3 6.0 %encode_blocks.1 = (bf16[1664,128]{1,0:T(8,128)(2,1)S(1)}, bf16[4992,128]{1,0:T(8,128)(2,1)}, s32[96]{0:T(128)}) custom-call(s32[3]{0:T(128)} %pad_add_fusion.refs_0_, s32[96]{0:T(128)} %bitcast.42, s32[96]{0:T(128)} %refs_2_.2, bf16[64,12288]{1,0:T(8,128)(2,1)} %refs_3_.2, bf16[2,12288]{1,0:T(2,128)(2,1)} %offset_ref.1), custom_call_target="tpu_custom_call" | custom-call | tf_op jit(solution)/shard_map/encode_blocks/pallas_call | solution.py:584
  7.4 5.2 %all-to-all-start.6 = ((bf16[8,624,128]{2,1,0:T(8,128)(2,1)}), bf16[8,624,128]{2,1,0:T(8,128)(2,1)S(1)}, u32[]{:S(2)}, u32[]{:S(2)}) async-start(bf16[8,624,128]{2,1,0:T(8,128)(2,1)} %bitcast.38), calls=%async_computation.6 | async-start | bytes 2555904 | tf_op jit(solution)/shard_map/all_to_all | solution.py:531
  13.7 16.2 %all-to-all-done.6 = bf16[8,624,128]{2,1,0:T(8,128)(2,1)S(1)} async-done(((bf16[8,624,128]{2,1,0:T(8,128)(2,1)}), bf16[8,624,128]{2,1,0:T(8,128)(2,1)S(1)}, u32[]{:S(2)}, u32[]{:S(2)}) %all-to-all-start.6) | async-done | bytes 1277984 | tf_op jit(solution)/shard_map/all_to_all | solution.py:531
  30.3 1.9 %gather_planes.1 = (bf16[800,128]{1,0:T(8,128)(2,1)S(1)}, bf16[800,128]{1,0:T(8,128)(2,1)S(1)}, bf16[800,128]{1,0:T(8,128)(2,1)S(1)}) custom-call(s32[144]{0:T(256)S(1)} %reshape.64.refs_0_, bf16[4992,128]{1,0:T(8,128)(2,1)S(1)} %bitcast.23), custom_call_target="tpu_custom_call" | custom-call | tf_op jit(solution)/shard_map/gather_planes/pallas_call | solution.py:614
  32.2 3.7 %collective-permute-start = (bf16[800,128]{1,0:T(8,128)(2,1)S(1)}, bf16[800,128]{1,0:T(8,128)(2,1)S(1)}, u32[]{:S(2)}, u32[]{:S(2)}) collective-permute-start(bf16[800,128]{1,0:T(8,128)(2,1)S(1)} %get-tuple-element.28), channel_id=1, source_target_pairs={{0,6},{2,4},{4,2},{6,0},{1,7},{3,5},{5,3},{7,1},{8,14},{10,12},{12... | collective-permute-start | bytes 614408 | tf_op jit(solution)/shard_map/ppermute | solution.py:548
  35.9 0.8 collective-permute-start.2
  36.7 10.6 %conditional.2 = (bf16[1664,128]{1,0:T(8,128)(2,1)S(1)}) conditional(s32[]{:T(128)} %bitcast.11, bf16[1664,128]{1,0:T(8,128)(2,1)S(1)} %get-tuple-element.29, bf16[1664,128]{1,0:T(8,128)(2,1)S(1)} %get-tuple-element.29), branch_computations={%region_0.1_spmd, %region_1.2_spmd} | conditional | bytes 3407880 | solution.py:543
  36.7 10.6 %all_to_all.36 = bf16[8,208,128]{2,1,0:T(8,128)(2,1)S(1)} all-to-all(bf16[8,208,128]{2,1,0:T(8,128)(2,1)S(1)} %bitcast.33), channel_id=1, replica_groups=mesh['lat'=4,'z'=4,'x'=2] {'lat','x'}, dimensions={0} | all-to-all | bytes 851968 | tf_op jit(solution)/shard_map/cond/branch_1_fun/all_to_all | solution.py:531
  47.6 1.1 gather_own.1.refs_0_
  48.8 4.4 %collective-permute-done.1.refs_2_ = bf16[800,128]{1,0:T(8,128)(2,1)S(1)} collective-permute-done((bf16[800,128]{1,0:T(8,128)(2,1)S(1)}, bf16[800,128]{1,0:T(8,128)(2,1)S(1)}, u32[]{:S(2)}, u32[]{:S(2)}) %collective-permute-start.1) | collective-permute-done | bytes 204832 | tf_op jit(solution)/shard_map/ppermute | solution.py:548
  53.7 1.7 %collective-permute-start.4 = (bf16[4,48,256]{2,1,0:T(8,128)(2,1)S(1)}, bf16[4,48,256]{2,1,0:T(8,128)(2,1)S(1)}, u32[]{:S(2)}, u32[]{:S(2)}) collective-permute-start(bf16[4,48,256]{2,1,0:T(8,128)(2,1)S(1)} %get-tuple-element.39), channel_id=1, source_target_pairs={{8,0},{16,8},{24,16},{0,24},{9,1},{17,9},{25,17},{1,25},{10,2},{18... | collective-permute-start | bytes 294920 | tf_op jit(solution)/shard_map/ppermute | solution.py:518
  55.4 2.3 %collective-permute-done.3 = bf16[4,48,256]{2,1,0:T(8,128)(2,1)S(1)} collective-permute-done((bf16[4,48,256]{2,1,0:T(8,128)(2,1)S(1)}, bf16[4,48,256]{2,1,0:T(8,128)(2,1)S(1)}, u32[]{:S(2)}, u32[]{:S(2)}) %collective-permute-start.3) | collective-permute-done | bytes 98336 | tf_op jit(solution)/shard_map/ppermute | solution.py:517
  57.8 1.0 collective-permute-start.5
  58.8 3.8 %collective-permute-start.6 = (bf16[40,4,256]{2,1,0:T(4,128)(2,1)S(1)}, bf16[40,4,256]{2,1,0:T(4,128)(2,1)S(1)}, u32[]{:S(2)}, u32[]{:S(2)}) collective-permute-start(bf16[40,4,256]{2,1,0:T(4,128)(2,1)S(1)} %get-tuple-element.37), channel_id=1, source_target_pairs={{1,0},{2,1},{3,2},{4,3},{5,4},{6,5},{7,6},{0,7},{9,8},{10,9},{11,1... | collective-permute-start | bytes 245768 | tf_op jit(solution)/shard_map/ppermute | solution.py:518
  62.6 4.6 %inner_block.1 = (bf16[16,32,256]{2,1,0:T(8,128)(2,1)S(1)}, bf16[256,128]{1,0:T(8,128)(2,1)S(1)}, f32[24,40,256]{2,1,0:T(8,128)S(1)}) custom-call(bf16[32,48,256]{2,1,0:T(8,128)(2,1)S(1)} %start_tile.1.start_ref, f32[1,256]{1,0:T(1,128)S(1)} %bitcast.28, bf16[256,768]{1,0:T(8,128)(2,1)S(1)} %copy-done.7, bf16[256,256]{1,0:T(8,128)(2,1)S(1)} %copy-done.8, ...), custom_call_target="tpu_custom_call" | custom-call | flops 6000000000 | bytes 10000000 | tf_op jit(solution)/shard_map/inner_block/pallas_call | solution.py:672
  67.9 7.8 %outer_block.1 = (bf16[32,48,256]{2,1,0:T(8,128)(2,1)}, bf16[768,128]{1,0:T(8,128)(2,1)S(1)}) custom-call(s32[3]{0:T(128)S(1)} %copy-done.3, f32[40,56,256]{2,1,0:T(8,128)S(1)} %maximum_convert_fusion.refs_1_, bf16[16,32,256]{2,1,0:T(8,128)(2,1)S(1)} %get-tuple-element.30.refs_2_, bf16[256,128]{1,0:T(8,128)(2,1)S(1)} %get-tuple-element.31.refs_3_, ...), custom_call_target="tpu_custom_call" | custom-call | flops 8000000000 | bytes 10000000 | tf_op jit(solution)/shard_map/outer_block/pallas_call | solution.py:688
  75.7 1.4 %collective-permute-start.8 = (bf16[768,128]{1,0:T(8,128)(2,1)S(1)}, bf16[768,128]{1,0:T(8,128)(2,1)S(1)}, u32[]{:S(2)}, u32[]{:S(2)}) collective-permute-start(bf16[768,128]{1,0:T(8,128)(2,1)S(1)} %get-tuple-element.35.refs_1_), channel_id=1, source_target_pairs={{0,4},{2,6},{4,0},{6,2},{1,5},{3,7},{5,1},{7,3},{8,12},{10,14},{12... | collective-permute-start | bytes 589832 | tf_op jit(solution)/shard_map/ppermute | solution.py:548
  77.1 2.9 %collective-permute-start.9 = (bf16[768,128]{1,0:T(8,128)(2,1)S(1)}, bf16[768,128]{1,0:T(8,128)(2,1)S(1)}, u32[]{:S(2)}, u32[]{:S(2)}) collective-permute-start(bf16[768,128]{1,0:T(8,128)(2,1)S(1)} %get-tuple-element.35.refs_1_), channel_id=1, source_target_pairs={{0,6},{2,4},{4,2},{6,0},{1,7},{3,5},{5,3},{7,1},{8,14},{10,12},{12... | collective-permute-start | bytes 589832 | tf_op jit(solution)/shard_map/ppermute | solution.py:548
  80.8 10.4 %conditional.3 = (bf16[1536,128]{1,0:T(8,128)(2,1)S(1)}) conditional(s32[]{:T(128)} %bitcast.11, bf16[1536,128]{1,0:T(8,128)(2,1)S(1)} %reply_near.1, bf16[1536,128]{1,0:T(8,128)(2,1)S(1)} %reply_near.1), branch_computations={%region_2.3_spmd, %region_3.4_spmd} | conditional | bytes 3145736 | solution.py:543
  80.8 10.4 %all_to_all.39 = bf16[8,192,128]{2,1,0:T(8,128)(2,1)S(1)} all-to-all(bf16[8,192,128]{2,1,0:T(8,128)(2,1)S(1)} %bitcast.35), channel_id=1, replica_groups=mesh['lat'=4,'z'=4,'x'=2] {'lat','x'}, dimensions={0} | all-to-all | bytes 786432 | tf_op jit(solution)/shard_map/cond/branch_1_fun/all_to_all | solution.py:531
  91.2 1.6 %collective-permute-done.8.refs_2_ = bf16[768,128]{1,0:T(8,128)(2,1)S(1)} collective-permute-done((bf16[768,128]{1,0:T(8,128)(2,1)S(1)}, bf16[768,128]{1,0:T(8,128)(2,1)S(1)}, u32[]{:S(2)}, u32[]{:S(2)}) %collective-permute-start.8) | collective-permute-done | bytes 196640 | tf_op jit(solution)/shard_map/ppermute | solution.py:548
  92.8 1.0 reply_far.1
  93.8 19.2 %all_to_all.40 = bf16[8,576,128]{2,1,0:T(8,128)(2,1)S(1)} all-to-all(bf16[8,576,128]{2,1,0:T(8,128)(2,1)S(1)} %bitcast.25), channel_id=1, replica_groups=mesh['lat'=4,'z'=4,'x'=2] {'lat','x'}, dimensions={0} | all-to-all | bytes 2359296 | tf_op jit(solution)/shard_map/all_to_all | solution.py:531
  113.0 3.8 %decode_blocks.1 = bf16[64,12288]{1,0:T(8,128)(2,1)} custom-call(s32[96]{0:T(128)S(1)} %copy-done.4, bf16[2,12288]{1,0:T(2,128)(2,1)S(1)} %copy-done.1, bf16[1536,128]{1,0:T(8,128)(2,1)S(1)} %get-tuple-element.41.near_ref, bf16[4608,128]{1,0:T(8,128)(2,1)S(1)} %bitcast.24), custom_call_target="tpu_custom_call" | custom-call | tf_op jit(solution)/shard_map/decode_blocks/pallas_call | solution.py:723
  (47 shorter events, 3.7 us)
Async XLA Ops:
  0.6 11.9 %copy-start.10 = (f32[256]{0:T(256)S(1)}, f32[256]{0:T(256)}, u32[]{:S(2)}) copy-start(f32[256]{0:T(256)} %param.23) | copy-start | bytes 3076
  7.4 22.6 %all-to-all-start.6 = ((bf16[8,624,128]{2,1,0:T(8,128)(2,1)}), bf16[8,624,128]{2,1,0:T(8,128)(2,1)S(1)}, u32[]{:S(2)}, u32[]{:S(2)}) async-start(bf16[8,624,128]{2,1,0:T(8,128)(2,1)} %bitcast.38), calls=%async_computation.6 | async-start | bytes 2555904 | tf_op jit(solution)/shard_map/all_to_all | solution.py:531
  32.2 15.3 %copy-start.7 = (bf16[256,768]{1,0:T(8,128)(2,1)S(1)}, bf16[256,768]{1,0:T(8,128)(2,1)}, u32[]{:S(2)}) copy-start(bf16[256,768]{1,0:T(8,128)(2,1)} %refs_6_.1) | copy-start | bytes 1179652
  32.2 15.3 %copy-start.8 = (bf16[256,256]{1,0:T(8,128)(2,1)S(1)}, bf16[256,256]{1,0:T(8,128)(2,1)}, u32[]{:S(2)}) copy-start(bf16[256,256]{1,0:T(8,128)(2,1)} %refs_7_.1) | copy-start | bytes 393220
  32.2 16.5 %collective-permute-start = (bf16[800,128]{1,0:T(8,128)(2,1)S(1)}, bf16[800,128]{1,0:T(8,128)(2,1)S(1)}, u32[]{:S(2)}, u32[]{:S(2)}) collective-permute-start(bf16[800,128]{1,0:T(8,128)(2,1)S(1)} %get-tuple-element.28), channel_id=1, source_target_pairs={{0,6},{2,4},{4,2},{6,0},{1,7},{3,5},{5,3},{7,1},{8,14},{10,12},{12... | collective-permute-start | bytes 614408 | tf_op jit(solution)/shard_map/ppermute | solution.py:548
  35.9 17.2 %collective-permute-start.1 = (bf16[800,128]{1,0:T(8,128)(2,1)S(1)}, bf16[800,128]{1,0:T(8,128)(2,1)S(1)}, u32[]{:S(2)}, u32[]{:S(2)}) collective-permute-start(bf16[800,128]{1,0:T(8,128)(2,1)S(1)} %get-tuple-element.27), channel_id=1, source_target_pairs={{0,4},{2,6},{4,0},{6,2},{1,5},{3,7},{5,1},{7,3},{8,12},{10,14},{12... | collective-permute-start | bytes 614408 | tf_op jit(solution)/shard_map/ppermute | solution.py:548
  35.9 17.2 %collective-permute-start.2 = (bf16[800,128]{1,0:T(8,128)(2,1)S(1)}, bf16[800,128]{1,0:T(8,128)(2,1)S(1)}, u32[]{:S(2)}, u32[]{:S(2)}) collective-permute-start(bf16[800,128]{1,0:T(8,128)(2,1)S(1)} %get-tuple-element.26), channel_id=1, source_target_pairs={{0,2},{2,0},{4,6},{6,4},{1,3},{3,1},{5,7},{7,5},{8,10},{10,8},{12,... | collective-permute-start | bytes 614408 | tf_op jit(solution)/shard_map/ppermute | solution.py:548
  47.3 5.8 %copy-start = (bf16[32,48,256]{2,1,0:T(8,128)(2,1)S(1)}, bf16[32,48,256]{2,1,0:T(8,128)(2,1)}, u32[]{:S(2)}) copy-start(bf16[32,48,256]{2,1,0:T(8,128)(2,1)} %refs_5_.1) | copy-start | bytes 2359300
  47.3 5.8 %copy-start.2 = (bf16[64,256]{1,0:T(8,128)(2,1)S(1)}, bf16[64,256]{1,0:T(8,128)(2,1)}, u32[]{:S(2)}) copy-start(bf16[64,256]{1,0:T(8,128)(2,1)} %refs_4_.3) | copy-start | bytes 98308
  48.7 13.8 %copy-start.5 = (bf16[256,1024]{1,0:T(8,128)(2,1)S(1)}, bf16[256,1024]{1,0:T(8,128)(2,1)}, u32[]{:S(2)}) copy-start(bf16[256,1024]{1,0:T(8,128)(2,1)} %refs_9_.1) | copy-start | bytes 1572868
  48.7 13.8 %copy-start.6 = (bf16[1024,256]{1,0:T(8,128)(2,1)S(1)}, bf16[1024,256]{1,0:T(8,128)(2,1)}, u32[]{:S(2)}) copy-start(bf16[1024,256]{1,0:T(8,128)(2,1)} %refs_10_.1) | copy-start | bytes 1572868
  48.7 13.8 %copy-start.9 = (bf16[256,64]{0,1:T(8,128)(2,1)S(1)}, bf16[256,64]{0,1:T(8,128)(2,1)}, u32[]{:S(2)}) copy-start(bf16[256,64]{0,1:T(8,128)(2,1)} %param.29) | copy-start | bytes 98308
  48.8 13.8 %copy-start.11 = (f32[256]{0:T(256)S(1)}, f32[256]{0:T(256)}, u32[]{:S(2)}) copy-start(f32[256]{0:T(256)} %param.26) | copy-start | bytes 3076
  53.6 4.1 %collective-permute-start.3 = (bf16[4,48,256]{2,1,0:T(8,128)(2,1)S(1)}, bf16[4,48,256]{2,1,0:T(8,128)(2,1)S(1)}, u32[]{:S(2)}, u32[]{:S(2)}) collective-permute-start(bf16[4,48,256]{2,1,0:T(8,128)(2,1)S(1)} %get-tuple-element.38), channel_id=1, source_target_pairs={{0,8},{8,16},{16,24},{24,0},{1,9},{9,17},{17,25},{25,1},{2,10},{10... | collective-permute-start | bytes 294920 | tf_op jit(solution)/shard_map/ppermute | solution.py:517
  53.7 4.0 %collective-permute-start.4 = (bf16[4,48,256]{2,1,0:T(8,128)(2,1)S(1)}, bf16[4,48,256]{2,1,0:T(8,128)(2,1)S(1)}, u32[]{:S(2)}, u32[]{:S(2)}) collective-permute-start(bf16[4,48,256]{2,1,0:T(8,128)(2,1)S(1)} %get-tuple-element.39), channel_id=1, source_target_pairs={{8,0},{16,8},{24,16},{0,24},{9,1},{17,9},{25,17},{1,25},{10,2},{18... | collective-permute-start | bytes 294920 | tf_op jit(solution)/shard_map/ppermute | solution.py:518
  57.8 9.4 %collective-permute-start.5 = (bf16[40,4,256]{2,1,0:T(4,128)(2,1)S(1)}, bf16[40,4,256]{2,1,0:T(4,128)(2,1)S(1)}, u32[]{:S(2)}, u32[]{:S(2)}) collective-permute-start(bf16[40,4,256]{2,1,0:T(4,128)(2,1)S(1)} %get-tuple-element.36), channel_id=1, source_target_pairs={{0,1},{1,2},{2,3},{3,4},{4,5},{5,6},{6,7},{7,0},{8,9},{9,10},{10,1... | collective-permute-start | bytes 245768 | tf_op jit(solution)/shard_map/ppermute | solution.py:517
  58.8 8.4 %collective-permute-start.6 = (bf16[40,4,256]{2,1,0:T(4,128)(2,1)S(1)}, bf16[40,4,256]{2,1,0:T(4,128)(2,1)S(1)}, u32[]{:S(2)}, u32[]{:S(2)}) collective-permute-start(bf16[40,4,256]{2,1,0:T(4,128)(2,1)S(1)} %get-tuple-element.37), channel_id=1, source_target_pairs={{1,0},{2,1},{3,2},{4,3},{5,4},{6,5},{7,6},{0,7},{9,8},{10,9},{11,1... | collective-permute-start | bytes 245768 | tf_op jit(solution)/shard_map/ppermute | solution.py:518
  67.2 0.7 copy-start.3
  75.7 15.5 %collective-permute-start.7 = (bf16[768,128]{1,0:T(8,128)(2,1)S(1)}, bf16[768,128]{1,0:T(8,128)(2,1)S(1)}, u32[]{:S(2)}, u32[]{:S(2)}) collective-permute-start(bf16[768,128]{1,0:T(8,128)(2,1)S(1)} %get-tuple-element.35.refs_1_), channel_id=1, source_target_pairs={{0,2},{2,0},{4,6},{6,4},{1,3},{3,1},{5,7},{7,5},{8,10},{10,8},{12,... | collective-permute-start | bytes 589832 | tf_op jit(solution)/shard_map/ppermute | solution.py:548
  75.7 17.1 %collective-permute-start.8 = (bf16[768,128]{1,0:T(8,128)(2,1)S(1)}, bf16[768,128]{1,0:T(8,128)(2,1)S(1)}, u32[]{:S(2)}, u32[]{:S(2)}) collective-permute-start(bf16[768,128]{1,0:T(8,128)(2,1)S(1)} %get-tuple-element.35.refs_1_), channel_id=1, source_target_pairs={{0,4},{2,6},{4,0},{6,2},{1,5},{3,7},{5,1},{7,3},{8,12},{10,14},{12... | collective-permute-start | bytes 589832 | tf_op jit(solution)/shard_map/ppermute | solution.py:548
  77.1 15.7 %collective-permute-start.9 = (bf16[768,128]{1,0:T(8,128)(2,1)S(1)}, bf16[768,128]{1,0:T(8,128)(2,1)S(1)}, u32[]{:S(2)}, u32[]{:S(2)}) collective-permute-start(bf16[768,128]{1,0:T(8,128)(2,1)S(1)} %get-tuple-element.35.refs_1_), channel_id=1, source_target_pairs={{0,6},{2,4},{4,2},{6,0},{1,7},{3,5},{5,3},{7,1},{8,14},{10,12},{12... | collective-permute-start | bytes 589832 | tf_op jit(solution)/shard_map/ppermute | solution.py:548
  91.2 21.8 %copy-start.1 = (bf16[2,12288]{1,0:T(2,128)(2,1)S(1)}, bf16[2,12288]{1,0:T(2,128)(2,1)}, u32[]{:S(2)}) copy-start(bf16[2,12288]{1,0:T(2,128)(2,1)} %offset_ref.1) | copy-start | bytes 147460
  91.2 21.8 %copy-start.4 = (s32[96]{0:T(128)S(1)}, s32[96]{0:T(128)}, u32[]{:S(2)}) copy-start(s32[96]{0:T(128)} %get-tuple-element.34.slot_ref) | copy-start | bytes 1156

commit v7 on v6

--- a/solution.py
+++ b/solution.py
@@ -56,11 +56,12 @@
 
 
 def encode_blocks(
-    capacity, shape, place_ref, tile_hbm, patch_hbm, feat_hbm, offset_hbm, near_ref, far_ref,
+    capacity, shape, tile_hbm, patch_hbm, feat_hbm, offset_hbm, near_ref, far_ref,
     slot_ref, send_ref, tile_ref, patch_ref, feat_ref, offset_ref, count_ref, sems,
 ):
     lat, depth, width = shape
     devices = lat * depth * width
+    plane_id = lax.axis_index("z")
     feat_width = feat_ref.shape[0]
     blocks = feat_ref.shape[1] // BLK
     step = sems.shape[0] - 3
@@ -95,13 +96,13 @@
         tile = tile_ref[b]
         rank = count_ref[tile]
         count_ref[tile] = rank + 1
-        lon = tile % (depth * width)
-        partner = tile // (depth * width) * width + lon % width
-        hop = lon // width ^ place_ref[1]
+        lon = lax.rem(tile, depth * width)
+        partner = lax.div(tile, depth * width) * width + lax.rem(lon, width)
+        hop = lax.div(lon, width) ^ plane_id
         piece = jnp.where(hop == 0, partner, lat * width + partner * (depth - 1) + hop - 1)
         slot_ref[b] = piece * capacity + rank
-        pair = rank // 2
-        half = rank % 2
+        pair = lax.div(rank, 2)
+        half = lax.rem(rank, 2)
         col = pl.multiple_of(b * BLK, BLK)
         feat = jnp.concatenate([feat_ref[:, pl.ds(col, BLK)], ones], axis=0)
         weights = block_weights(offset_ref[:, pl.ds(col, BLK)].astype(jnp.float32))
@@ -392,7 +393,7 @@
 
 
 def outer_block(
-    lat_cells, place_ref, ext_ref, inner_latent_ref, inner_proj_ref, inner_mixed_ref, norm_ref, qkv_ref, out_ref,
+    lat_cells, ext_ref, inner_latent_ref, inner_proj_ref, inner_mixed_ref, norm_ref, qkv_ref, out_ref,
     mlp_ref, up_ref, down_ref, decode_ref, latent_ref, proj_ref, mixed_ref, turned_ref, key_ref,
     pack_ref, att_ref, score_ref, prob_ref,
 ):
@@ -401,7 +402,7 @@
     margin = WIN // 2
     feat_width = decode_ref.shape[0]
     last_row, last_col = ext_rows - WIN, ext_cols - WIN
-    top = place_ref[2] * tile_rows - margin
+    top = lax.axis_index("lat") * tile_rows - margin
     turn_weights(qkv_ref, turned_ref)
 
     def place(windows, side):
@@ -477,34 +478,38 @@
                 out_ref[at : at + feat_width, :] = pair.astype(jnp.bfloat16)
 
 
-def decode_blocks(slot_ref, offset_ref, near_ref, far_ref, out_ref, back_ref):
+def decode_blocks(slot_ref, offset_ref, near_ref, far_ref, out_hbm, back_ref, out_ref, sems):
+    feat_width, count = out_ref.shape
+    blocks = count // BLK
+    step = sems.shape[0]
+    size = blocks // step
     back_ref[: near_ref.shape[0], :] = near_ref[...]
     back_ref[near_ref.shape[0] :, :] = far_ref[...]
-    feat_width, count = out_ref.shape
-    blocks = count // BLK
 
     def one(b):
         slot = slot_ref[b]
-        col = pl.multiple_of(b * BLK, BLK)
-        weights = block_weights(offset_ref[:, pl.ds(col, BLK)].astype(jnp.float32))
+        span = slice(b * BLK, (b + 1) * BLK)
+        weights = block_weights(offset_ref[:, span].astype(jnp.float32))
         total = jnp.sum(weights.astype(jnp.float32), axis=0, keepdims=True)
         nothing = jnp.zeros_like(weights)
-        low = slot % 2 == 0
+        low = lax.rem(slot, 2) == 0
         both = jnp.concatenate(
             [jnp.where(low, weights, nothing), jnp.where(low, nothing, weights)], axis=0
         )
-        values = back_ref[pl.ds(pl.multiple_of(slot // 2 * feat_width, 16), feat_width), :]
+        row = pl.multiple_of(lax.div(slot, 2) * feat_width, 16)
+        values = back_ref[pl.ds(row, feat_width), :]
         mean = jnp.dot(values, both, preferred_element_type=jnp.float32) * (1.0 / total)
-        out_ref[:, pl.ds(col, BLK)] = mean.astype(jnp.bfloat16)
-
-    unroll = 32 if blocks % 32 == 0 else 1
-
-    def body(i, _):
-        for u in range(unroll):
-            one(i * unroll + u)
-        return 0
-
-    lax.fori_loop(0, blocks // unroll, body, 0)
+        out_ref[:, span] = mean.astype(jnp.bfloat16)
+
+    copies = []
+    for i in range(step):
+        for b in range(i * size, (i + 1) * size):
+            one(b)
+        span = pl.ds(i * size * BLK, size * BLK)
+        copies.append(pltpu.make_async_copy(out_ref.at[:, span], out_hbm.at[:, span], sems.at[i]))
+        copies[i].start()
+    for copy in copies:
+        copy.wait()
 
 
 def with_halo(array, sides, width):
@@ -575,11 +580,6 @@
     patch_total = (tile_rows // PATCH) * (tile_cols // PATCH)
     chunk = pairs * feat_width + meta_rows(pairs)
     dense = dense_rows(patch_total // 2, feat_width)
-    lat_id = lax.axis_index("lat").astype(jnp.int32)
-    place = jnp.stack(
-        [lat_id * width + lax.axis_index("x"), lax.axis_index("z"), lat_id]
-    ).astype(jnp.int32)
-
     steps = 3 if blocks % 3 == 0 else 1
     send_near, send_far, slots = pl.pallas_call(
         lambda *refs: encode_blocks(capacity, (lat, depth, width), *refs),
@@ -588,7 +588,7 @@
             jax.ShapeDtypeStruct((plane * hops * chunk, LANES), jnp.bfloat16),
             jax.ShapeDtypeStruct((blocks,), jnp.int32),
         ),
-        in_specs=[smem()] + [pl.BlockSpec(memory_space=pltpu.HBM)] * 4,
+        in_specs=[pl.BlockSpec(memory_space=pltpu.HBM)] * 4,
         out_specs=(vmem(), vmem(), smem()),
         scratch_shapes=[
             pltpu.VMEM((devices * chunk, LANES), jnp.bfloat16),
@@ -601,7 +601,7 @@
         ],
         compiler_params=params(61),
         name="encode_blocks",
-    )(place, block_tile.reshape(blocks), block_patch, obs_feat, obs_offset)
+    )(block_tile.reshape(blocks), block_patch, obs_feat, obs_offset)
 
     def ids_of(recv, tiles):
         at = pairs * feat_width + 2 * pairs
@@ -691,14 +691,14 @@
             jax.ShapeDtypeStruct(grid_base.shape, jnp.bfloat16),
             jax.ShapeDtypeStruct((patch_total // 2 * feat_width, LANES), jnp.bfloat16),
         ),
-        in_specs=[smem()] + [vmem()] * 11,
+        in_specs=[vmem()] * 11,
         out_specs=(vmem(), vmem()),
         scratch_shapes=[pltpu.VMEM((ext_rows, ext_cols, channels), jnp.float32)]
         + scratch(max(ext_cols // WIN, 2 * (ext_rows // WIN - 2))),
         compiler_params=params(20),
         cost_estimate=pl.CostEstimate(flops=8 * 10**9, bytes_accessed=10**7, transcendentals=0),
         name="outer_block",
-    )(place, ext, latent_inner, proj_inner, mixed_inner, *weights)
+    )(ext, latent_inner, proj_inner, mixed_inner, *weights)
 
     def reply(ids, tiles, name):
         count = len(tiles)
@@ -724,9 +724,13 @@
         decode_blocks,
         out_shape=jax.ShapeDtypeStruct((feat_width, obs_count), jnp.bfloat16),
         in_specs=[smem(), vmem()] + [vmem()] * 2,
-        out_specs=vmem(),
-        scratch_shapes=[pltpu.VMEM((devices * pairs * feat_width, LANES), jnp.bfloat16)],
-        compiler_params=params(10),
+        out_specs=pl.BlockSpec(memory_space=pltpu.HBM),
+        scratch_shapes=[
+            pltpu.VMEM((devices * pairs * feat_width, LANES), jnp.bfloat16),
+            pltpu.VMEM((feat_width, obs_count), jnp.bfloat16),
+            pltpu.SemaphoreType.DMA((steps,)),
+        ],
+        compiler_params=params(12),
         name="decode_blocks",
     )(slots, obs_offset, near_back, far_back)
     return (latent, obs_out)

time: 119 us -> 116 us (0.975)
  Pallas kernels: 27.5 us -> 25.3 us
where the time goes in v7:
time: 116 us; the launch traced here: 114 us
  blocking collectives  40.4 us (35%)
  Pallas kernels  25.3 us (22%)
  waiting for transfers between devices  24.5 us (21%)
  starting transfers between devices  20.6 us (18%)
  between operations  1.66 us (1%)
    all_to_all x3, blocking collectives, swap_in_plane(): lax.all_to_all(parts, ('lat', 'x'), split_axis=0, concat_axis=0, tiled=True)  40.4 us
    all_to_all x1, waiting for transfers between devices, swap_in_plane(): lax.all_to_all(parts, ('lat', 'x'), split_axis=0, concat_axis=0, tiled=True)  16.2 us
    ppermute x6, starting transfers between devices, swap_planes(): return lax.ppermute(array, 'z', [(i, i ^ hop) for i in range(depth)])  8.84 us
    pallas_call x1, Pallas kernels, local(): pl.pallas_call(lambda *refs: outer_block(tile_rows * lat, *refs), out_sha...  7.26 us
    ppermute x6, waiting for transfers between devices, swap_planes(): return lax.ppermute(array, 'z', [(i, i ^ hop) for i in range(depth)])  5.98 us
    ppermute x2, starting transfers between devices, with_halo(): after = lax.ppermute(initial, axis, down)  5.51 us
    all_to_all x1, starting transfers between devices, swap_in_plane(): lax.all_to_all(parts, ('lat', 'x'), split_axis=0, concat_axis=0, tiled=True)  5.18 us
    pallas_call x1, Pallas kernels, local(): pl.pallas_call(lambda *refs: encode_blocks(capacity, (lat, depth, width),...  4.87 us
  transfers between devices with their start and end apart: 11, of which 4 were waited for; matrix products, arithmetic and copies ran while one was open for 1% of the time, Pallas kernels for 6%

profile of v7, /device:TPU:0, one launch (start us, length us, event | category | flops | bytes accessed | tf_op | source)
XLA Modules:
  0.0 114.1 jit_solution(15776711389233869581)
XLA Ops:
  0.6 4.9 %encode_blocks.1 = (bf16[1664,128]{1,0:T(8,128)(2,1)S(1)}, bf16[4992,128]{1,0:T(8,128)(2,1)}, s32[96]{0:T(128)}) custom-call(s32[96]{0:T(128)} %bitcast.39, s32[96]{0:T(128)} %refs_1_.1, bf16[64,12288]{1,0:T(8,128)(2,1)} %refs_2_.2, bf16[2,12288]{1,0:T(2,128)(2,1)} %offset_ref.1), custom_call_target="tpu_custom_call" | custom-call | tf_op jit(solution)/shard_map/encode_blocks/pallas_call | solution.py:584
  5.5 5.2 %all-to-all-start.6 = ((bf16[8,624,128]{2,1,0:T(8,128)(2,1)}), bf16[8,624,128]{2,1,0:T(8,128)(2,1)S(1)}, u32[]{:S(2)}, u32[]{:S(2)}) async-start(bf16[8,624,128]{2,1,0:T(8,128)(2,1)} %bitcast.35), calls=%async_computation.6 | async-start | bytes 2555904 | tf_op jit(solution)/shard_map/all_to_all | solution.py:536
  11.9 16.2 %all-to-all-done.6 = bf16[8,624,128]{2,1,0:T(8,128)(2,1)S(1)} async-done(((bf16[8,624,128]{2,1,0:T(8,128)(2,1)}), bf16[8,624,128]{2,1,0:T(8,128)(2,1)S(1)}, u32[]{:S(2)}, u32[]{:S(2)}) %all-to-all-start.6) | async-done | bytes 1277984 | tf_op jit(solution)/shard_map/all_to_all | solution.py:536
  28.4 1.9 %gather_planes.1 = (bf16[800,128]{1,0:T(8,128)(2,1)S(1)}, bf16[800,128]{1,0:T(8,128)(2,1)S(1)}, bf16[800,128]{1,0:T(8,128)(2,1)S(1)}) custom-call(s32[144]{0:T(256)S(1)} %reshape.64.refs_0_, bf16[4992,128]{1,0:T(8,128)(2,1)S(1)} %bitcast.20), custom_call_target="tpu_custom_call" | custom-call | tf_op jit(solution)/shard_map/gather_planes/pallas_call | solution.py:614
  30.4 3.7 %collective-permute-start = (bf16[800,128]{1,0:T(8,128)(2,1)S(1)}, bf16[800,128]{1,0:T(8,128)(2,1)S(1)}, u32[]{:S(2)}, u32[]{:S(2)}) collective-permute-start(bf16[800,128]{1,0:T(8,128)(2,1)S(1)} %get-tuple-element.28), channel_id=1, source_target_pairs={{0,6},{2,4},{4,2},{6,0},{1,7},{3,5},{5,3},{7,1},{8,14},{10,12},{12... | collective-permute-start | bytes 614408 | tf_op jit(solution)/shard_map/ppermute | solution.py:553
  34.0 0.8 collective-permute-start.2
  34.8 10.6 %conditional.2 = (bf16[1664,128]{1,0:T(8,128)(2,1)S(1)}) conditional(s32[]{:T(128)} %bitcast.8, bf16[1664,128]{1,0:T(8,128)(2,1)S(1)} %get-tuple-element.29, bf16[1664,128]{1,0:T(8,128)(2,1)S(1)} %get-tuple-element.29), branch_computations={%region_0.1_spmd, %region_1.2_spmd} | conditional | bytes 3407880 | solution.py:548
  34.8 10.6 %all_to_all.36 = bf16[8,208,128]{2,1,0:T(8,128)(2,1)S(1)} all-to-all(bf16[8,208,128]{2,1,0:T(8,128)(2,1)S(1)} %bitcast.30), channel_id=1, replica_groups=mesh['lat'=4,'z'=4,'x'=2] {'lat','x'}, dimensions={0} | all-to-all | bytes 851968 | tf_op jit(solution)/shard_map/cond/branch_1_fun/all_to_all | solution.py:536
  45.7 1.1 gather_own.1.refs_0_
  46.9 4.4 %collective-permute-done.1.refs_2_ = bf16[800,128]{1,0:T(8,128)(2,1)S(1)} collective-permute-done((bf16[800,128]{1,0:T(8,128)(2,1)S(1)}, bf16[800,128]{1,0:T(8,128)(2,1)S(1)}, u32[]{:S(2)}, u32[]{:S(2)}) %collective-permute-start.1) | collective-permute-done | bytes 204832 | tf_op jit(solution)/shard_map/ppermute | solution.py:553
  51.8 1.7 %collective-permute-start.4 = (bf16[4,48,256]{2,1,0:T(8,128)(2,1)S(1)}, bf16[4,48,256]{2,1,0:T(8,128)(2,1)S(1)}, u32[]{:S(2)}, u32[]{:S(2)}) collective-permute-start(bf16[4,48,256]{2,1,0:T(8,128)(2,1)S(1)} %get-tuple-element.39), channel_id=1, source_target_pairs={{8,0},{16,8},{24,16},{0,24},{9,1},{17,9},{25,17},{1,25},{10,2},{18... | collective-permute-start | bytes 294920 | tf_op jit(solution)/shard_map/ppermute | solution.py:523
  53.5 2.3 %collective-permute-done.3 = bf16[4,48,256]{2,1,0:T(8,128)(2,1)S(1)} collective-permute-done((bf16[4,48,256]{2,1,0:T(8,128)(2,1)S(1)}, bf16[4,48,256]{2,1,0:T(8,128)(2,1)S(1)}, u32[]{:S(2)}, u32[]{:S(2)}) %collective-permute-start.3) | collective-permute-done | bytes 98336 | tf_op jit(solution)/shard_map/ppermute | solution.py:522
  55.9 1.0 collective-permute-start.5
  56.9 3.8 %collective-permute-start.6 = (bf16[40,4,256]{2,1,0:T(4,128)(2,1)S(1)}, bf16[40,4,256]{2,1,0:T(4,128)(2,1)S(1)}, u32[]{:S(2)}, u32[]{:S(2)}) collective-permute-start(bf16[40,4,256]{2,1,0:T(4,128)(2,1)S(1)} %get-tuple-element.37), channel_id=1, source_target_pairs={{1,0},{2,1},{3,2},{4,3},{5,4},{6,5},{7,6},{0,7},{9,8},{10,9},{11,1... | collective-permute-start | bytes 245768 | tf_op jit(solution)/shard_map/ppermute | solution.py:523
  60.7 4.6 %inner_block.1 = (bf16[16,32,256]{2,1,0:T(8,128)(2,1)S(1)}, bf16[256,128]{1,0:T(8,128)(2,1)S(1)}, f32[24,40,256]{2,1,0:T(8,128)S(1)}) custom-call(bf16[32,48,256]{2,1,0:T(8,128)(2,1)S(1)} %start_tile.1.start_ref, f32[1,256]{1,0:T(1,128)S(1)} %bitcast.25, bf16[256,768]{1,0:T(8,128)(2,1)S(1)} %copy-done.6, bf16[256,256]{1,0:T(8,128)(2,1)S(1)} %copy-done.7, ...), custom_call_target="tpu_custom_call" | custom-call | flops 6000000000 | bytes 10000000 | tf_op jit(solution)/shard_map/inner_block/pallas_call | solution.py:672
  65.8 7.3 %outer_block.1 = (bf16[32,48,256]{2,1,0:T(8,128)(2,1)}, bf16[768,128]{1,0:T(8,128)(2,1)S(1)}) custom-call(f32[40,56,256]{2,1,0:T(8,128)S(1)} %maximum_convert_fusion.refs_0_, bf16[16,32,256]{2,1,0:T(8,128)(2,1)S(1)} %get-tuple-element.30.refs_1_, bf16[256,128]{1,0:T(8,128)(2,1)S(1)} %get-tuple-element.31.refs_2_, ...), custom_call_target="tpu_custom_call" | custom-call | flops 8000000000 | bytes 10000000 | tf_op jit(solution)/shard_map/outer_block/pallas_call | solution.py:688
  73.1 1.6 %collective-permute-start.8 = (bf16[768,128]{1,0:T(8,128)(2,1)S(1)}, bf16[768,128]{1,0:T(8,128)(2,1)S(1)}, u32[]{:S(2)}, u32[]{:S(2)}) collective-permute-start(bf16[768,128]{1,0:T(8,128)(2,1)S(1)} %get-tuple-element.35.refs_1_), channel_id=1, source_target_pairs={{0,4},{2,6},{4,0},{6,2},{1,5},{3,7},{5,1},{7,3},{8,12},{10,14},{12... | collective-permute-start | bytes 589832 | tf_op jit(solution)/shard_map/ppermute | solution.py:553
  74.7 2.7 %collective-permute-start.9 = (bf16[768,128]{1,0:T(8,128)(2,1)S(1)}, bf16[768,128]{1,0:T(8,128)(2,1)S(1)}, u32[]{:S(2)}, u32[]{:S(2)}) collective-permute-start(bf16[768,128]{1,0:T(8,128)(2,1)S(1)} %get-tuple-element.35.refs_1_), channel_id=1, source_target_pairs={{0,6},{2,4},{4,2},{6,0},{1,7},{3,5},{5,3},{7,1},{8,14},{10,12},{12... | collective-permute-start | bytes 589832 | tf_op jit(solution)/shard_map/ppermute | solution.py:553
  78.2 10.4 %conditional.3 = (bf16[1536,128]{1,0:T(8,128)(2,1)S(1)}) conditional(s32[]{:T(128)} %bitcast.8, bf16[1536,128]{1,0:T(8,128)(2,1)S(1)} %reply_near.1, bf16[1536,128]{1,0:T(8,128)(2,1)S(1)} %reply_near.1), branch_computations={%region_2.3_spmd, %region_3.4_spmd} | conditional | bytes 3145736 | solution.py:548
  78.2 10.4 %all_to_all.39 = bf16[8,192,128]{2,1,0:T(8,128)(2,1)S(1)} all-to-all(bf16[8,192,128]{2,1,0:T(8,128)(2,1)S(1)} %bitcast.32), channel_id=1, replica_groups=mesh['lat'=4,'z'=4,'x'=2] {'lat','x'}, dimensions={0} | all-to-all | bytes 786432 | tf_op jit(solution)/shard_map/cond/branch_1_fun/all_to_all | solution.py:536
  88.6 1.6 %collective-permute-done.8.refs_2_ = bf16[768,128]{1,0:T(8,128)(2,1)S(1)} collective-permute-done((bf16[768,128]{1,0:T(8,128)(2,1)S(1)}, bf16[768,128]{1,0:T(8,128)(2,1)S(1)}, u32[]{:S(2)}, u32[]{:S(2)}) %collective-permute-start.8) | collective-permute-done | bytes 196640 | tf_op jit(solution)/shard_map/ppermute | solution.py:553
  90.2 1.0 reply_far.1
  91.2 19.4 %all_to_all.40 = bf16[8,576,128]{2,1,0:T(8,128)(2,1)S(1)} all-to-all(bf16[8,576,128]{2,1,0:T(8,128)(2,1)S(1)} %bitcast.22), channel_id=1, replica_groups=mesh['lat'=4,'z'=4,'x'=2] {'lat','x'}, dimensions={0} | all-to-all | bytes 2359296 | tf_op jit(solution)/shard_map/all_to_all | solution.py:536
  110.6 3.4 %decode_blocks.1 = bf16[64,12288]{1,0:T(8,128)(2,1)} custom-call(s32[96]{0:T(128)S(1)} %copy-done.3, bf16[2,12288]{1,0:T(2,128)(2,1)S(1)} %copy-done.1, bf16[1536,128]{1,0:T(8,128)(2,1)S(1)} %get-tuple-element.41.near_ref, bf16[4608,128]{1,0:T(8,128)(2,1)S(1)} %bitcast.21), custom_call_target="tpu_custom_call" | custom-call | tf_op jit(solution)/shard_map/decode_blocks/pallas_call | solution.py:723
  (44 shorter events, 2.9 us)
Async XLA Ops:
  0.6 10.1 %copy-start.9 = (f32[256]{0:T(256)S(1)}, f32[256]{0:T(256)}, u32[]{:S(2)}) copy-start(f32[256]{0:T(256)} %param.23) | copy-start | bytes 3076
  5.5 22.6 %all-to-all-start.6 = ((bf16[8,624,128]{2,1,0:T(8,128)(2,1)}), bf16[8,624,128]{2,1,0:T(8,128)(2,1)S(1)}, u32[]{:S(2)}, u32[]{:S(2)}) async-start(bf16[8,624,128]{2,1,0:T(8,128)(2,1)} %bitcast.35), calls=%async_computation.6 | async-start | bytes 2555904 | tf_op jit(solution)/shard_map/all_to_all | solution.py:536
  30.4 15.3 %copy-start.6 = (bf16[256,768]{1,0:T(8,128)(2,1)S(1)}, bf16[256,768]{1,0:T(8,128)(2,1)}, u32[]{:S(2)}) copy-start(bf16[256,768]{1,0:T(8,128)(2,1)} %refs_5_.3) | copy-start | bytes 1179652
  30.4 15.3 %copy-start.7 = (bf16[256,256]{1,0:T(8,128)(2,1)S(1)}, bf16[256,256]{1,0:T(8,128)(2,1)}, u32[]{:S(2)}) copy-start(bf16[256,256]{1,0:T(8,128)(2,1)} %refs_6_.1) | copy-start | bytes 393220
  30.4 16.5 %collective-permute-start = (bf16[800,128]{1,0:T(8,128)(2,1)S(1)}, bf16[800,128]{1,0:T(8,128)(2,1)S(1)}, u32[]{:S(2)}, u32[]{:S(2)}) collective-permute-start(bf16[800,128]{1,0:T(8,128)(2,1)S(1)} %get-tuple-element.28), channel_id=1, source_target_pairs={{0,6},{2,4},{4,2},{6,0},{1,7},{3,5},{5,3},{7,1},{8,14},{10,12},{12... | collective-permute-start | bytes 614408 | tf_op jit(solution)/shard_map/ppermute | solution.py:553
  34.0 17.2 %collective-permute-start.1 = (bf16[800,128]{1,0:T(8,128)(2,1)S(1)}, bf16[800,128]{1,0:T(8,128)(2,1)S(1)}, u32[]{:S(2)}, u32[]{:S(2)}) collective-permute-start(bf16[800,128]{1,0:T(8,128)(2,1)S(1)} %get-tuple-element.27), channel_id=1, source_target_pairs={{0,4},{2,6},{4,0},{6,2},{1,5},{3,7},{5,1},{7,3},{8,12},{10,14},{12... | collective-permute-start | bytes 614408 | tf_op jit(solution)/shard_map/ppermute | solution.py:553
  34.0 17.2 %collective-permute-start.2 = (bf16[800,128]{1,0:T(8,128)(2,1)S(1)}, bf16[800,128]{1,0:T(8,128)(2,1)S(1)}, u32[]{:S(2)}, u32[]{:S(2)}) collective-permute-start(bf16[800,128]{1,0:T(8,128)(2,1)S(1)} %get-tuple-element.26), channel_id=1, source_target_pairs={{0,2},{2,0},{4,6},{6,4},{1,3},{3,1},{5,7},{7,5},{8,10},{10,8},{12,... | collective-permute-start | bytes 614408 | tf_op jit(solution)/shard_map/ppermute | solution.py:553
  45.5 5.8 %copy-start = (bf16[32,48,256]{2,1,0:T(8,128)(2,1)S(1)}, bf16[32,48,256]{2,1,0:T(8,128)(2,1)}, u32[]{:S(2)}) copy-start(bf16[32,48,256]{2,1,0:T(8,128)(2,1)} %refs_5_.2) | copy-start | bytes 2359300
  45.5 5.8 %copy-start.2 = (bf16[64,256]{1,0:T(8,128)(2,1)S(1)}, bf16[64,256]{1,0:T(8,128)(2,1)}, u32[]{:S(2)}) copy-start(bf16[64,256]{1,0:T(8,128)(2,1)} %refs_4_.1) | copy-start | bytes 98308
  46.9 13.8 %copy-start.4 = (bf16[256,1024]{1,0:T(8,128)(2,1)S(1)}, bf16[256,1024]{1,0:T(8,128)(2,1)}, u32[]{:S(2)}) copy-start(bf16[256,1024]{1,0:T(8,128)(2,1)} %refs_8_.1) | copy-start | bytes 1572868
  46.9 13.8 %copy-start.5 = (bf16[1024,256]{1,0:T(8,128)(2,1)S(1)}, bf16[1024,256]{1,0:T(8,128)(2,1)}, u32[]{:S(2)}) copy-start(bf16[1024,256]{1,0:T(8,128)(2,1)} %refs_9_.1) | copy-start | bytes 1572868
  46.9 13.8 %copy-start.8 = (bf16[256,64]{0,1:T(8,128)(2,1)S(1)}, bf16[256,64]{0,1:T(8,128)(2,1)}, u32[]{:S(2)}) copy-start(bf16[256,64]{0,1:T(8,128)(2,1)} %param.29) | copy-start | bytes 98308
  46.9 13.8 %copy-start.10 = (f32[256]{0:T(256)S(1)}, f32[256]{0:T(256)}, u32[]{:S(2)}) copy-start(f32[256]{0:T(256)} %param.26) | copy-start | bytes 3076
  51.7 4.1 %collective-permute-start.3 = (bf16[4,48,256]{2,1,0:T(8,128)(2,1)S(1)}, bf16[4,48,256]{2,1,0:T(8,128)(2,1)S(1)}, u32[]{:S(2)}, u32[]{:S(2)}) collective-permute-start(bf16[4,48,256]{2,1,0:T(8,128)(2,1)S(1)} %get-tuple-element.38), channel_id=1, source_target_pairs={{0,8},{8,16},{16,24},{24,0},{1,9},{9,17},{17,25},{25,1},{2,10},{10... | collective-permute-start | bytes 294920 | tf_op jit(solution)/shard_map/ppermute | solution.py:522
  51.8 4.0 %collective-permute-start.4 = (bf16[4,48,256]{2,1,0:T(8,128)(2,1)S(1)}, bf16[4,48,256]{2,1,0:T(8,128)(2,1)S(1)}, u32[]{:S(2)}, u32[]{:S(2)}) collective-permute-start(bf16[4,48,256]{2,1,0:T(8,128)(2,1)S(1)} %get-tuple-element.39), channel_id=1, source_target_pairs={{8,0},{16,8},{24,16},{0,24},{9,1},{17,9},{25,17},{1,25},{10,2},{18... | collective-permute-start | bytes 294920 | tf_op jit(solution)/shard_map/ppermute | solution.py:523
  55.9 9.4 %collective-permute-start.5 = (bf16[40,4,256]{2,1,0:T(4,128)(2,1)S(1)}, bf16[40,4,256]{2,1,0:T(4,128)(2,1)S(1)}, u32[]{:S(2)}, u32[]{:S(2)}) collective-permute-start(bf16[40,4,256]{2,1,0:T(4,128)(2,1)S(1)} %get-tuple-element.36), channel_id=1, source_target_pairs={{0,1},{1,2},{2,3},{3,4},{4,5},{5,6},{6,7},{7,0},{8,9},{9,10},{10,1... | collective-permute-start | bytes 245768 | tf_op jit(solution)/shard_map/ppermute | solution.py:522
  56.9 8.4 %collective-permute-start.6 = (bf16[40,4,256]{2,1,0:T(4,128)(2,1)S(1)}, bf16[40,4,256]{2,1,0:T(4,128)(2,1)S(1)}, u32[]{:S(2)}, u32[]{:S(2)}) collective-permute-start(bf16[40,4,256]{2,1,0:T(4,128)(2,1)S(1)} %get-tuple-element.37), channel_id=1, source_target_pairs={{1,0},{2,1},{3,2},{4,3},{5,4},{6,5},{7,6},{0,7},{9,8},{10,9},{11,1... | collective-permute-start | bytes 245768 | tf_op jit(solution)/shard_map/ppermute | solution.py:523
  73.1 15.5 %collective-permute-start.7 = (bf16[768,128]{1,0:T(8,128)(2,1)S(1)}, bf16[768,128]{1,0:T(8,128)(2,1)S(1)}, u32[]{:S(2)}, u32[]{:S(2)}) collective-permute-start(bf16[768,128]{1,0:T(8,128)(2,1)S(1)} %get-tuple-element.35.refs_1_), channel_id=1, source_target_pairs={{0,2},{2,0},{4,6},{6,4},{1,3},{3,1},{5,7},{7,5},{8,10},{10,8},{12,... | collective-permute-start | bytes 589832 | tf_op jit(solution)/shard_map/ppermute | solution.py:553
  73.1 17.1 %collective-permute-start.8 = (bf16[768,128]{1,0:T(8,128)(2,1)S(1)}, bf16[768,128]{1,0:T(8,128)(2,1)S(1)}, u32[]{:S(2)}, u32[]{:S(2)}) collective-permute-start(bf16[768,128]{1,0:T(8,128)(2,1)S(1)} %get-tuple-element.35.refs_1_), channel_id=1, source_target_pairs={{0,4},{2,6},{4,0},{6,2},{1,5},{3,7},{5,1},{7,3},{8,12},{10,14},{12... | collective-permute-start | bytes 589832 | tf_op jit(solution)/shard_map/ppermute | solution.py:553
  74.7 15.5 %collective-permute-start.9 = (bf16[768,128]{1,0:T(8,128)(2,1)S(1)}, bf16[768,128]{1,0:T(8,128)(2,1)S(1)}, u32[]{:S(2)}, u32[]{:S(2)}) collective-permute-start(bf16[768,128]{1,0:T(8,128)(2,1)S(1)} %get-tuple-element.35.refs_1_), channel_id=1, source_target_pairs={{0,6},{2,4},{4,2},{6,0},{1,7},{3,5},{5,3},{7,1},{8,14},{10,12},{12... | collective-permute-start | bytes 589832 | tf_op jit(solution)/shard_map/ppermute | solution.py:553
  88.6 22.0 %copy-start.1 = (bf16[2,12288]{1,0:T(2,128)(2,1)S(1)}, bf16[2,12288]{1,0:T(2,128)(2,1)}, u32[]{:S(2)}) copy-start(bf16[2,12288]{1,0:T(2,128)(2,1)} %offset_ref.1) | copy-start | bytes 147460
  88.6 22.0 %copy-start.3 = (s32[96]{0:T(128)S(1)}, s32[96]{0:T(128)}, u32[]{:S(2)}) copy-start(s32[96]{0:T(128)} %get-tuple-element.34.slot_ref) | copy-start | bytes 1156

commit v8 on v7

--- a/solution.py
+++ b/solution.py
@@ -236,7 +236,7 @@
 
 
 def attend(
-    cells_ref, windows, side, norm_gain, qkv_ref, out_ref, turned_ref, key_ref, pack_ref, att_ref,
+    cells_ref, windows, sides, norm_gain, qkv_ref, out_ref, turned_ref, key_ref, pack_ref, att_ref,
     score_ref, prob_ref,
 ):
     channels = qkv_ref.shape[0]
@@ -266,11 +266,13 @@
     pack_ref[:, :size] = lax.dot_general(
         turned_ref[...], normed, NT, preferred_element_type=jnp.float32
     ).astype(jnp.bfloat16)
-    if side is not None:
-        key_row = lax.broadcasted_iota(jnp.int32, (tokens, LANES), 0) // WIN
-        query_row = lax.broadcasted_iota(jnp.int32, (tokens, LANES), 1) % tokens // WIN
-        bias = jnp.where(side(key_row) == side(query_row), 0.0, -1e30)
-        bias = jnp.concatenate([bias] * heads, axis=1)
+    key_row = lax.broadcasted_iota(jnp.int32, (tokens, LANES), 0) // WIN
+    query_row = lax.broadcasted_iota(jnp.int32, (tokens, LANES), 1) % tokens // WIN
+    bias = [None] * count
+    for p, side in enumerate(sides):
+        if side is not None:
+            apart = jnp.where(side(key_row) == side(query_row), 0.0, -1e30)
+            bias[p] = jnp.concatenate([apart] * heads, axis=1)
     parts = [(p, g) for p in range(count) for g in range(channels // group)]
     for n, (p, g) in enumerate(parts):
         span = slice(p * LANES, (p + 1) * LANES)
@@ -291,7 +293,7 @@
         )
         scores = jnp.dot(key_ref[span, at], stack, preferred_element_type=jnp.float32)
         scores = jnp.where(own, scores[:tokens], scores[tokens:])
-        score_ref[n] = scores if side is None else scores + bias
+        score_ref[n] = scores if bias[p] is None else scores + bias[p]
     for n in range(len(parts)):
         scores = score_ref[n]
         peak = jnp.max(scores, axis=0, keepdims=True)
@@ -341,12 +343,17 @@
 
 
 def patch_order(patch_rows, patch_cols):
-    inner = lambda r, c: 0 < r < patch_rows - 1 and 0 < c < patch_cols - 1
     every = [(r, c) for r in range(patch_rows) for c in range(patch_cols)]
-    first = [at for at in every if inner(*at)]
-    sides = [at for at in every if 0 < at[0] < patch_rows - 1 and not inner(*at)]
-    ends = [at for at in every if not 0 < at[0] < patch_rows - 1]
-    return first, sides, ends
+    middle = [(r, c) for r, c in every if 0 < c < patch_cols - 1]
+    first = [(r, c) for r, c in middle if 0 < r < patch_rows - 1]
+    ends = [at for at in middle if at not in first]
+    return first, ends, [at for at in every if at not in middle]
+
+
+def edge_side(top, row, lat_cells):
+    return lambda r: (top + row + r >= 0).astype(jnp.int32) + (
+        top + row + r >= lat_cells
+    ).astype(jnp.int32)
 
 
 def inner_block(
@@ -361,7 +368,7 @@
     for row in range(0, tile_rows - WIN, WIN):
         cols = range(0, tile_cols - WIN, WIN)
         mixed = attend(
-            cells_ref, [(row + margin, col + margin) for col in cols], None, norm_ref[...],
+            cells_ref, [(row + margin, col + margin) for col in cols], [], norm_ref[...],
             qkv_ref, out_ref, turned_ref, key_ref, pack_ref, att_ref, score_ref, prob_ref,
         )
         for col, block in zip(cols, mixed):
@@ -392,10 +399,59 @@
             done += feat_width
 
 
+def tall_block(
+    lat_cells, tall_ref, inner_mixed_ref, norm_ref, qkv_ref, out_ref, mlp_ref, up_ref, down_ref,
+    decode_ref, latent_ref, proj_ref, mixed_ref, cells_ref, turned_ref, key_ref, pack_ref,
+    att_ref, score_ref, prob_ref,
+):
+    rows, tile_cols, channels = tall_ref.shape
+    margin = WIN // 2
+    tile_rows = rows - 2 * margin
+    feat_width = decode_ref.shape[0]
+    last = rows - WIN
+    top = lax.axis_index("lat") * tile_rows - margin
+    turn_weights(qkv_ref, turned_ref)
+    for part in (slice(0, 2 * WIN), slice(rows - 2 * WIN, rows)):
+        cells_ref[part] = tall_ref[part].astype(jnp.float32)
+    cols = range(0, tile_cols - WIN, WIN)
+    for i, row in enumerate((0, last)):
+        mixed = attend(
+            cells_ref, [(row, col + margin) for col in cols],
+            [edge_side(top, row, lat_cells)] * -(-len(cols) // 2), norm_ref[...], qkv_ref,
+            out_ref, turned_ref, key_ref, pack_ref, att_ref, score_ref, prob_ref,
+        )
+        for col, block in zip(cols, mixed):
+            mixed_ref[i * WIN : (i + 1) * WIN, col : col + WIN, :] = block
+    here = range(1, tile_cols // PATCH - 1)
+    done = 0
+    for i, row in enumerate((margin, last - margin)):
+        begun, mixed = [], []
+        for c in here:
+            span = slice(c * PATCH - margin, (c + 1) * PATCH - margin)
+            begun.append(cells_ref[row : row + PATCH, c * PATCH : (c + 1) * PATCH, :])
+            if i == 0:
+                halves = [mixed_ref[margin:WIN, span, :], inner_mixed_ref[:margin, span, :]]
+            else:
+                halves = [
+                    inner_mixed_ref[tile_rows - WIN - margin :, span, :],
+                    mixed_ref[WIN : WIN + margin, span, :],
+                ]
+            mixed.append(jnp.concatenate(halves, axis=0))
+        latent, turned = finish(begun, mixed, mlp_ref[...], up_ref, down_ref, decode_ref)
+        placed = latent.reshape(len(here), PATCH, PATCH, channels).transpose(1, 0, 2, 3)
+        latent_ref[i * PATCH : (i + 1) * PATCH] = placed.reshape(
+            PATCH, len(here) * PATCH, channels
+        ).astype(jnp.bfloat16)
+        for pair in turned:
+            proj_ref[done : done + feat_width, :] = pair
+            done += feat_width
+
+
 def outer_block(
-    lat_cells, ext_ref, inner_latent_ref, inner_proj_ref, inner_mixed_ref, norm_ref, qkv_ref, out_ref,
-    mlp_ref, up_ref, down_ref, decode_ref, latent_ref, proj_ref, mixed_ref, turned_ref, key_ref,
-    pack_ref, att_ref, score_ref, prob_ref,
+    lat_cells, ext_ref, inner_latent_ref, inner_proj_ref, inner_mixed_ref, tall_latent_ref,
+    tall_proj_ref, tall_mixed_ref, norm_ref, qkv_ref, out_ref, mlp_ref, up_ref, down_ref,
+    decode_ref, latent_ref, proj_ref, mixed_ref, turned_ref, key_ref, pack_ref, att_ref,
+    score_ref, prob_ref,
 ):
     ext_rows, ext_cols, channels = ext_ref.shape
     tile_rows, tile_cols, _ = latent_ref.shape
@@ -404,56 +460,50 @@
     last_row, last_col = ext_rows - WIN, ext_cols - WIN
     top = lax.axis_index("lat") * tile_rows - margin
     turn_weights(qkv_ref, turned_ref)
-
-    def place(windows, side):
-        mixed = attend(
-            ext_ref, windows, side, norm_ref[...], qkv_ref, out_ref, turned_ref, key_ref,
-            pack_ref, att_ref, score_ref, prob_ref,
-        )
-        for (row, col), block in zip(windows, mixed):
-            mixed_ref[row : row + WIN, col : col + WIN, :] = block
-
-    for row in (0, last_row):
-        side = lambda r: (top + row + r >= 0).astype(jnp.int32) + (
-            top + row + r >= lat_cells
-        ).astype(jnp.int32)
-        place([(row, col) for col in range(0, ext_cols, WIN)], side)
-    place([(row, col) for row in range(WIN, last_row, WIN) for col in (0, last_col)], None)
     mixed_ref[WIN:last_row, WIN:last_col, :] = inner_mixed_ref[...]
-    _, sides, ends = patch_order(tile_rows // PATCH, tile_cols // PATCH)
+    mixed_ref[:WIN, WIN:last_col, :] = tall_mixed_ref[:WIN]
+    mixed_ref[last_row:, WIN:last_col, :] = tall_mixed_ref[WIN:]
+    windows = [(row, col) for row in range(0, ext_rows, WIN) for col in (0, last_col)]
+    sides = [
+        edge_side(top, row, lat_cells) if row in (0, last_row) else None
+        for row in range(0, ext_rows, WIN)
+    ]
+    mixed = attend(
+        ext_ref, windows, sides, norm_ref[...], qkv_ref, out_ref, turned_ref, key_ref, pack_ref,
+        att_ref, score_ref, prob_ref,
+    )
+    for (row, col), block in zip(windows, mixed):
+        mixed_ref[row : row + WIN, col : col + WIN, :] = block
     done = inner_proj_ref.shape[0]
     proj_ref[:done, :] = inner_proj_ref[...]
-
-    def patches(here):
-        at = [
-            (
-                slice(r * PATCH + margin, (r + 1) * PATCH + margin),
-                slice(c * PATCH + margin, (c + 1) * PATCH + margin),
-            )
-            for r, c in here
-        ]
-        latent, turned = finish(
-            [ext_ref[r, c, :] for r, c in at],
-            [mixed_ref[r, c, :] for r, c in at],
-            mlp_ref[...], up_ref, down_ref, decode_ref,
+    proj_ref[done : done + tall_proj_ref.shape[0], :] = tall_proj_ref[...]
+    done += tall_proj_ref.shape[0]
+    patch_rows = tile_rows // PATCH
+    _, _, here = patch_order(patch_rows, tile_cols // PATCH)
+    at = [
+        (
+            slice(r * PATCH + margin, (r + 1) * PATCH + margin),
+            slice(c * PATCH + margin, (c + 1) * PATCH + margin),
         )
-        for i, pair in enumerate(turned):
-            at = done + i * feat_width
-            proj_ref[at : at + feat_width, :] = pair
-        return latent.reshape(len(here), PATCH, PATCH, channels), len(turned) * feat_width
-
-    latent, used = patches(sides)
-    done += used
-    for pr in sorted(set(r for r, _ in sides)):
-        left, right = [latent[i] for i, (r, _) in enumerate(sides) if r == pr]
-        inner = inner_latent_ref[(pr - 1) * PATCH : pr * PATCH].astype(jnp.float32)
-        whole = jnp.concatenate([left, inner, right], axis=1)
+        for r, c in here
+    ]
+    latent, turned = finish(
+        [ext_ref[r, c, :] for r, c in at],
+        [mixed_ref[r, c, :] for r, c in at],
+        mlp_ref[...], up_ref, down_ref, decode_ref,
+    )
+    for pair in turned:
+        proj_ref[done : done + feat_width, :] = pair
+        done += feat_width
+    latent = latent.reshape(len(here), PATCH, PATCH, channels)
+    for pr in range(patch_rows):
+        left, right = [latent[i] for i, (r, _) in enumerate(here) if r == pr]
+        if 0 < pr < patch_rows - 1:
+            middle = inner_latent_ref[(pr - 1) * PATCH : pr * PATCH]
+        else:
+            middle = tall_latent_ref[:PATCH] if pr == 0 else tall_latent_ref[PATCH:]
+        whole = jnp.concatenate([left, middle.astype(jnp.float32), right], axis=1)
         latent_ref[pr * PATCH : (pr + 1) * PATCH] = whole.astype(jnp.bfloat16)
-    for pr in sorted(set(r for r, _ in ends)):
-        latent, used = patches([at for at in ends if at[0] == pr])
-        done += used
-        placed = latent.transpose(1, 0, 2, 3).reshape(PATCH, tile_cols, channels)
-        latent_ref[pr * PATCH : (pr + 1) * PATCH] = placed.astype(jnp.bfloat16)
 
 
 def reply_patches(capacity, plane, tiles, order, feat_width, id_ref, *refs):
@@ -512,17 +562,15 @@
         copy.wait()
 
 
-def with_halo(array, sides, width):
-    for axis, dim in sides:
-        size, length = (axis_count(axis), array.shape[dim])
-        up = [(i, (i + 1) % size) for i in range(size)]
-        down = [(j, i) for i, j in up]
-        last = lax.slice_in_dim(array, length - width, length, axis=dim)
-        initial = lax.slice_in_dim(array, 0, width, axis=dim)
-        before = lax.ppermute(last, axis, up)
-        after = lax.ppermute(initial, axis, down)
-        array = jnp.concatenate([before, array, after], axis=dim)
-    return array
+def with_halo(array, axis, dim, width):
+    size, length = (axis_count(axis), array.shape[dim])
+    up = [(i, (i + 1) % size) for i in range(size)]
+    down = [(j, i) for i, j in up]
+    last = lax.slice_in_dim(array, length - width, length, axis=dim)
+    initial = lax.slice_in_dim(array, 0, width, axis=dim)
+    before = lax.ppermute(last, axis, up)
+    after = lax.ppermute(initial, axis, down)
+    return jnp.concatenate([before, array, after], axis=dim)
 
 
 def axis_count(axes):
@@ -645,14 +693,14 @@
     )(own, *parts, embed_weight, grid_base)
 
     margin = WIN // 2
-    ext = with_halo(start, (("lat", 0), (("z", "x"), 1)), margin).astype(jnp.float32)
-    ext_rows, ext_cols, _ = ext.shape
+    ext_rows, ext_cols = tile_rows + 2 * margin, tile_cols + 2 * margin
+    tall = with_halo(start, "lat", 0, margin)
     group = 128
     gains = (norm_gain.reshape(1, channels), mlp_gain.reshape(1, channels))
     weights = (gains[0], qkv_weight, out_weight, gains[1], up_weight, down_weight, decode_weight.T)
     patch_rows, patch_cols = tile_rows // PATCH, tile_cols // PATCH
-    inner, sides, ends = patch_order(patch_rows, patch_cols)
-    order = [r * patch_cols + c for r, c in inner + sides + ends]
+    inner, ends, sides = patch_order(patch_rows, patch_cols)
+    order = [r * patch_cols + c for r, c in inner + ends + sides]
     inner_cells = (tile_rows - 2 * PATCH, tile_cols - 2 * PATCH, channels)
     inner_mixed = (tile_rows - WIN, tile_cols - WIN, channels)
 
@@ -685,20 +733,40 @@
         name="inner_block",
     )(start, *weights)
 
+    tall, proj_inner = lax.optimization_barrier((tall, proj_inner))
+    ext = with_halo(tall, ("z", "x"), 1, margin).astype(jnp.float32)
+
+    latent_tall, proj_tall, mixed_tall = pl.pallas_call(
+        lambda *refs: tall_block(tile_rows * lat, *refs),
+        out_shape=(
+            jax.ShapeDtypeStruct((2 * PATCH,) + inner_cells[1:], jnp.bfloat16),
+            jax.ShapeDtypeStruct((len(ends) // 2 * feat_width, LANES), jnp.bfloat16),
+            jax.ShapeDtypeStruct((2 * WIN,) + inner_mixed[1:], jnp.float32),
+        ),
+        in_specs=[vmem()] * 9,
+        out_specs=(vmem(), vmem(), vmem()),
+        scratch_shapes=[pltpu.VMEM(tall.shape, jnp.float32)] + scratch(tile_cols // WIN - 1),
+        compiler_params=params(16),
+        cost_estimate=pl.CostEstimate(flops=5 * 10**9, bytes_accessed=10**7, transcendentals=0),
+        name="tall_block",
+    )(tall, mixed_inner, *weights)
+
     latent, projected = pl.pallas_call(
         lambda *refs: outer_block(tile_rows * lat, *refs),
         out_shape=(
             jax.ShapeDtypeStruct(grid_base.shape, jnp.bfloat16),
             jax.ShapeDtypeStruct((patch_total // 2 * feat_width, LANES), jnp.bfloat16),
         ),
-        in_specs=[vmem()] * 11,
+        in_specs=[vmem()] * 14,
         out_specs=(vmem(), vmem()),
         scratch_shapes=[pltpu.VMEM((ext_rows, ext_cols, channels), jnp.float32)]
-        + scratch(max(ext_cols // WIN, 2 * (ext_rows // WIN - 2))),
+        + scratch(2 * (ext_rows // WIN)),
         compiler_params=params(20),
-        cost_estimate=pl.CostEstimate(flops=8 * 10**9, bytes_accessed=10**7, transcendentals=0),
+        cost_estimate=pl.CostEstimate(flops=5 * 10**9, bytes_accessed=10**7, transcendentals=0),
         name="outer_block",
-    )(ext, latent_inner, proj_inner, mixed_inner, *weights)
+    )(
+        ext, latent_inner, proj_inner, mixed_inner, latent_tall, proj_tall, mixed_tall, *weights
+    )
 
     def reply(ids, tiles, name):
         count = len(tiles)

time: 116 us -> 113 us (0.974)
  starting transfers between devices: 20.6 us -> 17.5 us
    pallas_call x0 -> x1, Pallas kernels: none -> 3.67 us  [local(): pl.pallas_call(lambda *refs: tall_block(tile_rows * lat, *refs), out_shap...]
    pallas_call x1, Pallas kernels: 7.26 us -> 3.87 us  [local(): pl.pallas_call(lambda *refs: outer_block(tile_rows * lat, *refs), out_sha...]
    ppermute x2, starting transfers between devices: 5.51 us -> 3.24 us  [with_halo(): after = lax.ppermute(initial, axis, down)]
    ppermute x2, waiting for transfers between devices: 2.3 us -> 3.51 us  [with_halo(): before = lax.ppermute(last, axis, up)]
  transfers between devices with their start and end apart: 11 -> 11, of which waited for: 4 -> 4; matrix products, arithmetic and copies ran while one was open for 1% -> 1% of each run, Pallas kernels for 6% -> 9%
where the time goes in v8:
time: 113 us; the launch traced here: 112 us
  blocking collectives  40.1 us (35%)
  Pallas kernels  25.6 us (23%)
  waiting for transfers between devices  25.4 us (22%)
  starting transfers between devices  17.5 us (15%)
  between operations  1.69 us (1%)
  local copies, waits for them, and re-layouts  1.15 us (1%)
    all_to_all x3, blocking collectives, swap_in_plane(): lax.all_to_all(parts, ('lat', 'x'), split_axis=0, concat_axis=0, tiled=True)  40.1 us
    all_to_all x1, waiting for transfers between devices, swap_in_plane(): lax.all_to_all(parts, ('lat', 'x'), split_axis=0, concat_axis=0, tiled=True)  16.2 us
    ppermute x6, starting transfers between devices, swap_planes(): return lax.ppermute(array, 'z', [(i, i ^ hop) for i in range(depth)])  8.84 us
    ppermute x6, waiting for transfers between devices, swap_planes(): return lax.ppermute(array, 'z', [(i, i ^ hop) for i in range(depth)])  5.67 us
    all_to_all x1, starting transfers between devices, swap_in_plane(): lax.all_to_all(parts, ('lat', 'x'), split_axis=0, concat_axis=0, tiled=True)  5.18 us
    pallas_call x1, Pallas kernels, local(): pl.pallas_call(lambda *refs: encode_blocks(capacity, (lat, depth, width),...  4.88 us
    pallas_call x1, Pallas kernels, local(): pl.pallas_call(inner_block, out_shape=(jax.ShapeDtypeStruct(inner_cells,...  4.59 us
    pallas_call x1, Pallas kernels, local(): pl.pallas_call(lambda *refs: outer_block(tile_rows * lat, *refs), out_sha...  3.87 us
  transfers between devices with their start and end apart: 11, of which 4 were waited for; matrix products, arithmetic and copies ran while one was open for 1% of the time, Pallas kernels for 9%

profile of v8, /device:TPU:0, one launch (start us, length us, event | category | flops | bytes accessed | tf_op | source)
XLA Modules:
  0.0 112.0 jit_solution(2966320847804017163)
XLA Ops:
  0.6 4.9 %encode_blocks.1 = (bf16[1664,128]{1,0:T(8,128)(2,1)S(1)}, bf16[4992,128]{1,0:T(8,128)(2,1)}, s32[96]{0:T(128)}) custom-call(s32[96]{0:T(128)} %bitcast.42, s32[96]{0:T(128)} %refs_1_.1, bf16[64,12288]{1,0:T(8,128)(2,1)} %refs_2_.2, bf16[2,12288]{1,0:T(2,128)(2,1)} %offset_ref.1), custom_call_target="tpu_custom_call" | custom-call | tf_op jit(solution)/shard_map/encode_blocks/pallas_call | solution.py:632
  5.5 5.2 %all-to-all-start.6 = ((bf16[8,624,128]{2,1,0:T(8,128)(2,1)}), bf16[8,624,128]{2,1,0:T(8,128)(2,1)S(1)}, u32[]{:S(2)}, u32[]{:S(2)}) async-start(bf16[8,624,128]{2,1,0:T(8,128)(2,1)} %bitcast.38), calls=%async_computation.6 | async-start | bytes 2555904 | tf_op jit(solution)/shard_map/all_to_all | solution.py:584
  10.7 0.5 slice.22
  11.9 16.2 %all-to-all-done.6 = bf16[8,624,128]{2,1,0:T(8,128)(2,1)S(1)} async-done(((bf16[8,624,128]{2,1,0:T(8,128)(2,1)}), bf16[8,624,128]{2,1,0:T(8,128)(2,1)S(1)}, u32[]{:S(2)}, u32[]{:S(2)}) %all-to-all-start.6) | async-done | bytes 1277984 | tf_op jit(solution)/shard_map/all_to_all | solution.py:584
  28.4 1.9 %gather_planes.1 = (bf16[800,128]{1,0:T(8,128)(2,1)S(1)}, bf16[800,128]{1,0:T(8,128)(2,1)S(1)}, bf16[800,128]{1,0:T(8,128)(2,1)S(1)}) custom-call(s32[144]{0:T(256)S(1)} %reshape.64.refs_0_, bf16[4992,128]{1,0:T(8,128)(2,1)S(1)} %bitcast.20), custom_call_target="tpu_custom_call" | custom-call | tf_op jit(solution)/shard_map/gather_planes/pallas_call | solution.py:662
  30.3 3.7 %collective-permute-start = (bf16[800,128]{1,0:T(8,128)(2,1)S(1)}, bf16[800,128]{1,0:T(8,128)(2,1)S(1)}, u32[]{:S(2)}, u32[]{:S(2)}) collective-permute-start(bf16[800,128]{1,0:T(8,128)(2,1)S(1)} %get-tuple-element.33), channel_id=1, source_target_pairs={{0,6},{2,4},{4,2},{6,0},{1,7},{3,5},{5,3},{7,1},{8,14},{10,12},{12... | collective-permute-start | bytes 614408 | tf_op jit(solution)/shard_map/ppermute | solution.py:601
  34.0 0.8 collective-permute-start.2
  34.8 10.8 %conditional.2 = (bf16[1664,128]{1,0:T(8,128)(2,1)S(1)}) conditional(s32[]{:T(128)} %bitcast.8, bf16[1664,128]{1,0:T(8,128)(2,1)S(1)} %get-tuple-element.34, bf16[1664,128]{1,0:T(8,128)(2,1)S(1)} %get-tuple-element.34), branch_computations={%region_0.1_spmd, %region_1.2_spmd} | conditional | bytes 3407880 | solution.py:596
  34.8 10.8 %all_to_all.36 = bf16[8,208,128]{2,1,0:T(8,128)(2,1)S(1)} all-to-all(bf16[8,208,128]{2,1,0:T(8,128)(2,1)S(1)} %bitcast.33), channel_id=1, replica_groups=mesh['lat'=4,'z'=4,'x'=2] {'lat','x'}, dimensions={0} | all-to-all | bytes 851968 | tf_op jit(solution)/shard_map/cond/branch_1_fun/all_to_all | solution.py:584
  45.8 1.1 %gather_own.1.refs_0_ = f32[12,72,128]{2,1,0:T(8,128)S(1)} custom-call(s32[48]{0:T(128)S(1)} %reshape.67.refs_0_, bf16[1664,128]{1,0:T(8,128)(2,1)S(1)} %get-tuple-element.50.refs_1_, bf16[256,768]{1,0:T(8,128)(2,1)S(1)} %copy-done.6, bf16[256,256]{1,0:T(8,128)(2,1)S(1)} %copy-done.7), custom_call_target="tpu_custom_call" | custom-call | flops 1000000000 | bytes 10000000 | tf_op jit(solution)/shard_map/gather_own/pallas_call | solution.py:675
  47.0 4.2 %collective-permute-done.1.refs_2_ = bf16[800,128]{1,0:T(8,128)(2,1)S(1)} collective-permute-done((bf16[800,128]{1,0:T(8,128)(2,1)S(1)}, bf16[800,128]{1,0:T(8,128)(2,1)S(1)}, u32[]{:S(2)}, u32[]{:S(2)}) %collective-permute-start.1) | collective-permute-done | bytes 204832 | tf_op jit(solution)/shard_map/ppermute | solution.py:601
  52.3 4.6 %inner_block.1 = (bf16[16,32,256]{2,1,0:T(8,128)(2,1)S(1)}, bf16[256,128]{1,0:T(8,128)(2,1)S(1)}, f32[24,40,256]{2,1,0:T(8,128)S(1)}) custom-call(bf16[32,48,256]{2,1,0:T(8,128)(2,1)S(1)} %start_tile.1.start_ref, f32[1,256]{1,0:T(1,128)S(1)} %bitcast.26, bf16[256,768]{1,0:T(8,128)(2,1)S(1)} %copy-done.6, bf16[256,256]{1,0:T(8,128)(2,1)S(1)} %copy-done.7, ...), custom_call_target="tpu_custom_call" | custom-call | flops 6000000000 | bytes 10000000 | tf_op jit(solution)/shard_map/inner_block/pallas_call | solution.py:720
  57.1 2.9 %collective-permute-start.6 = (bf16[40,4,256]{2,1,0:T(4,128)(2,1)S(1)}, bf16[40,4,256]{2,1,0:T(4,128)(2,1)S(1)}, u32[]{:S(2)}, u32[]{:S(2)}) collective-permute-start(bf16[40,4,256]{2,1,0:T(4,128)(2,1)S(1)} %get-tuple-element.47), channel_id=1, source_target_pairs={{1,0},{2,1},{3,2},{4,3},{5,4},{6,5},{7,6},{0,7},{9,8},{10,9},{11,1... | collective-permute-start | bytes 245768 | tf_op jit(solution)/shard_map/ppermute | solution.py:572
  60.1 3.7 %tall_block.1 = (bf16[16,32,256]{2,1,0:T(8,128)(2,1)S(1)}, bf16[256,128]{1,0:T(8,128)(2,1)S(1)}, f32[16,40,256]{2,1,0:T(8,128)S(1)}) custom-call(bf16[40,48,256]{2,1,0:T(8,128)(2,1)S(1)} %pad_maximum_fusion.refs_0_, f32[24,40,256]{2,1,0:T(8,128)S(1)} %get-tuple-element.39.refs_1_.refs_3_, f32[1,256]{1,0:T(1,128)S(1)} %bitcast.27, ...), custom_call_target="tpu_custom_call" | custom-call | flops 5000000000 | bytes 10000000 | tf_op jit(solution)/shard_map/tall_block/pallas_call | solution.py:739
  63.7 3.5 %collective-permute-done.5 = bf16[40,4,256]{2,1,0:T(4,128)(2,1)S(1)} collective-permute-done((bf16[40,4,256]{2,1,0:T(4,128)(2,1)S(1)}, bf16[40,4,256]{2,1,0:T(4,128)(2,1)S(1)}, u32[]{:S(2)}, u32[]{:S(2)}) %collective-permute-start.5) | collective-permute-done | bytes 81952 | tf_op jit(solution)/shard_map/ppermute | solution.py:571
  67.7 3.9 %outer_block.1 = (bf16[32,48,256]{2,1,0:T(8,128)(2,1)}, bf16[768,128]{1,0:T(8,128)(2,1)S(1)}) custom-call(f32[40,56,256]{2,1,0:T(8,128)S(1)} %maximum_convert_fusion.refs_0_, bf16[16,32,256]{2,1,0:T(8,128)(2,1)S(1)} %get-tuple-element.37.refs_1_, bf16[256,128]{1,0:T(8,128)(2,1)S(1)} %get-tuple-element.38.refs_2_, ...), custom_call_target="tpu_custom_call" | custom-call | flops 5000000000 | bytes 10000000 | tf_op jit(solution)/shard_map/outer_block/pallas_call | solution.py:754
  71.6 4.4 %collective-permute-start.9 = (bf16[768,128]{1,0:T(8,128)(2,1)S(1)}, bf16[768,128]{1,0:T(8,128)(2,1)S(1)}, u32[]{:S(2)}, u32[]{:S(2)}) collective-permute-start(bf16[768,128]{1,0:T(8,128)(2,1)S(1)} %get-tuple-element.45.refs_1_), channel_id=1, source_target_pairs={{0,6},{2,4},{4,2},{6,0},{1,7},{3,5},{5,3},{7,1},{8,14},{10,12},{12... | collective-permute-start | bytes 589832 | tf_op jit(solution)/shard_map/ppermute | solution.py:601
  76.0 0.7 reply_near.1
  76.7 10.4 %conditional.3 = (bf16[1536,128]{1,0:T(8,128)(2,1)S(1)}) conditional(s32[]{:T(128)} %bitcast.8, bf16[1536,128]{1,0:T(8,128)(2,1)S(1)} %reply_near.1, bf16[1536,128]{1,0:T(8,128)(2,1)S(1)} %reply_near.1), branch_computations={%region_2.3_spmd, %region_3.4_spmd} | conditional | bytes 3145736 | solution.py:596
  76.7 10.4 %all_to_all.39 = bf16[8,192,128]{2,1,0:T(8,128)(2,1)S(1)} all-to-all(bf16[8,192,128]{2,1,0:T(8,128)(2,1)S(1)} %bitcast.35), channel_id=1, replica_groups=mesh['lat'=4,'z'=4,'x'=2] {'lat','x'}, dimensions={0} | all-to-all | bytes 786432 | tf_op jit(solution)/shard_map/cond/branch_1_fun/all_to_all | solution.py:584
  87.1 1.4 %collective-permute-done.8.refs_2_ = bf16[768,128]{1,0:T(8,128)(2,1)S(1)} collective-permute-done((bf16[768,128]{1,0:T(8,128)(2,1)S(1)}, bf16[768,128]{1,0:T(8,128)(2,1)S(1)}, u32[]{:S(2)}, u32[]{:S(2)}) %collective-permute-start.8) | collective-permute-done | bytes 196640 | tf_op jit(solution)/shard_map/ppermute | solution.py:601
  88.6 1.0 reply_far.1
  89.6 18.9 %all_to_all.40 = bf16[8,576,128]{2,1,0:T(8,128)(2,1)S(1)} all-to-all(bf16[8,576,128]{2,1,0:T(8,128)(2,1)S(1)} %bitcast.22), channel_id=1, replica_groups=mesh['lat'=4,'z'=4,'x'=2] {'lat','x'}, dimensions={0} | all-to-all | bytes 2359296 | tf_op jit(solution)/shard_map/all_to_all | solution.py:584
  108.5 3.4 %decode_blocks.1 = bf16[64,12288]{1,0:T(8,128)(2,1)} custom-call(s32[96]{0:T(128)S(1)} %copy-done.3, bf16[2,12288]{1,0:T(2,128)(2,1)S(1)} %copy-done.1, bf16[1536,128]{1,0:T(8,128)(2,1)S(1)} %get-tuple-element.51.near_ref, bf16[4608,128]{1,0:T(8,128)(2,1)S(1)} %bitcast.21), custom_call_target="tpu_custom_call" | custom-call | tf_op jit(solution)/shard_map/decode_blocks/pallas_call | solution.py:791
  (46 shorter events, 2.3 us)
Async XLA Ops:
  5.5 5.2 %copy-start.9 = (f32[256]{0:T(256)S(1)}, f32[256]{0:T(256)}, u32[]{:S(2)}) copy-start(f32[256]{0:T(256)} %param.23) | copy-start | bytes 3076
  5.5 22.6 %all-to-all-start.6 = ((bf16[8,624,128]{2,1,0:T(8,128)(2,1)}), bf16[8,624,128]{2,1,0:T(8,128)(2,1)S(1)}, u32[]{:S(2)}, u32[]{:S(2)}) async-start(bf16[8,624,128]{2,1,0:T(8,128)(2,1)} %bitcast.38), calls=%async_computation.6 | async-start | bytes 2555904 | tf_op jit(solution)/shard_map/all_to_all | solution.py:584
  30.3 16.7 %collective-permute-start = (bf16[800,128]{1,0:T(8,128)(2,1)S(1)}, bf16[800,128]{1,0:T(8,128)(2,1)S(1)}, u32[]{:S(2)}, u32[]{:S(2)}) collective-permute-start(bf16[800,128]{1,0:T(8,128)(2,1)S(1)} %get-tuple-element.33), channel_id=1, source_target_pairs={{0,6},{2,4},{4,2},{6,0},{1,7},{3,5},{5,3},{7,1},{8,14},{10,12},{12... | collective-permute-start | bytes 614408 | tf_op jit(solution)/shard_map/ppermute | solution.py:601
  34.0 17.2 %collective-permute-start.1 = (bf16[800,128]{1,0:T(8,128)(2,1)S(1)}, bf16[800,128]{1,0:T(8,128)(2,1)S(1)}, u32[]{:S(2)}, u32[]{:S(2)}) collective-permute-start(bf16[800,128]{1,0:T(8,128)(2,1)S(1)} %get-tuple-element.32), channel_id=1, source_target_pairs={{0,4},{2,6},{4,0},{6,2},{1,5},{3,7},{5,1},{7,3},{8,12},{10,14},{12... | collective-permute-start | bytes 614408 | tf_op jit(solution)/shard_map/ppermute | solution.py:601
  34.0 17.2 %collective-permute-start.2 = (bf16[800,128]{1,0:T(8,128)(2,1)S(1)}, bf16[800,128]{1,0:T(8,128)(2,1)S(1)}, u32[]{:S(2)}, u32[]{:S(2)}) collective-permute-start(bf16[800,128]{1,0:T(8,128)(2,1)S(1)} %get-tuple-element.31), channel_id=1, source_target_pairs={{0,2},{2,0},{4,6},{6,4},{1,3},{3,1},{5,7},{7,5},{8,10},{10,8},{12,... | collective-permute-start | bytes 614408 | tf_op jit(solution)/shard_map/ppermute | solution.py:601
  34.8 11.0 %copy-start.6 = (bf16[256,768]{1,0:T(8,128)(2,1)S(1)}, bf16[256,768]{1,0:T(8,128)(2,1)}, u32[]{:S(2)}) copy-start(bf16[256,768]{1,0:T(8,128)(2,1)} %refs_8_.1) | copy-start | bytes 1179652
  34.8 11.0 %copy-start.7 = (bf16[256,256]{1,0:T(8,128)(2,1)S(1)}, bf16[256,256]{1,0:T(8,128)(2,1)}, u32[]{:S(2)}) copy-start(bf16[256,256]{1,0:T(8,128)(2,1)} %refs_9_.1) | copy-start | bytes 393220
  45.8 5.5 %copy-start = (bf16[32,48,256]{2,1,0:T(8,128)(2,1)S(1)}, bf16[32,48,256]{2,1,0:T(8,128)(2,1)}, u32[]{:S(2)}) copy-start(bf16[32,48,256]{2,1,0:T(8,128)(2,1)} %refs_5_.1) | copy-start | bytes 2359300
  45.8 5.4 %copy-start.2 = (bf16[64,256]{1,0:T(8,128)(2,1)S(1)}, bf16[64,256]{1,0:T(8,128)(2,1)}, u32[]{:S(2)}) copy-start(bf16[64,256]{1,0:T(8,128)(2,1)} %refs_4_.2) | copy-start | bytes 98308
  47.0 5.3 %copy-start.4 = (bf16[256,1024]{1,0:T(8,128)(2,1)S(1)}, bf16[256,1024]{1,0:T(8,128)(2,1)}, u32[]{:S(2)}) copy-start(bf16[256,1024]{1,0:T(8,128)(2,1)} %refs_11_.1) | copy-start | bytes 1572868
  47.0 5.3 %copy-start.5 = (bf16[1024,256]{1,0:T(8,128)(2,1)S(1)}, bf16[1024,256]{1,0:T(8,128)(2,1)}, u32[]{:S(2)}) copy-start(bf16[1024,256]{1,0:T(8,128)(2,1)} %refs_12_.1) | copy-start | bytes 1572868
  47.0 5.3 %copy-start.8 = (bf16[256,64]{0,1:T(8,128)(2,1)S(1)}, bf16[256,64]{0,1:T(8,128)(2,1)}, u32[]{:S(2)}) copy-start(bf16[256,64]{0,1:T(8,128)(2,1)} %param.29) | copy-start | bytes 98308
  47.0 5.3 %copy-start.10 = (f32[256]{0:T(256)S(1)}, f32[256]{0:T(256)}, u32[]{:S(2)}) copy-start(f32[256]{0:T(256)} %param.26) | copy-start | bytes 3076
  51.7 5.2 %collective-permute-start.4 = (bf16[4,48,256]{2,1,0:T(8,128)(2,1)S(1)}, bf16[4,48,256]{2,1,0:T(8,128)(2,1)S(1)}, u32[]{:S(2)}, u32[]{:S(2)}) collective-permute-start(bf16[4,48,256]{2,1,0:T(8,128)(2,1)S(1)} %get-tuple-element.49), channel_id=1, source_target_pairs={{8,0},{16,8},{24,16},{0,24},{9,1},{17,9},{25,17},{1,25},{10,2},{18... | collective-permute-start | bytes 294920 | tf_op jit(solution)/shard_map/ppermute | solution.py:572
  52.1 4.9 %collective-permute-start.3 = (bf16[4,48,256]{2,1,0:T(8,128)(2,1)S(1)}, bf16[4,48,256]{2,1,0:T(8,128)(2,1)S(1)}, u32[]{:S(2)}, u32[]{:S(2)}) collective-permute-start(bf16[4,48,256]{2,1,0:T(8,128)(2,1)S(1)} %get-tuple-element.48), channel_id=1, source_target_pairs={{0,8},{8,16},{16,24},{24,0},{1,9},{9,17},{17,25},{25,1},{2,10},{10... | collective-permute-start | bytes 294920 | tf_op jit(solution)/shard_map/ppermute | solution.py:571
  57.1 6.6 %collective-permute-start.6 = (bf16[40,4,256]{2,1,0:T(4,128)(2,1)S(1)}, bf16[40,4,256]{2,1,0:T(4,128)(2,1)S(1)}, u32[]{:S(2)}, u32[]{:S(2)}) collective-permute-start(bf16[40,4,256]{2,1,0:T(4,128)(2,1)S(1)} %get-tuple-element.47), channel_id=1, source_target_pairs={{1,0},{2,1},{3,2},{4,3},{5,4},{6,5},{7,6},{0,7},{9,8},{10,9},{11,1... | collective-permute-start | bytes 245768 | tf_op jit(solution)/shard_map/ppermute | solution.py:572
  60.1 7.2 %collective-permute-start.5 = (bf16[40,4,256]{2,1,0:T(4,128)(2,1)S(1)}, bf16[40,4,256]{2,1,0:T(4,128)(2,1)S(1)}, u32[]{:S(2)}, u32[]{:S(2)}) collective-permute-start(bf16[40,4,256]{2,1,0:T(4,128)(2,1)S(1)} %get-tuple-element.46), channel_id=1, source_target_pairs={{0,1},{1,2},{2,3},{3,4},{4,5},{5,6},{6,7},{7,0},{8,9},{9,10},{10,1... | collective-permute-start | bytes 245768 | tf_op jit(solution)/shard_map/ppermute | solution.py:571
  71.6 15.5 %collective-permute-start.7 = (bf16[768,128]{1,0:T(8,128)(2,1)S(1)}, bf16[768,128]{1,0:T(8,128)(2,1)S(1)}, u32[]{:S(2)}, u32[]{:S(2)}) collective-permute-start(bf16[768,128]{1,0:T(8,128)(2,1)S(1)} %get-tuple-element.45.refs_1_), channel_id=1, source_target_pairs={{0,2},{2,0},{4,6},{6,4},{1,3},{3,1},{5,7},{7,5},{8,10},{10,8},{12,... | collective-permute-start | bytes 589832 | tf_op jit(solution)/shard_map/ppermute | solution.py:601
  71.6 17.0 %collective-permute-start.8 = (bf16[768,128]{1,0:T(8,128)(2,1)S(1)}, bf16[768,128]{1,0:T(8,128)(2,1)S(1)}, u32[]{:S(2)}, u32[]{:S(2)}) collective-permute-start(bf16[768,128]{1,0:T(8,128)(2,1)S(1)} %get-tuple-element.45.refs_1_), channel_id=1, source_target_pairs={{0,4},{2,6},{4,0},{6,2},{1,5},{3,7},{5,1},{7,3},{8,12},{10,14},{12... | collective-permute-start | bytes 589832 | tf_op jit(solution)/shard_map/ppermute | solution.py:601
  71.6 17.0 %collective-permute-start.9 = (bf16[768,128]{1,0:T(8,128)(2,1)S(1)}, bf16[768,128]{1,0:T(8,128)(2,1)S(1)}, u32[]{:S(2)}, u32[]{:S(2)}) collective-permute-start(bf16[768,128]{1,0:T(8,128)(2,1)S(1)} %get-tuple-element.45.refs_1_), channel_id=1, source_target_pairs={{0,6},{2,4},{4,2},{6,0},{1,7},{3,5},{5,3},{7,1},{8,14},{10,12},{12... | collective-permute-start | bytes 589832 | tf_op jit(solution)/shard_map/ppermute | solution.py:601
  89.6 18.9 %copy-start.1 = (bf16[2,12288]{1,0:T(2,128)(2,1)S(1)}, bf16[2,12288]{1,0:T(2,128)(2,1)}, u32[]{:S(2)}) copy-start(bf16[2,12288]{1,0:T(2,128)(2,1)} %offset_ref.1) | copy-start | bytes 147460
  89.6 18.9 %copy-start.3 = (s32[96]{0:T(128)S(1)}, s32[96]{0:T(128)}, u32[]{:S(2)}) copy-start(s32[96]{0:T(128)} %get-tuple-element.44.slot_ref) | copy-start | bytes 1156

commit v9 on v8

--- a/solution.py
+++ b/solution.py
@@ -325,10 +325,15 @@
 def finish(begun, mixed, mlp_gain, up_ref, down_ref, decode_ref):
     residual = jnp.concatenate([a.reshape(CELLS, -1) + b.reshape(CELLS, -1) for a, b in zip(begun, mixed)])
     normed = normalize(residual, mlp_gain).astype(jnp.bfloat16)
-    hidden = jax.nn.gelu(jnp.dot(normed, up_ref[...], preferred_element_type=jnp.float32))
-    latent = residual + jnp.dot(
-        hidden.astype(jnp.bfloat16), down_ref[...], preferred_element_type=jnp.float32
-    )
+    latent = residual
+    units = up_ref.shape[1]
+    step = min(units, 256)
+    for at in range(0, units, step):
+        span = slice(at, at + step)
+        hidden = jax.nn.gelu(jnp.dot(normed, up_ref[:, span], preferred_element_type=jnp.float32))
+        latent = latent + jnp.dot(
+            hidden.astype(jnp.bfloat16), down_ref[span, :], preferred_element_type=jnp.float32
+        )
     rounded = latent.astype(jnp.bfloat16)
     turned = [
         lax.dot_general(
@@ -668,7 +673,7 @@
         compiler_params=params(14),
         name="gather_planes",
     )(far_ids, far)
-    parts = [swap_planes(sums[hop - 1], hop) for hop in range(hops, 0, -1)]
+    parts = [swap_planes(sums[hop - 1], hop) for hop in range(1, depth)]
     send_near, _ = lax.optimization_barrier((send_near, sums))
     near = swap_at_once(norm_gain, send_near)
     near_ids = ids_of(near, 1)
@@ -783,7 +788,7 @@
             name=name,
         )(ids, *tiles)
 
-    others = [swap_planes(projected, hop) for hop in range(hops, 0, -1)][::-1]
+    others = [swap_planes(projected, hop) for hop in range(1, depth)]
     near_reply = reply(near_ids, [projected], "reply_near")
     near_back = swap_at_once(norm_gain, near_reply)
     far_back = swap_in_plane(reply(far_ids, others, "reply_far"))

time: 113 us -> 112 us (level)
  no operation moved by 1% of the time
where the time goes in v9:
time: 112 us; the launch traced here: 111 us
  blocking collectives  40.6 us (36%)
  Pallas kernels  25.1 us (22%)
  waiting for transfers between devices  24.5 us (22%)
  starting transfers between devices  17.5 us (16%)
  between operations  1.7 us (2%)
  local copies, waits for them, and re-layouts  1.15 us (1%)
    all_to_all x3, blocking collectives, swap_in_plane(): lax.all_to_all(parts, ('lat', 'x'), split_axis=0, concat_axis=0, tiled=True)  40.6 us
    all_to_all x1, waiting for transfers between devices, swap_in_plane(): lax.all_to_all(parts, ('lat', 'x'), split_axis=0, concat_axis=0, tiled=True)  16.2 us
    ppermute x6, starting transfers between devices, swap_planes(): return lax.ppermute(array, 'z', [(i, i ^ hop) for i in range(depth)])  8.84 us
    all_to_all x1, starting transfers between devices, swap_in_plane(): lax.all_to_all(parts, ('lat', 'x'), split_axis=0, concat_axis=0, tiled=True)  5.18 us
    pallas_call x1, Pallas kernels, local(): pl.pallas_call(lambda *refs: encode_blocks(capacity, (lat, depth, width),...  4.87 us
    ppermute x6, waiting for transfers between devices, swap_planes(): return lax.ppermute(array, 'z', [(i, i ^ hop) for i in range(depth)])  4.55 us
    pallas_call x1, Pallas kernels, local(): pl.pallas_call(inner_block, out_shape=(jax.ShapeDtypeStruct(inner_cells,...  4.35 us
    pallas_call x1, Pallas kernels, local(): pl.pallas_call(lambda *refs: outer_block(tile_rows * lat, *refs), out_sha...  3.86 us
  transfers between devices with their start and end apart: 11, of which 4 were waited for; matrix products, arithmetic and copies ran while one was open for 1% of the time, Pallas kernels for 9%

profile of v9, /device:TPU:0, one launch (start us, length us, event | category | flops | bytes accessed | tf_op | source)
XLA Modules:
  0.0 111.2 jit_solution(18098111455162517239)
XLA Ops:
  0.6 4.9 %encode_blocks.1 = (bf16[1664,128]{1,0:T(8,128)(2,1)S(1)}, bf16[4992,128]{1,0:T(8,128)(2,1)}, s32[96]{0:T(128)}) custom-call(s32[96]{0:T(128)} %bitcast.42, s32[96]{0:T(128)} %refs_1_.1, bf16[64,12288]{1,0:T(8,128)(2,1)} %refs_2_.2, bf16[2,12288]{1,0:T(2,128)(2,1)} %offset_ref.1), custom_call_target="tpu_custom_call" | custom-call | tf_op jit(solution)/shard_map/encode_blocks/pallas_call | solution.py:637
  5.5 5.2 %all-to-all-start.6 = ((bf16[8,624,128]{2,1,0:T(8,128)(2,1)}), bf16[8,624,128]{2,1,0:T(8,128)(2,1)S(1)}, u32[]{:S(2)}, u32[]{:S(2)}) async-start(bf16[8,624,128]{2,1,0:T(8,128)(2,1)} %bitcast.38), calls=%async_computation.6 | async-start | bytes 2555904 | tf_op jit(solution)/shard_map/all_to_all | solution.py:589
  11.9 16.2 %all-to-all-done.6 = bf16[8,624,128]{2,1,0:T(8,128)(2,1)S(1)} async-done(((bf16[8,624,128]{2,1,0:T(8,128)(2,1)}), bf16[8,624,128]{2,1,0:T(8,128)(2,1)S(1)}, u32[]{:S(2)}, u32[]{:S(2)}) %all-to-all-start.6) | async-done | bytes 1277984 | tf_op jit(solution)/shard_map/all_to_all | solution.py:589
  28.4 1.9 %gather_planes.1 = (bf16[800,128]{1,0:T(8,128)(2,1)S(1)}, bf16[800,128]{1,0:T(8,128)(2,1)S(1)}, bf16[800,128]{1,0:T(8,128)(2,1)S(1)}) custom-call(s32[144]{0:T(256)S(1)} %reshape.64.refs_0_, bf16[4992,128]{1,0:T(8,128)(2,1)S(1)} %bitcast.20), custom_call_target="tpu_custom_call" | custom-call | tf_op jit(solution)/shard_map/gather_planes/pallas_call | solution.py:667
  30.3 1.6 %collective-permute-start = (bf16[800,128]{1,0:T(8,128)(2,1)S(1)}, bf16[800,128]{1,0:T(8,128)(2,1)S(1)}, u32[]{:S(2)}, u32[]{:S(2)}) collective-permute-start(bf16[800,128]{1,0:T(8,128)(2,1)S(1)} %get-tuple-element.31), channel_id=1, source_target_pairs={{0,2},{2,0},{4,6},{6,4},{1,3},{3,1},{5,7},{7,5},{8,10},{10,8},{12,... | collective-permute-start | bytes 614408 | tf_op jit(solution)/shard_map/ppermute | solution.py:606
  32.0 2.6 %collective-permute-start.1 = (bf16[800,128]{1,0:T(8,128)(2,1)S(1)}, bf16[800,128]{1,0:T(8,128)(2,1)S(1)}, u32[]{:S(2)}, u32[]{:S(2)}) collective-permute-start(bf16[800,128]{1,0:T(8,128)(2,1)S(1)} %get-tuple-element.32), channel_id=1, source_target_pairs={{0,4},{2,6},{4,0},{6,2},{1,5},{3,7},{5,1},{7,3},{8,12},{10,14},{12... | collective-permute-start | bytes 614408 | tf_op jit(solution)/shard_map/ppermute | solution.py:606
  34.8 10.8 %conditional.2 = (bf16[1664,128]{1,0:T(8,128)(2,1)S(1)}) conditional(s32[]{:T(128)} %bitcast.8, bf16[1664,128]{1,0:T(8,128)(2,1)S(1)} %get-tuple-element.34, bf16[1664,128]{1,0:T(8,128)(2,1)S(1)} %get-tuple-element.34), branch_computations={%region_0.1_spmd, %region_1.2_spmd} | conditional | bytes 3407880 | solution.py:601
  34.8 10.8 %all_to_all.36 = bf16[8,208,128]{2,1,0:T(8,128)(2,1)S(1)} all-to-all(bf16[8,208,128]{2,1,0:T(8,128)(2,1)S(1)} %bitcast.33), channel_id=1, replica_groups=mesh['lat'=4,'z'=4,'x'=2] {'lat','x'}, dimensions={0} | all-to-all | bytes 851968 | tf_op jit(solution)/shard_map/cond/branch_1_fun/all_to_all | solution.py:589
  45.8 1.1 %gather_own.1.refs_0_ = f32[12,72,128]{2,1,0:T(8,128)S(1)} custom-call(s32[48]{0:T(128)S(1)} %reshape.67.refs_0_, bf16[1664,128]{1,0:T(8,128)(2,1)S(1)} %get-tuple-element.50.refs_1_, bf16[256,768]{1,0:T(8,128)(2,1)S(1)} %copy-done.6, bf16[256,256]{1,0:T(8,128)(2,1)S(1)} %copy-done.7), custom_call_target="tpu_custom_call" | custom-call | flops 1000000000 | bytes 10000000 | tf_op jit(solution)/shard_map/gather_own/pallas_call | solution.py:680
  47.0 2.6 %collective-permute-done.1.refs_2_ = bf16[800,128]{1,0:T(8,128)(2,1)S(1)} collective-permute-done((bf16[800,128]{1,0:T(8,128)(2,1)S(1)}, bf16[800,128]{1,0:T(8,128)(2,1)S(1)}, u32[]{:S(2)}, u32[]{:S(2)}) %collective-permute-start.1) | collective-permute-done | bytes 204832 | tf_op jit(solution)/shard_map/ppermute | solution.py:606
  50.7 4.4 %inner_block.1 = (bf16[16,32,256]{2,1,0:T(8,128)(2,1)S(1)}, bf16[256,128]{1,0:T(8,128)(2,1)S(1)}, f32[24,40,256]{2,1,0:T(8,128)S(1)}) custom-call(bf16[32,48,256]{2,1,0:T(8,128)(2,1)S(1)} %start_tile.1.start_ref, f32[1,256]{1,0:T(1,128)S(1)} %bitcast.26, bf16[256,768]{1,0:T(8,128)(2,1)S(1)} %copy-done.6, bf16[256,256]{1,0:T(8,128)(2,1)S(1)} %copy-done.7, ...), custom_call_target="tpu_custom_call" | custom-call | flops 6000000000 | bytes 10000000 | tf_op jit(solution)/shard_map/inner_block/pallas_call | solution.py:725
  55.3 3.0 %collective-permute-start.6 = (bf16[40,4,256]{2,1,0:T(4,128)(2,1)S(1)}, bf16[40,4,256]{2,1,0:T(4,128)(2,1)S(1)}, u32[]{:S(2)}, u32[]{:S(2)}) collective-permute-start(bf16[40,4,256]{2,1,0:T(4,128)(2,1)S(1)} %get-tuple-element.47), channel_id=1, source_target_pairs={{1,0},{2,1},{3,2},{4,3},{5,4},{6,5},{7,6},{0,7},{9,8},{10,9},{11,1... | collective-permute-start | bytes 245768 | tf_op jit(solution)/shard_map/ppermute | solution.py:577
  58.3 3.4 %tall_block.1 = (bf16[16,32,256]{2,1,0:T(8,128)(2,1)S(1)}, bf16[256,128]{1,0:T(8,128)(2,1)S(1)}, f32[16,40,256]{2,1,0:T(8,128)S(1)}) custom-call(bf16[40,48,256]{2,1,0:T(8,128)(2,1)S(1)} %pad_maximum_fusion.refs_0_, f32[24,40,256]{2,1,0:T(8,128)S(1)} %get-tuple-element.39.refs_1_.refs_3_, f32[1,256]{1,0:T(1,128)S(1)} %bitcast.27, ...), custom_call_target="tpu_custom_call" | custom-call | flops 5000000000 | bytes 10000000 | tf_op jit(solution)/shard_map/tall_block/pallas_call | solution.py:744
  61.7 3.7 %collective-permute-done.5 = bf16[40,4,256]{2,1,0:T(4,128)(2,1)S(1)} collective-permute-done((bf16[40,4,256]{2,1,0:T(4,128)(2,1)S(1)}, bf16[40,4,256]{2,1,0:T(4,128)(2,1)S(1)}, u32[]{:S(2)}, u32[]{:S(2)}) %collective-permute-start.5) | collective-permute-done | bytes 81952 | tf_op jit(solution)/shard_map/ppermute | solution.py:576
  65.9 3.9 %outer_block.1 = (bf16[32,48,256]{2,1,0:T(8,128)(2,1)}, bf16[768,128]{1,0:T(8,128)(2,1)S(1)}) custom-call(f32[40,56,256]{2,1,0:T(8,128)S(1)} %maximum_convert_fusion.refs_0_, bf16[16,32,256]{2,1,0:T(8,128)(2,1)S(1)} %get-tuple-element.37.refs_1_, bf16[256,128]{1,0:T(8,128)(2,1)S(1)} %get-tuple-element.38.refs_2_, ...), custom_call_target="tpu_custom_call" | custom-call | flops 5000000000 | bytes 10000000 | tf_op jit(solution)/shard_map/outer_block/pallas_call | solution.py:759
  70.0 1.9 %collective-permute-start.8 = (bf16[768,128]{1,0:T(8,128)(2,1)S(1)}, bf16[768,128]{1,0:T(8,128)(2,1)S(1)}, u32[]{:S(2)}, u32[]{:S(2)}) collective-permute-start(bf16[768,128]{1,0:T(8,128)(2,1)S(1)} %get-tuple-element.45.refs_1_), channel_id=1, source_target_pairs={{0,4},{2,6},{4,0},{6,2},{1,5},{3,7},{5,1},{7,3},{8,12},{10,14},{12... | collective-permute-start | bytes 589832 | tf_op jit(solution)/shard_map/ppermute | solution.py:606
  71.9 2.2 %collective-permute-start.9 = (bf16[768,128]{1,0:T(8,128)(2,1)S(1)}, bf16[768,128]{1,0:T(8,128)(2,1)S(1)}, u32[]{:S(2)}, u32[]{:S(2)}) collective-permute-start(bf16[768,128]{1,0:T(8,128)(2,1)S(1)} %get-tuple-element.45.refs_1_), channel_id=1, source_target_pairs={{0,6},{2,4},{4,2},{6,0},{1,7},{3,5},{5,3},{7,1},{8,14},{10,12},{12... | collective-permute-start | bytes 589832 | tf_op jit(solution)/shard_map/ppermute | solution.py:606
  74.1 0.7 reply_near.1
  74.9 10.4 %conditional.3 = (bf16[1536,128]{1,0:T(8,128)(2,1)S(1)}) conditional(s32[]{:T(128)} %bitcast.8, bf16[1536,128]{1,0:T(8,128)(2,1)S(1)} %reply_near.1, bf16[1536,128]{1,0:T(8,128)(2,1)S(1)} %reply_near.1), branch_computations={%region_2.3_spmd, %region_3.4_spmd} | conditional | bytes 3145736 | solution.py:601
  74.9 10.4 %all_to_all.39 = bf16[8,192,128]{2,1,0:T(8,128)(2,1)S(1)} all-to-all(bf16[8,192,128]{2,1,0:T(8,128)(2,1)S(1)} %bitcast.35), channel_id=1, replica_groups=mesh['lat'=4,'z'=4,'x'=2] {'lat','x'}, dimensions={0} | all-to-all | bytes 786432 | tf_op jit(solution)/shard_map/cond/branch_1_fun/all_to_all | solution.py:589
  85.3 1.9 %collective-permute-done.8.refs_2_ = bf16[768,128]{1,0:T(8,128)(2,1)S(1)} collective-permute-done((bf16[768,128]{1,0:T(8,128)(2,1)S(1)}, bf16[768,128]{1,0:T(8,128)(2,1)S(1)}, u32[]{:S(2)}, u32[]{:S(2)}) %collective-permute-start.8) | collective-permute-done | bytes 196640 | tf_op jit(solution)/shard_map/ppermute | solution.py:606
  87.2 1.0 reply_far.1
  88.2 19.5 %all_to_all.40 = bf16[8,576,128]{2,1,0:T(8,128)(2,1)S(1)} all-to-all(bf16[8,576,128]{2,1,0:T(8,128)(2,1)S(1)} %bitcast.22), channel_id=1, replica_groups=mesh['lat'=4,'z'=4,'x'=2] {'lat','x'}, dimensions={0} | all-to-all | bytes 2359296 | tf_op jit(solution)/shard_map/all_to_all | solution.py:589
  107.7 3.4 %decode_blocks.1 = bf16[64,12288]{1,0:T(8,128)(2,1)} custom-call(s32[96]{0:T(128)S(1)} %copy-done.3, bf16[2,12288]{1,0:T(2,128)(2,1)S(1)} %copy-done.1, bf16[1536,128]{1,0:T(8,128)(2,1)S(1)} %get-tuple-element.51.near_ref, bf16[4608,128]{1,0:T(8,128)(2,1)S(1)} %bitcast.21), custom_call_target="tpu_custom_call" | custom-call | tf_op jit(solution)/shard_map/decode_blocks/pallas_call | solution.py:796
  (46 shorter events, 3.2 us)
Async XLA Ops:
  5.5 5.2 %copy-start.9 = (f32[256]{0:T(256)S(1)}, f32[256]{0:T(256)}, u32[]{:S(2)}) copy-start(f32[256]{0:T(256)} %param.23) | copy-start | bytes 3076
  5.5 22.6 %all-to-all-start.6 = ((bf16[8,624,128]{2,1,0:T(8,128)(2,1)}), bf16[8,624,128]{2,1,0:T(8,128)(2,1)S(1)}, u32[]{:S(2)}, u32[]{:S(2)}) async-start(bf16[8,624,128]{2,1,0:T(8,128)(2,1)} %bitcast.38), calls=%async_computation.6 | async-start | bytes 2555904 | tf_op jit(solution)/shard_map/all_to_all | solution.py:589
  30.3 16.7 %collective-permute-start = (bf16[800,128]{1,0:T(8,128)(2,1)S(1)}, bf16[800,128]{1,0:T(8,128)(2,1)S(1)}, u32[]{:S(2)}, u32[]{:S(2)}) collective-permute-start(bf16[800,128]{1,0:T(8,128)(2,1)S(1)} %get-tuple-element.31), channel_id=1, source_target_pairs={{0,2},{2,0},{4,6},{6,4},{1,3},{3,1},{5,7},{7,5},{8,10},{10,8},{12,... | collective-permute-start | bytes 614408 | tf_op jit(solution)/shard_map/ppermute | solution.py:606
  32.0 17.7 %collective-permute-start.1 = (bf16[800,128]{1,0:T(8,128)(2,1)S(1)}, bf16[800,128]{1,0:T(8,128)(2,1)S(1)}, u32[]{:S(2)}, u32[]{:S(2)}) collective-permute-start(bf16[800,128]{1,0:T(8,128)(2,1)S(1)} %get-tuple-element.32), channel_id=1, source_target_pairs={{0,4},{2,6},{4,0},{6,2},{1,5},{3,7},{5,1},{7,3},{8,12},{10,14},{12... | collective-permute-start | bytes 614408 | tf_op jit(solution)/shard_map/ppermute | solution.py:606
  34.6 15.1 %collective-permute-start.2 = (bf16[800,128]{1,0:T(8,128)(2,1)S(1)}, bf16[800,128]{1,0:T(8,128)(2,1)S(1)}, u32[]{:S(2)}, u32[]{:S(2)}) collective-permute-start(bf16[800,128]{1,0:T(8,128)(2,1)S(1)} %get-tuple-element.33), channel_id=1, source_target_pairs={{0,6},{2,4},{4,2},{6,0},{1,7},{3,5},{5,3},{7,1},{8,14},{10,12},{12... | collective-permute-start | bytes 614408 | tf_op jit(solution)/shard_map/ppermute | solution.py:606
  34.8 11.0 %copy-start.6 = (bf16[256,768]{1,0:T(8,128)(2,1)S(1)}, bf16[256,768]{1,0:T(8,128)(2,1)}, u32[]{:S(2)}) copy-start(bf16[256,768]{1,0:T(8,128)(2,1)} %refs_8_.1) | copy-start | bytes 1179652
  34.8 11.0 %copy-start.7 = (bf16[256,256]{1,0:T(8,128)(2,1)S(1)}, bf16[256,256]{1,0:T(8,128)(2,1)}, u32[]{:S(2)}) copy-start(bf16[256,256]{1,0:T(8,128)(2,1)} %refs_9_.1) | copy-start | bytes 393220
  45.8 3.9 %copy-start = (bf16[32,48,256]{2,1,0:T(8,128)(2,1)S(1)}, bf16[32,48,256]{2,1,0:T(8,128)(2,1)}, u32[]{:S(2)}) copy-start(bf16[32,48,256]{2,1,0:T(8,128)(2,1)} %refs_5_.1) | copy-start | bytes 2359300
  45.8 3.9 %copy-start.2 = (bf16[64,256]{1,0:T(8,128)(2,1)S(1)}, bf16[64,256]{1,0:T(8,128)(2,1)}, u32[]{:S(2)}) copy-start(bf16[64,256]{1,0:T(8,128)(2,1)} %refs_4_.2) | copy-start | bytes 98308
  47.0 3.7 %copy-start.4 = (bf16[256,1024]{1,0:T(8,128)(2,1)S(1)}, bf16[256,1024]{1,0:T(8,128)(2,1)}, u32[]{:S(2)}) copy-start(bf16[256,1024]{1,0:T(8,128)(2,1)} %refs_11_.1) | copy-start | bytes 1572868
  47.0 3.7 %copy-start.5 = (bf16[1024,256]{1,0:T(8,128)(2,1)S(1)}, bf16[1024,256]{1,0:T(8,128)(2,1)}, u32[]{:S(2)}) copy-start(bf16[1024,256]{1,0:T(8,128)(2,1)} %refs_12_.1) | copy-start | bytes 1572868
  47.0 3.7 %copy-start.8 = (bf16[256,64]{0,1:T(8,128)(2,1)S(1)}, bf16[256,64]{0,1:T(8,128)(2,1)}, u32[]{:S(2)}) copy-start(bf16[256,64]{0,1:T(8,128)(2,1)} %param.29) | copy-start | bytes 98308
  47.0 3.7 %copy-start.10 = (f32[256]{0:T(256)S(1)}, f32[256]{0:T(256)}, u32[]{:S(2)}) copy-start(f32[256]{0:T(256)} %param.26) | copy-start | bytes 3076
  50.1 4.9 %collective-permute-start.4 = (bf16[4,48,256]{2,1,0:T(8,128)(2,1)S(1)}, bf16[4,48,256]{2,1,0:T(8,128)(2,1)S(1)}, u32[]{:S(2)}, u32[]{:S(2)}) collective-permute-start(bf16[4,48,256]{2,1,0:T(8,128)(2,1)S(1)} %get-tuple-element.49), channel_id=1, source_target_pairs={{8,0},{16,8},{24,16},{0,24},{9,1},{17,9},{25,17},{1,25},{10,2},{18... | collective-permute-start | bytes 294920 | tf_op jit(solution)/shard_map/ppermute | solution.py:577
  50.2 4.9 %collective-permute-start.3 = (bf16[4,48,256]{2,1,0:T(8,128)(2,1)S(1)}, bf16[4,48,256]{2,1,0:T(8,128)(2,1)S(1)}, u32[]{:S(2)}, u32[]{:S(2)}) collective-permute-start(bf16[4,48,256]{2,1,0:T(8,128)(2,1)S(1)} %get-tuple-element.48), channel_id=1, source_target_pairs={{0,8},{8,16},{16,24},{24,0},{1,9},{9,17},{17,25},{25,1},{2,10},{10... | collective-permute-start | bytes 294920 | tf_op jit(solution)/shard_map/ppermute | solution.py:576
  55.3 6.4 %collective-permute-start.6 = (bf16[40,4,256]{2,1,0:T(4,128)(2,1)S(1)}, bf16[40,4,256]{2,1,0:T(4,128)(2,1)S(1)}, u32[]{:S(2)}, u32[]{:S(2)}) collective-permute-start(bf16[40,4,256]{2,1,0:T(4,128)(2,1)S(1)} %get-tuple-element.47), channel_id=1, source_target_pairs={{1,0},{2,1},{3,2},{4,3},{5,4},{6,5},{7,6},{0,7},{9,8},{10,9},{11,1... | collective-permute-start | bytes 245768 | tf_op jit(solution)/shard_map/ppermute | solution.py:577
  58.3 7.1 %collective-permute-start.5 = (bf16[40,4,256]{2,1,0:T(4,128)(2,1)S(1)}, bf16[40,4,256]{2,1,0:T(4,128)(2,1)S(1)}, u32[]{:S(2)}, u32[]{:S(2)}) collective-permute-start(bf16[40,4,256]{2,1,0:T(4,128)(2,1)S(1)} %get-tuple-element.46), channel_id=1, source_target_pairs={{0,1},{1,2},{2,3},{3,4},{4,5},{5,6},{6,7},{7,0},{8,9},{9,10},{10,1... | collective-permute-start | bytes 245768 | tf_op jit(solution)/shard_map/ppermute | solution.py:576
  69.7 15.5 %collective-permute-start.7 = (bf16[768,128]{1,0:T(8,128)(2,1)S(1)}, bf16[768,128]{1,0:T(8,128)(2,1)S(1)}, u32[]{:S(2)}, u32[]{:S(2)}) collective-permute-start(bf16[768,128]{1,0:T(8,128)(2,1)S(1)} %get-tuple-element.45.refs_1_), channel_id=1, source_target_pairs={{0,2},{2,0},{4,6},{6,4},{1,3},{3,1},{5,7},{7,5},{8,10},{10,8},{12,... | collective-permute-start | bytes 589832 | tf_op jit(solution)/shard_map/ppermute | solution.py:606
  70.0 17.2 %collective-permute-start.8 = (bf16[768,128]{1,0:T(8,128)(2,1)S(1)}, bf16[768,128]{1,0:T(8,128)(2,1)S(1)}, u32[]{:S(2)}, u32[]{:S(2)}) collective-permute-start(bf16[768,128]{1,0:T(8,128)(2,1)S(1)} %get-tuple-element.45.refs_1_), channel_id=1, source_target_pairs={{0,4},{2,6},{4,0},{6,2},{1,5},{3,7},{5,1},{7,3},{8,12},{10,14},{12... | collective-permute-start | bytes 589832 | tf_op jit(solution)/shard_map/ppermute | solution.py:606
  71.9 15.3 %collective-permute-start.9 = (bf16[768,128]{1,0:T(8,128)(2,1)S(1)}, bf16[768,128]{1,0:T(8,128)(2,1)S(1)}, u32[]{:S(2)}, u32[]{:S(2)}) collective-permute-start(bf16[768,128]{1,0:T(8,128)(2,1)S(1)} %get-tuple-element.45.refs_1_), channel_id=1, source_target_pairs={{0,6},{2,4},{4,2},{6,0},{1,7},{3,5},{5,3},{7,1},{8,14},{10,12},{12... | collective-permute-start | bytes 589832 | tf_op jit(solution)/shard_map/ppermute | solution.py:606
  88.2 19.5 %copy-start.1 = (bf16[2,12288]{1,0:T(2,128)(2,1)S(1)}, bf16[2,12288]{1,0:T(2,128)(2,1)}, u32[]{:S(2)}) copy-start(bf16[2,12288]{1,0:T(2,128)(2,1)} %offset_ref.1) | copy-start | bytes 147460
  88.2 19.5 %copy-start.3 = (s32[96]{0:T(128)S(1)}, s32[96]{0:T(128)}, u32[]{:S(2)}) copy-start(s32[96]{0:T(128)} %get-tuple-element.44.slot_ref) | copy-start | bytes 1156

commit v10 on v9

--- a/solution.py
+++ b/solution.py
@@ -350,9 +350,7 @@
 def patch_order(patch_rows, patch_cols):
     every = [(r, c) for r in range(patch_rows) for c in range(patch_cols)]
     middle = [(r, c) for r, c in every if 0 < c < patch_cols - 1]
-    first = [(r, c) for r, c in middle if 0 < r < patch_rows - 1]
-    ends = [at for at in middle if at not in first]
-    return first, ends, [at for at in every if at not in middle]
+    return middle, [at for at in every if at not in middle]
 
 
 def edge_side(top, row, lat_cells):
@@ -362,12 +360,11 @@
 
 
 def inner_block(
-    start_ref, norm_ref, qkv_ref, out_ref, mlp_ref, up_ref, down_ref, decode_ref, latent_ref,
-    proj_ref, mixed_ref, cells_ref, turned_ref, key_ref, pack_ref, att_ref, score_ref, prob_ref,
+    start_ref, norm_ref, qkv_ref, out_ref, mixed_ref, cells_ref, turned_ref, key_ref, pack_ref,
+    att_ref, score_ref, prob_ref,
 ):
-    tile_rows, tile_cols, channels = cells_ref.shape
+    tile_rows, tile_cols, _ = cells_ref.shape
     margin = WIN // 2
-    feat_width = decode_ref.shape[0]
     cells_ref[...] = start_ref[...].astype(jnp.float32)
     turn_weights(qkv_ref, turned_ref)
     for row in range(0, tile_rows - WIN, WIN):
@@ -378,30 +375,6 @@
         )
         for col, block in zip(cols, mixed):
             mixed_ref[row : row + WIN, col : col + WIN, :] = block
-    first, _, _ = patch_order(tile_rows // PATCH, tile_cols // PATCH)
-    done = 0
-    for pr in sorted(set(r for r, _ in first)):
-        here = [c for r, c in first if r == pr]
-        row = pr * PATCH
-        latent, turned = finish(
-            [cells_ref[row : row + PATCH, c * PATCH : (c + 1) * PATCH, :] for c in here],
-            [
-                mixed_ref[
-                    row - margin : row - margin + PATCH,
-                    c * PATCH - margin : c * PATCH - margin + PATCH,
-                    :,
-                ]
-                for c in here
-            ],
-            mlp_ref[...], up_ref, down_ref, decode_ref,
-        )
-        placed = latent.reshape(len(here), PATCH, PATCH, channels).transpose(1, 0, 2, 3)
-        latent_ref[row - PATCH : row] = placed.reshape(PATCH, len(here) * PATCH, channels).astype(
-            jnp.bfloat16
-        )
-        for pair in turned:
-            proj_ref[done : done + feat_width, :] = pair
-            done += feat_width
 
 
 def tall_block(
@@ -416,8 +389,7 @@
     last = rows - WIN
     top = lax.axis_index("lat") * tile_rows - margin
     turn_weights(qkv_ref, turned_ref)
-    for part in (slice(0, 2 * WIN), slice(rows - 2 * WIN, rows)):
-        cells_ref[part] = tall_ref[part].astype(jnp.float32)
+    cells_ref[...] = tall_ref[...].astype(jnp.float32)
     cols = range(0, tile_cols - WIN, WIN)
     for i, row in enumerate((0, last)):
         mixed = attend(
@@ -429,22 +401,25 @@
             mixed_ref[i * WIN : (i + 1) * WIN, col : col + WIN, :] = block
     here = range(1, tile_cols // PATCH - 1)
     done = 0
-    for i, row in enumerate((margin, last - margin)):
+    for pr in range(tile_rows // PATCH):
+        row = pr * PATCH + margin
         begun, mixed = [], []
         for c in here:
             span = slice(c * PATCH - margin, (c + 1) * PATCH - margin)
             begun.append(cells_ref[row : row + PATCH, c * PATCH : (c + 1) * PATCH, :])
-            if i == 0:
+            if pr == 0:
                 halves = [mixed_ref[margin:WIN, span, :], inner_mixed_ref[:margin, span, :]]
-            else:
+            elif row == last - margin:
                 halves = [
                     inner_mixed_ref[tile_rows - WIN - margin :, span, :],
                     mixed_ref[WIN : WIN + margin, span, :],
                 ]
+            else:
+                halves = [inner_mixed_ref[row - WIN : row - WIN + PATCH, span, :]]
             mixed.append(jnp.concatenate(halves, axis=0))
         latent, turned = finish(begun, mixed, mlp_ref[...], up_ref, down_ref, decode_ref)
         placed = latent.reshape(len(here), PATCH, PATCH, channels).transpose(1, 0, 2, 3)
-        latent_ref[i * PATCH : (i + 1) * PATCH] = placed.reshape(
+        latent_ref[pr * PATCH : (pr + 1) * PATCH] = placed.reshape(
             PATCH, len(here) * PATCH, channels
         ).astype(jnp.bfloat16)
         for pair in turned:
@@ -453,8 +428,7 @@
 
 
 def outer_block(
-    lat_cells, ext_ref, inner_latent_ref, inner_proj_ref, inner_mixed_ref, tall_latent_ref,
-    tall_proj_ref, tall_mixed_ref, norm_ref, qkv_ref, out_ref, mlp_ref, up_ref, down_ref,
+    lat_cells, ext_ref, inner_mixed_ref, tall_latent_ref, tall_proj_ref, tall_mixed_ref, norm_ref, qkv_ref, out_ref, mlp_ref, up_ref, down_ref,
     decode_ref, latent_ref, proj_ref, mixed_ref, turned_ref, key_ref, pack_ref, att_ref,
     score_ref, prob_ref,
 ):
@@ -479,12 +453,10 @@
     )
     for (row, col), block in zip(windows, mixed):
         mixed_ref[row : row + WIN, col : col + WIN, :] = block
-    done = inner_proj_ref.shape[0]
-    proj_ref[:done, :] = inner_proj_ref[...]
-    proj_ref[done : done + tall_proj_ref.shape[0], :] = tall_proj_ref[...]
-    done += tall_proj_ref.shape[0]
+    done = tall_proj_ref.shape[0]
+    proj_ref[:done, :] = tall_proj_ref[...]
     patch_rows = tile_rows // PATCH
-    _, _, here = patch_order(patch_rows, tile_cols // PATCH)
+    _, here = patch_order(patch_rows, tile_cols // PATCH)
     at = [
         (
             slice(r * PATCH + margin, (r + 1) * PATCH + margin),
@@ -503,10 +475,7 @@
     latent = latent.reshape(len(here), PATCH, PATCH, channels)
     for pr in range(patch_rows):
         left, right = [latent[i] for i, (r, _) in enumerate(here) if r == pr]
-        if 0 < pr < patch_rows - 1:
-            middle = inner_latent_ref[(pr - 1) * PATCH : pr * PATCH]
-        else:
-            middle = tall_latent_ref[:PATCH] if pr == 0 else tall_latent_ref[PATCH:]
+        middle = tall_latent_ref[pr * PATCH : (pr + 1) * PATCH]
         whole = jnp.concatenate([left, middle.astype(jnp.float32), right], axis=1)
         latent_ref[pr * PATCH : (pr + 1) * PATCH] = whole.astype(jnp.bfloat16)
 
@@ -704,9 +673,8 @@
     gains = (norm_gain.reshape(1, channels), mlp_gain.reshape(1, channels))
     weights = (gains[0], qkv_weight, out_weight, gains[1], up_weight, down_weight, decode_weight.T)
     patch_rows, patch_cols = tile_rows // PATCH, tile_cols // PATCH
-    inner, ends, sides = patch_order(patch_rows, patch_cols)
-    order = [r * patch_cols + c for r, c in inner + ends + sides]
-    inner_cells = (tile_rows - 2 * PATCH, tile_cols - 2 * PATCH, channels)
+    middle, sides = patch_order(patch_rows, patch_cols)
+    order = [r * patch_cols + c for r, c in middle + sides]
     inner_mixed = (tile_rows - WIN, tile_cols - WIN, channels)
 
     def scratch(windows):
@@ -722,30 +690,25 @@
             pltpu.VMEM((parts, LANES, lanes), jnp.bfloat16),
         ]
 
-    latent_inner, proj_inner, mixed_inner = pl.pallas_call(
+    mixed_inner = pl.pallas_call(
         inner_block,
-        out_shape=(
-            jax.ShapeDtypeStruct(inner_cells, jnp.bfloat16),
-            jax.ShapeDtypeStruct((len(inner) // 2 * feat_width, LANES), jnp.bfloat16),
-            jax.ShapeDtypeStruct(inner_mixed, jnp.float32),
-        ),
-        in_specs=[vmem()] * 8,
-        out_specs=(vmem(), vmem(), vmem()),
+        out_shape=jax.ShapeDtypeStruct(inner_mixed, jnp.float32),
+        in_specs=[vmem()] * 4,
+        out_specs=vmem(),
         scratch_shapes=[pltpu.VMEM(grid_base.shape, jnp.float32)]
         + scratch(tile_cols // WIN - 1),
         compiler_params=params(16),
-        cost_estimate=pl.CostEstimate(flops=6 * 10**9, bytes_accessed=10**7, transcendentals=0),
+        cost_estimate=pl.CostEstimate(flops=5 * 10**9, bytes_accessed=10**7, transcendentals=0),
         name="inner_block",
-    )(start, *weights)
-
-    tall, proj_inner = lax.optimization_barrier((tall, proj_inner))
+    )(start, *weights[:3])
+    tall, mixed_inner = lax.optimization_barrier((tall, mixed_inner))
     ext = with_halo(tall, ("z", "x"), 1, margin).astype(jnp.float32)
 
     latent_tall, proj_tall, mixed_tall = pl.pallas_call(
         lambda *refs: tall_block(tile_rows * lat, *refs),
         out_shape=(
-            jax.ShapeDtypeStruct((2 * PATCH,) + inner_cells[1:], jnp.bfloat16),
-            jax.ShapeDtypeStruct((len(ends) // 2 * feat_width, LANES), jnp.bfloat16),
+            jax.ShapeDtypeStruct((tile_rows, tile_cols - 2 * PATCH, channels), jnp.bfloat16),
+            jax.ShapeDtypeStruct((len(middle) // 2 * feat_width, LANES), jnp.bfloat16),
             jax.ShapeDtypeStruct((2 * WIN,) + inner_mixed[1:], jnp.float32),
         ),
         in_specs=[vmem()] * 9,
@@ -762,7 +725,7 @@
             jax.ShapeDtypeStruct(grid_base.shape, jnp.bfloat16),
             jax.ShapeDtypeStruct((patch_total // 2 * feat_width, LANES), jnp.bfloat16),
         ),
-        in_specs=[vmem()] * 14,
+        in_specs=[vmem()] * 12,
         out_specs=(vmem(), vmem()),
         scratch_shapes=[pltpu.VMEM((ext_rows, ext_cols, channels), jnp.float32)]
         + scratch(2 * (ext_rows // WIN)),
@@ -770,7 +733,7 @@
         cost_estimate=pl.CostEstimate(flops=5 * 10**9, bytes_accessed=10**7, transcendentals=0),
         name="outer_block",
     )(
-        ext, latent_inner, proj_inner, mixed_inner, latent_tall, proj_tall, mixed_tall, *weights
+        ext, mixed_inner, latent_tall, proj_tall, mixed_tall, *weights
     )
 
     def reply(ids, tiles, name):

time: 112 us -> 112 us (level)
    pallas_call x1, Pallas kernels: 3.38 us -> 4.72 us  [local(): pl.pallas_call(lambda *refs: tall_block(tile_rows * lat, *refs), out_shap...]
  transfers between devices with their start and end apart: 11 -> 11, of which waited for: 4 -> 5; matrix products, arithmetic and copies ran while one was open for 1% -> 1% of each run, Pallas kernels for 9% -> 9%
where the time goes in v10:
time: 112 us; the launch traced here: 111 us
  blocking collectives  40.9 us (37%)
  Pallas kernels  25.4 us (23%)
  waiting for transfers between devices  23.8 us (21%)
  starting transfers between devices  17.6 us (16%)
  between operations  1.7 us (2%)
  local copies, waits for them, and re-layouts  1.15 us (1%)
    all_to_all x3, blocking collectives, swap_in_plane(): lax.all_to_all(parts, ('lat', 'x'), split_axis=0, concat_axis=0, tiled=True)  40.9 us
    all_to_all x1, waiting for transfers between devices, swap_in_plane(): lax.all_to_all(parts, ('lat', 'x'), split_axis=0, concat_axis=0, tiled=True)  16.2 us
    ppermute x6, starting transfers between devices, swap_planes(): return lax.ppermute(array, 'z', [(i, i ^ hop) for i in range(depth)])  8.84 us
    all_to_all x1, starting transfers between devices, swap_in_plane(): lax.all_to_all(parts, ('lat', 'x'), split_axis=0, concat_axis=0, tiled=True)  5.18 us
    ppermute x6, waiting for transfers between devices, swap_planes(): return lax.ppermute(array, 'z', [(i, i ^ hop) for i in range(depth)])  4.93 us
    pallas_call x1, Pallas kernels, local(): pl.pallas_call(lambda *refs: encode_blocks(capacity, (lat, depth, width),...  4.87 us
    pallas_call x1, Pallas kernels, local(): pl.pallas_call(lambda *refs: tall_block(tile_rows * lat, *refs), out_shap...  4.72 us
    pallas_call x1, Pallas kernels, local(): pl.pallas_call(lambda *refs: outer_block(tile_rows * lat, *refs), out_sha...  3.86 us
  transfers between devices with their start and end apart: 11, of which 5 were waited for; matrix products, arithmetic and copies ran while one was open for 1% of the time, Pallas kernels for 9%

profile of v10, /device:TPU:0, one launch (start us, length us, event | category | flops | bytes accessed | tf_op | source)
XLA Modules:
  0.0 111.1 jit_solution(11844495237818006285)
XLA Ops:
  0.6 4.9 %encode_blocks.1 = (bf16[1664,128]{1,0:T(8,128)(2,1)S(1)}, bf16[4992,128]{1,0:T(8,128)(2,1)}, s32[96]{0:T(128)}) custom-call(s32[96]{0:T(128)} %bitcast.40, s32[96]{0:T(128)} %refs_1_.1, bf16[64,12288]{1,0:T(8,128)(2,1)} %refs_2_.2, bf16[2,12288]{1,0:T(2,128)(2,1)} %offset_ref.1), custom_call_target="tpu_custom_call" | custom-call | tf_op jit(solution)/shard_map/encode_blocks/pallas_call | solution.py:606
  5.5 5.2 %all-to-all-start.6 = ((bf16[8,624,128]{2,1,0:T(8,128)(2,1)}), bf16[8,624,128]{2,1,0:T(8,128)(2,1)S(1)}, u32[]{:S(2)}, u32[]{:S(2)}) async-start(bf16[8,624,128]{2,1,0:T(8,128)(2,1)} %bitcast.36), calls=%async_computation.6 | async-start | bytes 2555904 | tf_op jit(solution)/shard_map/all_to_all | solution.py:558
  11.9 16.2 %all-to-all-done.6 = bf16[8,624,128]{2,1,0:T(8,128)(2,1)S(1)} async-done(((bf16[8,624,128]{2,1,0:T(8,128)(2,1)}), bf16[8,624,128]{2,1,0:T(8,128)(2,1)S(1)}, u32[]{:S(2)}, u32[]{:S(2)}) %all-to-all-start.6) | async-done | bytes 1277984 | tf_op jit(solution)/shard_map/all_to_all | solution.py:558
  28.4 1.9 %gather_planes.1 = (bf16[800,128]{1,0:T(8,128)(2,1)S(1)}, bf16[800,128]{1,0:T(8,128)(2,1)S(1)}, bf16[800,128]{1,0:T(8,128)(2,1)S(1)}) custom-call(s32[144]{0:T(256)S(1)} %reshape.64.refs_0_, bf16[4992,128]{1,0:T(8,128)(2,1)S(1)} %bitcast.20), custom_call_target="tpu_custom_call" | custom-call | tf_op jit(solution)/shard_map/gather_planes/pallas_call | solution.py:636
  30.3 1.6 %collective-permute-start = (bf16[800,128]{1,0:T(8,128)(2,1)S(1)}, bf16[800,128]{1,0:T(8,128)(2,1)S(1)}, u32[]{:S(2)}, u32[]{:S(2)}) collective-permute-start(bf16[800,128]{1,0:T(8,128)(2,1)S(1)} %get-tuple-element.28), channel_id=1, source_target_pairs={{0,2},{2,0},{4,6},{6,4},{1,3},{3,1},{5,7},{7,5},{8,10},{10,8},{12,... | collective-permute-start | bytes 614408 | tf_op jit(solution)/shard_map/ppermute | solution.py:575
  32.0 2.6 %collective-permute-start.1 = (bf16[800,128]{1,0:T(8,128)(2,1)S(1)}, bf16[800,128]{1,0:T(8,128)(2,1)S(1)}, u32[]{:S(2)}, u32[]{:S(2)}) collective-permute-start(bf16[800,128]{1,0:T(8,128)(2,1)S(1)} %get-tuple-element.29), channel_id=1, source_target_pairs={{0,4},{2,6},{4,0},{6,2},{1,5},{3,7},{5,1},{7,3},{8,12},{10,14},{12... | collective-permute-start | bytes 614408 | tf_op jit(solution)/shard_map/ppermute | solution.py:575
  34.8 10.8 %conditional.2 = (bf16[1664,128]{1,0:T(8,128)(2,1)S(1)}) conditional(s32[]{:T(128)} %bitcast.8, bf16[1664,128]{1,0:T(8,128)(2,1)S(1)} %get-tuple-element.31, bf16[1664,128]{1,0:T(8,128)(2,1)S(1)} %get-tuple-element.31), branch_computations={%region_0.1_spmd, %region_1.2_spmd} | conditional | bytes 3407880 | solution.py:570
  34.8 10.8 %all_to_all.36 = bf16[8,208,128]{2,1,0:T(8,128)(2,1)S(1)} all-to-all(bf16[8,208,128]{2,1,0:T(8,128)(2,1)S(1)} %bitcast.31), channel_id=1, replica_groups=mesh['lat'=4,'z'=4,'x'=2] {'lat','x'}, dimensions={0} | all-to-all | bytes 851968 | tf_op jit(solution)/shard_map/cond/branch_1_fun/all_to_all | solution.py:558
  45.8 1.1 %gather_own.1.refs_0_ = f32[12,72,128]{2,1,0:T(8,128)S(1)} custom-call(s32[48]{0:T(128)S(1)} %reshape.67.refs_0_, bf16[1664,128]{1,0:T(8,128)(2,1)S(1)} %get-tuple-element.44.refs_1_, bf16[256,768]{1,0:T(8,128)(2,1)S(1)} %copy-done.6, bf16[256,256]{1,0:T(8,128)(2,1)S(1)} %copy-done.7), custom_call_target="tpu_custom_call" | custom-call | flops 1000000000 | bytes 10000000 | tf_op jit(solution)/shard_map/gather_own/pallas_call | solution.py:649
  47.0 2.7 %collective-permute-done.1.refs_2_ = bf16[800,128]{1,0:T(8,128)(2,1)S(1)} collective-permute-done((bf16[800,128]{1,0:T(8,128)(2,1)S(1)}, bf16[800,128]{1,0:T(8,128)(2,1)S(1)}, u32[]{:S(2)}, u32[]{:S(2)}) %collective-permute-start.1) | collective-permute-done | bytes 204832 | tf_op jit(solution)/shard_map/ppermute | solution.py:575
  50.7 3.3 %inner_block.1.refs_1_ = f32[24,40,256]{2,1,0:T(8,128)S(1)} custom-call(bf16[32,48,256]{2,1,0:T(8,128)(2,1)S(1)} %start_tile.1.start_ref, f32[1,256]{1,0:T(1,128)S(1)} %bitcast.25, bf16[256,768]{1,0:T(8,128)(2,1)S(1)} %copy-done.6, bf16[256,256]{1,0:T(8,128)(2,1)S(1)} %copy-done.7), custom_call_target="tpu_custom_call" | custom-call | flops 5000000000 | bytes 10000000 | tf_op jit(solution)/shard_map/inner_block/pallas_call | solution.py:693
  54.6 3.0 %collective-permute-start.6 = (bf16[40,4,256]{2,1,0:T(4,128)(2,1)S(1)}, bf16[40,4,256]{2,1,0:T(4,128)(2,1)S(1)}, u32[]{:S(2)}, u32[]{:S(2)}) collective-permute-start(bf16[40,4,256]{2,1,0:T(4,128)(2,1)S(1)} %get-tuple-element.41), channel_id=1, source_target_pairs={{1,0},{2,1},{3,2},{4,3},{5,4},{6,5},{7,6},{0,7},{9,8},{10,9},{11,1... | collective-permute-start | bytes 245768 | tf_op jit(solution)/shard_map/ppermute | solution.py:546
  57.6 4.7 %tall_block.1 = (bf16[32,32,256]{2,1,0:T(8,128)(2,1)S(1)}, bf16[512,128]{1,0:T(8,128)(2,1)S(1)}, f32[16,40,256]{2,1,0:T(8,128)S(1)}) custom-call(bf16[40,48,256]{2,1,0:T(8,128)(2,1)S(1)} %pad_maximum_fusion.refs_0_, f32[24,40,256]{2,1,0:T(8,128)S(1)} %inner_block.1.refs_1_, f32[1,256]{1,0:T(1,128)S(1)} %bitcast.26, bf16[256,768]{1,0:T(8,128)(2,1)S(1)} %copy-done.6, ...), custom_call_target="tpu_custom_call" | custom-call | flops 5000000000 | bytes 10000000 | tf_op jit(solution)/shard_map/tall_block/pallas_call | solution.py:707
  62.3 2.4 %collective-permute-done.5 = bf16[40,4,256]{2,1,0:T(4,128)(2,1)S(1)} collective-permute-done((bf16[40,4,256]{2,1,0:T(4,128)(2,1)S(1)}, bf16[40,4,256]{2,1,0:T(4,128)(2,1)S(1)}, u32[]{:S(2)}, u32[]{:S(2)}) %collective-permute-start.5) | collective-permute-done | bytes 81952 | tf_op jit(solution)/shard_map/ppermute | solution.py:545
  65.2 3.9 %outer_block.1 = (bf16[32,48,256]{2,1,0:T(8,128)(2,1)}, bf16[768,128]{1,0:T(8,128)(2,1)S(1)}) custom-call(f32[40,56,256]{2,1,0:T(8,128)S(1)} %maximum_convert_fusion.refs_0_, f32[24,40,256]{2,1,0:T(8,128)S(1)} %inner_block.1.refs_1_, bf16[32,32,256]{2,1,0:T(8,128)(2,1)S(1)} %get-tuple-element.34.refs_2_, bf16[512,128]{1,0:T(8,128)(2,1)S(1)} %get-tuple-element.35.refs_3_, ...), custom_call_target="tpu_custom_call" | custom-call | flops 5000000000 | bytes 10000000 | tf_op jit(solution)/shard_map/outer_block/pallas_call | solution.py:722
  69.8 1.5 %collective-permute-start.8 = (bf16[768,128]{1,0:T(8,128)(2,1)S(1)}, bf16[768,128]{1,0:T(8,128)(2,1)S(1)}, u32[]{:S(2)}, u32[]{:S(2)}) collective-permute-start(bf16[768,128]{1,0:T(8,128)(2,1)S(1)} %get-tuple-element.39.refs_1_), channel_id=1, source_target_pairs={{0,4},{2,6},{4,0},{6,2},{1,5},{3,7},{5,1},{7,3},{8,12},{10,14},{12... | collective-permute-start | bytes 589832 | tf_op jit(solution)/shard_map/ppermute | solution.py:575
  71.3 2.1 %collective-permute-start.9 = (bf16[768,128]{1,0:T(8,128)(2,1)S(1)}, bf16[768,128]{1,0:T(8,128)(2,1)S(1)}, u32[]{:S(2)}, u32[]{:S(2)}) collective-permute-start(bf16[768,128]{1,0:T(8,128)(2,1)S(1)} %get-tuple-element.39.refs_1_), channel_id=1, source_target_pairs={{0,6},{2,4},{4,2},{6,0},{1,7},{3,5},{5,3},{7,1},{8,14},{10,12},{12... | collective-permute-start | bytes 589832 | tf_op jit(solution)/shard_map/ppermute | solution.py:575
  73.4 0.7 reply_near.1
  74.2 10.5 %conditional.3 = (bf16[1536,128]{1,0:T(8,128)(2,1)S(1)}) conditional(s32[]{:T(128)} %bitcast.8, bf16[1536,128]{1,0:T(8,128)(2,1)S(1)} %reply_near.1, bf16[1536,128]{1,0:T(8,128)(2,1)S(1)} %reply_near.1), branch_computations={%region_2.3_spmd, %region_3.4_spmd} | conditional | bytes 3145736 | solution.py:570
  74.2 10.5 %all_to_all.39 = bf16[8,192,128]{2,1,0:T(8,128)(2,1)S(1)} all-to-all(bf16[8,192,128]{2,1,0:T(8,128)(2,1)S(1)} %bitcast.33), channel_id=1, replica_groups=mesh['lat'=4,'z'=4,'x'=2] {'lat','x'}, dimensions={0} | all-to-all | bytes 786432 | tf_op jit(solution)/shard_map/cond/branch_1_fun/all_to_all | solution.py:558
  84.7 2.2 %collective-permute-done.8.refs_2_ = bf16[768,128]{1,0:T(8,128)(2,1)S(1)} collective-permute-done((bf16[768,128]{1,0:T(8,128)(2,1)S(1)}, bf16[768,128]{1,0:T(8,128)(2,1)S(1)}, u32[]{:S(2)}, u32[]{:S(2)}) %collective-permute-start.8) | collective-permute-done | bytes 196640 | tf_op jit(solution)/shard_map/ppermute | solution.py:575
  86.9 1.0 reply_far.1
  88.0 19.6 %all_to_all.40 = bf16[8,576,128]{2,1,0:T(8,128)(2,1)S(1)} all-to-all(bf16[8,576,128]{2,1,0:T(8,128)(2,1)S(1)} %bitcast.22), channel_id=1, replica_groups=mesh['lat'=4,'z'=4,'x'=2] {'lat','x'}, dimensions={0} | all-to-all | bytes 2359296 | tf_op jit(solution)/shard_map/all_to_all | solution.py:558
  107.6 3.4 %decode_blocks.1 = bf16[64,12288]{1,0:T(8,128)(2,1)} custom-call(s32[96]{0:T(128)S(1)} %copy-done.3, bf16[2,12288]{1,0:T(2,128)(2,1)S(1)} %copy-done.1, bf16[1536,128]{1,0:T(8,128)(2,1)S(1)} %get-tuple-element.45.near_ref, bf16[4608,128]{1,0:T(8,128)(2,1)S(1)} %bitcast.21), custom_call_target="tpu_custom_call" | custom-call | tf_op jit(solution)/shard_map/decode_blocks/pallas_call | solution.py:759
  (46 shorter events, 4.0 us)
Async XLA Ops:
  5.5 5.2 %copy-start.9 = (f32[256]{0:T(256)S(1)}, f32[256]{0:T(256)}, u32[]{:S(2)}) copy-start(f32[256]{0:T(256)} %param.23) | copy-start | bytes 3076
  5.5 22.6 %all-to-all-start.6 = ((bf16[8,624,128]{2,1,0:T(8,128)(2,1)}), bf16[8,624,128]{2,1,0:T(8,128)(2,1)S(1)}, u32[]{:S(2)}, u32[]{:S(2)}) async-start(bf16[8,624,128]{2,1,0:T(8,128)(2,1)} %bitcast.36), calls=%async_computation.6 | async-start | bytes 2555904 | tf_op jit(solution)/shard_map/all_to_all | solution.py:558
  30.3 16.6 %collective-permute-start = (bf16[800,128]{1,0:T(8,128)(2,1)S(1)}, bf16[800,128]{1,0:T(8,128)(2,1)S(1)}, u32[]{:S(2)}, u32[]{:S(2)}) collective-permute-start(bf16[800,128]{1,0:T(8,128)(2,1)S(1)} %get-tuple-element.28), channel_id=1, source_target_pairs={{0,2},{2,0},{4,6},{6,4},{1,3},{3,1},{5,7},{7,5},{8,10},{10,8},{12,... | collective-permute-start | bytes 614408 | tf_op jit(solution)/shard_map/ppermute | solution.py:575
  32.0 17.7 %collective-permute-start.1 = (bf16[800,128]{1,0:T(8,128)(2,1)S(1)}, bf16[800,128]{1,0:T(8,128)(2,1)S(1)}, u32[]{:S(2)}, u32[]{:S(2)}) collective-permute-start(bf16[800,128]{1,0:T(8,128)(2,1)S(1)} %get-tuple-element.29), channel_id=1, source_target_pairs={{0,4},{2,6},{4,0},{6,2},{1,5},{3,7},{5,1},{7,3},{8,12},{10,14},{12... | collective-permute-start | bytes 614408 | tf_op jit(solution)/shard_map/ppermute | solution.py:575
  34.6 15.1 %collective-permute-start.2 = (bf16[800,128]{1,0:T(8,128)(2,1)S(1)}, bf16[800,128]{1,0:T(8,128)(2,1)S(1)}, u32[]{:S(2)}, u32[]{:S(2)}) collective-permute-start(bf16[800,128]{1,0:T(8,128)(2,1)S(1)} %get-tuple-element.30), channel_id=1, source_target_pairs={{0,6},{2,4},{4,2},{6,0},{1,7},{3,5},{5,3},{7,1},{8,14},{10,12},{12... | collective-permute-start | bytes 614408 | tf_op jit(solution)/shard_map/ppermute | solution.py:575
  34.8 11.0 %copy-start.6 = (bf16[256,768]{1,0:T(8,128)(2,1)S(1)}, bf16[256,768]{1,0:T(8,128)(2,1)}, u32[]{:S(2)}) copy-start(bf16[256,768]{1,0:T(8,128)(2,1)} %refs_6_.3) | copy-start | bytes 1179652
  34.8 11.0 %copy-start.7 = (bf16[256,256]{1,0:T(8,128)(2,1)S(1)}, bf16[256,256]{1,0:T(8,128)(2,1)}, u32[]{:S(2)}) copy-start(bf16[256,256]{1,0:T(8,128)(2,1)} %refs_7_.3) | copy-start | bytes 393220
  45.8 3.9 %copy-start = (bf16[32,48,256]{2,1,0:T(8,128)(2,1)S(1)}, bf16[32,48,256]{2,1,0:T(8,128)(2,1)}, u32[]{:S(2)}) copy-start(bf16[32,48,256]{2,1,0:T(8,128)(2,1)} %refs_5_.1) | copy-start | bytes 2359300
  45.8 3.9 %copy-start.2 = (bf16[64,256]{1,0:T(8,128)(2,1)S(1)}, bf16[64,256]{1,0:T(8,128)(2,1)}, u32[]{:S(2)}) copy-start(bf16[64,256]{1,0:T(8,128)(2,1)} %refs_4_.2) | copy-start | bytes 98308
  50.2 3.9 %collective-permute-start.4 = (bf16[4,48,256]{2,1,0:T(8,128)(2,1)S(1)}, bf16[4,48,256]{2,1,0:T(8,128)(2,1)S(1)}, u32[]{:S(2)}, u32[]{:S(2)}) collective-permute-start(bf16[4,48,256]{2,1,0:T(8,128)(2,1)S(1)} %get-tuple-element.43), channel_id=1, source_target_pairs={{8,0},{16,8},{24,16},{0,24},{9,1},{17,9},{25,17},{1,25},{10,2},{18... | collective-permute-start | bytes 294920 | tf_op jit(solution)/shard_map/ppermute | solution.py:546
  50.2 4.2 %collective-permute-start.3 = (bf16[4,48,256]{2,1,0:T(8,128)(2,1)S(1)}, bf16[4,48,256]{2,1,0:T(8,128)(2,1)S(1)}, u32[]{:S(2)}, u32[]{:S(2)}) collective-permute-start(bf16[4,48,256]{2,1,0:T(8,128)(2,1)S(1)} %get-tuple-element.42), channel_id=1, source_target_pairs={{0,8},{8,16},{16,24},{24,0},{1,9},{9,17},{17,25},{25,1},{2,10},{10... | collective-permute-start | bytes 294920 | tf_op jit(solution)/shard_map/ppermute | solution.py:545
  54.0 3.5 %copy-start.4 = (bf16[256,1024]{1,0:T(8,128)(2,1)S(1)}, bf16[256,1024]{1,0:T(8,128)(2,1)}, u32[]{:S(2)}) copy-start(bf16[256,1024]{1,0:T(8,128)(2,1)} %refs_9_.1) | copy-start | bytes 1572868
  54.0 3.5 %copy-start.5 = (bf16[1024,256]{1,0:T(8,128)(2,1)S(1)}, bf16[1024,256]{1,0:T(8,128)(2,1)}, u32[]{:S(2)}) copy-start(bf16[1024,256]{1,0:T(8,128)(2,1)} %refs_10_.1) | copy-start | bytes 1572868
  54.1 3.5 %copy-start.8 = (bf16[256,64]{0,1:T(8,128)(2,1)S(1)}, bf16[256,64]{0,1:T(8,128)(2,1)}, u32[]{:S(2)}) copy-start(bf16[256,64]{0,1:T(8,128)(2,1)} %param.29) | copy-start | bytes 98308
  54.1 3.5 %copy-start.10 = (f32[256]{0:T(256)S(1)}, f32[256]{0:T(256)}, u32[]{:S(2)}) copy-start(f32[256]{0:T(256)} %param.26) | copy-start | bytes 3076
  54.6 7.7 %collective-permute-start.6 = (bf16[40,4,256]{2,1,0:T(4,128)(2,1)S(1)}, bf16[40,4,256]{2,1,0:T(4,128)(2,1)S(1)}, u32[]{:S(2)}, u32[]{:S(2)}) collective-permute-start(bf16[40,4,256]{2,1,0:T(4,128)(2,1)S(1)} %get-tuple-element.41), channel_id=1, source_target_pairs={{1,0},{2,1},{3,2},{4,3},{5,4},{6,5},{7,6},{0,7},{9,8},{10,9},{11,1... | collective-permute-start | bytes 245768 | tf_op jit(solution)/shard_map/ppermute | solution.py:546
  57.6 7.1 %collective-permute-start.5 = (bf16[40,4,256]{2,1,0:T(4,128)(2,1)S(1)}, bf16[40,4,256]{2,1,0:T(4,128)(2,1)S(1)}, u32[]{:S(2)}, u32[]{:S(2)}) collective-permute-start(bf16[40,4,256]{2,1,0:T(4,128)(2,1)S(1)} %get-tuple-element.40), channel_id=1, source_target_pairs={{0,1},{1,2},{2,3},{3,4},{4,5},{5,6},{6,7},{7,0},{8,9},{9,10},{10,1... | collective-permute-start | bytes 245768 | tf_op jit(solution)/shard_map/ppermute | solution.py:545
  69.0 15.7 %collective-permute-start.7 = (bf16[768,128]{1,0:T(8,128)(2,1)S(1)}, bf16[768,128]{1,0:T(8,128)(2,1)S(1)}, u32[]{:S(2)}, u32[]{:S(2)}) collective-permute-start(bf16[768,128]{1,0:T(8,128)(2,1)S(1)} %get-tuple-element.39.refs_1_), channel_id=1, source_target_pairs={{0,2},{2,0},{4,6},{6,4},{1,3},{3,1},{5,7},{7,5},{8,10},{10,8},{12,... | collective-permute-start | bytes 589832 | tf_op jit(solution)/shard_map/ppermute | solution.py:575
  69.8 17.2 %collective-permute-start.8 = (bf16[768,128]{1,0:T(8,128)(2,1)S(1)}, bf16[768,128]{1,0:T(8,128)(2,1)S(1)}, u32[]{:S(2)}, u32[]{:S(2)}) collective-permute-start(bf16[768,128]{1,0:T(8,128)(2,1)S(1)} %get-tuple-element.39.refs_1_), channel_id=1, source_target_pairs={{0,4},{2,6},{4,0},{6,2},{1,5},{3,7},{5,1},{7,3},{8,12},{10,14},{12... | collective-permute-start | bytes 589832 | tf_op jit(solution)/shard_map/ppermute | solution.py:575
  71.3 15.6 %collective-permute-start.9 = (bf16[768,128]{1,0:T(8,128)(2,1)S(1)}, bf16[768,128]{1,0:T(8,128)(2,1)S(1)}, u32[]{:S(2)}, u32[]{:S(2)}) collective-permute-start(bf16[768,128]{1,0:T(8,128)(2,1)S(1)} %get-tuple-element.39.refs_1_), channel_id=1, source_target_pairs={{0,6},{2,4},{4,2},{6,0},{1,7},{3,5},{5,3},{7,1},{8,14},{10,12},{12... | collective-permute-start | bytes 589832 | tf_op jit(solution)/shard_map/ppermute | solution.py:575
  88.0 19.6 %copy-start.1 = (bf16[2,12288]{1,0:T(2,128)(2,1)S(1)}, bf16[2,12288]{1,0:T(2,128)(2,1)}, u32[]{:S(2)}) copy-start(bf16[2,12288]{1,0:T(2,128)(2,1)} %offset_ref.1) | copy-start | bytes 147460
  88.0 19.6 %copy-start.3 = (s32[96]{0:T(128)S(1)}, s32[96]{0:T(128)}, u32[]{:S(2)}) copy-start(s32[96]{0:T(128)} %get-tuple-element.38.slot_ref) | copy-start | bytes 1156

commit v11 on v10

--- a/solution.py
+++ b/solution.py
@@ -139,7 +139,7 @@
 
 
 def dense_rows(pairs, feat_width):
-    return pairs * feat_width + -(-2 * pairs // 16) * 16
+    return pairs * feat_width + -(-pairs // 16) * 16
 
 
 def add_chunk(capacity, feat_width, id_ref, slot, recv_ref, base, low_ref, high_ref):
@@ -184,9 +184,8 @@
             )
             masses.append(pair[feat_width : feat_width + 1])
         masses = jnp.concatenate(masses, axis=0)
-        high = masses.astype(jnp.bfloat16).astype(jnp.float32)
-        spare = outs[hop].shape[0] - patch_pairs * (feat_width + 2)
-        rows = [high, masses - high] + ([jnp.zeros((spare, LANES), jnp.float32)] if spare else [])
+        spare = outs[hop].shape[0] - patch_pairs * (feat_width + 1)
+        rows = [masses] + ([jnp.zeros((spare, LANES), jnp.float32)] if spare else [])
         outs[hop][patch_pairs * feat_width :, :] = jnp.concatenate(rows, axis=0).astype(jnp.bfloat16)
 
 
@@ -220,7 +219,7 @@
             sums, mass = pair[:feat_width], pair[feat_width : feat_width + 1]
             for part, rows in zip(parts, mass_rows):
                 sums = sums + part[j * feat_width : (j + 1) * feat_width, :].astype(jnp.float32)
-                mass = mass + (rows[j : j + 1] + rows[patch_pairs + j : patch_pairs + j + 1])
+                mass = mass + rows[j : j + 1]
             encoded = (sums * (1.0 / (1.0 + mass))).astype(jnp.bfloat16)
             lifted.append(lax.dot_general(encoded, embed, TN, preferred_element_type=jnp.float32))
         lifted = jnp.concatenate(lifted, axis=0).reshape(patch_cols, PATCH, PATCH, channels)

time: 112 us -> 111 us (level)
  no operation moved by 1% of the time
where the time goes in v11:
time: 111 us
  blocking collectives  40.9 us (37%)
  Pallas kernels  25.4 us (23%)
  waiting for transfers between devices  23.5 us (21%)
  starting transfers between devices  17.6 us (16%)
  between operations  1.7 us (2%)
  local copies, waits for them, and re-layouts  1.15 us (1%)
    all_to_all x3, blocking collectives, swap_in_plane(): lax.all_to_all(parts, ('lat', 'x'), split_axis=0, concat_axis=0, tiled=True)  40.9 us
    all_to_all x1, waiting for transfers between devices, swap_in_plane(): lax.all_to_all(parts, ('lat', 'x'), split_axis=0, concat_axis=0, tiled=True)  16.2 us
    ppermute x6, starting transfers between devices, swap_planes(): return lax.ppermute(array, 'z', [(i, i ^ hop) for i in range(depth)])  8.84 us
    all_to_all x1, starting transfers between devices, swap_in_plane(): lax.all_to_all(parts, ('lat', 'x'), split_axis=0, concat_axis=0, tiled=True)  5.18 us
    pallas_call x1, Pallas kernels, local(): pl.pallas_call(lambda *refs: encode_blocks(capacity, (lat, depth, width),...  4.87 us
    pallas_call x1, Pallas kernels, local(): pl.pallas_call(lambda *refs: tall_block(tile_rows * lat, *refs), out_shap...  4.71 us
    ppermute x6, waiting for transfers between devices, swap_planes(): return lax.ppermute(array, 'z', [(i, i ^ hop) for i in range(depth)])  4.59 us
    pallas_call x1, Pallas kernels, local(): pl.pallas_call(lambda *refs: outer_block(tile_rows * lat, *refs), out_sha...  3.88 us
  transfers between devices with their start and end apart: 11, of which 5 were waited for; matrix products, arithmetic and copies ran while one was open for 1% of the time, Pallas kernels for 9%

profile of v11, /device:TPU:0, one launch (start us, length us, event | category | flops | bytes accessed | tf_op | source)
XLA Modules:
  0.0 110.8 jit_solution(16786926311353271071)
XLA Ops:
  0.6 4.9 %encode_blocks.1 = (bf16[1664,128]{1,0:T(8,128)(2,1)S(1)}, bf16[4992,128]{1,0:T(8,128)(2,1)}, s32[96]{0:T(128)}) custom-call(s32[96]{0:T(128)} %bitcast.40, s32[96]{0:T(128)} %refs_1_.1, bf16[64,12288]{1,0:T(8,128)(2,1)} %refs_2_.2, bf16[2,12288]{1,0:T(2,128)(2,1)} %offset_ref.1), custom_call_target="tpu_custom_call" | custom-call | tf_op jit(solution)/shard_map/encode_blocks/pallas_call | solution.py:605
  5.5 5.2 %all-to-all-start.6 = ((bf16[8,624,128]{2,1,0:T(8,128)(2,1)}), bf16[8,624,128]{2,1,0:T(8,128)(2,1)S(1)}, u32[]{:S(2)}, u32[]{:S(2)}) async-start(bf16[8,624,128]{2,1,0:T(8,128)(2,1)} %bitcast.36), calls=%async_computation.6 | async-start | bytes 2555904 | tf_op jit(solution)/shard_map/all_to_all | solution.py:557
  11.9 16.2 %all-to-all-done.6 = bf16[8,624,128]{2,1,0:T(8,128)(2,1)S(1)} async-done(((bf16[8,624,128]{2,1,0:T(8,128)(2,1)}), bf16[8,624,128]{2,1,0:T(8,128)(2,1)S(1)}, u32[]{:S(2)}, u32[]{:S(2)}) %all-to-all-start.6) | async-done | bytes 1277984 | tf_op jit(solution)/shard_map/all_to_all | solution.py:557
  28.4 1.9 %gather_planes.1 = (bf16[784,128]{1,0:T(8,128)(2,1)S(1)}, bf16[784,128]{1,0:T(8,128)(2,1)S(1)}, bf16[784,128]{1,0:T(8,128)(2,1)S(1)}) custom-call(s32[144]{0:T(256)S(1)} %reshape.64.refs_0_, bf16[4992,128]{1,0:T(8,128)(2,1)S(1)} %bitcast.20), custom_call_target="tpu_custom_call" | custom-call | tf_op jit(solution)/shard_map/gather_planes/pallas_call | solution.py:635
  30.3 1.6 %collective-permute-start = (bf16[784,128]{1,0:T(8,128)(2,1)S(1)}, bf16[784,128]{1,0:T(8,128)(2,1)S(1)}, u32[]{:S(2)}, u32[]{:S(2)}) collective-permute-start(bf16[784,128]{1,0:T(8,128)(2,1)S(1)} %get-tuple-element.28), channel_id=1, source_target_pairs={{0,2},{2,0},{4,6},{6,4},{1,3},{3,1},{5,7},{7,5},{8,10},{10,8},{12,... | collective-permute-start | bytes 602120 | tf_op jit(solution)/shard_map/ppermute | solution.py:574
  32.0 2.6 %collective-permute-start.1 = (bf16[784,128]{1,0:T(8,128)(2,1)S(1)}, bf16[784,128]{1,0:T(8,128)(2,1)S(1)}, u32[]{:S(2)}, u32[]{:S(2)}) collective-permute-start(bf16[784,128]{1,0:T(8,128)(2,1)S(1)} %get-tuple-element.29), channel_id=1, source_target_pairs={{0,4},{2,6},{4,0},{6,2},{1,5},{3,7},{5,1},{7,3},{8,12},{10,14},{12... | collective-permute-start | bytes 602120 | tf_op jit(solution)/shard_map/ppermute | solution.py:574
  34.8 10.8 %conditional.2 = (bf16[1664,128]{1,0:T(8,128)(2,1)S(1)}) conditional(s32[]{:T(128)} %bitcast.8, bf16[1664,128]{1,0:T(8,128)(2,1)S(1)} %get-tuple-element.31, bf16[1664,128]{1,0:T(8,128)(2,1)S(1)} %get-tuple-element.31), branch_computations={%region_0.1_spmd, %region_1.2_spmd} | conditional | bytes 3407880 | solution.py:569
  34.8 10.8 %all_to_all.36 = bf16[8,208,128]{2,1,0:T(8,128)(2,1)S(1)} all-to-all(bf16[8,208,128]{2,1,0:T(8,128)(2,1)S(1)} %bitcast.31), channel_id=1, replica_groups=mesh['lat'=4,'z'=4,'x'=2] {'lat','x'}, dimensions={0} | all-to-all | bytes 851968 | tf_op jit(solution)/shard_map/cond/branch_1_fun/all_to_all | solution.py:557
  45.8 1.1 %gather_own.1.refs_0_ = f32[12,72,128]{2,1,0:T(8,128)S(1)} custom-call(s32[48]{0:T(128)S(1)} %reshape.67.refs_0_, bf16[1664,128]{1,0:T(8,128)(2,1)S(1)} %get-tuple-element.44.refs_1_, bf16[256,768]{1,0:T(8,128)(2,1)S(1)} %copy-done.6, bf16[256,256]{1,0:T(8,128)(2,1)S(1)} %copy-done.7), custom_call_target="tpu_custom_call" | custom-call | flops 1000000000 | bytes 10000000 | tf_op jit(solution)/shard_map/gather_own/pallas_call | solution.py:648
  47.0 2.4 %collective-permute-done.1.refs_2_ = bf16[784,128]{1,0:T(8,128)(2,1)S(1)} collective-permute-done((bf16[784,128]{1,0:T(8,128)(2,1)S(1)}, bf16[784,128]{1,0:T(8,128)(2,1)S(1)}, u32[]{:S(2)}, u32[]{:S(2)}) %collective-permute-start.1) | collective-permute-done | bytes 200736 | tf_op jit(solution)/shard_map/ppermute | solution.py:574
  50.4 3.3 %inner_block.1.refs_1_ = f32[24,40,256]{2,1,0:T(8,128)S(1)} custom-call(bf16[32,48,256]{2,1,0:T(8,128)(2,1)S(1)} %start_tile.1.start_ref, f32[1,256]{1,0:T(1,128)S(1)} %bitcast.25, bf16[256,768]{1,0:T(8,128)(2,1)S(1)} %copy-done.6, bf16[256,256]{1,0:T(8,128)(2,1)S(1)} %copy-done.7), custom_call_target="tpu_custom_call" | custom-call | flops 5000000000 | bytes 10000000 | tf_op jit(solution)/shard_map/inner_block/pallas_call | solution.py:692
  54.3 3.0 %collective-permute-start.6 = (bf16[40,4,256]{2,1,0:T(4,128)(2,1)S(1)}, bf16[40,4,256]{2,1,0:T(4,128)(2,1)S(1)}, u32[]{:S(2)}, u32[]{:S(2)}) collective-permute-start(bf16[40,4,256]{2,1,0:T(4,128)(2,1)S(1)} %get-tuple-element.41), channel_id=1, source_target_pairs={{1,0},{2,1},{3,2},{4,3},{5,4},{6,5},{7,6},{0,7},{9,8},{10,9},{11,1... | collective-permute-start | bytes 245768 | tf_op jit(solution)/shard_map/ppermute | solution.py:545
  57.3 4.7 %tall_block.1 = (bf16[32,32,256]{2,1,0:T(8,128)(2,1)S(1)}, bf16[512,128]{1,0:T(8,128)(2,1)S(1)}, f32[16,40,256]{2,1,0:T(8,128)S(1)}) custom-call(bf16[40,48,256]{2,1,0:T(8,128)(2,1)S(1)} %pad_maximum_fusion.refs_0_, f32[24,40,256]{2,1,0:T(8,128)S(1)} %inner_block.1.refs_1_, f32[1,256]{1,0:T(1,128)S(1)} %bitcast.26, bf16[256,768]{1,0:T(8,128)(2,1)S(1)} %copy-done.6, ...), custom_call_target="tpu_custom_call" | custom-call | flops 5000000000 | bytes 10000000 | tf_op jit(solution)/shard_map/tall_block/pallas_call | solution.py:706
  62.1 2.4 %collective-permute-done.5 = bf16[40,4,256]{2,1,0:T(4,128)(2,1)S(1)} collective-permute-done((bf16[40,4,256]{2,1,0:T(4,128)(2,1)S(1)}, bf16[40,4,256]{2,1,0:T(4,128)(2,1)S(1)}, u32[]{:S(2)}, u32[]{:S(2)}) %collective-permute-start.5) | collective-permute-done | bytes 81952 | tf_op jit(solution)/shard_map/ppermute | solution.py:544
  64.9 3.9 %outer_block.1 = (bf16[32,48,256]{2,1,0:T(8,128)(2,1)}, bf16[768,128]{1,0:T(8,128)(2,1)S(1)}) custom-call(f32[40,56,256]{2,1,0:T(8,128)S(1)} %maximum_convert_fusion.refs_0_, f32[24,40,256]{2,1,0:T(8,128)S(1)} %inner_block.1.refs_1_, bf16[32,32,256]{2,1,0:T(8,128)(2,1)S(1)} %get-tuple-element.34.refs_2_, bf16[512,128]{1,0:T(8,128)(2,1)S(1)} %get-tuple-element.35.refs_3_, ...), custom_call_target="tpu_custom_call" | custom-call | flops 5000000000 | bytes 10000000 | tf_op jit(solution)/shard_map/outer_block/pallas_call | solution.py:721
  69.4 1.5 %collective-permute-start.8 = (bf16[768,128]{1,0:T(8,128)(2,1)S(1)}, bf16[768,128]{1,0:T(8,128)(2,1)S(1)}, u32[]{:S(2)}, u32[]{:S(2)}) collective-permute-start(bf16[768,128]{1,0:T(8,128)(2,1)S(1)} %get-tuple-element.39.refs_1_), channel_id=1, source_target_pairs={{0,4},{2,6},{4,0},{6,2},{1,5},{3,7},{5,1},{7,3},{8,12},{10,14},{12... | collective-permute-start | bytes 589832 | tf_op jit(solution)/shard_map/ppermute | solution.py:574
  70.9 2.2 %collective-permute-start.9 = (bf16[768,128]{1,0:T(8,128)(2,1)S(1)}, bf16[768,128]{1,0:T(8,128)(2,1)S(1)}, u32[]{:S(2)}, u32[]{:S(2)}) collective-permute-start(bf16[768,128]{1,0:T(8,128)(2,1)S(1)} %get-tuple-element.39.refs_1_), channel_id=1, source_target_pairs={{0,6},{2,4},{4,2},{6,0},{1,7},{3,5},{5,3},{7,1},{8,14},{10,12},{12... | collective-permute-start | bytes 589832 | tf_op jit(solution)/shard_map/ppermute | solution.py:574
  73.2 0.7 reply_near.1
  73.9 10.5 %conditional.3 = (bf16[1536,128]{1,0:T(8,128)(2,1)S(1)}) conditional(s32[]{:T(128)} %bitcast.8, bf16[1536,128]{1,0:T(8,128)(2,1)S(1)} %reply_near.1, bf16[1536,128]{1,0:T(8,128)(2,1)S(1)} %reply_near.1), branch_computations={%region_2.3_spmd, %region_3.4_spmd} | conditional | bytes 3145736 | solution.py:569
  73.9 10.5 %all_to_all.39 = bf16[8,192,128]{2,1,0:T(8,128)(2,1)S(1)} all-to-all(bf16[8,192,128]{2,1,0:T(8,128)(2,1)S(1)} %bitcast.33), channel_id=1, replica_groups=mesh['lat'=4,'z'=4,'x'=2] {'lat','x'}, dimensions={0} | all-to-all | bytes 786432 | tf_op jit(solution)/shard_map/cond/branch_1_fun/all_to_all | solution.py:557
  84.4 2.2 %collective-permute-done.8.refs_2_ = bf16[768,128]{1,0:T(8,128)(2,1)S(1)} collective-permute-done((bf16[768,128]{1,0:T(8,128)(2,1)S(1)}, bf16[768,128]{1,0:T(8,128)(2,1)S(1)}, u32[]{:S(2)}, u32[]{:S(2)}) %collective-permute-start.8) | collective-permute-done | bytes 196640 | tf_op jit(solution)/shard_map/ppermute | solution.py:574
  86.6 1.0 reply_far.1
  87.6 19.6 %all_to_all.40 = bf16[8,576,128]{2,1,0:T(8,128)(2,1)S(1)} all-to-all(bf16[8,576,128]{2,1,0:T(8,128)(2,1)S(1)} %bitcast.22), channel_id=1, replica_groups=mesh['lat'=4,'z'=4,'x'=2] {'lat','x'}, dimensions={0} | all-to-all | bytes 2359296 | tf_op jit(solution)/shard_map/all_to_all | solution.py:557
  107.2 3.4 %decode_blocks.1 = bf16[64,12288]{1,0:T(8,128)(2,1)} custom-call(s32[96]{0:T(128)S(1)} %copy-done.3, bf16[2,12288]{1,0:T(2,128)(2,1)S(1)} %copy-done.1, bf16[1536,128]{1,0:T(8,128)(2,1)S(1)} %get-tuple-element.45.near_ref, bf16[4608,128]{1,0:T(8,128)(2,1)S(1)} %bitcast.21), custom_call_target="tpu_custom_call" | custom-call | tf_op jit(solution)/shard_map/decode_blocks/pallas_call | solution.py:758
  (46 shorter events, 3.9 us)
Async XLA Ops:
  5.5 5.2 %copy-start.9 = (f32[256]{0:T(256)S(1)}, f32[256]{0:T(256)}, u32[]{:S(2)}) copy-start(f32[256]{0:T(256)} %param.23) | copy-start | bytes 3076
  5.5 22.6 %all-to-all-start.6 = ((bf16[8,624,128]{2,1,0:T(8,128)(2,1)}), bf16[8,624,128]{2,1,0:T(8,128)(2,1)S(1)}, u32[]{:S(2)}, u32[]{:S(2)}) async-start(bf16[8,624,128]{2,1,0:T(8,128)(2,1)} %bitcast.36), calls=%async_computation.6 | async-start | bytes 2555904 | tf_op jit(solution)/shard_map/all_to_all | solution.py:557
  30.3 16.6 %collective-permute-start = (bf16[784,128]{1,0:T(8,128)(2,1)S(1)}, bf16[784,128]{1,0:T(8,128)(2,1)S(1)}, u32[]{:S(2)}, u32[]{:S(2)}) collective-permute-start(bf16[784,128]{1,0:T(8,128)(2,1)S(1)} %get-tuple-element.28), channel_id=1, source_target_pairs={{0,2},{2,0},{4,6},{6,4},{1,3},{3,1},{5,7},{7,5},{8,10},{10,8},{12,... | collective-permute-start | bytes 602120 | tf_op jit(solution)/shard_map/ppermute | solution.py:574
  32.0 17.4 %collective-permute-start.1 = (bf16[784,128]{1,0:T(8,128)(2,1)S(1)}, bf16[784,128]{1,0:T(8,128)(2,1)S(1)}, u32[]{:S(2)}, u32[]{:S(2)}) collective-permute-start(bf16[784,128]{1,0:T(8,128)(2,1)S(1)} %get-tuple-element.29), channel_id=1, source_target_pairs={{0,4},{2,6},{4,0},{6,2},{1,5},{3,7},{5,1},{7,3},{8,12},{10,14},{12... | collective-permute-start | bytes 602120 | tf_op jit(solution)/shard_map/ppermute | solution.py:574
  34.6 14.8 %collective-permute-start.2 = (bf16[784,128]{1,0:T(8,128)(2,1)S(1)}, bf16[784,128]{1,0:T(8,128)(2,1)S(1)}, u32[]{:S(2)}, u32[]{:S(2)}) collective-permute-start(bf16[784,128]{1,0:T(8,128)(2,1)S(1)} %get-tuple-element.30), channel_id=1, source_target_pairs={{0,6},{2,4},{4,2},{6,0},{1,7},{3,5},{5,3},{7,1},{8,14},{10,12},{12... | collective-permute-start | bytes 602120 | tf_op jit(solution)/shard_map/ppermute | solution.py:574
  34.8 11.0 %copy-start.6 = (bf16[256,768]{1,0:T(8,128)(2,1)S(1)}, bf16[256,768]{1,0:T(8,128)(2,1)}, u32[]{:S(2)}) copy-start(bf16[256,768]{1,0:T(8,128)(2,1)} %refs_6_.3) | copy-start | bytes 1179652
  34.8 11.0 %copy-start.7 = (bf16[256,256]{1,0:T(8,128)(2,1)S(1)}, bf16[256,256]{1,0:T(8,128)(2,1)}, u32[]{:S(2)}) copy-start(bf16[256,256]{1,0:T(8,128)(2,1)} %refs_7_.3) | copy-start | bytes 393220
  45.8 3.6 %copy-start = (bf16[32,48,256]{2,1,0:T(8,128)(2,1)S(1)}, bf16[32,48,256]{2,1,0:T(8,128)(2,1)}, u32[]{:S(2)}) copy-start(bf16[32,48,256]{2,1,0:T(8,128)(2,1)} %refs_5_.1) | copy-start | bytes 2359300
  45.8 3.6 %copy-start.2 = (bf16[64,256]{1,0:T(8,128)(2,1)S(1)}, bf16[64,256]{1,0:T(8,128)(2,1)}, u32[]{:S(2)}) copy-start(bf16[64,256]{1,0:T(8,128)(2,1)} %refs_4_.2) | copy-start | bytes 98308
  49.9 3.9 %collective-permute-start.4 = (bf16[4,48,256]{2,1,0:T(8,128)(2,1)S(1)}, bf16[4,48,256]{2,1,0:T(8,128)(2,1)S(1)}, u32[]{:S(2)}, u32[]{:S(2)}) collective-permute-start(bf16[4,48,256]{2,1,0:T(8,128)(2,1)S(1)} %get-tuple-element.43), channel_id=1, source_target_pairs={{8,0},{16,8},{24,16},{0,24},{9,1},{17,9},{25,17},{1,25},{10,2},{18... | collective-permute-start | bytes 294920 | tf_op jit(solution)/shard_map/ppermute | solution.py:545
  49.9 4.2 %collective-permute-start.3 = (bf16[4,48,256]{2,1,0:T(8,128)(2,1)S(1)}, bf16[4,48,256]{2,1,0:T(8,128)(2,1)S(1)}, u32[]{:S(2)}, u32[]{:S(2)}) collective-permute-start(bf16[4,48,256]{2,1,0:T(8,128)(2,1)S(1)} %get-tuple-element.42), channel_id=1, source_target_pairs={{0,8},{8,16},{16,24},{24,0},{1,9},{9,17},{17,25},{25,1},{2,10},{10... | collective-permute-start | bytes 294920 | tf_op jit(solution)/shard_map/ppermute | solution.py:544
  53.8 3.6 %copy-start.4 = (bf16[256,1024]{1,0:T(8,128)(2,1)S(1)}, bf16[256,1024]{1,0:T(8,128)(2,1)}, u32[]{:S(2)}) copy-start(bf16[256,1024]{1,0:T(8,128)(2,1)} %refs_9_.1) | copy-start | bytes 1572868
  53.8 3.5 %copy-start.5 = (bf16[1024,256]{1,0:T(8,128)(2,1)S(1)}, bf16[1024,256]{1,0:T(8,128)(2,1)}, u32[]{:S(2)}) copy-start(bf16[1024,256]{1,0:T(8,128)(2,1)} %refs_10_.1) | copy-start | bytes 1572868
  53.8 3.5 %copy-start.8 = (bf16[256,64]{0,1:T(8,128)(2,1)S(1)}, bf16[256,64]{0,1:T(8,128)(2,1)}, u32[]{:S(2)}) copy-start(bf16[256,64]{0,1:T(8,128)(2,1)} %param.29) | copy-start | bytes 98308
  53.8 3.5 %copy-start.10 = (f32[256]{0:T(256)S(1)}, f32[256]{0:T(256)}, u32[]{:S(2)}) copy-start(f32[256]{0:T(256)} %param.26) | copy-start | bytes 3076
  54.3 7.7 %collective-permute-start.6 = (bf16[40,4,256]{2,1,0:T(4,128)(2,1)S(1)}, bf16[40,4,256]{2,1,0:T(4,128)(2,1)S(1)}, u32[]{:S(2)}, u32[]{:S(2)}) collective-permute-start(bf16[40,4,256]{2,1,0:T(4,128)(2,1)S(1)} %get-tuple-element.41), channel_id=1, source_target_pairs={{1,0},{2,1},{3,2},{4,3},{5,4},{6,5},{7,6},{0,7},{9,8},{10,9},{11,1... | collective-permute-start | bytes 245768 | tf_op jit(solution)/shard_map/ppermute | solution.py:545
  57.3 7.1 %collective-permute-start.5 = (bf16[40,4,256]{2,1,0:T(4,128)(2,1)S(1)}, bf16[40,4,256]{2,1,0:T(4,128)(2,1)S(1)}, u32[]{:S(2)}, u32[]{:S(2)}) collective-permute-start(bf16[40,4,256]{2,1,0:T(4,128)(2,1)S(1)} %get-tuple-element.40), channel_id=1, source_target_pairs={{0,1},{1,2},{2,3},{3,4},{4,5},{5,6},{6,7},{7,0},{8,9},{9,10},{10,1... | collective-permute-start | bytes 245768 | tf_op jit(solution)/shard_map/ppermute | solution.py:544
  68.8 15.7 %collective-permute-start.7 = (bf16[768,128]{1,0:T(8,128)(2,1)S(1)}, bf16[768,128]{1,0:T(8,128)(2,1)S(1)}, u32[]{:S(2)}, u32[]{:S(2)}) collective-permute-start(bf16[768,128]{1,0:T(8,128)(2,1)S(1)} %get-tuple-element.39.refs_1_), channel_id=1, source_target_pairs={{0,2},{2,0},{4,6},{6,4},{1,3},{3,1},{5,7},{7,5},{8,10},{10,8},{12,... | collective-permute-start | bytes 589832 | tf_op jit(solution)/shard_map/ppermute | solution.py:574
  69.4 17.2 %collective-permute-start.8 = (bf16[768,128]{1,0:T(8,128)(2,1)S(1)}, bf16[768,128]{1,0:T(8,128)(2,1)S(1)}, u32[]{:S(2)}, u32[]{:S(2)}) collective-permute-start(bf16[768,128]{1,0:T(8,128)(2,1)S(1)} %get-tuple-element.39.refs_1_), channel_id=1, source_target_pairs={{0,4},{2,6},{4,0},{6,2},{1,5},{3,7},{5,1},{7,3},{8,12},{10,14},{12... | collective-permute-start | bytes 589832 | tf_op jit(solution)/shard_map/ppermute | solution.py:574
  70.9 15.7 %collective-permute-start.9 = (bf16[768,128]{1,0:T(8,128)(2,1)S(1)}, bf16[768,128]{1,0:T(8,128)(2,1)S(1)}, u32[]{:S(2)}, u32[]{:S(2)}) collective-permute-start(bf16[768,128]{1,0:T(8,128)(2,1)S(1)} %get-tuple-element.39.refs_1_), channel_id=1, source_target_pairs={{0,6},{2,4},{4,2},{6,0},{1,7},{3,5},{5,3},{7,1},{8,14},{10,12},{12... | collective-permute-start | bytes 589832 | tf_op jit(solution)/shard_map/ppermute | solution.py:574
  87.6 19.6 %copy-start.1 = (bf16[2,12288]{1,0:T(2,128)(2,1)S(1)}, bf16[2,12288]{1,0:T(2,128)(2,1)}, u32[]{:S(2)}) copy-start(bf16[2,12288]{1,0:T(2,128)(2,1)} %offset_ref.1) | copy-start | bytes 147460
  87.6 19.6 %copy-start.3 = (s32[96]{0:T(128)S(1)}, s32[96]{0:T(128)}, u32[]{:S(2)}) copy-start(s32[96]{0:T(128)} %get-tuple-element.38.slot_ref) | copy-start | bytes 1156
